TPU v7x, 128 devices: a whole 4x4x4 slice. The times are simulated.
128 devices in a mesh: row: 8 (over y_lo, x), col: 16 (over y_hi, z, core).
Axes of the slice: x: 4, y: 4 (y_hi: 2, y_lo: 2; y = y_hi * 2 + y_lo), z: 4, core: 2. Of those that a mesh axis runs over, the one named last changes fastest.
Arguments:
- pair_tensor: bfloat16 [2048, 2048, 128], P('row', 'col'), may hold values from -6 to 6
- token_single: bfloat16 [2048, 768], P('row'), may hold values from -6 to 6
- atom_single: bfloat16 [16384, 128], P(('row', 'col')), may hold values from -6 to 6
- atom_token: int32 [16384], replicated, may hold values from 0 to 2047, as said below
- chain_index: int32 [2048], replicated, may hold values from 0 to 15, never falling along the last dimension, each value on 1 to 512 neighbouring positions
- pair_up: bfloat16 [128, 512], replicated, may hold values from -0.5 to 0.5
- pair_down: bfloat16 [256, 128], replicated, may hold values from -0.75 to 0.75
- bias_heads: bfloat16 [128, 20], replicated, may hold values from -0.5 to 0.5
- atom_gain: float32 [128], replicated, may hold values from 0.1 to 1.9
- atom_proj: bfloat16 [128, 512], replicated, may hold values from -0.5 to 0.5
- atom_exit: bfloat16 [128, 128], replicated, may hold values from -0.5 to 0.5
- atom_pool: bfloat16 [128, 768], replicated, may hold values from -0.5 to 0.5
- token_gain: float32 [768], replicated, may hold values from 0.1 to 1.9
- token_proj: bfloat16 [768, 3072], replicated, may hold values from -0.21875 to 0.21875
- token_exit: bfloat16 [768, 768], replicated, may hold values from -0.21875 to 0.21875
- chain_bias: float32 [16], replicated, may hold values from -2 to 115
- token_back: bfloat16 [768, 128], replicated, may hold values from -0.21875 to 0.21875
Outputs:
- token_update: bfloat16 [2048, 768], P('row')
- atom_update: bfloat16 [16384, 128], P(('row', 'col'))
Inputs may be any that keep to these rules, and one draw needn't show every extreme that they name: `atom_token`: Non-decreasing. For every r, the atoms r * 8 * 256 to (r + 1) * 8 * 256 - 1 belong to the tokens r * 256 to (r + 1) * 256 - 1, and every token has one atom or more.
All inputs are finite; a program needn't handle non-finite values.
Results may differ from a plain program's by a relative error of at most 0.0085.
Values may be sent and summed in bfloat16 or wider, within the bound.
No kernel may reach another device: no remote copies, remote signals or barrier semaphores. Data moves between devices by JAX's collectives and lax.ppermute only.
A program may use at most 128 MiB of HBM per device.

v0:
```python
import jax
import jax.numpy as jnp
from jax import lax
from jax.sharding import PartitionSpec as P

CZ = 128
CS = 768
CA = 128
HT = 16
HA = 4
PH = 256
QB = 32
KW = 128
EDGE = 48
HDA = 32
HDT = 48
HB = 20


EPS = 1e-05


def with_halo(cells, sides, width):
    for axis, dim in sides:
        count = lax.axis_size(axis)
        ends = count - 1
        head = lax.slice_in_dim(cells, 0, width, axis=dim)
        tail = lax.slice_in_dim(cells, cells.shape[dim] - width, cells.shape[dim], axis=dim)
        cells = jnp.concatenate(
            [
                lax.ppermute(tail, axis, [(i, (i + 1) % count) for i in range(ends)]),
                cells,
                lax.ppermute(head, axis, [((i + 1) % count, i) for i in range(ends)]),
            ],
            axis=dim,
        )
    return cells


def joined(value, axis, join):
    pieces = jax.tree.map(lambda part: lax.all_gather(part, axis), value)
    head = jax.tree.map(lambda part: part[0], pieces)
    tail = jax.tree.map(lambda part: part[1:], pieces)
    total, _ = lax.scan(lambda total, piece: (join(total, piece), None), head, tail)
    return total


def standardize(features):
    features = features.astype(jnp.float32)
    center = features - jnp.mean(features, axis=-1, keepdims=True)
    spread = jnp.mean(center * center, axis=-1, keepdims=True)
    return center * lax.rsqrt(spread + EPS)


def normalize(features, gain_vec):
    return standardize(features) * gain_vec


def merge_parts(earlier, later):
    top_early, sum_early, out_early = earlier
    top_late, sum_late, out_late = later
    row_top = jnp.maximum(top_early, top_late)
    scale_early = jnp.exp(top_early - row_top)
    scale_late = jnp.exp(top_late - row_top)
    head_width = out_early.shape[1] // top_early.shape[0]
    merged_out = out_early * jnp.repeat(scale_early.T, head_width, axis=1) + out_late * jnp.repeat(
        scale_late.T, head_width, axis=1
    )
    return (row_top, sum_early * scale_early + sum_late * scale_late, merged_out)


def local(
    pair_tensor,
    token_single,
    atom_single,
    atom_token,
    chain_index,
    pair_up,
    pair_down,
    bias_heads,
    atom_gain,
    atom_proj,
    atom_exit,
    atom_pool,
    token_gain,
    token_proj,
    token_exit,
    chain_bias,
    token_back,
):
    tok_rows = token_single.shape[0]
    tok_cols = pair_tensor.shape[1]
    atom_rows = atom_single.shape[0]
    row_count = lax.axis_size("row")
    col_count = lax.axis_size("col")
    row_index = lax.axis_index("row")
    col_index = lax.axis_index("col")
    row_start = row_index * tok_rows
    rows_per = tok_rows // 16
    pair_blocks = pair_tensor.reshape(16, rows_per * tok_cols, CZ)

    def pair_step(pair_part):
        normed = standardize(pair_part).astype(jnp.bfloat16)
        mixed_up = jnp.dot(normed, pair_up, preferred_element_type=jnp.float32)
        hidden = (jax.nn.silu(mixed_up[:, :PH]) * mixed_up[:, PH:]).astype(jnp.bfloat16)
        updated = pair_part.astype(jnp.float32) + jnp.dot(
            hidden, pair_down, preferred_element_type=jnp.float32
        )
        normed_two = standardize(updated).astype(jnp.bfloat16)
        return jnp.einsum(
            "nc,ch->hn", normed_two, bias_heads, preferred_element_type=jnp.float32
        ).astype(jnp.bfloat16)

    biases = lax.map(pair_step, pair_blocks).reshape(16, HB, rows_per, tok_cols)
    biases = jnp.transpose(biases, (1, 0, 2, 3)).reshape(HB, tok_rows, tok_cols)
    atom_bias = biases[:HA]
    token_bias = biases[HA:]
    band_bias = lax.all_gather(atom_bias, "col", axis=2, tiled=True)
    atom_normed = normalize(atom_single, atom_gain).astype(jnp.bfloat16)
    atom_projected = jnp.dot(atom_normed, atom_proj, preferred_element_type=jnp.float32)
    queries = atom_projected[:, :CA].astype(jnp.bfloat16)
    keyvals = atom_projected[:, CA : 3 * CA].astype(jnp.bfloat16)
    atom_gate = atom_projected[:, 3 * CA :]
    extended = with_halo(keyvals, ((("row", "col"), 0),), EDGE)
    nblocks = atom_rows // QB
    windows = jnp.stack(
        [
            lax.slice_in_dim(extended, QB * block_id, QB * block_id + KW, axis=0)
            for block_id in range(nblocks)
        ]
    )
    total_atoms = atom_rows * col_count * row_count
    atom_base = (row_index * col_count + col_index) * atom_rows
    positions = (
        atom_base
        + QB * jnp.arange(nblocks, dtype=jnp.int32)[:, None]
        - EDGE
        + jnp.arange(KW, dtype=jnp.int32)[None, :]
    )
    in_range = (positions >= 0) & (positions < total_atoms)
    key_tokens = atom_token[jnp.clip(positions, 0, total_atoms - 1)]
    query_tokens = lax.dynamic_slice_in_dim(atom_token, atom_base, atom_rows).reshape(nblocks, QB)
    q_first = jnp.clip(query_tokens[:, 0] - row_start, 0, band_bias.shape[1] - QB)
    k_first = jnp.clip(key_tokens[:, 0], 0, band_bias.shape[2] - KW)

    def tile_at(q_at, k_at):
        return lax.dynamic_slice(band_bias, (jnp.int32(0), q_at, k_at), (HA, QB, KW))

    tile_stack = jax.vmap(tile_at)(q_first, k_first)
    q_onehot = (
        (query_tokens - row_start - q_first[:, None])[:, :, None]
        == jnp.arange(QB, dtype=jnp.int32)[None, None, :]
    ).astype(jnp.bfloat16)
    k_onehot = (
        (key_tokens - k_first[:, None])[:, :, None]
        == jnp.arange(KW, dtype=jnp.int32)[None, None, :]
    ).astype(jnp.bfloat16)
    rows_sel = jnp.einsum(
        "bia,bhac->bhic", q_onehot, tile_stack, preferred_element_type=jnp.float32
    ).astype(jnp.bfloat16)
    bias_tile = jnp.einsum("bhic,bjc->bhij", rows_sel, k_onehot, preferred_element_type=jnp.float32)
    query_heads = queries.reshape(nblocks, QB, HA, CA // HA)
    keys_win = windows[:, :, :CA].reshape(nblocks, KW, HA, CA // HA)
    vals_win = windows[:, :, CA:].reshape(nblocks, KW, HA, CA // HA)
    scores = (
        jnp.einsum("bihd,bjhd->bhij", query_heads, keys_win, preferred_element_type=jnp.float32)
        * HDA ** (-0.5)
        + bias_tile
    )
    scores = jnp.where(in_range[:, None, None, :], scores, -1e30)
    row_top = jnp.max(scores, axis=-1, keepdims=True)
    weights_full = jnp.exp(scores - row_top)
    denominator = jnp.sum(weights_full, axis=-1)
    attended = jnp.einsum(
        "bhij,bjhd->bihd",
        weights_full.astype(jnp.bfloat16),
        vals_win,
        preferred_element_type=jnp.float32,
    )
    attended = (attended / jnp.transpose(denominator, (0, 2, 1))[..., None]).reshape(atom_rows, CA)
    atom_gated = (attended * jax.nn.sigmoid(atom_gate)).astype(jnp.bfloat16)
    atom_mid = (
        atom_single.astype(jnp.float32)
        + jnp.dot(atom_gated, atom_exit, preferred_element_type=jnp.float32)
    ).astype(jnp.bfloat16)
    atom_pooled = jax.nn.relu(
        jnp.dot(atom_mid, atom_pool, preferred_element_type=jnp.float32)
    ).astype(jnp.bfloat16)
    local_tok = query_tokens.reshape(atom_rows) - row_start
    onehot = (local_tok[:, None] == jnp.arange(tok_rows, dtype=jnp.int32)[None, :]).astype(
        jnp.bfloat16
    )
    partial_value = jnp.einsum("at,ac->tc", onehot, atom_pooled, preferred_element_type=jnp.float32)
    row_atoms = lax.dynamic_slice_in_dim(
        atom_token, row_index * atom_rows * col_count, atom_rows * col_count
    )
    counts = jnp.sum(
        (row_atoms[None, :] - row_start == jnp.arange(tok_rows, dtype=jnp.int32)[:, None]).astype(
            jnp.float32
        ),
        axis=1,
    )
    summed = lax.psum(partial_value, "col")
    token_mid = (token_single.astype(jnp.float32) + summed / counts[:, None]).astype(jnp.bfloat16)
    token_normed = normalize(token_mid, token_gain).astype(jnp.bfloat16)
    row_proj = jnp.dot(token_normed, token_proj[:, : 2 * CS], preferred_element_type=jnp.float32)
    row_query = row_proj[:, :CS].astype(jnp.bfloat16)
    token_gate = row_proj[:, CS:]
    every_token = lax.all_gather(token_normed, "row", axis=0, tiled=True)
    col_tokens = lax.dynamic_slice_in_dim(every_token, col_index * tok_cols, tok_cols)
    col_proj = jnp.dot(
        col_tokens, token_proj[:, 2 * CS :], preferred_element_type=jnp.float32
    ).astype(jnp.bfloat16)
    col_keys = col_proj[:, :CS].reshape(tok_cols, HT, HDT)
    col_values = col_proj[:, CS:].reshape(tok_cols, HT, HDT)
    row_chain = lax.dynamic_slice_in_dim(chain_index, row_start, tok_rows)
    col_chain = lax.dynamic_slice_in_dim(chain_index, col_index * tok_cols, tok_cols)
    same_chain = (row_chain[:, None] == col_chain[None, :]).astype(jnp.float32)
    token_scores = (
        jnp.einsum(
            "ihd,jhd->hij",
            row_query.reshape(tok_rows, HT, HDT),
            col_keys,
            preferred_element_type=jnp.float32,
        )
        * HDT ** (-0.5)
        + token_bias.astype(jnp.float32)
        + chain_bias[:, None, None] * same_chain[None]
    )
    local_top = jnp.max(token_scores, axis=-1)
    local_exp = jnp.exp(token_scores - local_top[:, :, None])
    local_sum = jnp.sum(local_exp, axis=-1)
    local_out = jnp.einsum(
        "hij,jhd->ihd",
        local_exp.astype(jnp.bfloat16),
        col_values,
        preferred_element_type=jnp.float32,
    ).reshape(tok_rows, CS)
    merged_top, merged_sum, merged_out = joined(
        (local_top, local_sum, local_out), "col", merge_parts
    )
    token_attended = merged_out / jnp.repeat(merged_sum.T, HDT, axis=1)
    token_gated = (token_attended * jax.nn.sigmoid(token_gate)).astype(jnp.bfloat16)
    token_update = (
        token_mid.astype(jnp.float32)
        + jnp.dot(token_gated, token_exit, preferred_element_type=jnp.float32)
    ).astype(jnp.bfloat16)
    token_sent = jnp.dot(token_update, token_back, preferred_element_type=jnp.float32).astype(
        jnp.bfloat16
    )
    atom_added = jnp.dot(onehot, token_sent, preferred_element_type=jnp.float32)
    atom_update = (atom_mid.astype(jnp.float32) + atom_added).astype(jnp.bfloat16)
    return (token_update, atom_update)


def solution(mesh):
    placed = (
        P("row", "col", None),
        P("row", None),
        P(("row", "col"), None),
        P(),
        P(),
        P(),
        P(),
        P(),
        P(),
        P(),
        P(),
        P(),
        P(),
        P(),
        P(),
        P(),
        P(),
    )
    return jax.shard_map(
        local,
        mesh=mesh,
        in_specs=placed,
        out_specs=(P("row", None), P(("row", "col"), None)),
        check_vma=False,
    )
```

profile of v0, /device:TPU:1, one launch (start us, length us, event | category | flops | bytes accessed | tf_op | source)
XLA Modules:
  0.0 551.2 jit_solution(14883822240512350784)
XLA Ops:
  7.2 69.6 %while.25 = (s32[]{:T(128)}, bf16[16,20,2048]{2,1,0:T(8,128)(2,1)}, bf16[16,2048,128]{2,1,0:T(8,128)(2,1)}, bf16[128,512]{1,0:T(8,128)(2,1)}, bf16[256,128]{1,0:...) while((s32[]{:T(128)}, bf16[16,20,2048]{2,1,0:T(8,128)(2,1)}, bf16[16,2048,128]{2,1,0:T(8,128)(2,1)}, ...), condition=%wide.region_7.8_spmd, body=%wide.region_2.7_spmd.sunk | while | flops 421310464 | bytes 16983216 | solution.py:114
  7.3 1.2 constant_dynamic-slice_fusion.6
  76.8 3.5 reshape.301
  80.3 1.7 copy.87
  84.1 4.9 collective-permute-start
  89.1 1.9 collective-permute-start.1
  91.3 3.1 gather_fusion
  96.3 47.3 %all-gather.6.cloned.1.call-done = bf16[4,256,2048]{2,1,0:T(8,128)(2,1)} async-done(((bf16[4,256,128]{2,1,0:T(8,128)(2,1)}), bf16[4,256,2048]{2,1,0:T(8,128)(2,1)}) %all-gather.6.cloned.1.call-update) | async-done | bytes 4194320 | tf_op jit(solution)/shard_map/all_gather | solution.py:118
  143.6 11.5 %while.27 = (s32[]{:T(128)}, bf16[4,256,2048]{2,1,0:T(8,128)(2,1)}, s32[4,3]{1,0:T(4,128)S(1)}, bf16[4,4,32,128]{3,2,1,0:T(8,128)(2,1)S(1)}, s32[]{:T(128)}) while((s32[]{:T(128)}, bf16[4,256,2048]{2,1,0:T(8,128)(2,1)}, s32[4,3]{1,0:T(4,128)S(1)}, bf16[4,4,32,128]{3,2,1,0:T(8,128)(2,1)S(1)}, s32[]{:T(128)}) %tuple.82), condition=%wide.while_cond, body=%wide.while_body.sunk | while | flops 2 | bytes 65661 | solution.py:147
  144.2 2.2 bitcast_dynamic-update-slice_fusion.2
  147.1 2.2 bitcast_dynamic-update-slice_fusion.2
  150.0 2.2 bitcast_dynamic-update-slice_fusion.2
  152.8 2.2 bitcast_dynamic-update-slice_fusion.2
  155.8 1.9 fusion.29
  160.1 2.2 fusion.30
  162.7 136.7 %all-reduce.2.cloned.1.call-done = f32[256,768]{1,0:T(8,128)} async-done(((f32[256,768]{1,0:T(8,128)}), f32[256,768]{1,0:T(8,128)}) %all-reduce.2.cloned.1.call-update) | async-done | bytes 786448 | tf_op jit(solution)/shard_map/psum | solution.py:203
  299.4 1.4 convert_reduce_fusion.2
  305.3 1.4 bitcast_convert_fusion
  306.7 1.8 copy.70
  309.3 2.6 fusion.22
  311.9 1.2 copy-done.15
  314.1 31.1 %all-gather.8.cloned.1.call-done = bf16[2048,768]{1,0:T(8,128)(2,1)} async-done(((bf16[256,768]{1,0:T(8,128)(2,1)}), bf16[2048,768]{1,0:T(8,128)(2,1)}) %all-gather.8.cloned.1.call-update) | async-done | bytes 3145744 | tf_op jit(solution)/shard_map/all_gather | solution.py:209
  345.2 2.3 convolution_convert_fusion.1
  348.5 2.5 fusion.108
  351.0 1.4 fusion.34
  352.4 2.4 copy.73
  354.8 28.6 %all-gather = f32[256,256]{1,0:T(8,128)S(1)} all-gather(f32[16,256]{1,0:T(8,128)S(1)} %get-tuple-element.181), channel_id=2, replica_groups=mesh['row'=8,'col'=16] {'col'}, dimensions={0}, use_global_device_ids=true | all-gather | bytes 278528 | tf_op jit(solution)/shard_map/all_gather | solution.py:41
  385.1 20.3 %all-gather.1 = f32[256,256]{1,0:T(8,128)S(1)} all-gather(f32[16,256]{1,0:T(8,128)S(1)} %fusion.25), channel_id=3, replica_groups=mesh['row'=8,'col'=16] {'col'}, dimensions={0}, use_global_device_ids=true | all-gather | bytes 278528 | tf_op jit(solution)/shard_map/all_gather | solution.py:41
  406.7 42.6 %all-gather.10.cloned.1.call-done = f32[16,256,768]{2,1,0:T(8,128)} async-done(((f32[1,256,768]{2,1,0:T(8,128)}), f32[16,256,768]{2,1,0:T(8,128)}) %all-gather.10.cloned.1.call-update) | async-done | bytes 12582928 | tf_op jit(solution)/shard_map/all_gather | solution.py:41
  450.8 9.7 %slice.172 = f32[15,256,768]{2,1,0:T(8,128)} slice(f32[16,256,768]{2,1,0:T(8,128)} %all-gather.10.cloned.1.call-done), slice={[1:16], [0:256], [0:768]} | slice | bytes 23592960 | tf_op jit(solution)/shard_map/slice | solution.py:43
  460.5 78.7 %while.26 = (s32[]{:T(128)}, f32[16,256]{1,0:T(8,128)S(1)}, f32[16,256]{1,0:T(8,128)}, f32[256,768]{0,1:T(8,128)S(1)}, f32[15,16,256]{2,1,0:T(8,128)}, /*index=5...) while((s32[]{:T(128)}, f32[16,256]{1,0:T(8,128)S(1)}, f32[16,256]{1,0:T(8,128)}, ...), condition=%wide.region_17.18_spmd, body=%wide.region_16.17_spmd.sunk | while | flops 618498 | bytes 5750889 | solution.py:44
  460.5 1.3 fusion.146
  461.8 1.4 fusion.147
  465.7 1.3 fusion.146
  467.1 1.4 fusion.147
  471.0 1.3 fusion.146
  472.3 1.4 fusion.147
  476.2 1.3 fusion.146
  477.5 1.4 fusion.147
  478.9 1.2 constant_dynamic-slice_fusion.7
  481.5 1.3 fusion.146
  482.8 1.4 fusion.147
  484.2 1.2 constant_dynamic-slice_fusion.7
  486.7 1.3 fusion.146
  488.0 1.4 fusion.147
  492.0 1.3 fusion.146
  493.3 1.4 fusion.147
  497.2 1.3 fusion.146
  498.5 1.4 fusion.147
  502.4 1.3 fusion.146
  503.8 1.4 fusion.147
  507.7 1.3 fusion.146
  509.0 1.4 fusion.147
  512.9 1.3 fusion.146
  514.3 1.4 fusion.147
  518.2 1.3 fusion.146
  519.5 1.4 fusion.147
  523.4 1.3 fusion.146
  524.8 1.4 fusion.147
  528.7 1.3 fusion.146
  530.0 1.4 fusion.147
  533.9 1.3 fusion.146
  535.2 1.4 fusion.147
  541.5 2.1 fusion.26
  (462 shorter events, 127.1 us)
Async XLA Ops:
  7.2 534.3 %copy-start = (bf16[768,768]{1,0:T(8,128)(2,1)S(1)}, bf16[768,768]{1,0:T(8,128)(2,1)}, u32[]{:S(2)}) copy-start(bf16[768,768]{1,0:T(8,128)(2,1)} %param.35) | copy-start | bytes 3538948
  7.2 136.4 %all-gather.6.cloned.1.call-start = ((), (), s32[]{:S(2)}) async-start(), calls=%async_computation | async-start | bytes 4456448 | tf_op jit(solution)/shard_map/all_gather | solution.py:118
  7.2 1.7 copy-start.4
  9.0 0.8 copy-start.21
  9.8 1.0 copy-start.11
  11.7 1.6 copy-start.4
  14.1 1.0 copy-start.11
  16.0 1.6 copy-start.4
  18.5 1.0 copy-start.11
  20.4 1.6 copy-start.4
  22.0 0.8 copy-start.21
  22.8 1.0 copy-start.11
  24.7 1.6 copy-start.4
  26.3 0.8 copy-start.21
  27.2 1.0 copy-start.11
  29.1 1.6 copy-start.4
  30.7 0.8 copy-start.21
  31.5 1.0 copy-start.11
  33.4 1.6 copy-start.4
  35.9 1.0 copy-start.11
  37.7 1.6 copy-start.4
  39.4 0.8 copy-start.21
  40.2 1.0 copy-start.11
  42.1 1.6 copy-start.4
  44.6 1.0 copy-start.11
  46.4 1.6 copy-start.4
  48.1 0.8 copy-start.21
  48.9 1.0 copy-start.11
  50.8 1.6 copy-start.4
  53.2 1.0 copy-start.11
  55.1 1.6 copy-start.4
  56.7 0.8 copy-start.21
  57.6 1.0 copy-start.11
  59.4 1.6 copy-start.4
  61.9 1.0 copy-start.11
  63.8 1.6 copy-start.4
  66.3 1.0 copy-start.11
  68.1 1.6 copy-start.4
  70.6 1.0 copy-start.11
  72.5 1.6 copy-start.4
  74.9 1.0 copy-start.11
  80.3 2.5 copy-start.8
  80.3 2.9 copy-start.12
  80.3 2.9 copy-start.19
  80.3 10.7 %copy-start.1 = (s32[16384]{0:T(1024)S(1)}, s32[16384]{0:T(1024)}, u32[]{:S(2)}) copy-start(s32[16384]{0:T(1024)} %param.24) | copy-start | bytes 196612
  82.8 216.5 %all-reduce.2.cloned.1.call-start = ((), (), s32[]{:S(2)}) async-start(), calls=%async_computation.1 | async-start | bytes 1572864 | tf_op jit(solution)/shard_map/psum | solution.py:203
  84.1 10.9 %collective-permute-start = (bf16[48,256]{1,0:T(8,128)(2,1)S(1)}, bf16[48,256]{1,0:T(8,128)(2,1)S(1)}, u32[]{:S(2)}, u32[]{:S(2)}) collective-permute-start(bf16[48,256]{1,0:T(8,128)(2,1)S(1)} %get-tuple-element.165), channel_id=1, source_target_pairs={{0,1},{1,2},{2,3},{3,4},{4,5},{5,6},{6,7},{7,8},{8,9},{9,10},{10,1... | collective-permute-start | bytes 73736 | tf_op jit(solution)/shard_map/ppermute | solution.py:31
  89.1 6.0 %collective-permute-start.1 = (bf16[48,256]{1,0:T(8,128)(2,1)S(1)}, bf16[48,256]{1,0:T(8,128)(2,1)S(1)}, u32[]{:S(2)}, u32[]{:S(2)}) collective-permute-start(bf16[48,256]{1,0:T(8,128)(2,1)S(1)} %get-tuple-element.166), channel_id=1, source_target_pairs={{1,0},{2,1},{3,2},{4,3},{5,4},{6,5},{7,6},{8,7},{9,8},{10,9},{11,1... | collective-permute-start | bytes 73736 | tf_op jit(solution)/shard_map/ppermute | solution.py:33
  91.1 69.0 %copy-start.16 = (s32[128]{0:T(128)}, s32[128]{0:T(128)S(1)}, u32[]{:S(2)}) copy-start(s32[128]{0:T(128)S(1)} %get-tuple-element.153) | copy-start | bytes 1540
  95.3 63.7 %copy-start.22 = (bf16[128,128]{1,0:T(8,128)(2,1)S(1)}, bf16[128,128]{1,0:T(8,128)(2,1)}, u32[]{:S(2)}) copy-start(bf16[128,128]{1,0:T(8,128)(2,1)} %param.31) | copy-start | bytes 98308
  155.8 143.5 %copy-start.7 = (bf16[256,768]{1,0:T(8,128)(2,1)S(1)}, bf16[256,768]{1,0:T(8,128)(2,1)}, u32[]{:S(2)}) copy-start(bf16[256,768]{1,0:T(8,128)(2,1)} %param.22) | copy-start | bytes 1179652
  159.0 142.5 %copy-start.18 = (f32[768]{0:T(1024)S(1)}, f32[768]{0:T(1024)}, u32[]{:S(2)}) copy-start(f32[768]{0:T(1024)} %param.33) | copy-start | bytes 9220
  160.0 142.5 %copy-start.13 = (bf16[128,128]{1,0:T(8,128)(2,1)}, bf16[128,128]{1,0:T(8,128)(2,1)S(1)}, u32[]{:S(2)}) copy-start(bf16[128,128]{1,0:T(8,128)(2,1)S(1)} %fusion.32) | copy-start | bytes 98308
  162.3 182.9 %all-gather.8.cloned.1.call-start = ((), (), s32[]{:S(2)}) async-start(), calls=%async_computation.2 | async-start | bytes 3538944 | tf_op jit(solution)/shard_map/all_gather | solution.py:209
  302.5 146.8 %all-gather.10.cloned.1.call-start = ((), (), s32[]{:S(2)}) async-start(), calls=%async_computation.3 | async-start | bytes 13369344 | tf_op jit(solution)/shard_map/all_gather | solution.py:41
  311.9 1.2 copy-start.15
  314.1 34.4 %copy-start.20 = (f32[16]{0:T(128)S(1)}, f32[16]{0:T(128)}, u32[]{:S(2)}) copy-start(f32[16]{0:T(128)} %param.36) | copy-start | bytes 196
  348.5 2.5 copy-start.5
  351.0 3.8 copy-start.9
  539.1 2.3 copy-start.3
  541.4 2.1 copy-start.10
  541.5 2.1 copy-start.14
  541.5 2.1 copy-start.17
  543.6 1.0 copy-start.6
  (10 other events, 8.3 us)
Sparse Core Ops, SparseCore 0:
  82.9 60.6 all-gather.5
  162.5 136.8 all-reduce.1
  302.7 42.5 all-gather.7
  354.9 94.3 all-gather.9
where the time goes:
time: 558 us; the launch traced here: 551 us
  waiting for transfers between devices  258 us (46%)
  local copies, waits for them, and re-layouts  93.6 us (17%)
  other arithmetic  70.2 us (13%)
  matrix products  57.5 us (10%)
  blocking collectives  48.9 us (9%)
  between operations  14.3 us (3%)
  starting transfers between devices  7.01 us (1%)
    psum x1, waiting for transfers between devices, local(): summed = lax.psum(partial_value, 'col')  137 us
    all_gather x2, blocking collectives, joined(): pieces = jax.tree.map(lambda part: lax.all_gather(part, axis), value)  48.9 us
    all_gather x1, waiting for transfers between devices, local(): band_bias = lax.all_gather(atom_bias, 'col', axis=2, tiled=True)  47.3 us
    all_gather x1, waiting for transfers between devices, joined(): pieces = jax.tree.map(lambda part: lax.all_gather(part, axis), value)  42.6 us
    transpose x30, other arithmetic, merge_parts(): merged_out = out_early * jnp.repeat(scale_early.T, head_width, axis=1) +...  40.7 us
    all_gather x1, waiting for transfers between devices, local(): every_token = lax.all_gather(token_normed, 'row', axis=0, tiled=True)  31.1 us
    dynamic_slice x30, local copies, waits for them, and re-layouts, joined(): lax.scan(lambda total, piece: (join(total, piece), None), head, tail)  21.7 us
    dynamic_slice x32, local copies, waits for them, and re-layouts, local(): biases = lax.map(pair_step, pair_blocks).reshape(16, HB, rows_per, tok_cols)  21.3 us
  transfers between devices with their start and end apart: 6, of which 4 were waited for; matrix products, arithmetic and copies ran while one was open for 4% of the time, Pallas kernels for 0%

commit v1 on v0

v1 whole, which is shorter than its diff:
```python
import functools

import jax
import jax.numpy as jnp
from jax import lax
from jax.experimental import pallas as pl
from jax.experimental.pallas import tpu as pltpu
from jax.sharding import PartitionSpec as P

CZ = 128
CS = 768
CA = 128
HT = 16
HA = 4
PH = 256
QB = 32
KW = 128
HDA = 32
HDT = 48
HB = 20
HALO = 64
CHUNK = 64
GROUP = 256
EPS = 1e-05

bf16 = jnp.bfloat16
f32 = jnp.float32


def dot(left, right):
    return jnp.dot(left, right, preferred_element_type=f32)


def dot_nt(left, right):
    return lax.dot_general(left, right, (((1,), (1,)), ((), ())), preferred_element_type=f32)


def dot_tn(left, right):
    return lax.dot_general(left, right, (((0,), (0,)), ((), ())), preferred_element_type=f32)


def centered(features):
    return features - jnp.mean(features, axis=-1, keepdims=True)


def scaled(center):
    spread = jnp.mean(center * center, axis=-1, keepdims=True)
    return center * lax.rsqrt(spread + EPS)


def sigmoid(value):
    return 0.5 + 0.5 * jnp.tanh(0.5 * value)


VMEM = pl.BlockSpec(memory_space=pltpu.VMEM)
SMEM = pl.BlockSpec(memory_space=pltpu.SMEM)


def pair_body(place, pair_ref, up_ref, down_ref, heads_ref, center_ref, *refs):
    refs = refs[-3:] if len(refs) in (3, 5) else refs[-2:]
    pair_part = pair_ref[...].reshape(-1, CZ)
    normed = scaled(dot(pair_part, center_ref[...])).astype(bf16)
    mixed = dot(normed, up_ref[...])
    gate, value = mixed[:, :PH], mixed[:, PH:]
    hidden = ((gate + gate * jnp.tanh(gate)) * value).astype(bf16)
    updated = pair_part.astype(f32) + dot(hidden, down_ref[...])
    normed_two = scaled(centered(updated)).astype(bf16)
    biases = dot_nt(heads_ref[...], normed_two)
    rows = pair_ref.shape[0]
    stacked = jnp.stack([biases[:, i * CZ : (i + 1) * CZ] for i in range(rows)], axis=0)
    stacked = jnp.swapaxes(stacked, 0, 1).astype(bf16)
    refs[0][...] = stacked[:HA]
    refs[1][...] = stacked[HA:HB]
    if len(refs) == 3:
        refs[2][...] = stacked[:HA]


def pair_chunks(place, pair, weights, before, count, where):
    rows, cols = pair.shape[:2]
    whole = lambda array: pl.BlockSpec(array.shape, lambda i, place: (0,) * array.ndim)
    out_shape = [
        jax.ShapeDtypeStruct((HA, rows, cols), bf16),
        jax.ShapeDtypeStruct((HT, rows, cols), bf16),
    ]
    out_specs = [
        pl.BlockSpec((HA, CHUNK, cols), lambda i, place: (0, where(i, place), 0)),
        pl.BlockSpec((HT, CHUNK, cols), lambda i, place: (0, where(i, place), 0)),
    ]
    in_specs = [pl.BlockSpec((CHUNK, cols, CZ), lambda i, place: (where(i, place), 0, 0))]
    in_specs += [whole(array) for array in weights]
    aliases = {}
    if before:
        aliases = {2 + len(weights): 0, 3 + len(weights): 1}
        in_specs += [pl.BlockSpec(memory_space=pl.ANY)] * 2
    else:
        out_shape.append(jax.ShapeDtypeStruct((HA, CHUNK, cols), bf16))
        out_specs.append(pl.BlockSpec((HA, CHUNK, cols), lambda i, place: (0, 0, 0)))
    cells = count * CHUNK * cols
    return pl.pallas_call(
        pair_body,
        grid_spec=pltpu.PrefetchScalarGridSpec(
            num_scalar_prefetch=1, grid=(count,), in_specs=in_specs, out_specs=out_specs
        ),
        out_shape=out_shape,
        input_output_aliases=aliases,
        compiler_params=pltpu.CompilerParams(vmem_limit_bytes=56 * 2**20),
        cost_estimate=pl.CostEstimate(
            flops=cells * 250000, bytes_accessed=cells * 300, transcendentals=cells * PH
        ),
        name="pair",
    )(place, pair, *weights, *before)


def project_body(ext_ref, gain_ref, proj_ref, query_ref, key_ref, value_ref, gate_ref):
    ext = ext_ref[...].astype(f32)
    normed = (scaled(centered(ext)) * gain_ref[...]).astype(bf16)
    atoms = query_ref.shape[0]
    own = normed[HALO : HALO + atoms]
    query_ref[...] = (dot(own, proj_ref[:, :CA]) * HDA ** (-0.5)).astype(bf16)
    key_ref[...] = dot(normed, proj_ref[:, CA : 2 * CA]).astype(bf16)
    value_ref[...] = dot(normed, proj_ref[:, 2 * CA : 3 * CA]).astype(bf16)
    gate_ref[...] = sigmoid(dot(own, proj_ref[:, 3 * CA :]))


def project_atoms(ext, gain, proj):
    total = ext.shape[0]
    atoms = total - 2 * HALO
    return pl.pallas_call(
        project_body,
        in_specs=[VMEM] * 3,
        out_specs=[VMEM] * 4,
        out_shape=[
            jax.ShapeDtypeStruct((atoms, CA), bf16),
            jax.ShapeDtypeStruct((total, CA), bf16),
            jax.ShapeDtypeStruct((total, CA), bf16),
            jax.ShapeDtypeStruct((atoms, CA), f32),
        ],
        compiler_params=pltpu.CompilerParams(vmem_limit_bytes=48 * 2**20),
        cost_estimate=pl.CostEstimate(flops=10**9, bytes_accessed=2**22, transcendentals=2**18),
        name="atom_projections",
    )(ext, gain, proj)


def atoms_body(
    place,
    half_ref,
    other_ref,
    query_ref,
    key_ref,
    value_ref,
    gate_ref,
    ext_ref,
    tokens_ref,
    exit_ref,
    pool_ref,
    single_ref,
    gain_ref,
    tproj_ref,
    mid_ref,
    tmid_ref,
    tquery_ref,
    tgate_ref,
    tkv_ref,
    bias_ref,
    look_ref,
    sums_ref,
):
    row, col, row_count = place[0], place[1], place[2]
    total = ext_ref.shape[0]
    atoms = query_ref.shape[0]
    rows = single_ref.shape[0]
    even = lax.rem(col, 2) == 0
    for h in range(HA):
        mine, theirs = half_ref[h], other_ref[h]
        first = jnp.where(even, mine, theirs)
        second = jnp.where(even, theirs, mine)
        base = h * 3 * KW
        bias_ref[:, base : base + KW] = first[:rows]
        bias_ref[:, base + KW : base + 2 * KW] = second[:rows]
        bias_ref[:, base + 2 * KW : base + 3 * KW] = jnp.concatenate(
            [first[rows:], jnp.zeros((rows - 2 * HALO, KW), bf16), second[rows:]], axis=0
        )
    lane = lax.broadcasted_iota(jnp.int32, (KW, 3 * KW), 1)
    for t in range(total // KW):
        at = slice(t * KW, (t + 1) * KW)
        tokens = jnp.broadcast_to(tokens_ref[:, at], (KW, KW)).astype(f32).T.astype(jnp.int32)
        tokens = jnp.concatenate([tokens] * 3, axis=1)
        tokens = jnp.where(tokens < 0, tokens + 3 * KW, tokens)
        look_ref[at, :CA] = key_ref[at, :]
        look_ref[at, CA:] = (tokens == lane).astype(f32).astype(bf16)
    head_of = lax.broadcasted_iota(jnp.int32, (QB, CA), 1) // HDA
    sums_ref[...] = jnp.zeros_like(sums_ref)
    row_lane = lax.broadcasted_iota(jnp.int32, (1, KW), 1)

    def group(g, counts):
        start = pl.multiple_of(g * GROUP, GROUP)
        own = pl.ds(start, GROUP)
        onehot = look_ref[pl.ds(pl.multiple_of(start + HALO, HALO), GROUP), CA : CA + 2 * KW]
        picked = dot(onehot, bias_ref[...]).astype(bf16)
        queries = query_ref[own, :]
        scores = []
        for b in range(GROUP // QB):
            part = slice(b * QB, (b + 1) * QB)
            left = jnp.concatenate(
                [
                    jnp.concatenate(
                        [
                            jnp.where(head_of == h, queries[part].astype(f32), 0.0).astype(bf16),
                            picked[part, h * 3 * KW : (h + 1) * 3 * KW],
                        ],
                        axis=1,
                    )
                    for h in range(HA)
                ],
                axis=0,
            )
            first = start + b * QB + HALO - (KW - QB) // 2
            window = look_ref[pl.ds(pl.multiple_of(first, 16), KW), :]
            at = row_lane + first
            inside = ((at >= HALO) | (row > 0)) & ((at < total - HALO) | (row < row_count - 1))
            scores.append(dot_nt(left, window) + jnp.where(inside, 0.0, -1e30))
        scores = jnp.concatenate(scores, axis=0)
        exps = jnp.exp(scores - jnp.max(scores, axis=-1, keepdims=True))
        inverse = 1.0 / jnp.sum(exps, axis=-1, keepdims=True)
        weights = exps.astype(bf16)
        attended = []
        for b in range(GROUP // QB):
            first = start + b * QB + HALO - (KW - QB) // 2
            part = slice(b * HA * QB, (b + 1) * HA * QB)
            out = dot(weights[part], value_ref[pl.ds(pl.multiple_of(first, 16), KW), :])
            out = out * inverse[part]
            merged = out[:QB]
            for h in range(1, HA):
                merged = jnp.where(head_of == h, out[h * QB : (h + 1) * QB], merged)
            attended.append(merged)
        attended = jnp.concatenate(attended, axis=0)
        gated = (attended * gate_ref[own, :]).astype(bf16)
        single = ext_ref[pl.ds(pl.multiple_of(start + HALO, HALO), GROUP), :].astype(f32)
        mid = (single + dot(gated, exit_ref[...])).astype(bf16)
        mid_ref[own, :] = mid
        pooled = jnp.maximum(dot(mid, pool_ref[...]), 0.0).astype(bf16)
        sums_ref[...] += dot_tn(onehot, pooled)
        return counts + jnp.sum(onehot.astype(f32).T, axis=1, keepdims=True)

    counts = lax.fori_loop(0, atoms // GROUP, group, jnp.zeros((rows, 1), f32))
    token_mid = (single_ref[...].astype(f32) + sums_ref[...] / counts).astype(bf16)
    tmid_ref[...] = token_mid
    normed = (scaled(centered(token_mid.astype(f32))) * gain_ref[...]).astype(bf16)

    def head_part(part):
        start = part * CS + col * HDT
        base = jnp.minimum(start // KW * KW, 4 * CS - 2 * KW)
        base = pl.multiple_of(base, KW)
        wide = dot(normed, tproj_ref[:, pl.ds(base, 2 * KW)])
        return pltpu.roll(wide, lax.rem(2 * KW - (start - base), 2 * KW), 1)[:, :KW]

    tquery_ref[...] = head_part(0)[:, :HDT].astype(bf16)
    tgate_ref[...] = sigmoid(head_part(1)[:, :HDT])
    tkv_ref[:HDT, :] = head_part(2).T[:HDT].astype(bf16)
    tkv_ref[HDT:, :] = head_part(3).T[:HDT].astype(bf16)


def atom_attention(place, half, other, parts, ext, tokens, exit_w, pool, single, gain, tproj):
    total = ext.shape[0]
    atoms = total - 2 * HALO
    rows = single.shape[0]
    return pl.pallas_call(
        atoms_body,
        in_specs=[SMEM] + [VMEM] * 13,
        out_specs=[VMEM] * 5,
        out_shape=[
            jax.ShapeDtypeStruct((atoms, CA), bf16),
            jax.ShapeDtypeStruct((rows, CS), bf16),
            jax.ShapeDtypeStruct((rows, HDT), bf16),
            jax.ShapeDtypeStruct((rows, HDT), f32),
            jax.ShapeDtypeStruct((2 * HDT, rows), bf16),
        ],
        scratch_shapes=[
            pltpu.VMEM((rows, HA * 3 * KW), bf16),
            pltpu.VMEM((total, CA + 3 * KW), bf16),
            pltpu.VMEM((rows, CS), f32),
        ],
        compiler_params=pltpu.CompilerParams(vmem_limit_bytes=48 * 2**20),
        cost_estimate=pl.CostEstimate(
            flops=10**10, bytes_accessed=2**24, transcendentals=2**22
        ),
        name="atoms",
    )(place, half, other, *parts, ext, tokens, exit_w, pool, single, gain, tproj)


def tokens_body(place, query_ref, gate_ref, kv_ref, bias_ref, mine_ref, chain_ref, strength, out_ref):
    col = place[1]
    rows = query_ref.shape[0]
    shards, cols = bias_ref.shape[0], bias_ref.shape[2]
    query = query_ref[...]
    strong = strength[col]
    scores = []
    for r in range(kv_ref.shape[0]):
        raw = dot(query, kv_ref[r, :HDT, :]) * HDT ** (-0.5)
        per = rows // cols
        bias = jnp.concatenate([bias_ref[r * per + k].astype(f32) for k in range(per)], axis=1)
        same = mine_ref[...] == chain_ref[:, r * rows : (r + 1) * rows]
        scores.append(raw + bias + jnp.where(same, strong, 0.0))
    top = scores[0]
    for part in scores[1:]:
        top = jnp.maximum(top, part)
    top = jnp.max(top, axis=-1, keepdims=True)
    exps = [jnp.exp(part - top) for part in scores]
    total = exps[0]
    for part in exps[1:]:
        total = total + part
    total = jnp.sum(total, axis=-1, keepdims=True)
    out = jnp.zeros((rows, HDT), f32)
    for r in range(kv_ref.shape[0]):
        out = out + dot_nt(exps[r].astype(bf16), kv_ref[r, HDT:, :])
    gated = out / total * gate_ref[...]
    wide = jnp.concatenate([gated, jnp.zeros((rows, KW - HDT), f32)], axis=1)
    gated = wide.T[:HDT].astype(bf16)
    for k in range(out_ref.shape[0]):
        out_ref[k] = gated


def token_attention(place, query, gate, kv, bias, mine, chain, strength):
    rows = query.shape[0]
    shards = bias.shape[0]
    return pl.pallas_call(
        tokens_body,
        in_specs=[SMEM] + [VMEM] * 6 + [SMEM],
        out_specs=VMEM,
        out_shape=jax.ShapeDtypeStruct((shards, HDT, rows), bf16),
        compiler_params=pltpu.CompilerParams(vmem_limit_bytes=48 * 2**20),
        cost_estimate=pl.CostEstimate(flops=10**9, bytes_accessed=2**22, transcendentals=2**19),
        name="tokens",
    )(place, query, gate, kv, bias, mine, chain, strength)


def update_body(place, gated_ref, exit_ref, tmid_ref, back_ref, mid_ref, tokens_ref, tout_ref, aout_ref):
    col = place[1]
    atoms, rows = aout_ref.shape[0], tmid_ref.shape[0]
    added = dot_tn(gated_ref[...], exit_ref[...])
    update = (tmid_ref[...].astype(f32) + added).astype(bf16)
    tout_ref[...] = update
    sent = dot(update, back_ref[...]).astype(bf16)
    own = tokens_ref[...]
    onehot = (lax.broadcasted_iota(jnp.int32, (rows, atoms), 0) == own).astype(f32).astype(bf16)
    at = pl.multiple_of(col * atoms, atoms)
    mid = mid_ref[pl.ds(at, atoms), :].astype(f32)
    aout_ref[...] = (mid + dot_tn(onehot, sent)).astype(bf16)


def updates(place, gated, exit_w, tmid, back, mid, tokens, atoms):
    rows = tmid.shape[0]
    return pl.pallas_call(
        update_body,
        in_specs=[SMEM] + [VMEM] * 6,
        out_specs=[VMEM] * 2,
        out_shape=[
            jax.ShapeDtypeStruct((rows, CS), bf16),
            jax.ShapeDtypeStruct((atoms, CA), bf16),
        ],
        compiler_params=pltpu.CompilerParams(vmem_limit_bytes=48 * 2**20),
        name="updates",
    )(place, gated, exit_w, tmid, back, mid, tokens)


def local(
    pair_tensor,
    token_single,
    atom_single,
    atom_token,
    chain_index,
    pair_up,
    pair_down,
    bias_heads,
    atom_gain,
    atom_proj,
    atom_exit,
    atom_pool,
    token_gain,
    token_proj,
    token_exit,
    chain_bias,
    token_back,
):
    rows, cols = pair_tensor.shape[:2]
    atom_rows = atom_single.shape[0]
    row_count = lax.axis_size("row")
    col_count = lax.axis_size("col")
    row = lax.axis_index("row")
    col = lax.axis_index("col")
    chips = col_count // 2
    row_atoms = atom_rows * col_count

    spread = lambda part, count: jnp.broadcast_to(part[None], (count,) + part.shape)
    atoms = lax.all_to_all(spread(atom_single, col_count), "col", 0, 0).reshape(row_atoms, CA)
    up = [(i, i + 1) for i in range(row_count - 1)]
    down = [(i + 1, i) for i in range(row_count - 1)]
    before = lax.ppermute(atoms[-HALO:], "row", up)
    after = lax.ppermute(atoms[:HALO], "row", down)
    ext = jnp.concatenate([before, atoms, after], axis=0)
    ext_tokens = lax.dynamic_slice_in_dim(
        jnp.pad(atom_token, (HALO, HALO)), row * row_atoms, row_atoms + 2 * HALO
    )
    ext_tokens = (ext_tokens - row * rows)[None, :]
    own_tokens = lax.dynamic_slice_in_dim(
        atom_token, row * row_atoms + col * atom_rows, atom_rows
    )
    own_tokens = (own_tokens - row * rows)[None, :]

    flip = ((col == 2 * row + 1) | (col == 2 * row + 2)).astype(jnp.int32)
    place = jnp.stack([row, col, jnp.int32(row_count), flip]).astype(jnp.int32)
    halved = jnp.concatenate([pair_up[:, :PH] * bf16(0.5), pair_up[:, PH:]], axis=1)
    heads = jnp.pad(bias_heads.T, ((0, 32 - HB), (0, 0)))
    center = (jnp.eye(CZ, dtype=f32) - 1.0 / CZ).astype(bf16)
    weights = (halved, pair_down, heads, center)
    chunks = rows // CHUNK
    atom_bias, token_bias, edge = pair_chunks(
        place, pair_tensor, weights, (), 1, lambda i, place: (chunks - 1) * place[3]
    )
    halo_pairs = [
        (r * col_count + 2 * r - 1, r * col_count + 2 * r) for r in range(1, row_count)
    ] + [(r * col_count + 2 * r + 2, r * col_count + 2 * r + 1) for r in range(row_count - 1)]
    edge = lax.ppermute(edge, ("row", "col"), halo_pairs)
    atom_bias, token_bias = pair_chunks(
        place,
        pair_tensor,
        weights,
        (atom_bias, token_bias),
        chunks - 1,
        lambda i, place: i + 1 - place[3],
    )
    head_bias = lax.all_to_all(token_bias, "col", 0, 0)

    half = jnp.concatenate([atom_bias, edge], axis=1)
    gathered = jnp.where(col // 2 == row, half, jnp.zeros_like(half))
    for step in range(1, chips):
        pairs = [
            (r * col_count + 2 * r + core, r * col_count + 2 * ((r + step) % chips) + core)
            for r in range(row_count)
            for core in range(2)
        ]
        gathered = gathered + lax.ppermute(half, ("row", "col"), pairs)
    other = lax.ppermute(gathered, "col", [(i, i ^ 1) for i in range(col_count)])

    parts = project_atoms(ext, atom_gain[None], atom_proj)
    atom_mid, token_mid, query, gate, keyvals = atom_attention(
        place,
        gathered,
        other,
        parts,
        ext,
        ext_tokens,
        atom_exit,
        atom_pool,
        token_single,
        token_gain[None],
        token_proj,
    )
    keyvals = lax.all_to_all(spread(keyvals, row_count), "row", 0, 0)
    mine = lax.dynamic_slice_in_dim(chain_index, row * rows, rows)
    gated = token_attention(
        place, query, gate, keyvals, head_bias, mine[:, None], chain_index[None], chain_bias
    )
    gated = lax.all_to_all(gated, "col", 0, 0).reshape(CS, rows)
    return tuple(
        updates(
            place, gated, token_exit, token_mid, token_back, atom_mid, own_tokens, atom_rows
        )
    )


def solution(mesh):
    placed = (
        P("row", "col", None),
        P("row", None),
        P(("row", "col"), None),
    ) + (P(),) * 14
    return jax.shard_map(
        local,
        mesh=mesh,
        in_specs=placed,
        out_specs=(P("row", None), P(("row", "col"), None)),
        check_vma=False,
    )
```

time: 558 us -> 146 us (0.26); the launches traced: 551 us -> 145 us
  waiting for transfers between devices: 258 us -> 29.7 us
  local copies, waits for them, and re-layouts: 93.6 us -> 9.74 us
  other arithmetic: 70.2 us -> 4.94 us
  matrix products: 57.5 us -> 0 us
  Pallas kernels: 0 us -> 49.5 us
  blocking collectives: 48.9 us -> 0 us
  starting transfers between devices: 7.01 us -> 50.5 us
  between operations: 14.3 us -> 0.98 us
    psum x1 -> x0, waiting for transfers between devices: 137 us -> none  [local(): summed = lax.psum(partial_value, 'col')]
    all_gather x3 -> x0, waiting for transfers between devices: 121 us -> none  [the longest x1 47.3 us: local(): band_bias = lax.all_gather(atom_bias, 'col', axis=2, tiled=True)]
    dot_general x60 -> x0, matrix products: 57.5 us -> none  [the longest x16 13.7 us: pair_step(): jnp.einsum('nc,ch->hn', normed_two, bias_heads, preferred_element_type=jn...]
    pallas_call x0 -> x6, Pallas kernels: none -> 49.5 us  [the longest x2 27.7 us: pair_chunks(): pl.pallas_call(pair_body, grid_spec=pltpu.PrefetchScalarGridSpec(num_scal...]
    all_gather x2 -> x0, blocking collectives: 48.9 us -> none  [joined(): pieces = jax.tree.map(lambda part: lax.all_gather(part, axis), value)]
    dynamic_slice x64 -> x1, local copies, waits for them, and re-layouts: 44.5 us -> 0.08 us  [local(): mine = lax.dynamic_slice_in_dim(chain_index, row * rows, rows)]
    transpose x30 -> x0, other arithmetic: 40.7 us -> none  [merge_parts(): merged_out = out_early * jnp.repeat(scale_early.T, head_width, axis=1) +...]
    all_to_all x0 -> x4, starting transfers between devices: none -> 26.7 us  [the longest x1 8.86 us: local(): lax.all_to_all(spread(atom_single, col_count), 'col', 0, 0)]
  transfers between devices with their start and end apart: 6 -> 15, of which waited for: 4 -> 4; matrix products, arithmetic and copies ran while one was open for 4% -> 3% of each run, Pallas kernels for 0% -> 25%
where the time goes in v1:
time: 146 us; the launch traced here: 145 us
  starting transfers between devices  50.5 us (35%)
  Pallas kernels  49.5 us (34%)
  waiting for transfers between devices  29.7 us (20%)
  local copies, waits for them, and re-layouts  9.74 us (7%)
  other arithmetic  4.94 us (3%)
    pallas_call x2, Pallas kernels, pair_chunks(): pl.pallas_call(pair_body, grid_spec=pltpu.PrefetchScalarGridSpec(num_scal...  27.7 us
    pallas_call x1, Pallas kernels, atom_attention(): pl.pallas_call(atoms_body, in_specs=[SMEM] + [VMEM] * 13, out_specs=[VMEM...  15.7 us
    ppermute x7, starting transfers between devices, local(): gathered = gathered + lax.ppermute(half, ('row', 'col'), pairs)  14.4 us
    ppermute x7, waiting for transfers between devices, local(): gathered = gathered + lax.ppermute(half, ('row', 'col'), pairs)  12.7 us
    all_to_all x1, waiting for transfers between devices, local(): gated = lax.all_to_all(gated, 'col', 0, 0).reshape(CS, rows)  9.13 us
    all_to_all x1, starting transfers between devices, local(): lax.all_to_all(spread(atom_single, col_count), 'col', 0, 0)  8.86 us
    all_to_all x1, starting transfers between devices, local(): gated = lax.all_to_all(gated, 'col', 0, 0).reshape(CS, rows)  8.61 us
    all_to_all x1, waiting for transfers between devices, local(): keyvals = lax.all_to_all(spread(keyvals, row_count), 'row', 0, 0)  7.88 us
  transfers between devices with their start and end apart: 15, of which 4 were waited for; matrix products, arithmetic and copies ran while one was open for 3% of the time, Pallas kernels for 25%

profile of v1, /device:TPU:1, one launch (start us, length us, event | category | flops | bytes accessed | tf_op | source)
XLA Modules:
  0.0 145.4 jit_solution(5454758872499084157)
XLA Ops:
  0.6 0.6 add_convert_fusion.center_ref
  1.3 0.9 slice_multiply_fusion
  2.1 0.7 pad_maximum_fusion.1.up_ref
  2.8 1.3 pad.8.heads_ref
  4.1 0.6 pad_add_fusion.place
  4.7 8.6 %pair.2 = (bf16[4,256,128]{2,1,0:T(8,128)(2,1)}, bf16[16,256,128]{2,1,0:T(8,128)(2,1)}, bf16[4,64,128]{2,1,0:T(8,128)(2,1)}) custom-call(s32[4]{0:T(128)} %pad_add_fusion.place, bf16[256,128,128]{2,1,0:T(8,128)(2,1)} %pair_ref.3, bf16[128,512]{1,0:T(8,128)(2,1)} %pad_maximum_fusion.1.up_ref, bf16[256,128]{1,0:T(8,128)(2,1)} %down_ref.3, ...), custom_call_target="tpu_custom_call" | custom-call | flops 2048000000 | bytes 2457600 | tf_op jit(solution)/shard_map/pair/pallas_call | solution.py:99
  13.3 1.3 collective-permute-start
  14.6 0.9 broadcast_in_dim.34
  15.5 8.9 %all-to-all-start = ((bf16[16,128,128]{2,1,0:T(8,128)(2,1)}), bf16[16,128,128]{2,1,0:T(8,128)(2,1)S(1)}, u32[]{:S(2)}, u32[]{:S(2)}) async-start(bf16[16,128,128]{2,1,0:T(8,128)(2,1)} %broadcast_in_dim.34), calls=%async_computation | async-start | bytes 1048576 | tf_op jit(solution)/shard_map/all_to_all | solution.py:395
  24.3 0.0 copy-start.17
  24.3 19.2 %pair.3 = (bf16[4,256,128]{2,1,0:T(8,128)(2,1)}, bf16[16,256,128]{2,1,0:T(8,128)(2,1)}) custom-call(s32[4]{0:T(128)} %pad_add_fusion.place, bf16[256,128,128]{2,1,0:T(8,128)(2,1)} %pair_ref.3, bf16[128,512]{1,0:T(8,128)(2,1)} %pad_maximum_fusion.1.up_ref, bf16[256,128]{1,0:T(8,128)(2,1)} %down_ref.3, ...), custom_call_target="tpu_custom_call", output_to_operand_aliasing={{0}: (6, {}), {1}: (7, {})} | custom-call | flops 6144000000 | bytes 7372800 | tf_op jit(solution)/shard_map/pair/pallas_call | solution.py:99
  43.5 1.0 constant_dynamic-update-slice_fusion.1
  44.5 0.0 collective-permute-done
  44.5 3.3 %collective-permute-start.1 = (bf16[4,320,128]{2,1,0:T(8,128)(2,1)S(1)}, bf16[4,320,128]{2,1,0:T(8,128)(2,1)S(1)}, u32[]{:S(2)}, u32[]{:S(2)}) collective-permute-start(bf16[4,320,128]{2,1,0:T(8,128)(2,1)S(1)} %constant_dynamic-update-slice_fusion), channel_id=1, source_target_pairs={{0,2},{1,3},{18,20},{19,21},{36,38},{37,39},{54,56},{55,57},{72,74... | collective-permute-start | bytes 983048 | tf_op jit(solution)/shard_map/ppermute | solution.py:442
  47.8 2.2 %collective-permute-start.2 = (bf16[4,320,128]{2,1,0:T(8,128)(2,1)S(1)}, bf16[4,320,128]{2,1,0:T(8,128)(2,1)S(1)}, u32[]{:S(2)}, u32[]{:S(2)}) collective-permute-start(bf16[4,320,128]{2,1,0:T(8,128)(2,1)S(1)} %constant_dynamic-update-slice_fusion), channel_id=1, source_target_pairs={{0,4},{1,5},{18,22},{19,23},{36,40},{37,41},{54,58},{55,59},{72,76... | collective-permute-start | bytes 983048 | tf_op jit(solution)/shard_map/ppermute | solution.py:442
  50.1 1.3 collective-permute-start.3
  51.4 1.3 collective-permute-start.4
  52.7 2.0 %collective-permute-start.5 = (bf16[4,320,128]{2,1,0:T(8,128)(2,1)S(1)}, bf16[4,320,128]{2,1,0:T(8,128)(2,1)}, u32[]{:S(2)}, u32[]{:S(2)}) collective-permute-start(bf16[4,320,128]{2,1,0:T(8,128)(2,1)S(1)} %constant_dynamic-update-slice_fusion), channel_id=1, source_target_pairs={{0,10},{1,11},{18,28},{19,29},{36,46},{37,47},{54,48},{55,49},{72,... | collective-permute-start | bytes 983048 | tf_op jit(solution)/shard_map/ppermute | solution.py:442
  54.7 0.0 collective-permute-done.1
  54.7 2.2 %collective-permute-start.6 = (bf16[4,320,128]{2,1,0:T(8,128)(2,1)S(1)}, bf16[4,320,128]{2,1,0:T(8,128)(2,1)}, u32[]{:S(2)}, u32[]{:S(2)}) collective-permute-start(bf16[4,320,128]{2,1,0:T(8,128)(2,1)S(1)} %constant_dynamic-update-slice_fusion), channel_id=1, source_target_pairs={{0,12},{1,13},{18,30},{19,31},{36,32},{37,33},{54,50},{55,51},{72,... | collective-permute-start | bytes 983048 | tf_op jit(solution)/shard_map/ppermute | solution.py:442
  56.9 4.7 %collective-permute-done.2 = bf16[4,320,128]{2,1,0:T(8,128)(2,1)S(1)} collective-permute-done((bf16[4,320,128]{2,1,0:T(8,128)(2,1)S(1)}, bf16[4,320,128]{2,1,0:T(8,128)(2,1)S(1)}, u32[]{:S(2)}, u32[]{:S(2)}) %collective-permute-start.2) | collective-permute-done | bytes 327712 | tf_op jit(solution)/shard_map/ppermute | solution.py:442
  61.6 2.0 %collective-permute-start.7 = (bf16[4,320,128]{2,1,0:T(8,128)(2,1)S(1)}, bf16[4,320,128]{2,1,0:T(8,128)(2,1)}, u32[]{:S(2)}, u32[]{:S(2)}) collective-permute-start(bf16[4,320,128]{2,1,0:T(8,128)(2,1)S(1)} %constant_dynamic-update-slice_fusion), channel_id=1, source_target_pairs={{0,14},{1,15},{18,16},{19,17},{36,34},{37,35},{54,52},{55,53},{72,... | collective-permute-start | bytes 983048 | tf_op jit(solution)/shard_map/ppermute | solution.py:442
  63.6 0.0 copy-done.15
  63.6 0.1 fusion
  63.7 0.0 all-to-all-done
  63.7 5.8 %all-to-all-start.2 = ((bf16[16,256,128]{2,1,0:T(8,128)(2,1)}), bf16[16,256,128]{2,1,0:T(8,128)(2,1)S(1)}, u32[]{:S(2)}, u32[]{:S(2)}) async-start(bf16[16,256,128]{2,1,0:T(8,128)(2,1)} %get-tuple-element.27), calls=%async_computation.2 | async-start | bytes 2097152 | tf_op jit(solution)/shard_map/all_to_all | solution.py:432
  69.6 0.0 collective-permute-done.3
  69.6 1.3 collective-permute-start.10
  70.9 0.0 collective-permute-done.4
  70.9 4.0 %collective-permute-start.9 = (bf16[64,128]{1,0:T(8,128)(2,1)S(1)}, bf16[64,128]{1,0:T(8,128)(2,1)S(1)}, u32[]{:S(2)}, u32[]{:S(2)}) collective-permute-start(bf16[64,128]{1,0:T(8,128)(2,1)S(1)} %get-tuple-element.30), channel_id=1, source_target_pairs={{0,16},{16,32},{32,48},{48,64},{64,80},{80,96},{96,112},{1,17},{17... | collective-permute-start | bytes 49160 | tf_op jit(solution)/shard_map/ppermute | solution.py:398
  74.9 0.0 collective-permute-done.5
  74.9 0.0 collective-permute-done.6
  74.9 8.0 %collective-permute-done.7 = bf16[4,320,128]{2,1,0:T(8,128)(2,1)} collective-permute-done((bf16[4,320,128]{2,1,0:T(8,128)(2,1)S(1)}, bf16[4,320,128]{2,1,0:T(8,128)(2,1)}, u32[]{:S(2)}, u32[]{:S(2)}) %collective-permute-start.7) | collective-permute-done | bytes 327712 | tf_op jit(solution)/shard_map/ppermute | solution.py:442
  82.9 1.3 add_add_fusion.half_ref
  84.2 0.0 copy-start.7
  84.2 0.0 copy-start.9
  84.2 2.8 %collective-permute-start.8 = (bf16[4,320,128]{2,1,0:T(8,128)(2,1)S(1)}, bf16[4,320,128]{2,1,0:T(8,128)(2,1)S(1)}, u32[]{:S(2)}, u32[]{:S(2)}) collective-permute-start(bf16[4,320,128]{2,1,0:T(8,128)(2,1)S(1)} %add_add_fusion.half_ref), channel_id=1, source_target_pairs={{0,1},{1,0},{2,3},{3,2},{4,5},{5,4},{6,7},{7,6},{8,9},{9,8},{10,11... | collective-permute-start | bytes 983048 | tf_op jit(solution)/shard_map/ppermute | solution.py:443
  87.1 0.0 collective-permute-done.10
  87.1 0.0 collective-permute-done.9
  87.1 0.0 copy-done.7
  87.1 0.0 copy-done.9
  87.1 0.0 copy-start.5
  87.2 0.0 copy-start.6
  87.2 0.0 copy-start.8
  87.2 1.1 atom_projections.1
  88.3 0.0 collective-permute-done.8.other_ref
  88.4 15.7 %atoms.1 = (bf16[2048,128]{1,0:T(8,128)(2,1)S(1)}, bf16[256,768]{1,0:T(8,128)(2,1)S(1)}, bf16[256,48]{1,0:T(8,128)(2,1)S(1)}, f32[256,48]{1,0:T(8,128)S(1)}, bf16[96,256]{1,0:T(8,128)(2,1)S(1)}) custom-call(s32[4]{0:T(128)S(1)} %copy-done.3, bf16[4,320,128]{2,1,0:T(8,128)(2,1)S(1)} %add_add_fusion.half_ref, ...), custom_call_target="tpu_custom_call" | custom-call | flops 10000000000 | bytes 16777216 | tf_op jit(solution)/shard_map/atoms/pallas_call | solution.py:267
  104.1 0.6 copy-done.11
  104.7 0.6 copy-done.13
  105.4 0.0 all-to-all-done.2.bias_ref
  105.4 0.8 broadcast_in_dim.38
  106.1 3.5 %all-to-all-start.1 = ((bf16[8,96,256]{2,1,0:T(8,128)(2,1)}), bf16[8,96,256]{2,1,0:T(8,128)(2,1)S(1)}, u32[]{:S(2)}, u32[]{:S(2)}) async-start(bf16[8,96,256]{2,1,0:T(8,128)(2,1)} %broadcast_in_dim.38), calls=%async_computation.1 | async-start | bytes 786432 | tf_op jit(solution)/shard_map/all_to_all | solution.py:459
  109.6 0.1 dynamic_slice.10
  109.7 0.8 copy.21.mine_ref
  110.5 7.9 %all-to-all-done.1.kv_ref = bf16[8,96,256]{2,1,0:T(8,128)(2,1)S(1)} async-done(((bf16[8,96,256]{2,1,0:T(8,128)(2,1)}), bf16[8,96,256]{2,1,0:T(8,128)(2,1)S(1)}, u32[]{:S(2)}, u32[]{:S(2)}) %all-to-all-start.1) | async-done | bytes 393248 | tf_op jit(solution)/shard_map/all_to_all | solution.py:459
  118.4 0.9 copy-done.2
  119.3 0.9 copy-done.12
  120.2 0.8 copy-done.14
  121.0 2.9 %tokens.1 = bf16[16,48,256]{2,1,0:T(8,128)(2,1)} custom-call(s32[4]{0:T(128)S(1)} %copy-done.3, bf16[256,48]{1,0:T(8,128)(2,1)S(1)} %copy-done.14, f32[256,48]{1,0:T(8,128)S(1)} %copy-done.12, bf16[8,96,256]{2,1,0:T(8,128)(2,1)S(1)} %all-to-all-done.1.kv_ref, bf16[16,256,128]{2,1,0:T(8,128)(2,1)S(1)} %all-to-all-done.2.bias_ref, s32[256,1]{1,0:T(8,128)S(1)} %copy-done.2, ...), custom_call_target="tpu_custom_call" | custom-call | flops 1000000000 | bytes 4194304 | tf_op jit(solution)/shard_map/tokens/pallas_call | solution.py:326
  123.9 8.6 %all-to-all-start.3 = ((bf16[16,48,256]{2,1,0:T(8,128)(2,1)}), bf16[16,48,256]{2,1,0:T(8,128)(2,1)S(1)}, u32[]{:S(2)}, u32[]{:S(2)}) async-start(bf16[16,48,256]{2,1,0:T(8,128)(2,1)} %tokens.1), calls=%async_computation.3 | async-start | bytes 786432 | tf_op jit(solution)/shard_map/all_to_all | solution.py:464
  132.5 0.8 subtract_bitcast_fusion.tokens_ref
  133.3 9.1 %all-to-all-done.3 = bf16[16,48,256]{2,1,0:T(8,128)(2,1)S(1)} async-done(((bf16[16,48,256]{2,1,0:T(8,128)(2,1)}), bf16[16,48,256]{2,1,0:T(8,128)(2,1)S(1)}, u32[]{:S(2)}, u32[]{:S(2)}) %all-to-all-start.3) | async-done | bytes 393248 | tf_op jit(solution)/shard_map/all_to_all | solution.py:464
  142.4 0.9 copy-done.1
  143.3 2.0 %updates.1 = (bf16[256,768]{1,0:T(8,128)(2,1)}, bf16[128,128]{1,0:T(8,128)(2,1)}) custom-call(s32[4]{0:T(128)S(1)} %copy-done.3, bf16[768,256]{1,0:T(8,128)(2,1)S(1)} %bitcast.11, bf16[768,768]{1,0:T(8,128)(2,1)S(1)} %copy-done, bf16[256,768]{1,0:T(8,128)(2,1)S(1)} %get-tuple-element.28.tmid_ref, bf16[768,128]{1,0:T(8,128)(2,1)S(1)} %copy-done.1, ...), custom_call_target="tpu_custom_call" | custom-call | tf_op jit(solution)/shard_map/updates/pallas_call | solution.py:353
  (26 shorter events, 0.1 us)
Async XLA Ops:
  4.7 9.9 %copy-start.16 = (bf16[128,128]{1,0:T(8,128)(2,1)S(1)}, bf16[128,128]{1,0:T(8,128)(2,1)}, u32[]{:S(2)}) copy-start(bf16[128,128]{1,0:T(8,128)(2,1)} %param.19) | copy-start | bytes 98308
  13.3 31.2 %collective-permute-start = (bf16[4,64,128]{2,1,0:T(8,128)(2,1)}, bf16[4,64,128]{2,1,0:T(8,128)(2,1)S(1)}, u32[]{:S(2)}, u32[]{:S(2)}) collective-permute-start(bf16[4,64,128]{2,1,0:T(8,128)(2,1)} %get-tuple-element.19), channel_id=1, source_target_pairs={{17,18},{35,36},{53,54},{71,72},{89,90},{107,108},{125,126},{2,1},... | collective-permute-start | bytes 196616 | tf_op jit(solution)/shard_map/ppermute | solution.py:423
  15.5 48.3 %all-to-all-start = ((bf16[16,128,128]{2,1,0:T(8,128)(2,1)}), bf16[16,128,128]{2,1,0:T(8,128)(2,1)S(1)}, u32[]{:S(2)}, u32[]{:S(2)}) async-start(bf16[16,128,128]{2,1,0:T(8,128)(2,1)} %broadcast_in_dim.34), calls=%async_computation | async-start | bytes 1048576 | tf_op jit(solution)/shard_map/all_to_all | solution.py:395
  24.3 39.3 %copy-start.15 = (s32[16384]{0:T(1024)S(1)}, s32[16384]{0:T(1024)}, u32[]{:S(2)}) copy-start(s32[16384]{0:T(1024)} %param.20) | copy-start | bytes 196612
  24.3 39.4 %copy-start.17 = (f32[768]{0:T(1024)S(1)}, f32[768]{0:T(1024)}, u32[]{:S(2)}) copy-start(f32[768]{0:T(1024)} %param.29) | copy-start | bytes 9220
  44.5 10.2 %collective-permute-start.1 = (bf16[4,320,128]{2,1,0:T(8,128)(2,1)S(1)}, bf16[4,320,128]{2,1,0:T(8,128)(2,1)S(1)}, u32[]{:S(2)}, u32[]{:S(2)}) collective-permute-start(bf16[4,320,128]{2,1,0:T(8,128)(2,1)S(1)} %constant_dynamic-update-slice_fusion), channel_id=1, source_target_pairs={{0,2},{1,3},{18,20},{19,21},{36,38},{37,39},{54,56},{55,57},{72,74... | collective-permute-start | bytes 983048 | tf_op jit(solution)/shard_map/ppermute | solution.py:442
  47.8 13.7 %collective-permute-start.2 = (bf16[4,320,128]{2,1,0:T(8,128)(2,1)S(1)}, bf16[4,320,128]{2,1,0:T(8,128)(2,1)S(1)}, u32[]{:S(2)}, u32[]{:S(2)}) collective-permute-start(bf16[4,320,128]{2,1,0:T(8,128)(2,1)S(1)} %constant_dynamic-update-slice_fusion), channel_id=1, source_target_pairs={{0,4},{1,5},{18,22},{19,23},{36,40},{37,41},{54,58},{55,59},{72,76... | collective-permute-start | bytes 983048 | tf_op jit(solution)/shard_map/ppermute | solution.py:442
  50.1 19.5 %collective-permute-start.3 = (bf16[4,320,128]{2,1,0:T(8,128)(2,1)S(1)}, bf16[4,320,128]{2,1,0:T(8,128)(2,1)S(1)}, u32[]{:S(2)}, u32[]{:S(2)}) collective-permute-start(bf16[4,320,128]{2,1,0:T(8,128)(2,1)S(1)} %constant_dynamic-update-slice_fusion), channel_id=1, source_target_pairs={{0,6},{1,7},{18,24},{19,25},{36,42},{37,43},{54,60},{55,61},{72,78... | collective-permute-start | bytes 983048 | tf_op jit(solution)/shard_map/ppermute | solution.py:442
  51.4 19.5 %collective-permute-start.4 = (bf16[4,320,128]{2,1,0:T(8,128)(2,1)S(1)}, bf16[4,320,128]{2,1,0:T(8,128)(2,1)S(1)}, u32[]{:S(2)}, u32[]{:S(2)}) collective-permute-start(bf16[4,320,128]{2,1,0:T(8,128)(2,1)S(1)} %constant_dynamic-update-slice_fusion), channel_id=1, source_target_pairs={{0,8},{1,9},{18,26},{19,27},{36,44},{37,45},{54,62},{55,63},{72,64... | collective-permute-start | bytes 983048 | tf_op jit(solution)/shard_map/ppermute | solution.py:442
  52.7 22.2 %collective-permute-start.5 = (bf16[4,320,128]{2,1,0:T(8,128)(2,1)S(1)}, bf16[4,320,128]{2,1,0:T(8,128)(2,1)}, u32[]{:S(2)}, u32[]{:S(2)}) collective-permute-start(bf16[4,320,128]{2,1,0:T(8,128)(2,1)S(1)} %constant_dynamic-update-slice_fusion), channel_id=1, source_target_pairs={{0,10},{1,11},{18,28},{19,29},{36,46},{37,47},{54,48},{55,49},{72,... | collective-permute-start | bytes 983048 | tf_op jit(solution)/shard_map/ppermute | solution.py:442
  54.7 20.2 %collective-permute-start.6 = (bf16[4,320,128]{2,1,0:T(8,128)(2,1)S(1)}, bf16[4,320,128]{2,1,0:T(8,128)(2,1)}, u32[]{:S(2)}, u32[]{:S(2)}) collective-permute-start(bf16[4,320,128]{2,1,0:T(8,128)(2,1)S(1)} %constant_dynamic-update-slice_fusion), channel_id=1, source_target_pairs={{0,12},{1,13},{18,30},{19,31},{36,32},{37,33},{54,50},{55,51},{72,... | collective-permute-start | bytes 983048 | tf_op jit(solution)/shard_map/ppermute | solution.py:442
  61.6 21.3 %collective-permute-start.7 = (bf16[4,320,128]{2,1,0:T(8,128)(2,1)S(1)}, bf16[4,320,128]{2,1,0:T(8,128)(2,1)}, u32[]{:S(2)}, u32[]{:S(2)}) collective-permute-start(bf16[4,320,128]{2,1,0:T(8,128)(2,1)S(1)} %constant_dynamic-update-slice_fusion), channel_id=1, source_target_pairs={{0,14},{1,15},{18,16},{19,17},{36,34},{37,35},{54,52},{55,53},{72,... | collective-permute-start | bytes 983048 | tf_op jit(solution)/shard_map/ppermute | solution.py:442
  63.7 41.6 %all-to-all-start.2 = ((bf16[16,256,128]{2,1,0:T(8,128)(2,1)}), bf16[16,256,128]{2,1,0:T(8,128)(2,1)S(1)}, u32[]{:S(2)}, u32[]{:S(2)}) async-start(bf16[16,256,128]{2,1,0:T(8,128)(2,1)} %get-tuple-element.27), calls=%async_computation.2 | async-start | bytes 2097152 | tf_op jit(solution)/shard_map/all_to_all | solution.py:432
  69.6 17.5 %collective-permute-start.10 = (bf16[64,128]{1,0:T(8,128)(2,1)S(1)}, bf16[64,128]{1,0:T(8,128)(2,1)S(1)}, u32[]{:S(2)}, u32[]{:S(2)}) collective-permute-start(bf16[64,128]{1,0:T(8,128)(2,1)S(1)} %get-tuple-element.31), channel_id=1, source_target_pairs={{16,0},{32,16},{48,32},{64,48},{80,64},{96,80},{112,96},{17,1},{33... | collective-permute-start | bytes 49160 | tf_op jit(solution)/shard_map/ppermute | solution.py:399
  70.9 16.2 %collective-permute-start.9 = (bf16[64,128]{1,0:T(8,128)(2,1)S(1)}, bf16[64,128]{1,0:T(8,128)(2,1)S(1)}, u32[]{:S(2)}, u32[]{:S(2)}) collective-permute-start(bf16[64,128]{1,0:T(8,128)(2,1)S(1)} %get-tuple-element.30), channel_id=1, source_target_pairs={{0,16},{16,32},{32,48},{48,64},{64,80},{80,96},{96,112},{1,17},{17... | collective-permute-start | bytes 49160 | tf_op jit(solution)/shard_map/ppermute | solution.py:398
  84.2 2.9 %copy-start.7 = (bf16[128,512]{1,0:T(8,128)(2,1)S(1)}, bf16[128,512]{1,0:T(8,128)(2,1)}, u32[]{:S(2)}) copy-start(bf16[128,512]{1,0:T(8,128)(2,1)} %proj_ref.1) | copy-start | bytes 393220
  84.2 2.9 %copy-start.9 = (f32[128]{0:T(128)S(1)}, f32[128]{0:T(128)}, u32[]{:S(2)}) copy-start(f32[128]{0:T(128)} %param.25) | copy-start | bytes 1540
  84.2 4.1 %collective-permute-start.8 = (bf16[4,320,128]{2,1,0:T(8,128)(2,1)S(1)}, bf16[4,320,128]{2,1,0:T(8,128)(2,1)S(1)}, u32[]{:S(2)}, u32[]{:S(2)}) collective-permute-start(bf16[4,320,128]{2,1,0:T(8,128)(2,1)S(1)} %add_add_fusion.half_ref), channel_id=1, source_target_pairs={{0,1},{1,0},{2,3},{3,2},{4,5},{5,4},{6,7},{7,6},{8,9},{9,8},{10,11... | collective-permute-start | bytes 983048 | tf_op jit(solution)/shard_map/ppermute | solution.py:443
  87.1 1.2 copy-start.3
  87.1 1.2 copy-start.5
  87.2 1.2 copy-start.6
  87.2 1.2 copy-start.8
  104.1 0.7 copy-start.11
  104.7 0.6 copy-start.13
  105.4 4.2 %copy-start.4 = (s32[2048]{0:T(1024)S(1)}, s32[2048]{0:T(1024)}, u32[]{:S(2)}) copy-start(s32[2048]{0:T(1024)} %param.21) | copy-start | bytes 24580
  105.4 13.0 %copy-start.10 = (f32[16]{0:T(128)S(1)}, f32[16]{0:T(128)}, u32[]{:S(2)}) copy-start(f32[16]{0:T(128)} %strength.1) | copy-start | bytes 196
  106.1 12.2 %all-to-all-start.1 = ((bf16[8,96,256]{2,1,0:T(8,128)(2,1)}), bf16[8,96,256]{2,1,0:T(8,128)(2,1)S(1)}, u32[]{:S(2)}, u32[]{:S(2)}) async-start(bf16[8,96,256]{2,1,0:T(8,128)(2,1)} %broadcast_in_dim.38), calls=%async_computation.1 | async-start | bytes 786432 | tf_op jit(solution)/shard_map/all_to_all | solution.py:459
  118.4 0.9 copy-start.2
  119.3 0.9 copy-start.12
  120.2 0.8 copy-start.14
  121.0 21.4 %copy-start = (bf16[768,768]{1,0:T(8,128)(2,1)S(1)}, bf16[768,768]{1,0:T(8,128)(2,1)}, u32[]{:S(2)}) copy-start(bf16[768,768]{1,0:T(8,128)(2,1)} %exit_ref.3) | copy-start | bytes 3538948
  123.9 18.5 %all-to-all-start.3 = ((bf16[16,48,256]{2,1,0:T(8,128)(2,1)}), bf16[16,48,256]{2,1,0:T(8,128)(2,1)S(1)}, u32[]{:S(2)}, u32[]{:S(2)}) async-start(bf16[16,48,256]{2,1,0:T(8,128)(2,1)} %tokens.1), calls=%async_computation.3 | async-start | bytes 786432 | tf_op jit(solution)/shard_map/all_to_all | solution.py:464
  142.4 0.9 copy-start.1

commit v2 on v1

--- a/solution.py
+++ b/solution.py
@@ -2,6 +2,7 @@
 
 import jax
 import jax.numpy as jnp
+import numpy as np
 from jax import lax
 from jax.experimental import pallas as pl
 from jax.experimental.pallas import tpu as pltpu
@@ -19,7 +20,7 @@
 HDT = 48
 HB = 20
 HALO = 64
-CHUNK = 64
+BANDS = (64, 80, 64)
 GROUP = 256
 EPS = 1e-05
 
@@ -52,69 +53,84 @@
     return 0.5 + 0.5 * jnp.tanh(0.5 * value)
 
 
-VMEM = pl.BlockSpec(memory_space=pltpu.VMEM)
 SMEM = pl.BlockSpec(memory_space=pltpu.SMEM)
 
 
-def pair_body(place, pair_ref, up_ref, down_ref, heads_ref, center_ref, *refs):
-    refs = refs[-3:] if len(refs) in (3, 5) else refs[-2:]
+def full(array):
+    return pl.BlockSpec(array.shape, lambda *_: (0,) * len(array.shape))
+
+
+def pair_body(place, pair_ref, up_ref, down_ref, heads_ref, center_ref, *refs, edges):
+    outs = refs[-2:] if edges else refs[-1:]
     pair_part = pair_ref[...].reshape(-1, CZ)
     normed = scaled(dot(pair_part, center_ref[...])).astype(bf16)
-    mixed = dot(normed, up_ref[...])
-    gate, value = mixed[:, :PH], mixed[:, PH:]
+    gate = dot(normed, up_ref[:, :PH] * bf16(0.5))
+    value = dot(normed, up_ref[:, PH:])
     hidden = ((gate + gate * jnp.tanh(gate)) * value).astype(bf16)
     updated = pair_part.astype(f32) + dot(hidden, down_ref[...])
     normed_two = scaled(centered(updated)).astype(bf16)
-    biases = dot_nt(heads_ref[...], normed_two)
+    heads = jnp.concatenate([heads_ref[...].astype(f32), jnp.zeros((CZ, CZ - HB), f32)], axis=1)
+    biases = dot_nt(heads.T[:32].astype(bf16), normed_two)
     rows = pair_ref.shape[0]
     stacked = jnp.stack([biases[:, i * CZ : (i + 1) * CZ] for i in range(rows)], axis=0)
     stacked = jnp.swapaxes(stacked, 0, 1).astype(bf16)
-    refs[0][...] = stacked[:HA]
-    refs[1][...] = stacked[HA:HB]
-    if len(refs) == 3:
-        refs[2][...] = stacked[:HA]
-
-
-def pair_chunks(place, pair, weights, before, count, where):
+    outs[0][...] = stacked[HA:HB]
+    if edges:
+        outs[1][...] = stacked[:HA]
+
+
+def pair_chunk(place, pair, weights, before, first, count, edges):
     rows, cols = pair.shape[:2]
-    whole = lambda array: pl.BlockSpec(array.shape, lambda i, place: (0,) * array.ndim)
-    out_shape = [
-        jax.ShapeDtypeStruct((HA, rows, cols), bf16),
-        jax.ShapeDtypeStruct((HT, rows, cols), bf16),
+
+    def start(place):
+        return pl.multiple_of(first + place[3] * (rows - 2 * first - count), 16)
+
+    in_specs = [
+        pl.BlockSpec(
+            (pl.Element(count), pl.Element(cols), pl.Element(CZ)),
+            lambda i, place: (start(place), 0, 0),
+        )
     ]
+    in_specs += [full(array) for array in weights]
+    out_shape = [jax.ShapeDtypeStruct((HT, rows, cols), bf16)]
     out_specs = [
-        pl.BlockSpec((HA, CHUNK, cols), lambda i, place: (0, where(i, place), 0)),
-        pl.BlockSpec((HT, CHUNK, cols), lambda i, place: (0, where(i, place), 0)),
+        pl.BlockSpec(
+            (pl.Element(HT), pl.Element(count), pl.Element(cols)),
+            lambda i, place: (0, start(place), 0),
+        )
     ]
-    in_specs = [pl.BlockSpec((CHUNK, cols, CZ), lambda i, place: (where(i, place), 0, 0))]
-    in_specs += [whole(array) for array in weights]
+    if edges:
+        out_shape.append(jax.ShapeDtypeStruct((HA, count, cols), bf16))
+        out_specs.append(full(out_shape[-1]))
     aliases = {}
     if before:
-        aliases = {2 + len(weights): 0, 3 + len(weights): 1}
-        in_specs += [pl.BlockSpec(memory_space=pl.ANY)] * 2
-    else:
-        out_shape.append(jax.ShapeDtypeStruct((HA, CHUNK, cols), bf16))
-        out_specs.append(pl.BlockSpec((HA, CHUNK, cols), lambda i, place: (0, 0, 0)))
-    cells = count * CHUNK * cols
+        aliases = {2 + len(weights): 0}
+        in_specs += [pl.BlockSpec(memory_space=pl.ANY)]
+    cells = count * cols
     return pl.pallas_call(
-        pair_body,
+        functools.partial(pair_body, edges=edges),
         grid_spec=pltpu.PrefetchScalarGridSpec(
-            num_scalar_prefetch=1, grid=(count,), in_specs=in_specs, out_specs=out_specs
+            num_scalar_prefetch=1, grid=(1,), in_specs=in_specs, out_specs=out_specs
         ),
         out_shape=out_shape,
         input_output_aliases=aliases,
         compiler_params=pltpu.CompilerParams(vmem_limit_bytes=56 * 2**20),
         cost_estimate=pl.CostEstimate(
-            flops=cells * 250000, bytes_accessed=cells * 300, transcendentals=cells * PH
+            flops=cells * 500000, bytes_accessed=cells * 300, transcendentals=cells * PH
         ),
         name="pair",
     )(place, pair, *weights, *before)
 
 
-def project_body(ext_ref, gain_ref, proj_ref, query_ref, key_ref, value_ref, gate_ref):
-    ext = ext_ref[...].astype(f32)
-    normed = (scaled(centered(ext)) * gain_ref[...]).astype(bf16)
+def project_body(shards_ref, gain_ref, proj_ref, ext_ref, query_ref, key_ref, value_ref, gate_ref):
+    shards = shards_ref.shape[0]
     atoms = query_ref.shape[0]
+    per = atoms // shards
+    ext_ref[:HALO] = shards_ref[0, per : per + HALO]
+    for k in range(shards):
+        ext_ref[HALO + k * per : HALO + (k + 1) * per] = shards_ref[k, :per]
+    ext_ref[HALO + atoms :] = shards_ref[shards - 1, per : per + HALO]
+    normed = (scaled(centered(ext_ref[...].astype(f32))) * gain_ref[...]).astype(bf16)
     own = normed[HALO : HALO + atoms]
     query_ref[...] = (dot(own, proj_ref[:, :CA]) * HDA ** (-0.5)).astype(bf16)
     key_ref[...] = dot(normed, proj_ref[:, CA : 2 * CA]).astype(bf16)
@@ -122,40 +138,44 @@
     gate_ref[...] = sigmoid(dot(own, proj_ref[:, 3 * CA :]))
 
 
-def project_atoms(ext, gain, proj):
-    total = ext.shape[0]
-    atoms = total - 2 * HALO
+def project_atoms(shards, gain, proj, atoms):
+    total = atoms + 2 * HALO
+    out_shape = [
+        jax.ShapeDtypeStruct((total, CA), bf16),
+        jax.ShapeDtypeStruct((atoms, CA), bf16),
+        jax.ShapeDtypeStruct((total, CA), bf16),
+        jax.ShapeDtypeStruct((total, CA), bf16),
+        jax.ShapeDtypeStruct((atoms, CA), f32),
+    ]
     return pl.pallas_call(
         project_body,
-        in_specs=[VMEM] * 3,
-        out_specs=[VMEM] * 4,
-        out_shape=[
-            jax.ShapeDtypeStruct((atoms, CA), bf16),
-            jax.ShapeDtypeStruct((total, CA), bf16),
-            jax.ShapeDtypeStruct((total, CA), bf16),
-            jax.ShapeDtypeStruct((atoms, CA), f32),
-        ],
+        grid=(1,),
+        in_specs=[full(shards), full(gain), full(proj)],
+        out_specs=[full(shape) for shape in out_shape],
+        out_shape=out_shape,
         compiler_params=pltpu.CompilerParams(vmem_limit_bytes=48 * 2**20),
         cost_estimate=pl.CostEstimate(flops=10**9, bytes_accessed=2**22, transcendentals=2**18),
         name="atom_projections",
-    )(ext, gain, proj)
+    )(shards, gain, proj)
 
 
 def atoms_body(
     place,
     half_ref,
     other_ref,
+    half_two_ref,
+    other_two_ref,
+    ext_ref,
     query_ref,
     key_ref,
     value_ref,
     gate_ref,
-    ext_ref,
     tokens_ref,
     exit_ref,
     pool_ref,
     single_ref,
     gain_ref,
-    tproj_ref,
+    tproj_hbm,
     mid_ref,
     tmid_ref,
     tquery_ref,
@@ -164,21 +184,33 @@
     bias_ref,
     look_ref,
     sums_ref,
+    tproj_ref,
+    sem,
 ):
     row, col, row_count = place[0], place[1], place[2]
     total = ext_ref.shape[0]
     atoms = query_ref.shape[0]
     rows = single_ref.shape[0]
     even = lax.rem(col, 2) == 0
+    copy = pltpu.make_async_copy(tproj_hbm, tproj_ref, sem)
+    copy.start()
+    near, mid, far = BANDS
     for h in range(HA):
         mine, theirs = half_ref[h], other_ref[h]
         first = jnp.where(even, mine, theirs)
         second = jnp.where(even, theirs, mine)
+        mine, theirs = half_two_ref[h], other_two_ref[h]
+        first_two = jnp.where(even, mine, theirs)
+        second_two = jnp.where(even, theirs, mine)
         base = h * 3 * KW
-        bias_ref[:, base : base + KW] = first[:rows]
-        bias_ref[:, base + KW : base + 2 * KW] = second[:rows]
+        rest = jnp.zeros((rows - near - mid - far, KW), bf16)
+        bias_ref[:, base : base + KW] = jnp.concatenate([first[: near + mid], first_two, rest], axis=0)
+        bias_ref[:, base + KW : base + 2 * KW] = jnp.concatenate(
+            [rest, second_two, second[near : near + mid], second[:near]], axis=0
+        )
         bias_ref[:, base + 2 * KW : base + 3 * KW] = jnp.concatenate(
-            [first[rows:], jnp.zeros((rows - 2 * HALO, KW), bf16), second[rows:]], axis=0
+            [first[near + mid :], jnp.zeros((rows - 2 * near, KW), bf16), second[near + mid :]],
+            axis=0,
         )
     lane = lax.broadcasted_iota(jnp.int32, (KW, 3 * KW), 1)
     for t in range(total // KW):
@@ -247,6 +279,8 @@
     tmid_ref[...] = token_mid
     normed = (scaled(centered(token_mid.astype(f32))) * gain_ref[...]).astype(bf16)
 
+    copy.wait()
+
     def head_part(part):
         start = part * CS + col * HDT
         base = jnp.minimum(start // KW * KW, 4 * CS - 2 * KW)
@@ -260,32 +294,37 @@
     tkv_ref[HDT:, :] = head_part(3).T[:HDT].astype(bf16)
 
 
-def atom_attention(place, half, other, parts, ext, tokens, exit_w, pool, single, gain, tproj):
-    total = ext.shape[0]
+def atom_attention(place, bands, parts, tokens, exit_w, pool, single, gain, tproj):
+    total = parts[0].shape[0]
     atoms = total - 2 * HALO
     rows = single.shape[0]
+    operands = (*bands, *parts, tokens, exit_w, pool, single, gain)
+    out_shape = [
+        jax.ShapeDtypeStruct((atoms, CA), bf16),
+        jax.ShapeDtypeStruct((rows, CS), bf16),
+        jax.ShapeDtypeStruct((rows, HDT), bf16),
+        jax.ShapeDtypeStruct((rows, HDT), f32),
+        jax.ShapeDtypeStruct((2 * HDT, rows), bf16),
+    ]
     return pl.pallas_call(
         atoms_body,
-        in_specs=[SMEM] + [VMEM] * 13,
-        out_specs=[VMEM] * 5,
-        out_shape=[
-            jax.ShapeDtypeStruct((atoms, CA), bf16),
-            jax.ShapeDtypeStruct((rows, CS), bf16),
-            jax.ShapeDtypeStruct((rows, HDT), bf16),
-            jax.ShapeDtypeStruct((rows, HDT), f32),
-            jax.ShapeDtypeStruct((2 * HDT, rows), bf16),
-        ],
+        grid=(1,),
+        in_specs=[SMEM] + [full(array) for array in operands] + [pl.BlockSpec(memory_space=pl.ANY)],
+        out_specs=[full(shape) for shape in out_shape],
+        out_shape=out_shape,
         scratch_shapes=[
             pltpu.VMEM((rows, HA * 3 * KW), bf16),
             pltpu.VMEM((total, CA + 3 * KW), bf16),
             pltpu.VMEM((rows, CS), f32),
+            pltpu.VMEM(tproj.shape, bf16),
+            pltpu.SemaphoreType.DMA,
         ],
-        compiler_params=pltpu.CompilerParams(vmem_limit_bytes=48 * 2**20),
+        compiler_params=pltpu.CompilerParams(vmem_limit_bytes=56 * 2**20),
         cost_estimate=pl.CostEstimate(
             flops=10**10, bytes_accessed=2**24, transcendentals=2**22
         ),
         name="atoms",
-    )(place, half, other, *parts, ext, tokens, exit_w, pool, single, gain, tproj)
+    )(place, *operands, tproj)
 
 
 def tokens_body(place, query_ref, gate_ref, kv_ref, bias_ref, mine_ref, chain_ref, strength, out_ref):
@@ -323,11 +362,13 @@
 def token_attention(place, query, gate, kv, bias, mine, chain, strength):
     rows = query.shape[0]
     shards = bias.shape[0]
+    out_shape = jax.ShapeDtypeStruct((shards, HDT, rows), bf16)
     return pl.pallas_call(
         tokens_body,
-        in_specs=[SMEM] + [VMEM] * 6 + [SMEM],
-        out_specs=VMEM,
-        out_shape=jax.ShapeDtypeStruct((shards, HDT, rows), bf16),
+        grid=(1,),
+        in_specs=[SMEM] + [full(a) for a in (query, gate, kv, bias, mine, chain)] + [SMEM],
+        out_specs=full(out_shape),
+        out_shape=out_shape,
         compiler_params=pltpu.CompilerParams(vmem_limit_bytes=48 * 2**20),
         cost_estimate=pl.CostEstimate(flops=10**9, bytes_accessed=2**22, transcendentals=2**19),
         name="tokens",
@@ -350,14 +391,16 @@
 
 def updates(place, gated, exit_w, tmid, back, mid, tokens, atoms):
     rows = tmid.shape[0]
+    out_shape = [
+        jax.ShapeDtypeStruct((rows, CS), bf16),
+        jax.ShapeDtypeStruct((atoms, CA), bf16),
+    ]
     return pl.pallas_call(
         update_body,
-        in_specs=[SMEM] + [VMEM] * 6,
-        out_specs=[VMEM] * 2,
-        out_shape=[
-            jax.ShapeDtypeStruct((rows, CS), bf16),
-            jax.ShapeDtypeStruct((atoms, CA), bf16),
-        ],
+        grid=(1,),
+        in_specs=[SMEM] + [full(a) for a in (gated, exit_w, tmid, back, mid, tokens)],
+        out_specs=[full(shape) for shape in out_shape],
+        out_shape=out_shape,
         compiler_params=pltpu.CompilerParams(vmem_limit_bytes=48 * 2**20),
         name="updates",
     )(place, gated, exit_w, tmid, back, mid, tokens)
@@ -392,12 +435,19 @@
     row_atoms = atom_rows * col_count
 
     spread = lambda part, count: jnp.broadcast_to(part[None], (count,) + part.shape)
-    atoms = lax.all_to_all(spread(atom_single, col_count), "col", 0, 0).reshape(row_atoms, CA)
-    up = [(i, i + 1) for i in range(row_count - 1)]
-    down = [(i + 1, i) for i in range(row_count - 1)]
-    before = lax.ppermute(atoms[-HALO:], "row", up)
-    after = lax.ppermute(atoms[:HALO], "row", down)
-    ext = jnp.concatenate([before, atoms, after], axis=0)
+    both = ("row", "col")
+    at = lambda r, k, core: r * col_count + 2 * k + core
+    last = col_count - 1
+
+    halo = lax.ppermute(
+        jnp.where(col == last, atom_single[-HALO:], atom_single[:HALO]),
+        both,
+        [(r * col_count + last, (r + 1) * col_count) for r in range(row_count - 1)]
+        + [((r + 1) * col_count, r * col_count + last) for r in range(row_count - 1)],
+    )
+    shards = lax.all_gather(
+        jnp.concatenate([atom_single, halo, jnp.zeros_like(halo)], axis=0), "col", axis=0
+    )
     ext_tokens = lax.dynamic_slice_in_dim(
         jnp.pad(atom_token, (HALO, HALO)), row * row_atoms, row_atoms + 2 * HALO
     )
@@ -409,46 +459,68 @@
 
     flip = ((col == 2 * row + 1) | (col == 2 * row + 2)).astype(jnp.int32)
     place = jnp.stack([row, col, jnp.int32(row_count), flip]).astype(jnp.int32)
-    halved = jnp.concatenate([pair_up[:, :PH] * bf16(0.5), pair_up[:, PH:]], axis=1)
-    heads = jnp.pad(bias_heads.T, ((0, 32 - HB), (0, 0)))
-    center = (jnp.eye(CZ, dtype=f32) - 1.0 / CZ).astype(bf16)
-    weights = (halved, pair_down, heads, center)
-    chunks = rows // CHUNK
-    atom_bias, token_bias, edge = pair_chunks(
-        place, pair_tensor, weights, (), 1, lambda i, place: (chunks - 1) * place[3]
-    )
-    halo_pairs = [
-        (r * col_count + 2 * r - 1, r * col_count + 2 * r) for r in range(1, row_count)
-    ] + [(r * col_count + 2 * r + 2, r * col_count + 2 * r + 1) for r in range(row_count - 1)]
-    edge = lax.ppermute(edge, ("row", "col"), halo_pairs)
-    atom_bias, token_bias = pair_chunks(
-        place,
-        pair_tensor,
-        weights,
-        (atom_bias, token_bias),
-        chunks - 1,
-        lambda i, place: i + 1 - place[3],
-    )
+    center = jnp.asarray((np.eye(CZ) - 1.0 / CZ).astype(bf16))
+    weights = (pair_up, pair_down, bias_heads, center)
+    near, mid, far = BANDS
+    token_bias, band_near = pair_chunk(place, pair_tensor, weights, (), 0, near, True)
+    edge = lax.ppermute(
+        band_near,
+        both,
+        [(at(r, r - 1, 1), at(r, r, 0)) for r in range(1, row_count)]
+        + [(at(r, r + 1, 0), at(r, r, 1)) for r in range(row_count - 1)],
+    )
+    token_bias, band_mid = pair_chunk(
+        place, pair_tensor, weights, (token_bias,), near, mid, True
+    )
+
+    here = col // 2 == row
+    ring = chips // 2
+    flat = lambda k, step: k // ring * ring + (k + step) % ring
+    across = lambda k: (k + ring) % chips
+
+    def over_y(band):
+        band = jnp.where(here, band, jnp.zeros_like(band))
+        return band + lax.ppermute(
+            band,
+            both,
+            [(at(r, r, core), at(r, across(r), core)) for r in range(row_count) for core in range(2)],
+        )
+
+    def over_z(band):
+        total = band
+        for step in range(1, ring):
+            total = total + lax.ppermute(
+                band,
+                both,
+                [
+                    (at(r, k, core), at(r, flat(k, step), core))
+                    for r in range(row_count)
+                    for k in (r, across(r))
+                    for core in range(2)
+                ],
+            )
+        return total, lax.ppermute(total, "col", [(i, i ^ 1) for i in range(col_count)])
+
+    part_one = over_y(jnp.concatenate([band_near, band_mid, edge], axis=1))
+    token_bias, band_far = pair_chunk(
+        place, pair_tensor, weights, (token_bias,), near + mid, far, True
+    )
+    part_two = over_y(band_far)
+    part_one, token_bias = lax.optimization_barrier((part_one, token_bias))
+    bands_one = over_z(part_one)
+    rest = near + mid + far
+    (token_bias,) = pair_chunk(
+        place, pair_tensor, weights, (token_bias,), rest, rows - rest, False
+    )
+    bands_two = over_z(part_two)
+    token_bias, bands_one, bands_two = lax.optimization_barrier((token_bias, bands_one, bands_two))
     head_bias = lax.all_to_all(token_bias, "col", 0, 0)
 
-    half = jnp.concatenate([atom_bias, edge], axis=1)
-    gathered = jnp.where(col // 2 == row, half, jnp.zeros_like(half))
-    for step in range(1, chips):
-        pairs = [
-            (r * col_count + 2 * r + core, r * col_count + 2 * ((r + step) % chips) + core)
-            for r in range(row_count)
-            for core in range(2)
-        ]
-        gathered = gathered + lax.ppermute(half, ("row", "col"), pairs)
-    other = lax.ppermute(gathered, "col", [(i, i ^ 1) for i in range(col_count)])
-
-    parts = project_atoms(ext, atom_gain[None], atom_proj)
+    parts = project_atoms(shards, atom_gain[None], atom_proj, row_atoms)
     atom_mid, token_mid, query, gate, keyvals = atom_attention(
         place,
-        gathered,
-        other,
+        (*bands_one, *bands_two),
         parts,
-        ext,
         ext_tokens,
         atom_exit,
         atom_pool,

time: 146 us -> 157 us (1.075)
  between operations: 0.98 us -> 14.4 us
  waiting for transfers between devices: 29.7 us -> 21.2 us
  Pallas kernels: 49.5 us -> 57.2 us
  starting transfers between devices: 50.5 us -> 43 us
  local copies, waits for them, and re-layouts: 9.74 us -> 15.6 us
    all_to_all x1 -> x0, starting transfers between devices: 8.86 us -> none  [local(): lax.all_to_all(spread(atom_single, col_count), 'col', 0, 0)]
    pallas_call x6 -> x8, Pallas kernels: 49.5 us -> 57.2 us  [the longest x4 34.8 us: pair_chunk(): pl.pallas_call(functools.partial(pair_body, edges=edges), grid_spec=pltpu...]
    ppermute x11 -> x12, waiting for transfers between devices: 12.7 us -> 5.25 us  [the longest x6 5.23 us: over_z(): lax.ppermute(band, both, [(at(r, k, core), at(r, flat(k, step), core)) fo...]
    all_to_all x1, starting transfers between devices: 3.45 us -> 8.16 us  [local(): keyvals = lax.all_to_all(spread(keyvals, row_count), 'row', 0, 0)]
    unnamed x37 -> x55, local copies, waits for them, and re-layouts: 5.87 us -> 10.5 us
    ppermute x11 -> x12, starting transfers between devices: 23.8 us -> 19.2 us  [the longest x6 7.79 us: over_z(): lax.ppermute(band, both, [(at(r, k, core), at(r, flat(k, step), core)) fo...]
    all_to_all x1, starting transfers between devices: 5.82 us -> 7.91 us  [local(): head_bias = lax.all_to_all(token_bias, 'col', 0, 0)]
    select_n x0 -> x3, other arithmetic: none -> 1.64 us  [the longest x2 0.89 us: over_y(): band = jnp.where(here, band, jnp.zeros_like(band))]
  transfers between devices with their start and end apart: 15 -> 16, of which waited for: 4 -> 3; matrix products, arithmetic and copies ran while one was open for 3% -> 6% of each run, Pallas kernels for 25% -> 33%
where the time goes in v2:
time: 157 us; the launch traced here: 156 us
  Pallas kernels  57.2 us (36%)
  starting transfers between devices  43 us (27%)
  waiting for transfers between devices  21.2 us (14%)
  local copies, waits for them, and re-layouts  15.6 us (10%)
  between operations  14.4 us (9%)
  other arithmetic  4.78 us (3%)
    pallas_call x4, Pallas kernels, pair_chunk(): pl.pallas_call(functools.partial(pair_body, edges=edges), grid_spec=pltpu...  34.8 us
    pallas_call x1, Pallas kernels, atom_attention(): pl.pallas_call(atoms_body, grid=(1,), in_specs=[SMEM] + [full(array) for...  16.3 us
    unnamed x55, local copies, waits for them, and re-layouts  10.5 us
    all_to_all x1, waiting for transfers between devices, local(): gated = lax.all_to_all(gated, 'col', 0, 0).reshape(CS, rows)  9.13 us
    all_to_all x1, starting transfers between devices, local(): keyvals = lax.all_to_all(spread(keyvals, row_count), 'row', 0, 0)  8.16 us
    all_to_all x1, starting transfers between devices, local(): head_bias = lax.all_to_all(token_bias, 'col', 0, 0)  7.91 us
    ppermute x6, starting transfers between devices, over_z(): lax.ppermute(band, both, [(at(r, k, core), at(r, flat(k, step), core)) fo...  7.79 us
    all_to_all x1, starting transfers between devices, local(): gated = lax.all_to_all(gated, 'col', 0, 0).reshape(CS, rows)  7.61 us
  transfers between devices with their start and end apart: 16, of which 3 were waited for; matrix products, arithmetic and copies ran while one was open for 6% of the time, Pallas kernels for 33%

profile of v2, /device:TPU:1, one launch (start us, length us, event | category | flops | bytes accessed | tf_op | source)
XLA Modules:
  0.0 156.2 jit_solution(7647256787692854204)
XLA Ops:
  7.2 0.0 all-gather.3.cloned.1.call-start
  7.2 0.7 slice_select_fusion
  8.0 0.7 collective-permute-start.11
  8.6 1.4 copy.30.heads_ref
  10.1 0.6 pad_add_fusion.place
  10.6 8.7 %pair.4 = (bf16[16,256,128]{2,1,0:T(8,128)(2,1)}, bf16[4,64,128]{2,1,0:T(8,128)(2,1)}) custom-call(s32[4]{0:T(128)} %pad_add_fusion.place, bf16[256,128,128]{2,1,0:T(8,128)(2,1)} %pair_ref.7, bf16[128,512]{1,0:T(8,128)(2,1)} %up_ref.7, bf16[256,128]{1,0:T(8,128)(2,1)} %down_ref.7, bf16[128,20]{1,0:T(8,128)(2,1)} %copy.30.heads_ref, ...), custom_call_target="tpu_custom_call" | custom-call | flops 4096000000 | bytes 2457600 | tf_op jit(solution)/shard_map/pair/pallas_call | solution.py:110
  19.4 1.5 collective-permute-start
  20.8 0.1 pad.7.clone
  20.9 0.0 collective-permute-done.11
  20.9 0.7 maximum_maximum_fusion
  21.7 0.0 all-gather.3.cloned.1.call-update
  21.7 10.0 %pair.5 = (bf16[16,256,128]{2,1,0:T(8,128)(2,1)}, bf16[4,80,128]{2,1,0:T(8,128)(2,1)}) custom-call(s32[4]{0:T(128)} %pad_add_fusion.place, bf16[256,128,128]{2,1,0:T(8,128)(2,1)} %pair_ref.7, bf16[128,512]{1,0:T(8,128)(2,1)} %up_ref.7, bf16[256,128]{1,0:T(8,128)(2,1)} %down_ref.7, bf16[128,20]{1,0:T(8,128)(2,1)} %copy.30.heads_ref, ...), custom_call_target="tpu_custom_call", output_to_operand_aliasing={{0}: (6, {})} | custom-call | flops 5120000000 | bytes 3072000 | tf_op jit(solution)/shard_map/pair/pallas_call | solution.py:110
  31.7 0.0 copy-start.24
  31.7 9.0 %pair.6 = (bf16[16,256,128]{2,1,0:T(8,128)(2,1)}, bf16[4,64,128]{2,1,0:T(8,128)(2,1)}) custom-call(s32[4]{0:T(128)} %pad_add_fusion.place, bf16[256,128,128]{2,1,0:T(8,128)(2,1)} %pair_ref.7, bf16[128,512]{1,0:T(8,128)(2,1)} %up_ref.7, bf16[256,128]{1,0:T(8,128)(2,1)} %down_ref.7, bf16[128,20]{1,0:T(8,128)(2,1)} %copy.30.heads_ref, ...), custom_call_target="tpu_custom_call", output_to_operand_aliasing={{0}: (6, {})} | custom-call | flops 4096000000 | bytes 2457600 | tf_op jit(solution)/shard_map/pair/pallas_call | solution.py:110
  40.7 0.8 broadcast_select_fusion
  41.5 4.2 %collective-permute-start.6 = (bf16[4,64,128]{2,1,0:T(8,128)(2,1)S(1)}, bf16[4,64,128]{2,1,0:T(8,128)(2,1)S(1)}, u32[]{:S(2)}, u32[]{:S(2)}) collective-permute-start(bf16[4,64,128]{2,1,0:T(8,128)(2,1)S(1)} %broadcast_select_fusion), channel_id=1, source_target_pairs={{0,8},{1,9},{18,26},{19,27},{36,44},{37,45},{54,62},{55,63},{72,64... | collective-permute-start | bytes 196616 | tf_op jit(solution)/shard_map/ppermute | solution.py:483
  45.8 1.3 collective-permute-start.1
  47.1 0.9 fusion.1
  48.0 1.3 collective-permute-start.7
  49.3 1.3 collective-permute-start.8
  50.6 1.3 collective-permute-start.9
  51.9 0.1 fusion
  52.0 0.6 broadcast_in_dim.37.tokens_ref
  52.6 0.6 broadcast_in_dim.38.gain_ref
  53.2 0.1 add.47
  53.3 1.3 collective-permute-start.2
  54.6 1.3 collective-permute-start.3
  55.9 0.0 collective-permute-done.7
  55.9 1.3 collective-permute-start.4
  57.2 0.0 collective-permute-done.9
  57.3 1.8 %collective-permute-start.10 = (bf16[4,64,128]{2,1,0:T(8,128)(2,1)S(1)}, bf16[4,64,128]{2,1,0:T(8,128)(2,1)S(1)}, u32[]{:S(2)}, u32[]{:S(2)}) collective-permute-start(bf16[4,64,128]{2,1,0:T(8,128)(2,1)S(1)} %add_add_fusion.1.half_two_ref), channel_id=1, source_target_pairs={{0,1},{1,0},{2,3},{3,2},{4,5},{5,4},{6,7},{7,6},{8,9},{9,8},{10,11... | collective-permute-start | bytes 196616 | tf_op jit(solution)/shard_map/ppermute | solution.py:502
  59.1 5.2 %collective-permute-done.3 = bf16[4,208,128]{2,1,0:T(8,128)(2,1)S(1)} collective-permute-done((bf16[4,208,128]{2,1,0:T(8,128)(2,1)S(1)}, bf16[4,208,128]{2,1,0:T(8,128)(2,1)S(1)}, u32[]{:S(2)}, u32[]{:S(2)}) %collective-permute-start.3) | collective-permute-done | bytes 213024 | tf_op jit(solution)/shard_map/ppermute | solution.py:492
  64.4 0.0 copy-start.8
  64.4 0.0 copy-start.9
  64.4 2.0 %collective-permute-start.5 = (bf16[4,208,128]{2,1,0:T(8,128)(2,1)S(1)}, bf16[4,208,128]{2,1,0:T(8,128)(2,1)S(1)}, u32[]{:S(2)}, u32[]{:S(2)}) collective-permute-start(bf16[4,208,128]{2,1,0:T(8,128)(2,1)S(1)} %add_add_fusion.half_ref), channel_id=1, source_target_pairs={{0,1},{1,0},{2,3},{3,2},{4,5},{5,4},{6,7},{7,6},{8,9},{9,8},{10,11... | collective-permute-start | bytes 638984 | tf_op jit(solution)/shard_map/ppermute | solution.py:502
  66.4 7.2 %pair.7 = bf16[16,256,128]{2,1,0:T(8,128)(2,1)} custom-call(s32[4]{0:T(128)} %pad_add_fusion.place, bf16[256,128,128]{2,1,0:T(8,128)(2,1)} %pair_ref.7, bf16[128,512]{1,0:T(8,128)(2,1)} %up_ref.7, bf16[256,128]{1,0:T(8,128)(2,1)} %down_ref.7, bf16[128,20]{1,0:T(8,128)(2,1)} %copy.30.heads_ref, ...), custom_call_target="tpu_custom_call", output_to_operand_aliasing={{}: (6, {})} | custom-call | flops 3072000000 | bytes 1843200 | tf_op jit(solution)/shard_map/pair/pallas_call | solution.py:110
  73.6 7.9 %all-to-all-start.1 = ((bf16[16,256,128]{2,1,0:T(8,128)(2,1)}), bf16[16,256,128]{2,1,0:T(8,128)(2,1)S(1)}, u32[]{:S(2)}, u32[]{:S(2)}) async-start(bf16[16,256,128]{2,1,0:T(8,128)(2,1)} %pair.7), calls=%async_computation.1 | async-start | bytes 2097152 | tf_op jit(solution)/shard_map/all_to_all | solution.py:517
  81.5 0.0 all-gather.3.cloned.1.call-done
  81.6 1.2 copy-done.7
  82.8 1.1 atom_projections.1
  83.9 1.0 copy-done.11
  84.9 0.8 copy-done.12
  85.7 0.8 copy-done.13
  86.5 0.8 copy-done.14
  87.3 0.8 copy-done.15
  88.1 0.0 copy-start.10
  88.2 16.3 %atoms.1 = (bf16[2048,128]{1,0:T(8,128)(2,1)}, bf16[256,768]{1,0:T(8,128)(2,1)}, bf16[256,48]{1,0:T(8,128)(2,1)}, f32[256,48]{1,0:T(8,128)}, bf16[96,256]{1,0:T(8,128)(2,1)}) custom-call(s32[4]{0:T(128)} %pad_add_fusion.place, bf16[4,208,128]{2,1,0:T(8,128)(2,1)} %copy-done.18, bf16[4,208,128]{2,1,0:T(8,128)(2,1)} %copy-done.25, ...), custom_call_target="tpu_custom_call" | custom-call | flops 10000000000 | bytes 16777216 | tf_op jit(solution)/shard_map/atoms/pallas_call | solution.py:309
  104.5 0.0 copy-start
  104.5 0.0 copy-start.2
  104.5 1.7 %broadcast_in_dim.39 = bf16[8,96,256]{2,1,0:T(8,128)(2,1)} broadcast(bf16[96,256]{1,0:T(8,128)(2,1)} %get-tuple-element.44), dimensions={1,2} | broadcast | bytes 442368 | tf_op jit(solution)/shard_map/broadcast_in_dim | solution.py:437
  106.2 8.2 %all-to-all-start = ((bf16[8,96,256]{2,1,0:T(8,128)(2,1)}), bf16[8,96,256]{2,1,0:T(8,128)(2,1)S(1)}, u32[]{:S(2)}, u32[]{:S(2)}) async-start(bf16[8,96,256]{2,1,0:T(8,128)(2,1)} %broadcast_in_dim.39), calls=%async_computation | async-start | bytes 786432 | tf_op jit(solution)/shard_map/all_to_all | solution.py:531
  114.4 0.6 dynamic_slice.10
  115.1 1.5 copy.31.mine_ref
  116.5 6.8 %all-to-all-done.kv_ref = bf16[8,96,256]{2,1,0:T(8,128)(2,1)S(1)} async-done(((bf16[8,96,256]{2,1,0:T(8,128)(2,1)}), bf16[8,96,256]{2,1,0:T(8,128)(2,1)S(1)}, u32[]{:S(2)}, u32[]{:S(2)}) %all-to-all-start) | async-done | bytes 393248 | tf_op jit(solution)/shard_map/all_to_all | solution.py:531
  123.3 0.9 copy-done.4
  124.2 0.9 copy-done.16
  125.1 0.8 copy-done.17
  125.9 2.9 %tokens.1 = bf16[16,48,256]{2,1,0:T(8,128)(2,1)} custom-call(s32[4]{0:T(128)S(1)} %copy-done.5, bf16[256,48]{1,0:T(8,128)(2,1)S(1)} %copy-done.17, f32[256,48]{1,0:T(8,128)S(1)} %copy-done.16, bf16[8,96,256]{2,1,0:T(8,128)(2,1)S(1)} %all-to-all-done.kv_ref, bf16[16,256,128]{2,1,0:T(8,128)(2,1)S(1)} %all-to-all-done.1.bias_ref, s32[256,1]{1,0:T(8,128)S(1)} %copy-done.4, ...), custom_call_target="tpu_custom_call" | custom-call | flops 1000000000 | bytes 4194304 | tf_op jit(solution)/shard_map/tokens/pallas_call | solution.py:366
  128.9 7.6 %all-to-all-start.2 = ((bf16[16,48,256]{2,1,0:T(8,128)(2,1)}), bf16[16,48,256]{2,1,0:T(8,128)(2,1)S(1)}, u32[]{:S(2)}, u32[]{:S(2)}) async-start(bf16[16,48,256]{2,1,0:T(8,128)(2,1)} %tokens.1), calls=%async_computation.2 | async-start | bytes 786432 | tf_op jit(solution)/shard_map/all_to_all | solution.py:536
  136.5 0.8 subtract_bitcast_fusion.tokens_ref
  137.2 9.1 %all-to-all-done.2 = bf16[16,48,256]{2,1,0:T(8,128)(2,1)S(1)} async-done(((bf16[16,48,256]{2,1,0:T(8,128)(2,1)}), bf16[16,48,256]{2,1,0:T(8,128)(2,1)S(1)}, u32[]{:S(2)}, u32[]{:S(2)}) %all-to-all-start.2) | async-done | bytes 393248 | tf_op jit(solution)/shard_map/all_to_all | solution.py:536
  146.4 0.0 copy-start.3
  146.4 0.9 copy-done.3
  147.3 2.0 %updates.1 = (bf16[256,768]{1,0:T(8,128)(2,1)}, bf16[128,128]{1,0:T(8,128)(2,1)}) custom-call(s32[4]{0:T(128)S(1)} %copy-done.5, bf16[768,256]{1,0:T(8,128)(2,1)S(1)} %bitcast.10, bf16[768,768]{1,0:T(8,128)(2,1)S(1)} %copy-done, bf16[256,768]{1,0:T(8,128)(2,1)S(1)} %copy-done.2, bf16[768,128]{1,0:T(8,128)(2,1)S(1)} %copy-done.3, ...), custom_call_target="tpu_custom_call" | custom-call | tf_op jit(solution)/shard_map/updates/pallas_call | solution.py:398
  (50 shorter events, 0.2 us)
Async XLA Ops:
  7.2 74.4 %all-gather.3.cloned.1.call-start = ((), (), s32[]{:S(2)}) async-start(), calls=%async_computation.3 | async-start | bytes 1114112 | tf_op jit(solution)/shard_map/all_gather | solution.py:448
  8.0 13.0 %collective-permute-start.11 = (bf16[64,128]{1,0:T(8,128)(2,1)S(1)}, bf16[64,128]{1,0:T(8,128)(2,1)S(1)}, u32[]{:S(2)}, u32[]{:S(2)}) collective-permute-start(bf16[64,128]{1,0:T(8,128)(2,1)S(1)} %slice_select_fusion), channel_id=1, source_target_pairs={{15,16},{31,32},{47,48},{63,64},{79,80},{95,96},{111,112},{16,15},... | collective-permute-start | bytes 49160 | tf_op jit(solution)/shard_map/ppermute | solution.py:442
  10.6 10.3 %copy-start.19 = (bf16[128,128]{1,0:T(8,128)(2,1)S(1)}, bf16[128,128]{1,0:T(8,128)(2,1)}, u32[]{:S(2)}) copy-start(bf16[128,128]{1,0:T(8,128)(2,1)} %param.20) | copy-start | bytes 98308
  19.4 26.4 %collective-permute-start = (bf16[4,64,128]{2,1,0:T(8,128)(2,1)}, bf16[4,64,128]{2,1,0:T(8,128)(2,1)S(1)}, u32[]{:S(2)}, u32[]{:S(2)}) collective-permute-start(bf16[4,64,128]{2,1,0:T(8,128)(2,1)} %get-tuple-element.25), channel_id=1, source_target_pairs={{17,18},{35,36},{53,54},{71,72},{89,90},{107,108},{125,126},{2,1},... | collective-permute-start | bytes 196616 | tf_op jit(solution)/shard_map/ppermute | solution.py:466
  31.7 14.1 %copy-start.20 = (bf16[4,80,128]{2,1,0:T(8,128)(2,1)S(1)}, bf16[4,80,128]{2,1,0:T(8,128)(2,1)}, u32[]{:S(2)}) copy-start(bf16[4,80,128]{2,1,0:T(8,128)(2,1)} %get-tuple-element.27) | copy-start | bytes 245764
  31.7 14.1 %copy-start.23 = (bf16[4,64,128]{2,1,0:T(8,128)(2,1)S(1)}, bf16[4,64,128]{2,1,0:T(8,128)(2,1)}, u32[]{:S(2)}) copy-start(bf16[4,64,128]{2,1,0:T(8,128)(2,1)} %get-tuple-element.25) | copy-start | bytes 196612
  31.7 20.2 %copy-start.21 = (s32[16384]{0:T(1024)S(1)}, s32[16384]{0:T(1024)}, u32[]{:S(2)}) copy-start(s32[16384]{0:T(1024)} %param.21) | copy-start | bytes 196612
  31.7 20.9 %copy-start.24 = (f32[768]{0:T(1024)S(1)}, f32[768]{0:T(1024)}, u32[]{:S(2)}) copy-start(f32[768]{0:T(1024)} %param.30) | copy-start | bytes 9220
  41.5 5.6 %collective-permute-start.6 = (bf16[4,64,128]{2,1,0:T(8,128)(2,1)S(1)}, bf16[4,64,128]{2,1,0:T(8,128)(2,1)S(1)}, u32[]{:S(2)}, u32[]{:S(2)}) collective-permute-start(bf16[4,64,128]{2,1,0:T(8,128)(2,1)S(1)} %broadcast_select_fusion), channel_id=1, source_target_pairs={{0,8},{1,9},{18,26},{19,27},{36,44},{37,45},{54,62},{55,63},{72,64... | collective-permute-start | bytes 196616 | tf_op jit(solution)/shard_map/ppermute | solution.py:483
  45.8 7.4 %collective-permute-start.1 = (bf16[4,208,128]{2,1,0:T(8,128)(2,1)S(1)}, bf16[4,208,128]{2,1,0:T(8,128)(2,1)S(1)}, u32[]{:S(2)}, u32[]{:S(2)}) collective-permute-start(bf16[4,208,128]{2,1,0:T(8,128)(2,1)S(1)} %maximum_select_fusion), channel_id=1, source_target_pairs={{0,8},{1,9},{18,26},{19,27},{36,44},{37,45},{54,62},{55,63},{72,64... | collective-permute-start | bytes 638984 | tf_op jit(solution)/shard_map/ppermute | solution.py:483
  48.0 7.9 %collective-permute-start.7 = (bf16[4,64,128]{2,1,0:T(8,128)(2,1)S(1)}, bf16[4,64,128]{2,1,0:T(8,128)(2,1)S(1)}, u32[]{:S(2)}, u32[]{:S(2)}) collective-permute-start(bf16[4,64,128]{2,1,0:T(8,128)(2,1)S(1)} %fusion.1), channel_id=1, source_target_pairs={{0,2},{1,3},{8,10},{9,11},{18,20},{19,21},{26,28},{27,29},{36,38},... | collective-permute-start | bytes 196616 | tf_op jit(solution)/shard_map/ppermute | solution.py:492
  49.3 7.9 %collective-permute-start.8 = (bf16[4,64,128]{2,1,0:T(8,128)(2,1)S(1)}, bf16[4,64,128]{2,1,0:T(8,128)(2,1)S(1)}, u32[]{:S(2)}, u32[]{:S(2)}) collective-permute-start(bf16[4,64,128]{2,1,0:T(8,128)(2,1)S(1)} %fusion.1), channel_id=1, source_target_pairs={{0,4},{1,5},{8,12},{9,13},{18,22},{19,23},{26,30},{27,31},{36,32},... | collective-permute-start | bytes 196616 | tf_op jit(solution)/shard_map/ppermute | solution.py:492
  50.6 6.6 %collective-permute-start.9 = (bf16[4,64,128]{2,1,0:T(8,128)(2,1)S(1)}, bf16[4,64,128]{2,1,0:T(8,128)(2,1)S(1)}, u32[]{:S(2)}, u32[]{:S(2)}) collective-permute-start(bf16[4,64,128]{2,1,0:T(8,128)(2,1)S(1)} %fusion.1), channel_id=1, source_target_pairs={{0,6},{1,7},{8,14},{9,15},{18,16},{19,17},{26,24},{27,25},{36,34},... | collective-permute-start | bytes 196616 | tf_op jit(solution)/shard_map/ppermute | solution.py:492
  53.3 5.8 %collective-permute-start.2 = (bf16[4,208,128]{2,1,0:T(8,128)(2,1)S(1)}, bf16[4,208,128]{2,1,0:T(8,128)(2,1)S(1)}, u32[]{:S(2)}, u32[]{:S(2)}) collective-permute-start(bf16[4,208,128]{2,1,0:T(8,128)(2,1)S(1)} %add.47), channel_id=1, source_target_pairs={{0,2},{1,3},{8,10},{9,11},{18,20},{19,21},{26,28},{27,29},{36,38},... | collective-permute-start | bytes 638984 | tf_op jit(solution)/shard_map/ppermute | solution.py:492
  54.6 9.7 %collective-permute-start.3 = (bf16[4,208,128]{2,1,0:T(8,128)(2,1)S(1)}, bf16[4,208,128]{2,1,0:T(8,128)(2,1)S(1)}, u32[]{:S(2)}, u32[]{:S(2)}) collective-permute-start(bf16[4,208,128]{2,1,0:T(8,128)(2,1)S(1)} %add.47), channel_id=1, source_target_pairs={{0,4},{1,5},{8,12},{9,13},{18,22},{19,23},{26,30},{27,31},{36,32},... | collective-permute-start | bytes 638984 | tf_op jit(solution)/shard_map/ppermute | solution.py:492
  55.9 8.4 %collective-permute-start.4 = (bf16[4,208,128]{2,1,0:T(8,128)(2,1)S(1)}, bf16[4,208,128]{2,1,0:T(8,128)(2,1)S(1)}, u32[]{:S(2)}, u32[]{:S(2)}) collective-permute-start(bf16[4,208,128]{2,1,0:T(8,128)(2,1)S(1)} %add.47), channel_id=1, source_target_pairs={{0,6},{1,7},{8,14},{9,15},{18,16},{19,17},{26,24},{27,25},{36,34},... | collective-permute-start | bytes 638984 | tf_op jit(solution)/shard_map/ppermute | solution.py:492
  57.2 16.3 %copy-start.22 = (bf16[4,64,128]{2,1,0:T(8,128)(2,1)}, bf16[4,64,128]{2,1,0:T(8,128)(2,1)S(1)}, u32[]{:S(2)}) copy-start(bf16[4,64,128]{2,1,0:T(8,128)(2,1)S(1)} %add_add_fusion.1.half_two_ref) | copy-start | bytes 196612
  57.3 16.3 %collective-permute-start.10 = (bf16[4,64,128]{2,1,0:T(8,128)(2,1)S(1)}, bf16[4,64,128]{2,1,0:T(8,128)(2,1)S(1)}, u32[]{:S(2)}, u32[]{:S(2)}) collective-permute-start(bf16[4,64,128]{2,1,0:T(8,128)(2,1)S(1)} %add_add_fusion.1.half_two_ref), channel_id=1, source_target_pairs={{0,1},{1,0},{2,3},{3,2},{4,5},{5,4},{6,7},{7,6},{8,9},{9,8},{10,11... | collective-permute-start | bytes 196616 | tf_op jit(solution)/shard_map/ppermute | solution.py:502
  64.3 9.2 %copy-start.18 = (bf16[4,208,128]{2,1,0:T(8,128)(2,1)}, bf16[4,208,128]{2,1,0:T(8,128)(2,1)S(1)}, u32[]{:S(2)}) copy-start(bf16[4,208,128]{2,1,0:T(8,128)(2,1)S(1)} %add_add_fusion.half_ref) | copy-start | bytes 638980
  64.4 17.2 %copy-start.8 = (bf16[128,512]{1,0:T(8,128)(2,1)S(1)}, bf16[128,512]{1,0:T(8,128)(2,1)}, u32[]{:S(2)}) copy-start(bf16[128,512]{1,0:T(8,128)(2,1)} %proj_ref.1) | copy-start | bytes 393220
  64.4 17.2 %copy-start.9 = (f32[128]{0:T(128)S(1)}, f32[128]{0:T(128)}, u32[]{:S(2)}) copy-start(f32[128]{0:T(128)} %param.26) | copy-start | bytes 1540
  64.4 9.2 %collective-permute-start.5 = (bf16[4,208,128]{2,1,0:T(8,128)(2,1)S(1)}, bf16[4,208,128]{2,1,0:T(8,128)(2,1)S(1)}, u32[]{:S(2)}, u32[]{:S(2)}) collective-permute-start(bf16[4,208,128]{2,1,0:T(8,128)(2,1)S(1)} %add_add_fusion.half_ref), channel_id=1, source_target_pairs={{0,1},{1,0},{2,3},{3,2},{4,5},{5,4},{6,7},{7,6},{8,9},{9,8},{10,11... | collective-permute-start | bytes 638984 | tf_op jit(solution)/shard_map/ppermute | solution.py:502
  73.6 14.6 %copy-start.26 = (bf16[4,64,128]{2,1,0:T(8,128)(2,1)}, bf16[4,64,128]{2,1,0:T(8,128)(2,1)S(1)}, u32[]{:S(2)}) copy-start(bf16[4,64,128]{2,1,0:T(8,128)(2,1)S(1)} %collective-permute-done.10.other_two_ref) | copy-start | bytes 196612
  73.6 14.6 %copy-start.25 = (bf16[4,208,128]{2,1,0:T(8,128)(2,1)}, bf16[4,208,128]{2,1,0:T(8,128)(2,1)S(1)}, u32[]{:S(2)}) copy-start(bf16[4,208,128]{2,1,0:T(8,128)(2,1)S(1)} %collective-permute-done.5.other_ref) | copy-start | bytes 638980
  73.6 30.9 %all-to-all-start.1 = ((bf16[16,256,128]{2,1,0:T(8,128)(2,1)}), bf16[16,256,128]{2,1,0:T(8,128)(2,1)S(1)}, u32[]{:S(2)}, u32[]{:S(2)}) async-start(bf16[16,256,128]{2,1,0:T(8,128)(2,1)} %pair.7), calls=%async_computation.1 | async-start | bytes 2097152 | tf_op jit(solution)/shard_map/all_to_all | solution.py:517
  81.5 1.2 copy-start.7
  83.9 1.0 copy-start.11
  84.9 0.8 copy-start.12
  85.7 0.8 copy-start.13
  86.5 0.8 copy-start.14
  87.3 0.8 copy-start.15
  88.1 26.3 %copy-start.6 = (s32[2048]{0:T(1024)S(1)}, s32[2048]{0:T(1024)}, u32[]{:S(2)}) copy-start(s32[2048]{0:T(1024)} %param.22) | copy-start | bytes 24580
  88.1 35.1 %copy-start.5 = (s32[4]{0:T(128)S(1)}, s32[4]{0:T(128)}, u32[]{:S(2)}) copy-start(s32[4]{0:T(128)} %pad_add_fusion.place) | copy-start | bytes 52
  88.1 35.1 %copy-start.10 = (f32[16]{0:T(128)S(1)}, f32[16]{0:T(128)}, u32[]{:S(2)}) copy-start(f32[16]{0:T(128)} %strength.1) | copy-start | bytes 196
  104.5 41.9 %copy-start = (bf16[768,768]{1,0:T(8,128)(2,1)S(1)}, bf16[768,768]{1,0:T(8,128)(2,1)}, u32[]{:S(2)}) copy-start(bf16[768,768]{1,0:T(8,128)(2,1)} %exit_ref.3) | copy-start | bytes 3538948
  104.5 41.9 %copy-start.1 = (bf16[2048,128]{1,0:T(8,128)(2,1)S(1)}, bf16[2048,128]{1,0:T(8,128)(2,1)}, u32[]{:S(2)}) copy-start(bf16[2048,128]{1,0:T(8,128)(2,1)} %get-tuple-element.47.mid_ref) | copy-start | bytes 1572868
  104.5 41.9 %copy-start.2 = (bf16[256,768]{1,0:T(8,128)(2,1)S(1)}, bf16[256,768]{1,0:T(8,128)(2,1)}, u32[]{:S(2)}) copy-start(bf16[256,768]{1,0:T(8,128)(2,1)} %get-tuple-element.46.tmid_ref) | copy-start | bytes 1179652
  106.2 17.0 %all-to-all-start = ((bf16[8,96,256]{2,1,0:T(8,128)(2,1)}), bf16[8,96,256]{2,1,0:T(8,128)(2,1)S(1)}, u32[]{:S(2)}, u32[]{:S(2)}) async-start(bf16[8,96,256]{2,1,0:T(8,128)(2,1)} %broadcast_in_dim.39), calls=%async_computation | async-start | bytes 786432 | tf_op jit(solution)/shard_map/all_to_all | solution.py:531
  123.3 0.9 copy-start.4
  124.2 0.9 copy-start.16
  125.1 0.8 copy-start.17
  128.9 17.5 %all-to-all-start.2 = ((bf16[16,48,256]{2,1,0:T(8,128)(2,1)}), bf16[16,48,256]{2,1,0:T(8,128)(2,1)S(1)}, u32[]{:S(2)}, u32[]{:S(2)}) async-start(bf16[16,48,256]{2,1,0:T(8,128)(2,1)} %tokens.1), calls=%async_computation.2 | async-start | bytes 786432 | tf_op jit(solution)/shard_map/all_to_all | solution.py:536
  146.4 0.9 copy-start.3
Sparse Core Ops, SparseCore 0:
  21.8 49.9 all-gather.2

commit v3 on v2

v3 whole, which is shorter than its diff:
```python
import functools

import jax
import jax.numpy as jnp
import numpy as np
from jax import lax
from jax.experimental import pallas as pl
from jax.experimental.pallas import tpu as pltpu
from jax.sharding import PartitionSpec as P

CZ = 128
CS = 768
CA = 128
HT = 16
HA = 4
PH = 256
QB = 32
KW = 128
HDA = 32
HDT = 48
HB = 20
HALO = 64
PART = 112
REACH = 208
GROUP = 1024
EPS = 1e-05

bf16 = jnp.bfloat16
f32 = jnp.float32


def dot(left, right):
    return jnp.dot(left, right, preferred_element_type=f32)


def dot_nt(left, right):
    return lax.dot_general(left, right, (((1,), (1,)), ((), ())), preferred_element_type=f32)


def dot_tn(left, right):
    return lax.dot_general(left, right, (((0,), (0,)), ((), ())), preferred_element_type=f32)


def centered(features):
    return features - jnp.mean(features, axis=-1, keepdims=True)


def scaled(center):
    spread = jnp.mean(center * center, axis=-1, keepdims=True)
    return center * lax.rsqrt(spread + EPS)


def sigmoid(value):
    return 0.5 + 0.5 * jnp.tanh(0.5 * value)


SMEM = pl.BlockSpec(memory_space=pltpu.SMEM)
ANY = pl.BlockSpec(memory_space=pl.ANY)


def full(array):
    return pl.BlockSpec(array.shape, lambda *_: (0,) * len(array.shape))


def held(arrays):
    return [pltpu.VMEM(a.shape, a.dtype) for a in arrays] + [
        pltpu.SemaphoreType.DMA((len(arrays),))
    ]


def fetch(sources, targets, sems):
    copies = [
        pltpu.make_async_copy(source, target, sems.at[i])
        for i, (source, target) in enumerate(zip(sources, targets))
    ]
    for copy in copies:
        copy.start()
    return copies


def pair_body(place, pair_ref, up_ref, down_ref, heads_ref, center_ref, *refs, bands):
    padded = refs[-1]
    outs = refs[-4:-1] if bands else refs[-2:-1]
    pair_part = pair_ref[...].reshape(-1, CZ)
    normed = scaled(dot(pair_part, center_ref[...])).astype(bf16)
    gate = dot(normed, up_ref[:, :PH] * bf16(0.5))
    value = dot(normed, up_ref[:, PH:])
    hidden = ((gate + gate * jnp.tanh(gate)) * value).astype(bf16)
    updated = pair_part.astype(f32) + dot(hidden, down_ref[...])
    normed_two = scaled(centered(updated)).astype(bf16)
    padded[...] = jnp.zeros_like(padded)
    padded[:HB, :] = heads_ref[...].astype(f32)
    biases = dot_nt(padded[...].astype(bf16), normed_two)
    rows = pair_ref.shape[0]
    stacked = jnp.stack([biases[:, i * CZ : (i + 1) * CZ] for i in range(rows)], axis=0)
    stacked = jnp.swapaxes(stacked, 0, 1)
    outs[0][...] = stacked[HA:HB].astype(bf16)
    if bands:
        outs[1][...] = stacked[:HA].astype(bf16)

        @pl.when(pl.program_id(0) == 0)
        def _():
            edge = jnp.where(place[3] == 1, stacked[:HA, rows - HALO :], stacked[:HA, :HALO])
            edge = pltpu.roll(edge.reshape(HA * HALO, CZ), HALO, 1)
            outs[2][...] = edge.reshape(HA, HALO, CZ).astype(bf16)


def pair_rows(place, pair, weights, before, first, size, count, bands):
    rows, cols = pair.shape[:2]

    def start(i, place):
        at = first + i * size
        return pl.multiple_of(at + place[3] * (rows - 2 * at - size), 16)

    in_specs = [
        pl.BlockSpec(
            (pl.Element(size), pl.Element(cols), pl.Element(CZ)),
            lambda i, place: (start(i, place), 0, 0),
        )
    ]
    in_specs += [full(array) for array in weights]
    out_shape = [jax.ShapeDtypeStruct((HT, rows, cols), bf16)]
    out_specs = [
        pl.BlockSpec(
            (pl.Element(HT), pl.Element(size), pl.Element(cols)),
            lambda i, place: (0, start(i, place), 0),
        )
    ]
    if bands:
        out_shape.append(jax.ShapeDtypeStruct((HA, size * count, cols), bf16))
        out_specs.append(
            pl.BlockSpec(
                (HA, size, cols),
                lambda i, place: (0, i + place[3] * (count - 1 - 2 * i), 0),
            )
        )
        out_shape.append(jax.ShapeDtypeStruct((HA, HALO, cols), bf16))
        out_specs.append(full(out_shape[-1]))
    aliases = {}
    if before:
        aliases = {2 + len(weights): 0}
        in_specs += [ANY]
    cells = size * count * cols
    return pl.pallas_call(
        functools.partial(pair_body, bands=bands),
        grid_spec=pltpu.PrefetchScalarGridSpec(
            num_scalar_prefetch=1,
            grid=(count,),
            in_specs=in_specs,
            out_specs=out_specs,
            scratch_shapes=[pltpu.VMEM((32, CZ), f32)],
        ),
        out_shape=out_shape,
        input_output_aliases=aliases,
        compiler_params=pltpu.CompilerParams(vmem_limit_bytes=56 * 2**20),
        cost_estimate=pl.CostEstimate(
            flops=cells * 500000, bytes_accessed=cells * 300, transcendentals=cells * PH
        ),
        name="pair",
    )(place, pair, *weights, *before)


def project_body(
    atoms_ref, before_ref, after_ref, gain_ref, proj_ref, ext_ref, query_ref, key_ref, value_ref, gate_ref
):
    atoms = atoms_ref.shape[0]
    ext_ref[:HALO] = before_ref[...]
    ext_ref[HALO : HALO + atoms] = atoms_ref[...]
    ext_ref[HALO + atoms :] = after_ref[...]
    normed = (scaled(centered(ext_ref[...].astype(f32))) * gain_ref[...]).astype(bf16)
    own = normed[HALO : HALO + atoms]
    query_ref[...] = (dot(own, proj_ref[:, :CA]) * HDA ** (-0.5)).astype(bf16)
    key_ref[...] = dot(normed, proj_ref[:, CA : 2 * CA]).astype(bf16)
    value_ref[...] = dot(normed, proj_ref[:, 2 * CA : 3 * CA]).astype(bf16)
    gate_ref[...] = sigmoid(dot(own, proj_ref[:, 3 * CA :]))


def project_atoms(atoms, before, after, gain, proj):
    count = atoms.shape[0]
    total = count + 2 * HALO
    operands = (atoms, before, after, gain, proj)
    out_shape = [
        jax.ShapeDtypeStruct((total, CA), bf16),
        jax.ShapeDtypeStruct((count, CA), bf16),
        jax.ShapeDtypeStruct((total, CA), bf16),
        jax.ShapeDtypeStruct((total, CA), bf16),
        jax.ShapeDtypeStruct((count, CA), f32),
    ]
    return pl.pallas_call(
        project_body,
        grid=(1,),
        in_specs=[full(array) for array in operands],
        out_specs=[full(shape) for shape in out_shape],
        out_shape=out_shape,
        compiler_params=pltpu.CompilerParams(vmem_limit_bytes=48 * 2**20),
        cost_estimate=pl.CostEstimate(flops=10**9, bytes_accessed=2**22, transcendentals=2**18),
        name="atom_projections",
    )(*operands)


def atoms_body(
    place,
    tokens_ref,
    exit_ref,
    pool_ref,
    single_ref,
    gain_ref,
    half_hbm,
    other_hbm,
    ext_hbm,
    query_hbm,
    key_hbm,
    value_hbm,
    gate_hbm,
    tproj_hbm,
    mid_ref,
    tmid_ref,
    tquery_ref,
    tgate_ref,
    tkv_ref,
    bias_ref,
    look_ref,
    sums_ref,
    half_ref,
    other_ref,
    ext_ref,
    query_ref,
    key_ref,
    value_ref,
    gate_ref,
    tproj_ref,
    sems,
):
    copies = fetch(
        (half_hbm, other_hbm, ext_hbm, query_hbm, key_hbm, value_hbm, gate_hbm, tproj_hbm),
        (half_ref, other_ref, ext_ref, query_ref, key_ref, value_ref, gate_ref, tproj_ref),
        sems,
    )
    for copy in copies[:-1]:
        copy.wait()
    row, col, row_count = place[0], place[1], place[2]
    total = ext_ref.shape[0]
    atoms = query_ref.shape[0]
    rows = single_ref.shape[0]
    even = lax.rem(col, 2) == 0
    rest = jnp.zeros((rows - REACH, KW), bf16)
    for h in range(HA):
        mine, theirs = half_ref[h], other_ref[h]
        first = jnp.where(even, mine, theirs)
        second = jnp.where(even, theirs, mine)
        base = h * 3 * KW
        bias_ref[:, base : base + KW] = jnp.concatenate([first, rest], axis=0)
        bias_ref[:, base + KW : base + 2 * KW] = jnp.concatenate([rest, second], axis=0)
        bias_ref[:, base + 2 * KW : base + 3 * KW] = jnp.concatenate(
            [first[REACH - HALO :], jnp.zeros((rows - 2 * HALO, KW), bf16), second[:HALO]], axis=0
        )
    lane = lax.broadcasted_iota(jnp.int32, (KW, 3 * KW), 1)
    for t in range(total // KW):
        at = slice(t * KW, (t + 1) * KW)
        tokens = jnp.broadcast_to(tokens_ref[:, at], (KW, KW)).astype(f32).T.astype(jnp.int32)
        tokens = jnp.concatenate([tokens] * 3, axis=1)
        tokens = jnp.where(
            tokens < 0,
            tokens + 2 * KW + HALO,
            jnp.where(tokens < 2 * KW, tokens, tokens + HALO),
        )
        look_ref[at, :CA] = key_ref[at, :]
        look_ref[at, CA:] = (tokens == lane).astype(f32).astype(bf16)
    head_of = lax.broadcasted_iota(jnp.int32, (QB, CA), 1) // HDA
    sums_ref[...] = jnp.zeros_like(sums_ref)
    row_lane = lax.broadcasted_iota(jnp.int32, (1, KW), 1)

    def group(g, counts):
        start = pl.multiple_of(g * GROUP, GROUP)
        own = pl.ds(start, GROUP)
        onehot = look_ref[pl.ds(pl.multiple_of(start + HALO, HALO), GROUP), CA : CA + 2 * KW]
        picked = dot(onehot, bias_ref[...]).astype(bf16)
        queries = query_ref[own, :]
        scores = []
        for b in range(GROUP // QB):
            part = slice(b * QB, (b + 1) * QB)
            left = jnp.concatenate(
                [
                    jnp.concatenate(
                        [
                            jnp.where(head_of == h, queries[part].astype(f32), 0.0).astype(bf16),
                            picked[part, h * 3 * KW : (h + 1) * 3 * KW],
                        ],
                        axis=1,
                    )
                    for h in range(HA)
                ],
                axis=0,
            )
            first = start + b * QB + HALO - (KW - QB) // 2
            window = look_ref[pl.ds(pl.multiple_of(first, 16), KW), :]
            at = row_lane + first
            inside = ((at >= HALO) | (row > 0)) & ((at < total - HALO) | (row < row_count - 1))
            scores.append(dot_nt(left, window) + jnp.where(inside, 0.0, -1e30))
        scores = jnp.concatenate(scores, axis=0)
        exps = jnp.exp(scores - jnp.max(scores, axis=-1, keepdims=True))
        inverse = 1.0 / jnp.sum(exps, axis=-1, keepdims=True)
        weights = exps.astype(bf16)
        attended = []
        for b in range(GROUP // QB):
            first = start + b * QB + HALO - (KW - QB) // 2
            part = slice(b * HA * QB, (b + 1) * HA * QB)
            out = dot(weights[part], value_ref[pl.ds(pl.multiple_of(first, 16), KW), :])
            out = out * inverse[part]
            merged = out[:QB]
            for h in range(1, HA):
                merged = jnp.where(head_of == h, out[h * QB : (h + 1) * QB], merged)
            attended.append(merged)
        attended = jnp.concatenate(attended, axis=0)
        gated = (attended * gate_ref[own, :]).astype(bf16)
        single = ext_ref[pl.ds(pl.multiple_of(start + HALO, HALO), GROUP), :].astype(f32)
        mid = (single + dot(gated, exit_ref[...])).astype(bf16)
        mid_ref[own, :] = mid
        pooled = jnp.maximum(dot(mid, pool_ref[...]), 0.0).astype(bf16)
        sums_ref[...] += dot_tn(onehot, pooled)
        return counts + jnp.sum(onehot.astype(f32).T, axis=1, keepdims=True)

    counts = lax.fori_loop(0, atoms // GROUP, group, jnp.zeros((rows, 1), f32))
    token_mid = (single_ref[...].astype(f32) + sums_ref[...] / counts).astype(bf16)
    tmid_ref[...] = token_mid
    normed = (scaled(centered(token_mid.astype(f32))) * gain_ref[...]).astype(bf16)

    copies[-1].wait()

    def head_part(part):
        start = part * CS + col * HDT
        base = jnp.minimum(start // KW * KW, 4 * CS - 2 * KW)
        base = pl.multiple_of(base, KW)
        wide = dot(normed, tproj_ref[:, pl.ds(base, 2 * KW)])
        return pltpu.roll(wide, lax.rem(2 * KW - (start - base), 2 * KW), 1)[:, :KW]

    tquery_ref[...] = head_part(0)[:, :HDT].astype(bf16)
    tgate_ref[...] = sigmoid(head_part(1)[:, :HDT])
    keyvals = jnp.concatenate([head_part(2).T[:HDT], head_part(3).T[:HDT]], axis=0).astype(bf16)
    for k in range(tkv_ref.shape[0]):
        tkv_ref[k] = keyvals


def atom_attention(place, bands, parts, tokens, exit_w, pool, single, gain, tproj, copies):
    total = parts[0].shape[0]
    atoms = total - 2 * HALO
    rows = single.shape[0]
    operands = (tokens, exit_w, pool, single, gain)
    fetched = (*bands, *parts, tproj)
    out_shape = [
        jax.ShapeDtypeStruct((atoms, CA), bf16),
        jax.ShapeDtypeStruct((rows, CS), bf16),
        jax.ShapeDtypeStruct((rows, HDT), bf16),
        jax.ShapeDtypeStruct((rows, HDT), f32),
        jax.ShapeDtypeStruct((copies, 2 * HDT, rows), bf16),
    ]
    return pl.pallas_call(
        atoms_body,
        grid=(1,),
        in_specs=[SMEM] + [full(array) for array in operands] + [ANY] * len(fetched),
        out_specs=[full(shape) for shape in out_shape],
        out_shape=out_shape,
        scratch_shapes=[
            pltpu.VMEM((rows, HA * 3 * KW), bf16),
            pltpu.VMEM((total, CA + 3 * KW), bf16),
            pltpu.VMEM((rows, CS), f32),
        ]
        + held(fetched),
        compiler_params=pltpu.CompilerParams(vmem_limit_bytes=56 * 2**20),
        cost_estimate=pl.CostEstimate(
            flops=10**10, bytes_accessed=2**24, transcendentals=2**22
        ),
        name="atoms",
    )(place, *operands, *fetched)


def tokens_body(
    place,
    strength,
    mine_ref,
    chain_ref,
    query_hbm,
    gate_hbm,
    kv_hbm,
    bias_hbm,
    out_ref,
    query_ref,
    gate_ref,
    kv_ref,
    bias_ref,
    sems,
):
    copies = fetch(
        (query_hbm, gate_hbm, kv_hbm, bias_hbm), (query_ref, gate_ref, kv_ref, bias_ref), sems
    )
    for copy in copies:
        copy.wait()
    col = place[1]
    rows = query_ref.shape[0]
    shards, cols = bias_ref.shape[0], bias_ref.shape[2]
    query = query_ref[...]
    strong = strength[col]
    scores = []
    for r in range(kv_ref.shape[0]):
        raw = dot(query, kv_ref[r, :HDT, :]) * HDT ** (-0.5)
        per = rows // cols
        bias = jnp.concatenate([bias_ref[r * per + k].astype(f32) for k in range(per)], axis=1)
        same = mine_ref[...] == chain_ref[:, r * rows : (r + 1) * rows]
        scores.append(raw + bias + jnp.where(same, strong, 0.0))
    top = scores[0]
    for part in scores[1:]:
        top = jnp.maximum(top, part)
    top = jnp.max(top, axis=-1, keepdims=True)
    exps = [jnp.exp(part - top) for part in scores]
    total = exps[0]
    for part in exps[1:]:
        total = total + part
    total = jnp.sum(total, axis=-1, keepdims=True)
    out = jnp.zeros((rows, HDT), f32)
    for r in range(kv_ref.shape[0]):
        out = out + dot_nt(exps[r].astype(bf16), kv_ref[r, HDT:, :])
    gated = out / total * gate_ref[...]
    wide = jnp.concatenate([gated, jnp.zeros((rows, KW - HDT), f32)], axis=1)
    gated = wide.T[:HDT].astype(bf16)
    for k in range(out_ref.shape[0]):
        out_ref[k] = gated


def token_attention(place, query, gate, kv, bias, mine, chain, strength):
    rows = query.shape[0]
    shards = bias.shape[0]
    out_shape = jax.ShapeDtypeStruct((shards, HDT, rows), bf16)
    return pl.pallas_call(
        tokens_body,
        grid=(1,),
        in_specs=[SMEM] * 2 + [full(mine), full(chain)] + [ANY] * 4,
        out_specs=full(out_shape),
        out_shape=out_shape,
        scratch_shapes=held((query, gate, kv, bias)),
        compiler_params=pltpu.CompilerParams(vmem_limit_bytes=48 * 2**20),
        cost_estimate=pl.CostEstimate(flops=10**9, bytes_accessed=2**22, transcendentals=2**19),
        name="tokens",
    )(place, strength, mine, chain, query, gate, kv, bias)


def update_body(
    place,
    exit_ref,
    back_ref,
    tokens_ref,
    gated_hbm,
    tmid_hbm,
    mid_hbm,
    tout_ref,
    aout_ref,
    gated_ref,
    tmid_ref,
    mid_ref,
    sems,
):
    col = place[1]
    atoms, rows = aout_ref.shape[0], tmid_ref.shape[0]
    at = pl.multiple_of(col * atoms, atoms)
    copies = fetch(
        (gated_hbm, tmid_hbm, mid_hbm.at[pl.ds(at, atoms)]), (gated_ref, tmid_ref, mid_ref), sems
    )
    for copy in copies:
        copy.wait()
    added = dot_tn(gated_ref[...], exit_ref[...])
    update = (tmid_ref[...].astype(f32) + added).astype(bf16)
    tout_ref[...] = update
    sent = dot(update, back_ref[...]).astype(bf16)
    own = tokens_ref[...]
    onehot = (lax.broadcasted_iota(jnp.int32, (rows, atoms), 0) == own).astype(f32).astype(bf16)
    aout_ref[...] = (mid_ref[...].astype(f32) + dot_tn(onehot, sent)).astype(bf16)


def updates(place, gated, exit_w, tmid, back, mid, tokens, atoms):
    rows = tmid.shape[0]
    out_shape = [
        jax.ShapeDtypeStruct((rows, CS), bf16),
        jax.ShapeDtypeStruct((atoms, CA), bf16),
    ]
    return pl.pallas_call(
        update_body,
        grid=(1,),
        in_specs=[SMEM] + [full(a) for a in (exit_w, back, tokens)] + [ANY] * 3,
        out_specs=[full(shape) for shape in out_shape],
        out_shape=out_shape,
        scratch_shapes=held((gated, tmid, jax.ShapeDtypeStruct((atoms, CA), bf16))),
        compiler_params=pltpu.CompilerParams(vmem_limit_bytes=48 * 2**20),
        name="updates",
    )(place, exit_w, back, tokens, gated, tmid, mid)


def local(
    pair_tensor,
    token_single,
    atom_single,
    atom_token,
    chain_index,
    pair_up,
    pair_down,
    bias_heads,
    atom_gain,
    atom_proj,
    atom_exit,
    atom_pool,
    token_gain,
    token_proj,
    token_exit,
    chain_bias,
    token_back,
):
    rows, cols = pair_tensor.shape[:2]
    atom_rows = atom_single.shape[0]
    row_count = lax.axis_size("row")
    col_count = lax.axis_size("col")
    row = lax.axis_index("row")
    col = lax.axis_index("col")
    chips = col_count // 2
    row_atoms = atom_rows * col_count

    both = ("row", "col")
    at = lambda r, k, core: r * col_count + 2 * k + core
    last = col_count - 1

    spread = jnp.broadcast_to(atom_single[None], (col_count,) + atom_single.shape)
    atoms = lax.all_to_all(spread, "col", 0, 0).reshape(row_atoms, CA)
    ext_tokens = lax.dynamic_slice_in_dim(
        jnp.pad(atom_token, (HALO, HALO)), row * row_atoms, row_atoms + 2 * HALO
    )
    ext_tokens = (ext_tokens - row * rows)[None, :]
    own_tokens = lax.dynamic_slice_in_dim(
        atom_token, row * row_atoms + col * atom_rows, atom_rows
    )
    own_tokens = (own_tokens - row * rows)[None, :]

    flip = ((col == 2 * row + 1) | (col == 2 * row + 2)).astype(jnp.int32)
    place = jnp.stack([row, col, jnp.int32(row_count), flip]).astype(jnp.int32)
    center = jnp.asarray((np.eye(CZ) - 1.0 / CZ).astype(bf16))
    weights = (pair_up, pair_down, bias_heads.T, center)
    token_bias, band, edge = pair_rows(place, pair_tensor, weights, (), 0, PART, 2, True)
    atoms, band, edge, token_bias = lax.optimization_barrier((atoms, band, edge, token_bias))

    up = [(i, i + 1) for i in range(row_count - 1)]
    down = [(i + 1, i) for i in range(row_count - 1)]
    before = lax.ppermute(atoms[-HALO:], "row", up)
    after = lax.ppermute(atoms[:HALO], "row", down)

    here = col // 2 == row
    even = col % 2 == 0
    ring = chips // 2
    flat = lambda k, step: k // ring * ring + (k + step) % ring
    across = lambda k: (k + ring) % chips
    band = jnp.where(
        here & even,
        band[:, :REACH],
        jnp.where(here, band[:, 2 * PART - REACH :], jnp.zeros_like(band[:, :REACH])),
    )
    band_y = lax.ppermute(
        band,
        both,
        [(at(r, r, core), at(r, across(r), core)) for r in range(row_count) for core in range(2)],
    )
    edges = [
        lax.ppermute(
            edge,
            both,
            [(at(r, r - 1, 1), at(r, to(r), 0)) for r in range(1, row_count)]
            + [(at(r, r + 1, 0), at(r, to(r), 1)) for r in range(row_count - 1)],
        )
        for to in (lambda r: r, across)
    ]
    (token_bias,) = pair_rows(
        place, pair_tensor, weights, (token_bias,), 2 * PART, rows - 2 * PART, 1, False
    )
    band_y, edges, before, after, token_bias = lax.optimization_barrier(
        (band_y, edges, before, after, token_bias)
    )
    edge = edges[0] + edges[1]
    blank = jnp.zeros((HA, REACH - HALO, cols), bf16)
    edge = jnp.where(
        even, jnp.concatenate([blank, edge], axis=1), jnp.concatenate([edge, blank], axis=1)
    )
    place_in = lax.broadcasted_iota(jnp.int32, band.shape, 1)
    lane = lax.broadcasted_iota(jnp.int32, band.shape, 2)
    spare = jnp.where(
        even, (place_in >= REACH - HALO) & (lane < HALO), (place_in < HALO) & (lane >= HALO)
    )
    band = jnp.where(spare, edge, band + band_y)
    sent = [
        lax.ppermute(
            band,
            both,
            [
                (at(r, k, core), at(r, flat(k, step), core))
                for r in range(row_count)
                for k in (r, across(r))
                for core in range(2)
            ],
        )
        for step in range(1, ring)
    ]
    parts = project_atoms(atoms, before, after, atom_gain[None], atom_proj)
    sent, parts = lax.optimization_barrier((sent, parts))
    band = band + sent[0] + sent[1] + sent[2]
    other = lax.ppermute(band, "col", [(i, i ^ 1) for i in range(col_count)])
    token_bias, band = lax.optimization_barrier((token_bias, band))
    head_bias = lax.all_to_all(token_bias, "col", 0, 0)

    atom_mid, token_mid, query, gate, keyvals = atom_attention(
        place,
        (band, other),
        parts,
        ext_tokens,
        atom_exit,
        atom_pool,
        token_single,
        token_gain[None],
        token_proj,
        row_count,
    )
    keyvals = lax.all_to_all(keyvals, "row", 0, 0)
    mine = lax.dynamic_slice_in_dim(chain_index, row * rows, rows)
    gated = token_attention(
        place, query, gate, keyvals, head_bias, mine[:, None], chain_index[None], chain_bias
    )
    gated = lax.all_to_all(gated, "col", 0, 0).reshape(CS, rows)
    return tuple(
        updates(
            place, gated, token_exit, token_mid, token_back, atom_mid, own_tokens, atom_rows
        )
    )


def solution(mesh):
    placed = (
        P("row", "col", None),
        P("row", None),
        P(("row", "col"), None),
    ) + (P(),) * 14
    return jax.shard_map(
        local,
        mesh=mesh,
        in_specs=placed,
        out_specs=(P("row", None), P(("row", "col"), None)),
        check_vma=False,
    )
```

time: 157 us -> 145 us (0.924)
  blocking collectives: 0 us -> 16.1 us
  between operations: 14.4 us -> 1.13 us
  Pallas kernels: 57.2 us -> 47.1 us
  starting transfers between devices: 43 us -> 38.5 us
  waiting for transfers between devices: 21.2 us -> 24.5 us
  local copies, waits for them, and re-layouts: 15.6 us -> 13.5 us
  other arithmetic: 4.78 us -> 2.81 us
    all_to_all x0 -> x1, blocking collectives: none -> 16.1 us  [local(): keyvals = lax.all_to_all(keyvals, 'row', 0, 0)]
    all_to_all x1, waiting for transfers between devices: 0.01 us -> 15.1 us  [local(): head_bias = lax.all_to_all(token_bias, 'col', 0, 0)]
    pallas_call x6 -> x4, Pallas kernels: 38.9 us -> 31.5 us  [the longest x2 26.9 us: pair_rows(): pl.pallas_call(functools.partial(pair_body, bands=bands), grid_spec=pltpu...]
    all_to_all x1, waiting for transfers between devices: 6.76 us -> 0.01 us  [local(): atoms = lax.all_to_all(spread, 'col', 0, 0).reshape(row_atoms, CA)]
    ppermute x12 -> x9, waiting for transfers between devices: 5.25 us -> 0.18 us  [the longest x3 0.16 us: local(): lax.ppermute(band, both, [(at(r, k, core), at(r, flat(k, step), core)) fo...]
    all_to_all x1, starting transfers between devices: 7.61 us -> 4.26 us  [local(): gated = lax.all_to_all(gated, 'col', 0, 0).reshape(CS, rows)]
    pallas_call x1, Pallas kernels: 16.3 us -> 13.1 us  [atom_attention(): pl.pallas_call(atoms_body, grid=(1,), in_specs=[SMEM] + [full(array) for...]
    all_to_all x1, starting transfers between devices: 7.91 us -> 5.72 us  [local(): head_bias = lax.all_to_all(token_bias, 'col', 0, 0)]
  transfers between devices with their start and end apart: 16 -> 12, of which waited for: 3 -> 3; matrix products, arithmetic and copies ran while one was open for 6% -> 4% of each run, Pallas kernels for 33% -> 20%
where the time goes in v3:
time: 145 us; the launch traced here: 144 us
  Pallas kernels  47.1 us (32%)
  starting transfers between devices  38.5 us (27%)
  waiting for transfers between devices  24.5 us (17%)
  blocking collectives  16.1 us (11%)
  local copies, waits for them, and re-layouts  13.5 us (9%)
  other arithmetic  2.81 us (2%)
    pallas_call x2, Pallas kernels, pair_rows(): pl.pallas_call(functools.partial(pair_body, bands=bands), grid_spec=pltpu...  26.9 us
    all_to_all x1, blocking collectives, local(): keyvals = lax.all_to_all(keyvals, 'row', 0, 0)  16.1 us
    all_to_all x1, waiting for transfers between devices, local(): head_bias = lax.all_to_all(token_bias, 'col', 0, 0)  15.1 us
    pallas_call x1, Pallas kernels, atom_attention(): pl.pallas_call(atoms_body, grid=(1,), in_specs=[SMEM] + [full(array) for...  13.1 us
    all_to_all x1, starting transfers between devices, local(): atoms = lax.all_to_all(spread, 'col', 0, 0).reshape(row_atoms, CA)  9.46 us
    all_to_all x1, waiting for transfers between devices, local(): gated = lax.all_to_all(gated, 'col', 0, 0).reshape(CS, rows)  9.21 us
    unnamed x44, local copies, waits for them, and re-layouts  8.55 us
    all_to_all x1, starting transfers between devices, local(): head_bias = lax.all_to_all(token_bias, 'col', 0, 0)  5.72 us
  transfers between devices with their start and end apart: 12, of which 3 were waited for; matrix products, arithmetic and copies ran while one was open for 4% of the time, Pallas kernels for 20%

profile of v3, /device:TPU:1, one launch (start us, length us, event | category | flops | bytes accessed | tf_op | source)
XLA Modules:
  0.0 143.7 jit_solution(948871876569685481)
XLA Ops:
  0.6 1.6 %broadcast_in_dim.33 = bf16[16,128,128]{2,1,0:T(8,128)(2,1)} broadcast(bf16[128,128]{1,0:T(8,128)(2,1)} %param.20), dimensions={1,2} | broadcast | bytes 557056 | tf_op jit(solution)/shard_map/broadcast_in_dim | solution.py:528
  2.3 9.5 %all-to-all-start = ((bf16[16,128,128]{2,1,0:T(8,128)(2,1)}), bf16[16,128,128]{2,1,0:T(8,128)(2,1)S(1)}, u32[]{:S(2)}, u32[]{:S(2)}) async-start(bf16[16,128,128]{2,1,0:T(8,128)(2,1)} %broadcast_in_dim.33), calls=%async_computation | async-start | bytes 1048576 | tf_op jit(solution)/shard_map/all_to_all | solution.py:529
  11.7 0.6 pad_add_fusion.place
  12.4 21.3 %pair.2 = (bf16[16,256,128]{2,1,0:T(8,128)(2,1)}, bf16[4,224,128]{2,1,0:T(8,128)(2,1)}, bf16[4,64,128]{2,1,0:T(8,128)(2,1)}) custom-call(s32[4]{0:T(128)} %pad_add_fusion.place, bf16[256,128,128]{2,1,0:T(8,128)(2,1)} %pair_ref.3, bf16[128,512]{1,0:T(8,128)(2,1)} %up_ref.3, bf16[256,128]{1,0:T(8,128)(2,1)} %down_ref.3, bf16[20,128]{1,0:T(8,128)(2,1)} %bitcast.16, ...), custom_call_target="tpu_custom_call" | custom-call | flops 14336000000 | bytes 8601600 | tf_op jit(solution)/shard_map/pair/pallas_call | solution.py:144
  33.8 0.0 all-to-all-done
  33.8 1.3 collective-permute-start.1
  35.1 0.7 collective-permute-start.2
  35.8 1.1 select_select_fusion.1
  36.8 4.8 %collective-permute-start = (bf16[4,208,128]{2,1,0:T(8,128)(2,1)S(1)}, bf16[4,208,128]{2,1,0:T(8,128)(2,1)S(1)}, u32[]{:S(2)}, u32[]{:S(2)}) collective-permute-start(bf16[4,208,128]{2,1,0:T(8,128)(2,1)S(1)} %select_select_fusion.1), channel_id=1, source_target_pairs={{0,8},{1,9},{18,26},{19,27},{36,44},{37,45},{54,62},{55,63},{72,64... | collective-permute-start | bytes 638984 | tf_op jit(solution)/shard_map/ppermute | solution.py:561
  41.7 3.6 %collective-permute-start.3 = (bf16[64,128]{1,0:T(8,128)(2,1)S(1)}, bf16[64,128]{1,0:T(8,128)(2,1)S(1)}, u32[]{:S(2)}, u32[]{:S(2)}) collective-permute-start(bf16[64,128]{1,0:T(8,128)(2,1)S(1)} %get-tuple-element.69), channel_id=1, source_target_pairs={{0,16},{16,32},{32,48},{48,64},{64,80},{80,96},{96,112},{1,17},{17... | collective-permute-start | bytes 49160 | tf_op jit(solution)/shard_map/ppermute | solution.py:548
  45.3 0.0 copy-start.17
  45.3 0.0 copy-start.7
  45.3 0.0 copy-start.8
  45.3 1.6 %collective-permute-start.4 = (bf16[64,128]{1,0:T(8,128)(2,1)S(1)}, bf16[64,128]{1,0:T(8,128)(2,1)S(1)}, u32[]{:S(2)}, u32[]{:S(2)}) collective-permute-start(bf16[64,128]{1,0:T(8,128)(2,1)S(1)} %get-tuple-element.68), channel_id=1, source_target_pairs={{16,0},{32,16},{48,32},{64,48},{80,64},{96,80},{112,96},{17,1},{33... | collective-permute-start | bytes 49160 | tf_op jit(solution)/shard_map/ppermute | solution.py:549
  47.0 5.5 %pair.3 = bf16[16,256,128]{2,1,0:T(8,128)(2,1)} custom-call(s32[4]{0:T(128)} %pad_add_fusion.place, bf16[256,128,128]{2,1,0:T(8,128)(2,1)} %pair_ref.3, bf16[128,512]{1,0:T(8,128)(2,1)} %up_ref.3, bf16[256,128]{1,0:T(8,128)(2,1)} %down_ref.3, bf16[20,128]{1,0:T(8,128)(2,1)} %bitcast.17, ...), custom_call_target="tpu_custom_call", output_to_operand_aliasing={{}: (6, {})} | custom-call | flops 2048000000 | bytes 1228800 | tf_op jit(solution)/shard_map/pair/pallas_call | solution.py:144
  52.5 0.0 collective-permute-done.3.before_ref
  52.5 0.0 collective-permute-done.4.after_ref
  52.5 0.0 collective-permute-done.1
  52.5 0.0 collective-permute-done.2
  52.5 0.0 collective-permute-done
  52.6 0.0 copy-done.17
  52.6 0.2 select_select_fusion
  52.8 2.6 %collective-permute-start.5 = (bf16[4,208,128]{2,1,0:T(8,128)(2,1)S(1)}, bf16[4,208,128]{2,1,0:T(8,128)(2,1)S(1)}, u32[]{:S(2)}, u32[]{:S(2)}) collective-permute-start(bf16[4,208,128]{2,1,0:T(8,128)(2,1)S(1)} %select_select_fusion), channel_id=1, source_target_pairs={{0,2},{1,3},{8,10},{9,11},{18,20},{19,21},{26,28},{27,29},{36,38},... | collective-permute-start | bytes 638984 | tf_op jit(solution)/shard_map/ppermute | solution.py:593
  55.4 1.3 collective-permute-start.6
  56.7 1.3 collective-permute-start.7
  58.0 0.0 copy-done.7
  58.0 1.1 atom_projections.1
  59.2 1.0 copy-done.10
  60.2 0.8 copy-done.11
  61.0 0.8 copy-done.12
  61.8 0.8 copy-done.13
  62.6 0.8 copy-done.14
  63.4 0.0 collective-permute-done.5
  63.4 0.2 collective-permute-done.6
  63.6 0.0 collective-permute-done.7
  63.6 0.1 add_add_fusion.half_hbm
  63.7 1.9 %collective-permute-start.8 = (bf16[4,208,128]{2,1,0:T(8,128)(2,1)S(1)}, bf16[4,208,128]{2,1,0:T(8,128)(2,1)S(1)}, u32[]{:S(2)}, u32[]{:S(2)}) collective-permute-start(bf16[4,208,128]{2,1,0:T(8,128)(2,1)S(1)} %add_add_fusion.half_hbm), channel_id=1, source_target_pairs={{0,1},{1,0},{2,3},{3,2},{4,5},{5,4},{6,7},{7,6},{8,9},{9,8},{10,11... | collective-permute-start | bytes 638984 | tf_op jit(solution)/shard_map/ppermute | solution.py:608
  65.5 0.0 copy-done.19
  65.5 0.1 fusion
  65.6 0.6 broadcast_in_dim.31.tokens_ref
  66.2 0.6 broadcast_in_dim.32.gain_ref
  66.8 0.0 collective-permute-done.8.other_hbm
  66.9 0.7 copy-done.21
  67.5 13.1 %atoms.1 = (bf16[2048,128]{1,0:T(8,128)(2,1)}, bf16[256,768]{1,0:T(8,128)(2,1)}, bf16[256,48]{1,0:T(8,128)(2,1)}, f32[256,48]{1,0:T(8,128)}, bf16[8,96,256]{2,1,0:T(8,128)(2,1)}) custom-call(s32[4]{0:T(128)} %pad_add_fusion.place, s32[1,2176]{1,0:T(1,128)} %broadcast_in_dim.31.tokens_ref, bf16[128,128]{1,0:T(8,128)(2,1)} %exit_ref.2, ...), custom_call_target="tpu_custom_call" | custom-call | flops 10000000000 | bytes 16777216 | tf_op jit(solution)/shard_map/atoms/pallas_call | solution.py:357
  80.7 0.0 copy-start
  80.7 0.0 copy-start.1
  80.7 0.0 copy-start.2
  80.7 16.1 %all_to_all.20.kv_hbm = bf16[8,96,256]{2,1,0:T(8,128)(2,1)S(1)} all-to-all(bf16[8,96,256]{2,1,0:T(8,128)(2,1)} %get-tuple-element.64), channel_id=1, replica_groups=mesh['row'=8,'col'=16] {'row'}, dimensions={0} | all-to-all | bytes 786432 | tf_op jit(solution)/shard_map/all_to_all | solution.py:624
  96.8 5.7 %all-to-all-start.2 = ((bf16[16,256,128]{2,1,0:T(8,128)(2,1)}), bf16[16,256,128]{2,1,0:T(8,128)(2,1)S(1)}, u32[]{:S(2)}, u32[]{:S(2)}) async-start(bf16[16,256,128]{2,1,0:T(8,128)(2,1)} %pair.3), calls=%async_computation.2 | async-start | bytes 2097152 | tf_op jit(solution)/shard_map/all_to_all | solution.py:610
  102.6 0.6 dynamic_slice.10
  103.2 1.5 %copy.21.mine_ref = s32[256,1]{1,0:T(8,128)} copy(s32[256,1]{0,1:T(1,128)} %bitcast.18) | data formatting | bytes 2048 | tf_op jit(solution)/shard_map/broadcast_in_dim | solution.py:627
  104.7 15.1 %all-to-all-done.2.bias_hbm = bf16[16,256,128]{2,1,0:T(8,128)(2,1)S(1)} async-done(((bf16[16,256,128]{2,1,0:T(8,128)(2,1)}), bf16[16,256,128]{2,1,0:T(8,128)(2,1)S(1)}, u32[]{:S(2)}, u32[]{:S(2)}) %all-to-all-start.2) | async-done | bytes 1048608 | tf_op jit(solution)/shard_map/all_to_all | solution.py:610
  119.8 0.0 copy-done.5
  119.8 0.9 copy-done.4
  120.7 0.9 copy-done.15
  121.6 0.8 copy-done.16
  122.4 3.4 %tokens.1 = bf16[16,48,256]{2,1,0:T(8,128)(2,1)} custom-call(s32[4]{0:T(128)S(1)} %copy-done.5, f32[16]{0:T(128)S(1)} %copy-done.9, s32[256,1]{1,0:T(8,128)S(1)} %copy-done.4, s32[1,2048]{1,0:T(1,128)S(1)} %bitcast.14, bf16[256,48]{1,0:T(8,128)(2,1)S(1)} %copy-done.16, f32[256,48]{1,0:T(8,128)S(1)} %copy-done.15, bf16[8,96,256]{2,1,0:T(8,128)(2,1)S(1)} %all_to_all.20.kv_hbm, ...), custom_call_target="tpu_custom_call" | custom-call | flops 1000000000 | bytes 4194304 | tf_op jit(solution)/shard_map/tokens/pallas_call | solution.py:433
  125.9 4.3 %all-to-all-start.3 = ((bf16[16,48,256]{2,1,0:T(8,128)(2,1)}), bf16[16,48,256]{2,1,0:T(8,128)(2,1)S(1)}, u32[]{:S(2)}, u32[]{:S(2)}) async-start(bf16[16,48,256]{2,1,0:T(8,128)(2,1)} %tokens.1), calls=%async_computation.3 | async-start | bytes 786432 | tf_op jit(solution)/shard_map/all_to_all | solution.py:629
  130.1 0.8 subtract_bitcast_fusion.tokens_ref
  130.9 9.2 %all-to-all-done.3 = bf16[16,48,256]{2,1,0:T(8,128)(2,1)S(1)} async-done(((bf16[16,48,256]{2,1,0:T(8,128)(2,1)}), bf16[16,48,256]{2,1,0:T(8,128)(2,1)S(1)}, u32[]{:S(2)}, u32[]{:S(2)}) %all-to-all-start.3) | async-done | bytes 393248 | tf_op jit(solution)/shard_map/all_to_all | solution.py:629
  140.1 0.0 copy-done.1
  140.1 0.0 copy-start.3
  140.1 0.9 copy-done.3
  141.0 2.5 %updates.1 = (bf16[256,768]{1,0:T(8,128)(2,1)}, bf16[128,128]{1,0:T(8,128)(2,1)}) custom-call(s32[4]{0:T(128)S(1)} %copy-done.5, bf16[768,768]{1,0:T(8,128)(2,1)S(1)} %copy-done, bf16[768,128]{1,0:T(8,128)(2,1)S(1)} %copy-done.3, s32[1,128]{1,0:T(1,128)S(1)} %subtract_bitcast_fusion.tokens_ref, bf16[768,256]{1,0:T(8,128)(2,1)S(1)} %bitcast.11, ...), custom_call_target="tpu_custom_call" | custom-call | tf_op jit(solution)/shard_map/updates/pallas_call | solution.py:484
  (26 shorter events, 0.1 us)
Async XLA Ops:
  2.3 31.5 %all-to-all-start = ((bf16[16,128,128]{2,1,0:T(8,128)(2,1)}), bf16[16,128,128]{2,1,0:T(8,128)(2,1)S(1)}, u32[]{:S(2)}, u32[]{:S(2)}) async-start(bf16[16,128,128]{2,1,0:T(8,128)(2,1)} %broadcast_in_dim.33), calls=%async_computation | async-start | bytes 1048576 | tf_op jit(solution)/shard_map/all_to_all | solution.py:529
  33.8 18.7 %collective-permute-start.1 = (bf16[4,64,128]{2,1,0:T(8,128)(2,1)}, bf16[4,64,128]{2,1,0:T(8,128)(2,1)S(1)}, u32[]{:S(2)}, u32[]{:S(2)}) collective-permute-start(bf16[4,64,128]{2,1,0:T(8,128)(2,1)} %get-tuple-element.39), channel_id=1, source_target_pairs={{17,18},{35,36},{53,54},{71,72},{89,90},{107,108},{125,126},{2,1},... | collective-permute-start | bytes 196616 | tf_op jit(solution)/shard_map/ppermute | solution.py:567
  35.1 17.4 %collective-permute-start.2 = (bf16[4,64,128]{2,1,0:T(8,128)(2,1)}, bf16[4,64,128]{2,1,0:T(8,128)(2,1)S(1)}, u32[]{:S(2)}, u32[]{:S(2)}) collective-permute-start(bf16[4,64,128]{2,1,0:T(8,128)(2,1)} %get-tuple-element.39), channel_id=1, source_target_pairs={{17,26},{35,44},{53,62},{71,64},{89,82},{107,100},{125,118},{2,9},... | collective-permute-start | bytes 196616 | tf_op jit(solution)/shard_map/ppermute | solution.py:567
  36.8 15.7 %collective-permute-start = (bf16[4,208,128]{2,1,0:T(8,128)(2,1)S(1)}, bf16[4,208,128]{2,1,0:T(8,128)(2,1)S(1)}, u32[]{:S(2)}, u32[]{:S(2)}) collective-permute-start(bf16[4,208,128]{2,1,0:T(8,128)(2,1)S(1)} %select_select_fusion.1), channel_id=1, source_target_pairs={{0,8},{1,9},{18,26},{19,27},{36,44},{37,45},{54,62},{55,63},{72,64... | collective-permute-start | bytes 638984 | tf_op jit(solution)/shard_map/ppermute | solution.py:561
  41.7 10.8 %collective-permute-start.3 = (bf16[64,128]{1,0:T(8,128)(2,1)S(1)}, bf16[64,128]{1,0:T(8,128)(2,1)S(1)}, u32[]{:S(2)}, u32[]{:S(2)}) collective-permute-start(bf16[64,128]{1,0:T(8,128)(2,1)S(1)} %get-tuple-element.69), channel_id=1, source_target_pairs={{0,16},{16,32},{32,48},{48,64},{64,80},{80,96},{96,112},{1,17},{17... | collective-permute-start | bytes 49160 | tf_op jit(solution)/shard_map/ppermute | solution.py:548
  45.3 7.3 %copy-start.17 = (bf16[4,224,128]{2,1,0:T(8,128)(2,1)S(1)}, bf16[4,224,128]{2,1,0:T(8,128)(2,1)}, u32[]{:S(2)}) copy-start(bf16[4,224,128]{2,1,0:T(8,128)(2,1)} %get-tuple-element.38) | copy-start | bytes 688132
  45.3 12.7 %copy-start.7 = (bf16[128,512]{1,0:T(8,128)(2,1)S(1)}, bf16[128,512]{1,0:T(8,128)(2,1)}, u32[]{:S(2)}) copy-start(bf16[128,512]{1,0:T(8,128)(2,1)} %proj_ref.1) | copy-start | bytes 393220
  45.3 12.7 %copy-start.8 = (f32[128]{0:T(128)S(1)}, f32[128]{0:T(128)}, u32[]{:S(2)}) copy-start(f32[128]{0:T(128)} %param.26) | copy-start | bytes 1540
  45.3 7.2 %collective-permute-start.4 = (bf16[64,128]{1,0:T(8,128)(2,1)S(1)}, bf16[64,128]{1,0:T(8,128)(2,1)S(1)}, u32[]{:S(2)}, u32[]{:S(2)}) collective-permute-start(bf16[64,128]{1,0:T(8,128)(2,1)S(1)} %get-tuple-element.68), channel_id=1, source_target_pairs={{16,0},{32,16},{48,32},{64,48},{80,64},{96,80},{112,96},{17,1},{33... | collective-permute-start | bytes 49160 | tf_op jit(solution)/shard_map/ppermute | solution.py:549
  52.5 13.0 %copy-start.19 = (s32[16384]{0:T(1024)S(1)}, s32[16384]{0:T(1024)}, u32[]{:S(2)}) copy-start(s32[16384]{0:T(1024)} %param.21) | copy-start | bytes 196612
  52.5 13.7 %copy-start.20 = (f32[768]{0:T(1024)S(1)}, f32[768]{0:T(1024)}, u32[]{:S(2)}) copy-start(f32[768]{0:T(1024)} %param.30) | copy-start | bytes 9220
  52.8 10.7 %collective-permute-start.5 = (bf16[4,208,128]{2,1,0:T(8,128)(2,1)S(1)}, bf16[4,208,128]{2,1,0:T(8,128)(2,1)S(1)}, u32[]{:S(2)}, u32[]{:S(2)}) collective-permute-start(bf16[4,208,128]{2,1,0:T(8,128)(2,1)S(1)} %select_select_fusion), channel_id=1, source_target_pairs={{0,2},{1,3},{8,10},{9,11},{18,20},{19,21},{26,28},{27,29},{36,38},... | collective-permute-start | bytes 638984 | tf_op jit(solution)/shard_map/ppermute | solution.py:593
  55.4 8.2 %collective-permute-start.6 = (bf16[4,208,128]{2,1,0:T(8,128)(2,1)S(1)}, bf16[4,208,128]{2,1,0:T(8,128)(2,1)S(1)}, u32[]{:S(2)}, u32[]{:S(2)}) collective-permute-start(bf16[4,208,128]{2,1,0:T(8,128)(2,1)S(1)} %select_select_fusion), channel_id=1, source_target_pairs={{0,4},{1,5},{8,12},{9,13},{18,22},{19,23},{26,30},{27,31},{36,32},... | collective-permute-start | bytes 638984 | tf_op jit(solution)/shard_map/ppermute | solution.py:593
  56.7 6.9 %collective-permute-start.7 = (bf16[4,208,128]{2,1,0:T(8,128)(2,1)S(1)}, bf16[4,208,128]{2,1,0:T(8,128)(2,1)S(1)}, u32[]{:S(2)}, u32[]{:S(2)}) collective-permute-start(bf16[4,208,128]{2,1,0:T(8,128)(2,1)S(1)} %select_select_fusion), channel_id=1, source_target_pairs={{0,6},{1,7},{8,14},{9,15},{18,16},{19,17},{26,24},{27,25},{36,34},... | collective-permute-start | bytes 638984 | tf_op jit(solution)/shard_map/ppermute | solution.py:593
  59.2 1.0 copy-start.10
  60.2 0.8 copy-start.11
  61.0 0.8 copy-start.12
  61.8 0.8 copy-start.13
  62.6 0.8 copy-start.14
  63.6 3.2 %copy-start.18 = (bf16[4,208,128]{2,1,0:T(8,128)(2,1)}, bf16[4,208,128]{2,1,0:T(8,128)(2,1)S(1)}, u32[]{:S(2)}) copy-start(bf16[4,208,128]{2,1,0:T(8,128)(2,1)S(1)} %add_add_fusion.half_hbm) | copy-start | bytes 638980
  63.7 3.2 %collective-permute-start.8 = (bf16[4,208,128]{2,1,0:T(8,128)(2,1)S(1)}, bf16[4,208,128]{2,1,0:T(8,128)(2,1)S(1)}, u32[]{:S(2)}, u32[]{:S(2)}) collective-permute-start(bf16[4,208,128]{2,1,0:T(8,128)(2,1)S(1)} %add_add_fusion.half_hbm), channel_id=1, source_target_pairs={{0,1},{1,0},{2,3},{3,2},{4,5},{5,4},{6,7},{7,6},{8,9},{9,8},{10,11... | collective-permute-start | bytes 638984 | tf_op jit(solution)/shard_map/ppermute | solution.py:608
  66.8 35.7 %copy-start.6 = (s32[2048]{0:T(1024)S(1)}, s32[2048]{0:T(1024)}, u32[]{:S(2)}) copy-start(s32[2048]{0:T(1024)} %param.22) | copy-start | bytes 24580
  66.8 52.9 %copy-start.5 = (s32[4]{0:T(128)S(1)}, s32[4]{0:T(128)}, u32[]{:S(2)}) copy-start(s32[4]{0:T(128)} %pad_add_fusion.place) | copy-start | bytes 52
  66.8 52.9 %copy-start.9 = (f32[16]{0:T(128)S(1)}, f32[16]{0:T(128)}, u32[]{:S(2)}) copy-start(f32[16]{0:T(128)} %strength.1) | copy-start | bytes 196
  66.8 0.7 copy-start.21
  80.7 59.4 %copy-start = (bf16[768,768]{1,0:T(8,128)(2,1)S(1)}, bf16[768,768]{1,0:T(8,128)(2,1)}, u32[]{:S(2)}) copy-start(bf16[768,768]{1,0:T(8,128)(2,1)} %exit_ref.3) | copy-start | bytes 3538948
  80.7 59.4 %copy-start.1 = (bf16[2048,128]{1,0:T(8,128)(2,1)S(1)}, bf16[2048,128]{1,0:T(8,128)(2,1)}, u32[]{:S(2)}) copy-start(bf16[2048,128]{1,0:T(8,128)(2,1)} %get-tuple-element.67.mid_hbm) | copy-start | bytes 1572868
  80.7 59.4 %copy-start.2 = (bf16[256,768]{1,0:T(8,128)(2,1)S(1)}, bf16[256,768]{1,0:T(8,128)(2,1)}, u32[]{:S(2)}) copy-start(bf16[256,768]{1,0:T(8,128)(2,1)} %get-tuple-element.66.tmid_hbm) | copy-start | bytes 1179652
  96.8 22.9 %all-to-all-start.2 = ((bf16[16,256,128]{2,1,0:T(8,128)(2,1)}), bf16[16,256,128]{2,1,0:T(8,128)(2,1)S(1)}, u32[]{:S(2)}, u32[]{:S(2)}) async-start(bf16[16,256,128]{2,1,0:T(8,128)(2,1)} %pair.3), calls=%async_computation.2 | async-start | bytes 2097152 | tf_op jit(solution)/shard_map/all_to_all | solution.py:610
  119.8 0.9 copy-start.4
  120.7 0.9 copy-start.15
  121.6 0.8 copy-start.16
  125.9 14.2 %all-to-all-start.3 = ((bf16[16,48,256]{2,1,0:T(8,128)(2,1)}), bf16[16,48,256]{2,1,0:T(8,128)(2,1)S(1)}, u32[]{:S(2)}, u32[]{:S(2)}) async-start(bf16[16,48,256]{2,1,0:T(8,128)(2,1)} %tokens.1), calls=%async_computation.3 | async-start | bytes 786432 | tf_op jit(solution)/shard_map/all_to_all | solution.py:629
  140.1 0.9 copy-start.3

commit v4 on v3

--- a/solution.py
+++ b/solution.py
@@ -56,6 +56,7 @@
 
 SMEM = pl.BlockSpec(memory_space=pltpu.SMEM)
 ANY = pl.BlockSpec(memory_space=pl.ANY)
+HBM = pl.BlockSpec(memory_space=pltpu.HBM)
 
 
 def full(array):
@@ -160,13 +161,14 @@
     )(place, pair, *weights, *before)
 
 
-def project_body(
-    atoms_ref, before_ref, after_ref, gain_ref, proj_ref, ext_ref, query_ref, key_ref, value_ref, gate_ref
-):
-    atoms = atoms_ref.shape[0]
-    ext_ref[:HALO] = before_ref[...]
-    ext_ref[HALO : HALO + atoms] = atoms_ref[...]
-    ext_ref[HALO + atoms :] = after_ref[...]
+def project_body(shards_ref, gain_ref, proj_ref, ext_ref, query_ref, key_ref, value_ref, gate_ref):
+    shards = shards_ref.shape[0]
+    atoms = query_ref.shape[0]
+    per = atoms // shards
+    ext_ref[:HALO] = shards_ref[0, per:]
+    for k in range(shards):
+        ext_ref[HALO + k * per : HALO + (k + 1) * per] = shards_ref[k, :per]
+    ext_ref[HALO + atoms :] = shards_ref[shards - 1, per:]
     normed = (scaled(centered(ext_ref[...].astype(f32))) * gain_ref[...]).astype(bf16)
     own = normed[HALO : HALO + atoms]
     query_ref[...] = (dot(own, proj_ref[:, :CA]) * HDA ** (-0.5)).astype(bf16)
@@ -175,10 +177,10 @@
     gate_ref[...] = sigmoid(dot(own, proj_ref[:, 3 * CA :]))
 
 
-def project_atoms(atoms, before, after, gain, proj):
-    count = atoms.shape[0]
+def project_atoms(shards, gain, proj):
+    count = shards.shape[0] * (shards.shape[1] - HALO)
     total = count + 2 * HALO
-    operands = (atoms, before, after, gain, proj)
+    operands = (shards, gain, proj)
     out_shape = [
         jax.ShapeDtypeStruct((total, CA), bf16),
         jax.ShapeDtypeStruct((count, CA), bf16),
@@ -192,7 +194,7 @@
         in_specs=[full(array) for array in operands],
         out_specs=[full(shape) for shape in out_shape],
         out_shape=out_shape,
-        compiler_params=pltpu.CompilerParams(vmem_limit_bytes=48 * 2**20),
+        compiler_params=pltpu.CompilerParams(vmem_limit_bytes=20 * 2**20),
         cost_estimate=pl.CostEstimate(flops=10**9, bytes_accessed=2**22, transcendentals=2**18),
         name="atom_projections",
     )(*operands)
@@ -215,8 +217,7 @@
     tproj_hbm,
     mid_ref,
     tmid_ref,
-    tquery_ref,
-    tgate_ref,
+    state_ref,
     tkv_ref,
     bias_ref,
     look_ref,
@@ -334,8 +335,7 @@
         wide = dot(normed, tproj_ref[:, pl.ds(base, 2 * KW)])
         return pltpu.roll(wide, lax.rem(2 * KW - (start - base), 2 * KW), 1)[:, :KW]
 
-    tquery_ref[...] = head_part(0)[:, :HDT].astype(bf16)
-    tgate_ref[...] = sigmoid(head_part(1)[:, :HDT])
+    state_ref[...] = jnp.concatenate([head_part(0), sigmoid(head_part(1))], axis=1)
     keyvals = jnp.concatenate([head_part(2).T[:HDT], head_part(3).T[:HDT]], axis=0).astype(bf16)
     for k in range(tkv_ref.shape[0]):
         tkv_ref[k] = keyvals
@@ -350,8 +350,7 @@
     out_shape = [
         jax.ShapeDtypeStruct((atoms, CA), bf16),
         jax.ShapeDtypeStruct((rows, CS), bf16),
-        jax.ShapeDtypeStruct((rows, HDT), bf16),
-        jax.ShapeDtypeStruct((rows, HDT), f32),
+        jax.ShapeDtypeStruct((rows, 2 * KW), f32),
         jax.ShapeDtypeStruct((copies, 2 * HDT, rows), bf16),
     ]
     return pl.pallas_call(
@@ -366,7 +365,7 @@
             pltpu.VMEM((rows, CS), f32),
         ]
         + held(fetched),
-        compiler_params=pltpu.CompilerParams(vmem_limit_bytes=56 * 2**20),
+        compiler_params=pltpu.CompilerParams(vmem_limit_bytes=44 * 2**20),
         cost_estimate=pl.CostEstimate(
             flops=10**10, bytes_accessed=2**24, transcendentals=2**22
         ),
@@ -375,37 +374,26 @@
 
 
 def tokens_body(
-    place,
-    strength,
-    mine_ref,
-    chain_ref,
-    query_hbm,
-    gate_hbm,
-    kv_hbm,
-    bias_hbm,
-    out_ref,
-    query_ref,
-    gate_ref,
-    kv_ref,
-    bias_ref,
-    sems,
+    place, strength, chain_ref, state_hbm, kv_hbm, bias_hbm, out_ref, state_ref, kv_ref, bias_ref, sems
 ):
-    copies = fetch(
-        (query_hbm, gate_hbm, kv_hbm, bias_hbm), (query_ref, gate_ref, kv_ref, bias_ref), sems
-    )
+    copies = fetch((state_hbm, kv_hbm, bias_hbm), (state_ref, kv_ref, bias_ref), sems)
+    col = place[1]
+    rows = state_ref.shape[0]
+    own = pl.multiple_of(place[0] * rows, rows)
+    mine = chain_ref[:, pl.ds(own, rows)].astype(f32)
+    mine = jnp.broadcast_to(mine, (KW, rows)).T
+    mine = jnp.concatenate([mine] * (rows // KW), axis=1).astype(jnp.int32)
     for copy in copies:
         copy.wait()
-    col = place[1]
-    rows = query_ref.shape[0]
+    query = state_ref[:, :HDT].astype(bf16)
     shards, cols = bias_ref.shape[0], bias_ref.shape[2]
-    query = query_ref[...]
     strong = strength[col]
     scores = []
     for r in range(kv_ref.shape[0]):
         raw = dot(query, kv_ref[r, :HDT, :]) * HDT ** (-0.5)
         per = rows // cols
         bias = jnp.concatenate([bias_ref[r * per + k].astype(f32) for k in range(per)], axis=1)
-        same = mine_ref[...] == chain_ref[:, r * rows : (r + 1) * rows]
+        same = mine == chain_ref[:, r * rows : (r + 1) * rows]
         scores.append(raw + bias + jnp.where(same, strong, 0.0))
     top = scores[0]
     for part in scores[1:]:
@@ -419,42 +407,43 @@
     out = jnp.zeros((rows, HDT), f32)
     for r in range(kv_ref.shape[0]):
         out = out + dot_nt(exps[r].astype(bf16), kv_ref[r, HDT:, :])
-    gated = out / total * gate_ref[...]
+    gated = out / total * state_ref[:, KW : KW + HDT]
     wide = jnp.concatenate([gated, jnp.zeros((rows, KW - HDT), f32)], axis=1)
     gated = wide.T[:HDT].astype(bf16)
     for k in range(out_ref.shape[0]):
         out_ref[k] = gated
 
 
-def token_attention(place, query, gate, kv, bias, mine, chain, strength):
-    rows = query.shape[0]
-    shards = bias.shape[0]
-    out_shape = jax.ShapeDtypeStruct((shards, HDT, rows), bf16)
+def token_attention(place, state, kv, bias, chain, strength):
+    rows = state.shape[0]
+    out_shape = jax.ShapeDtypeStruct((bias.shape[0], HDT, rows), bf16)
     return pl.pallas_call(
         tokens_body,
         grid=(1,),
-        in_specs=[SMEM] * 2 + [full(mine), full(chain)] + [ANY] * 4,
+        in_specs=[SMEM] * 2 + [full(chain)] + [HBM] * 3,
         out_specs=full(out_shape),
         out_shape=out_shape,
-        scratch_shapes=held((query, gate, kv, bias)),
-        compiler_params=pltpu.CompilerParams(vmem_limit_bytes=48 * 2**20),
+        scratch_shapes=held((state, kv, bias)),
+        compiler_params=pltpu.CompilerParams(vmem_limit_bytes=24 * 2**20),
         cost_estimate=pl.CostEstimate(flops=10**9, bytes_accessed=2**22, transcendentals=2**19),
         name="tokens",
-    )(place, strength, mine, chain, query, gate, kv, bias)
+    )(place, strength, chain, state, kv, bias)
 
 
 def update_body(
     place,
-    exit_ref,
-    back_ref,
     tokens_ref,
     gated_hbm,
+    exit_hbm,
     tmid_hbm,
+    back_hbm,
     mid_hbm,
     tout_ref,
     aout_ref,
     gated_ref,
+    exit_ref,
     tmid_ref,
+    back_ref,
     mid_ref,
     sems,
 ):
@@ -462,7 +451,9 @@
     atoms, rows = aout_ref.shape[0], tmid_ref.shape[0]
     at = pl.multiple_of(col * atoms, atoms)
     copies = fetch(
-        (gated_hbm, tmid_hbm, mid_hbm.at[pl.ds(at, atoms)]), (gated_ref, tmid_ref, mid_ref), sems
+        (gated_hbm, exit_hbm, tmid_hbm, back_hbm, mid_hbm.at[pl.ds(at, atoms)]),
+        (gated_ref, exit_ref, tmid_ref, back_ref, mid_ref),
+        sems,
     )
     for copy in copies:
         copy.wait()
@@ -484,13 +475,13 @@
     return pl.pallas_call(
         update_body,
         grid=(1,),
-        in_specs=[SMEM] + [full(a) for a in (exit_w, back, tokens)] + [ANY] * 3,
+        in_specs=[SMEM, full(tokens)] + [HBM] * 5,
         out_specs=[full(shape) for shape in out_shape],
         out_shape=out_shape,
-        scratch_shapes=held((gated, tmid, jax.ShapeDtypeStruct((atoms, CA), bf16))),
-        compiler_params=pltpu.CompilerParams(vmem_limit_bytes=48 * 2**20),
+        scratch_shapes=held((gated, exit_w, tmid, back, jax.ShapeDtypeStruct((atoms, CA), bf16))),
+        compiler_params=pltpu.CompilerParams(vmem_limit_bytes=24 * 2**20),
         name="updates",
-    )(place, exit_w, back, tokens, gated, tmid, mid)
+    )(place, tokens, gated, exit_w, tmid, back, mid)
 
 
 def local(
@@ -525,8 +516,15 @@
     at = lambda r, k, core: r * col_count + 2 * k + core
     last = col_count - 1
 
-    spread = jnp.broadcast_to(atom_single[None], (col_count,) + atom_single.shape)
-    atoms = lax.all_to_all(spread, "col", 0, 0).reshape(row_atoms, CA)
+    last = col_count - 1
+    halo = lax.ppermute(
+        jnp.where(col == last, atom_single[-HALO:], atom_single[:HALO]),
+        both,
+        [(r * col_count + last, (r + 1) * col_count) for r in range(row_count - 1)]
+        + [((r + 1) * col_count, r * col_count + last) for r in range(row_count - 1)],
+    )
+    packed = jnp.concatenate([atom_single, halo], axis=0)
+    spread = jnp.broadcast_to(packed[None], (col_count,) + packed.shape)
     ext_tokens = lax.dynamic_slice_in_dim(
         jnp.pad(atom_token, (HALO, HALO)), row * row_atoms, row_atoms + 2 * HALO
     )
@@ -538,15 +536,12 @@
 
     flip = ((col == 2 * row + 1) | (col == 2 * row + 2)).astype(jnp.int32)
     place = jnp.stack([row, col, jnp.int32(row_count), flip]).astype(jnp.int32)
+    spread, place = lax.optimization_barrier((spread, place))
+    shards = lax.all_to_all(spread, "col", 0, 0)
     center = jnp.asarray((np.eye(CZ) - 1.0 / CZ).astype(bf16))
     weights = (pair_up, pair_down, bias_heads.T, center)
     token_bias, band, edge = pair_rows(place, pair_tensor, weights, (), 0, PART, 2, True)
-    atoms, band, edge, token_bias = lax.optimization_barrier((atoms, band, edge, token_bias))
-
-    up = [(i, i + 1) for i in range(row_count - 1)]
-    down = [(i + 1, i) for i in range(row_count - 1)]
-    before = lax.ppermute(atoms[-HALO:], "row", up)
-    after = lax.ppermute(atoms[:HALO], "row", down)
+    shards, band, edge, token_bias = lax.optimization_barrier((shards, band, edge, token_bias))
 
     here = col // 2 == row
     even = col % 2 == 0
@@ -575,9 +570,7 @@
     (token_bias,) = pair_rows(
         place, pair_tensor, weights, (token_bias,), 2 * PART, rows - 2 * PART, 1, False
     )
-    band_y, edges, before, after, token_bias = lax.optimization_barrier(
-        (band_y, edges, before, after, token_bias)
-    )
+    band_y, edges, token_bias = lax.optimization_barrier((band_y, edges, token_bias))
     edge = edges[0] + edges[1]
     blank = jnp.zeros((HA, REACH - HALO, cols), bf16)
     edge = jnp.where(
@@ -602,14 +595,15 @@
         )
         for step in range(1, ring)
     ]
-    parts = project_atoms(atoms, before, after, atom_gain[None], atom_proj)
-    sent, parts = lax.optimization_barrier((sent, parts))
+    parts = project_atoms(shards, atom_gain[None], atom_proj)
+    gain = token_gain[None]
+    sent, parts, gain, ext_tokens = lax.optimization_barrier((sent, parts, gain, ext_tokens))
     band = band + sent[0] + sent[1] + sent[2]
     other = lax.ppermute(band, "col", [(i, i ^ 1) for i in range(col_count)])
     token_bias, band = lax.optimization_barrier((token_bias, band))
     head_bias = lax.all_to_all(token_bias, "col", 0, 0)
 
-    atom_mid, token_mid, query, gate, keyvals = atom_attention(
+    atom_mid, token_mid, state, keyvals = atom_attention(
         place,
         (band, other),
         parts,
@@ -617,15 +611,13 @@
         atom_exit,
         atom_pool,
         token_single,
-        token_gain[None],
+        gain,
         token_proj,
         row_count,
     )
+    keyvals, head_bias = lax.optimization_barrier((keyvals, head_bias))
     keyvals = lax.all_to_all(keyvals, "row", 0, 0)
-    mine = lax.dynamic_slice_in_dim(chain_index, row * rows, rows)
-    gated = token_attention(
-        place, query, gate, keyvals, head_bias, mine[:, None], chain_index[None], chain_bias
-    )
+    gated = token_attention(place, state, keyvals, head_bias, chain_index[None], chain_bias)
     gated = lax.all_to_all(gated, "col", 0, 0).reshape(CS, rows)
     return tuple(
         updates(

time: 145 us -> 138 us (0.952)
  waiting for transfers between devices: 24.5 us -> 12.5 us
  starting transfers between devices: 38.5 us -> 42.8 us
  local copies, waits for them, and re-layouts: 13.5 us -> 17 us
  Pallas kernels: 47.1 us -> 44.8 us
  blocking collectives: 16.1 us -> 13.9 us
    all_to_all x1, waiting for transfers between devices: 15.1 us -> 0.01 us  [local(): head_bias = lax.all_to_all(token_bias, 'col', 0, 0)]
    all_to_all x1, starting transfers between devices: 9.46 us -> 17.2 us  [local(): shards = lax.all_to_all(spread, 'col', 0, 0)]
    unnamed x44 -> x58, local copies, waits for them, and re-layouts: 8.55 us -> 15.9 us
    ppermute x2 -> x1, starting transfers between devices: 5.23 us -> 0.65 us  [local(): lax.ppermute(jnp.where(col == last, atom_single[-HALO:], atom_single[:HAL...]
    all_to_all x1, starting transfers between devices: 4.26 us -> 8.57 us  [local(): gated = lax.all_to_all(gated, 'col', 0, 0).reshape(CS, rows)]
    ppermute x3, waiting for transfers between devices: 0.16 us -> 3.36 us  [local(): lax.ppermute(band, both, [(at(r, k, core), at(r, flat(k, step), core)) fo...]
    broadcast_in_dim x3 -> x2, local copies, waits for them, and re-layouts: 3.7 us -> 1.06 us  [the longest x1 1.06 us: local(): spread = jnp.broadcast_to(packed[None], (col_count,) + packed.shape)]
    pallas_call x1, Pallas kernels: 13.1 us -> 10.6 us  [atom_attention(): pl.pallas_call(atoms_body, grid=(1,), in_specs=[SMEM] + [full(array) for...]
  transfers between devices with their start and end apart: 12 -> 11, of which waited for: 3 -> 2; matrix products, arithmetic and copies ran while one was open for 4% -> 1% of each run, Pallas kernels for 20% -> 28%
where the time goes in v4:
time: 138 us; the launch traced here: 136 us
  Pallas kernels  44.8 us (32%)
  starting transfers between devices  42.8 us (31%)
  local copies, waits for them, and re-layouts  17 us (12%)
  blocking collectives  13.9 us (10%)
  waiting for transfers between devices  12.5 us (9%)
  other arithmetic  4.26 us (3%)
    pallas_call x2, Pallas kernels, pair_rows(): pl.pallas_call(functools.partial(pair_body, bands=bands), grid_spec=pltpu...  26.9 us
    all_to_all x1, starting transfers between devices, local(): shards = lax.all_to_all(spread, 'col', 0, 0)  17.2 us
    unnamed x58, local copies, waits for them, and re-layouts  15.9 us
    all_to_all x1, blocking collectives, local(): keyvals = lax.all_to_all(keyvals, 'row', 0, 0)  13.9 us
    pallas_call x1, Pallas kernels, atom_attention(): pl.pallas_call(atoms_body, grid=(1,), in_specs=[SMEM] + [full(array) for...  10.6 us
    all_to_all x1, waiting for transfers between devices, local(): gated = lax.all_to_all(gated, 'col', 0, 0).reshape(CS, rows)  9.13 us
    all_to_all x1, starting transfers between devices, local(): gated = lax.all_to_all(gated, 'col', 0, 0).reshape(CS, rows)  8.57 us
    ppermute x1, starting transfers between devices, local(): lax.ppermute(band, both, [(at(r, r, core), at(r, across(r), core)) for r...  4.81 us
  transfers between devices with their start and end apart: 11, of which 2 were waited for; matrix products, arithmetic and copies ran while one was open for 1% of the time, Pallas kernels for 28%

profile of v4, /device:TPU:1, one launch (start us, length us, event | category | flops | bytes accessed | tf_op | source)
XLA Modules:
  0.0 136.4 jit_solution(9387845335179573176)
XLA Ops:
  0.6 0.7 slice_select_fusion
  1.4 0.7 collective-permute-start
  2.1 0.6 pad_add_fusion.place
  2.6 0.0 collective-permute-done
  2.6 0.8 pad_maximum_fusion
  3.4 1.1 broadcast_in_dim.25
  4.5 17.2 %all-to-all-start = ((bf16[16,192,128]{2,1,0:T(8,128)(2,1)}), bf16[16,192,128]{2,1,0:T(8,128)(2,1)S(1)}, u32[]{:S(2)}, u32[]{:S(2)}) async-start(bf16[16,192,128]{2,1,0:T(8,128)(2,1)} %broadcast_in_dim.25), calls=%async_computation | async-start | bytes 1572864 | tf_op jit(solution)/shard_map/all_to_all | solution.py:540
  21.7 21.3 %pair.2 = (bf16[16,256,128]{2,1,0:T(8,128)(2,1)}, bf16[4,224,128]{2,1,0:T(8,128)(2,1)}, bf16[4,64,128]{2,1,0:T(8,128)(2,1)}) custom-call(s32[4]{0:T(128)} %pad_add_fusion.place, bf16[256,128,128]{2,1,0:T(8,128)(2,1)} %pair_ref.3, bf16[128,512]{1,0:T(8,128)(2,1)} %up_ref.3, bf16[256,128]{1,0:T(8,128)(2,1)} %down_ref.3, bf16[20,128]{1,0:T(8,128)(2,1)} %bitcast.12, ...), custom_call_target="tpu_custom_call" | custom-call | flops 14336000000 | bytes 8601600 | tf_op jit(solution)/shard_map/pair/pallas_call | solution.py:145
  43.0 0.0 all-to-all-done.shards_ref
  43.0 1.1 select_select_fusion.1
  44.1 4.8 %collective-permute-start.1 = (bf16[4,208,128]{2,1,0:T(8,128)(2,1)S(1)}, bf16[4,208,128]{2,1,0:T(8,128)(2,1)S(1)}, u32[]{:S(2)}, u32[]{:S(2)}) collective-permute-start(bf16[4,208,128]{2,1,0:T(8,128)(2,1)S(1)} %select_select_fusion.1), channel_id=1, source_target_pairs={{0,8},{1,9},{18,26},{19,27},{36,44},{37,45},{54,62},{55,63},{72,64... | collective-permute-start | bytes 638984 | tf_op jit(solution)/shard_map/ppermute | solution.py:556
  48.9 0.0 copy-start.26
  48.9 0.0 copy-start.28
  48.9 0.0 copy-start.27
  48.9 0.0 copy-start.9
  49.0 0.0 copy-start.12
  49.0 0.8 collective-permute-start.3
  49.8 1.5 %collective-permute-start.2 = (bf16[4,64,128]{2,1,0:T(8,128)(2,1)}, bf16[4,64,128]{2,1,0:T(8,128)(2,1)S(1)}, u32[]{:S(2)}, u32[]{:S(2)}) collective-permute-start(bf16[4,64,128]{2,1,0:T(8,128)(2,1)} %get-tuple-element.44), channel_id=1, source_target_pairs={{17,18},{35,36},{53,54},{71,72},{89,90},{107,108},{125,126},{2,1},... | collective-permute-start | bytes 196616 | tf_op jit(solution)/shard_map/ppermute | solution.py:562
  51.2 5.6 %pair.3 = bf16[16,256,128]{2,1,0:T(8,128)(2,1)} custom-call(s32[4]{0:T(128)} %pad_add_fusion.place, bf16[256,128,128]{2,1,0:T(8,128)(2,1)} %pair_ref.3, bf16[128,512]{1,0:T(8,128)(2,1)} %up_ref.3, bf16[256,128]{1,0:T(8,128)(2,1)} %down_ref.3, bf16[20,128]{1,0:T(8,128)(2,1)} %bitcast.13, ...), custom_call_target="tpu_custom_call", output_to_operand_aliasing={{}: (6, {})} | custom-call | flops 2048000000 | bytes 1228800 | tf_op jit(solution)/shard_map/pair/pallas_call | solution.py:145
  56.8 0.0 collective-permute-done.3
  56.8 0.0 collective-permute-done.2
  56.8 0.0 collective-permute-done.1
  56.9 0.0 copy-done.26
  56.9 0.2 select_select_fusion
  57.0 1.3 collective-permute-start.6
  58.4 1.3 collective-permute-start.5
  59.7 1.3 collective-permute-start.4
  61.0 0.1 fusion
  61.1 1.1 atom_projections.1
  62.3 1.0 copy-done.14
  63.3 0.8 copy-done.18
  64.1 0.8 copy-done.20
  64.9 0.8 copy-done.22
  65.7 0.0 collective-permute-done.6
  65.7 0.0 collective-permute-done.5
  65.7 3.4 %collective-permute-done.4 = bf16[4,208,128]{2,1,0:T(8,128)(2,1)S(1)} collective-permute-done((bf16[4,208,128]{2,1,0:T(8,128)(2,1)S(1)}, bf16[4,208,128]{2,1,0:T(8,128)(2,1)S(1)}, u32[]{:S(2)}, u32[]{:S(2)}) %collective-permute-start.4) | collective-permute-done | bytes 213024 | tf_op jit(solution)/shard_map/ppermute | solution.py:586
  69.1 0.1 add_add_fusion.half_hbm
  69.1 0.0 copy-start.1
  69.1 0.7 collective-permute-start.7
  69.8 4.7 %all-to-all-start.1 = ((bf16[16,256,128]{2,1,0:T(8,128)(2,1)}), bf16[16,256,128]{2,1,0:T(8,128)(2,1)S(1)}, u32[]{:S(2)}, u32[]{:S(2)}) async-start(bf16[16,256,128]{2,1,0:T(8,128)(2,1)} %pair.3), calls=%async_computation.1 | async-start | bytes 2097152 | tf_op jit(solution)/shard_map/all_to_all | solution.py:604
  74.6 0.0 collective-permute-done.7.other_hbm
  74.6 0.7 copy-done.6
  75.3 0.9 copy-done.2
  76.2 1.0 copy-done.5
  77.2 0.9 copy-done.7
  78.1 0.9 copy-done.8
  79.1 1.2 copy-done.15
  80.3 1.1 copy-done.19
  81.3 1.1 copy-done.21
  82.4 1.1 copy-done.23
  83.4 1.0 copy-done.25
  84.5 10.6 %atoms.1 = (bf16[2048,128]{1,0:T(8,128)(2,1)S(1)}, bf16[256,768]{1,0:T(8,128)(2,1)S(1)}, f32[256,256]{1,0:T(8,128)S(1)}, bf16[8,96,256]{2,1,0:T(8,128)(2,1)S(1)}) custom-call(s32[4]{0:T(128)S(1)} %copy-done.4, s32[1,2176]{1,0:T(1,128)S(1)} %broadcast_in_dim.31.tokens_ref, bf16[128,128]{1,0:T(8,128)(2,1)S(1)} %copy-done.10, bf16[128,768]{1,0:T(8,128)(2,1)S(1)} %copy-done.8, ...), custom_call_target="tpu_custom_call" | custom-call | flops 10000000000 | bytes 16777216 | tf_op jit(solution)/shard_map/atoms/pallas_call | solution.py:356
  95.1 0.0 copy-start.16
  95.1 0.7 copy-done.16
  95.8 0.0 all-to-all-done.1.bias_hbm
  95.8 13.9 %all_to_all.20.kv_hbm = bf16[8,96,256]{2,1,0:T(8,128)(2,1)S(1)} all-to-all(bf16[8,96,256]{2,1,0:T(8,128)(2,1)S(1)} %get-tuple-element.70), channel_id=1, replica_groups=mesh['row'=8,'col'=16] {'row'}, dimensions={0} | all-to-all | bytes 786432 | tf_op jit(solution)/shard_map/all_to_all | solution.py:619
  109.7 0.0 copy-done.11
  109.7 0.9 copy-done.17
  110.7 3.2 %tokens.1 = bf16[16,48,256]{2,1,0:T(8,128)(2,1)} custom-call(s32[4]{0:T(128)S(1)} %copy-done.4, f32[16]{0:T(128)S(1)} %copy-done.13, s32[1,2048]{1,0:T(1,128)S(1)} %bitcast.10, f32[256,256]{1,0:T(8,128)S(1)} %copy-done.17, bf16[8,96,256]{2,1,0:T(8,128)(2,1)S(1)} %all_to_all.20.kv_hbm, bf16[16,256,128]{2,1,0:T(8,128)(2,1)S(1)} %all-to-all-done.1.bias_hbm), custom_call_target="tpu_custom_call" | custom-call | flops 1000000000 | bytes 4194304 | tf_op jit(solution)/shard_map/tokens/pallas_call | solution.py:420
  113.9 8.6 %all-to-all-start.3 = ((bf16[16,48,256]{2,1,0:T(8,128)(2,1)}), bf16[16,48,256]{2,1,0:T(8,128)(2,1)S(1)}, u32[]{:S(2)}, u32[]{:S(2)}) async-start(bf16[16,48,256]{2,1,0:T(8,128)(2,1)} %tokens.1), calls=%async_computation.3 | async-start | bytes 786432 | tf_op jit(solution)/shard_map/all_to_all | solution.py:621
  122.5 0.8 subtract_bitcast_fusion.tokens_ref
  123.2 9.1 %all-to-all-done.3 = bf16[16,48,256]{2,1,0:T(8,128)(2,1)S(1)} async-done(((bf16[16,48,256]{2,1,0:T(8,128)(2,1)}), bf16[16,48,256]{2,1,0:T(8,128)(2,1)S(1)}, u32[]{:S(2)}, u32[]{:S(2)}) %all-to-all-start.3) | async-done | bytes 393248 | tf_op jit(solution)/shard_map/all_to_all | solution.py:621
  132.4 0.9 copy-done.3
  133.3 3.0 %updates.1 = (bf16[256,768]{1,0:T(8,128)(2,1)}, bf16[128,128]{1,0:T(8,128)(2,1)}) custom-call(s32[4]{0:T(128)S(1)} %copy-done.4, s32[1,128]{1,0:T(1,128)S(1)} %subtract_bitcast_fusion.tokens_ref, bf16[768,256]{1,0:T(8,128)(2,1)S(1)} %bitcast.9, bf16[768,768]{1,0:T(8,128)(2,1)S(1)} %copy-done, bf16[256,768]{1,0:T(8,128)(2,1)S(1)} %get-tuple-element.72.tmid_hbm, ...), custom_call_target="tpu_custom_call" | custom-call | tf_op jit(solution)/shard_map/updates/pallas_call | solution.py:475
  (37 shorter events, 0.1 us)
Async XLA Ops:
  1.4 1.3 collective-permute-start
  4.5 38.5 %all-to-all-start = ((bf16[16,192,128]{2,1,0:T(8,128)(2,1)}), bf16[16,192,128]{2,1,0:T(8,128)(2,1)S(1)}, u32[]{:S(2)}, u32[]{:S(2)}) async-start(bf16[16,192,128]{2,1,0:T(8,128)(2,1)} %broadcast_in_dim.25), calls=%async_computation | async-start | bytes 1572864 | tf_op jit(solution)/shard_map/all_to_all | solution.py:540
  44.1 12.7 %collective-permute-start.1 = (bf16[4,208,128]{2,1,0:T(8,128)(2,1)S(1)}, bf16[4,208,128]{2,1,0:T(8,128)(2,1)S(1)}, u32[]{:S(2)}, u32[]{:S(2)}) collective-permute-start(bf16[4,208,128]{2,1,0:T(8,128)(2,1)S(1)} %select_select_fusion.1), channel_id=1, source_target_pairs={{0,8},{1,9},{18,26},{19,27},{36,44},{37,45},{54,62},{55,63},{72,64... | collective-permute-start | bytes 638984 | tf_op jit(solution)/shard_map/ppermute | solution.py:556
  48.9 8.0 %copy-start.26 = (bf16[4,224,128]{2,1,0:T(8,128)(2,1)S(1)}, bf16[4,224,128]{2,1,0:T(8,128)(2,1)}, u32[]{:S(2)}) copy-start(bf16[4,224,128]{2,1,0:T(8,128)(2,1)} %get-tuple-element.43) | copy-start | bytes 688132
  48.9 12.1 %copy-start.28 = (f32[768]{0:T(1024)S(1)}, f32[768]{0:T(1024)}, u32[]{:S(2)}) copy-start(f32[768]{0:T(1024)} %param.30) | copy-start | bytes 9220
  48.9 12.1 %copy-start.27 = (s32[16384]{0:T(1024)S(1)}, s32[16384]{0:T(1024)}, u32[]{:S(2)}) copy-start(s32[16384]{0:T(1024)} %param.21) | copy-start | bytes 196612
  48.9 12.2 %copy-start.9 = (bf16[128,512]{1,0:T(8,128)(2,1)S(1)}, bf16[128,512]{1,0:T(8,128)(2,1)}, u32[]{:S(2)}) copy-start(bf16[128,512]{1,0:T(8,128)(2,1)} %proj_ref.1) | copy-start | bytes 393220
  49.0 12.2 %copy-start.12 = (f32[128]{0:T(128)S(1)}, f32[128]{0:T(128)}, u32[]{:S(2)}) copy-start(f32[128]{0:T(128)} %param.26) | copy-start | bytes 1540
  49.0 7.8 %collective-permute-start.3 = (bf16[4,64,128]{2,1,0:T(8,128)(2,1)}, bf16[4,64,128]{2,1,0:T(8,128)(2,1)S(1)}, u32[]{:S(2)}, u32[]{:S(2)}) collective-permute-start(bf16[4,64,128]{2,1,0:T(8,128)(2,1)} %get-tuple-element.44), channel_id=1, source_target_pairs={{17,26},{35,44},{53,62},{71,64},{89,82},{107,100},{125,118},{2,9},... | collective-permute-start | bytes 196616 | tf_op jit(solution)/shard_map/ppermute | solution.py:562
  49.8 7.0 %collective-permute-start.2 = (bf16[4,64,128]{2,1,0:T(8,128)(2,1)}, bf16[4,64,128]{2,1,0:T(8,128)(2,1)S(1)}, u32[]{:S(2)}, u32[]{:S(2)}) collective-permute-start(bf16[4,64,128]{2,1,0:T(8,128)(2,1)} %get-tuple-element.44), channel_id=1, source_target_pairs={{17,18},{35,36},{53,54},{71,72},{89,90},{107,108},{125,126},{2,1},... | collective-permute-start | bytes 196616 | tf_op jit(solution)/shard_map/ppermute | solution.py:562
  56.8 18.5 %copy-start.4 = (s32[4]{0:T(128)S(1)}, s32[4]{0:T(128)}, u32[]{:S(2)}) copy-start(s32[4]{0:T(128)} %pad_add_fusion.place) | copy-start | bytes 52
  56.8 18.5 %copy-start.10 = (bf16[128,128]{1,0:T(8,128)(2,1)S(1)}, bf16[128,128]{1,0:T(8,128)(2,1)}, u32[]{:S(2)}) copy-start(bf16[128,128]{1,0:T(8,128)(2,1)} %exit_ref.1) | copy-start | bytes 98308
  57.0 8.7 %collective-permute-start.6 = (bf16[4,208,128]{2,1,0:T(8,128)(2,1)S(1)}, bf16[4,208,128]{2,1,0:T(8,128)(2,1)S(1)}, u32[]{:S(2)}, u32[]{:S(2)}) collective-permute-start(bf16[4,208,128]{2,1,0:T(8,128)(2,1)S(1)} %select_select_fusion), channel_id=1, source_target_pairs={{0,6},{1,7},{8,14},{9,15},{18,16},{19,17},{26,24},{27,25},{36,34},... | collective-permute-start | bytes 638984 | tf_op jit(solution)/shard_map/ppermute | solution.py:586
  58.4 7.3 %collective-permute-start.5 = (bf16[4,208,128]{2,1,0:T(8,128)(2,1)S(1)}, bf16[4,208,128]{2,1,0:T(8,128)(2,1)S(1)}, u32[]{:S(2)}, u32[]{:S(2)}) collective-permute-start(bf16[4,208,128]{2,1,0:T(8,128)(2,1)S(1)} %select_select_fusion), channel_id=1, source_target_pairs={{0,4},{1,5},{8,12},{9,13},{18,22},{19,23},{26,30},{27,31},{36,32},... | collective-permute-start | bytes 638984 | tf_op jit(solution)/shard_map/ppermute | solution.py:586
  59.7 9.4 %collective-permute-start.4 = (bf16[4,208,128]{2,1,0:T(8,128)(2,1)S(1)}, bf16[4,208,128]{2,1,0:T(8,128)(2,1)S(1)}, u32[]{:S(2)}, u32[]{:S(2)}) collective-permute-start(bf16[4,208,128]{2,1,0:T(8,128)(2,1)S(1)} %select_select_fusion), channel_id=1, source_target_pairs={{0,2},{1,3},{8,10},{9,11},{18,20},{19,21},{26,28},{27,29},{36,38},... | collective-permute-start | bytes 638984 | tf_op jit(solution)/shard_map/ppermute | solution.py:586
  62.3 1.0 copy-start.14
  63.3 0.8 copy-start.18
  64.1 0.8 copy-start.20
  64.9 0.8 copy-start.22
  65.7 8.9 %copy-start.24 = (bf16[2048,128]{1,0:T(8,128)(2,1)}, bf16[2048,128]{1,0:T(8,128)(2,1)S(1)}, u32[]{:S(2)}) copy-start(bf16[2048,128]{1,0:T(8,128)(2,1)S(1)} %get-tuple-element.63.query_hbm) | copy-start | bytes 1572868
  69.1 5.4 %copy-start.1 = (bf16[4,208,128]{2,1,0:T(8,128)(2,1)}, bf16[4,208,128]{2,1,0:T(8,128)(2,1)S(1)}, u32[]{:S(2)}) copy-start(bf16[4,208,128]{2,1,0:T(8,128)(2,1)S(1)} %add_add_fusion.half_hbm) | copy-start | bytes 638980
  69.1 5.4 %collective-permute-start.7 = (bf16[4,208,128]{2,1,0:T(8,128)(2,1)S(1)}, bf16[4,208,128]{2,1,0:T(8,128)(2,1)S(1)}, u32[]{:S(2)}, u32[]{:S(2)}) collective-permute-start(bf16[4,208,128]{2,1,0:T(8,128)(2,1)S(1)} %add_add_fusion.half_hbm), channel_id=1, source_target_pairs={{0,1},{1,0},{2,3},{3,2},{4,5},{5,4},{6,7},{7,6},{8,9},{9,8},{10,11... | collective-permute-start | bytes 638984 | tf_op jit(solution)/shard_map/ppermute | solution.py:602
  69.8 26.0 %all-to-all-start.1 = ((bf16[16,256,128]{2,1,0:T(8,128)(2,1)}), bf16[16,256,128]{2,1,0:T(8,128)(2,1)S(1)}, u32[]{:S(2)}, u32[]{:S(2)}) async-start(bf16[16,256,128]{2,1,0:T(8,128)(2,1)} %pair.3), calls=%async_computation.1 | async-start | bytes 2097152 | tf_op jit(solution)/shard_map/all_to_all | solution.py:604
  74.6 0.7 copy-start.6
  75.3 0.9 copy-start.2
  76.2 1.0 copy-start.5
  77.2 0.9 copy-start.7
  78.1 0.9 copy-start.8
  79.1 1.2 copy-start.15
  80.3 1.1 copy-start.19
  81.3 1.1 copy-start.21
  82.4 1.1 copy-start.23
  83.4 1.0 copy-start.25
  84.5 25.2 %copy-start.11 = (s32[2048]{0:T(1024)S(1)}, s32[2048]{0:T(1024)}, u32[]{:S(2)}) copy-start(s32[2048]{0:T(1024)} %param.22) | copy-start | bytes 24580
  84.5 25.2 %copy-start.13 = (f32[16]{0:T(128)S(1)}, f32[16]{0:T(128)}, u32[]{:S(2)}) copy-start(f32[16]{0:T(128)} %strength.1) | copy-start | bytes 196
  95.1 0.7 copy-start.16
  95.8 36.6 %copy-start = (bf16[768,768]{1,0:T(8,128)(2,1)S(1)}, bf16[768,768]{1,0:T(8,128)(2,1)}, u32[]{:S(2)}) copy-start(bf16[768,768]{1,0:T(8,128)(2,1)} %exit_hbm.1) | copy-start | bytes 3538948
  109.7 1.0 copy-start.17
  113.9 18.5 %all-to-all-start.3 = ((bf16[16,48,256]{2,1,0:T(8,128)(2,1)}), bf16[16,48,256]{2,1,0:T(8,128)(2,1)S(1)}, u32[]{:S(2)}, u32[]{:S(2)}) async-start(bf16[16,48,256]{2,1,0:T(8,128)(2,1)} %tokens.1), calls=%async_computation.3 | async-start | bytes 786432 | tf_op jit(solution)/shard_map/all_to_all | solution.py:621
  132.4 0.9 copy-start.3

commit v5 on v4

--- a/solution.py
+++ b/solution.py
@@ -57,6 +57,7 @@
 SMEM = pl.BlockSpec(memory_space=pltpu.SMEM)
 ANY = pl.BlockSpec(memory_space=pl.ANY)
 HBM = pl.BlockSpec(memory_space=pltpu.HBM)
+VMEM = pl.BlockSpec(memory_space=pltpu.VMEM)
 
 
 def full(array):
@@ -161,26 +162,28 @@
     )(place, pair, *weights, *before)
 
 
-def project_body(shards_ref, gain_ref, proj_ref, ext_ref, query_ref, key_ref, value_ref, gate_ref):
-    shards = shards_ref.shape[0]
-    atoms = query_ref.shape[0]
-    per = atoms // shards
-    ext_ref[:HALO] = shards_ref[0, per:]
-    for k in range(shards):
-        ext_ref[HALO + k * per : HALO + (k + 1) * per] = shards_ref[k, :per]
-    ext_ref[HALO + atoms :] = shards_ref[shards - 1, per:]
+def project_body(
+    atoms_ref, before_ref, after_ref, gain_ref, proj_ref, *refs
+):
+    outs, (ext_ref, query_ref, key_ref, value_ref, gate_ref, sems) = refs[:5], refs[5:]
+    atoms = atoms_ref.shape[0]
+    ext_ref[:HALO] = before_ref[...]
+    ext_ref[HALO : HALO + atoms] = atoms_ref[...]
+    ext_ref[HALO + atoms :] = after_ref[...]
     normed = (scaled(centered(ext_ref[...].astype(f32))) * gain_ref[...]).astype(bf16)
     own = normed[HALO : HALO + atoms]
     query_ref[...] = (dot(own, proj_ref[:, :CA]) * HDA ** (-0.5)).astype(bf16)
     key_ref[...] = dot(normed, proj_ref[:, CA : 2 * CA]).astype(bf16)
     value_ref[...] = dot(normed, proj_ref[:, 2 * CA : 3 * CA]).astype(bf16)
     gate_ref[...] = sigmoid(dot(own, proj_ref[:, 3 * CA :]))
-
-
-def project_atoms(shards, gain, proj):
-    count = shards.shape[0] * (shards.shape[1] - HALO)
+    for copy in fetch((ext_ref, query_ref, key_ref, value_ref, gate_ref), outs, sems):
+        copy.wait()
+
+
+def project_atoms(atoms, before, after, gain, proj):
+    count = atoms.shape[0]
     total = count + 2 * HALO
-    operands = (shards, gain, proj)
+    operands = (atoms, before, after, gain, proj)
     out_shape = [
         jax.ShapeDtypeStruct((total, CA), bf16),
         jax.ShapeDtypeStruct((count, CA), bf16),
@@ -192,9 +195,10 @@
         project_body,
         grid=(1,),
         in_specs=[full(array) for array in operands],
-        out_specs=[full(shape) for shape in out_shape],
+        out_specs=[HBM] * len(out_shape),
         out_shape=out_shape,
-        compiler_params=pltpu.CompilerParams(vmem_limit_bytes=20 * 2**20),
+        scratch_shapes=held(out_shape),
+        compiler_params=pltpu.CompilerParams(vmem_limit_bytes=24 * 2**20),
         cost_estimate=pl.CostEstimate(flops=10**9, bytes_accessed=2**22, transcendentals=2**18),
         name="atom_projections",
     )(*operands)
@@ -207,23 +211,21 @@
     pool_ref,
     single_ref,
     gain_ref,
-    half_hbm,
-    other_hbm,
+    half_ref,
+    other_ref,
     ext_hbm,
     query_hbm,
     key_hbm,
     value_hbm,
     gate_hbm,
     tproj_hbm,
-    mid_ref,
-    tmid_ref,
-    state_ref,
-    tkv_ref,
+    mid_hbm,
+    tmid_hbm,
+    state_hbm,
+    tkv_hbm,
     bias_ref,
     look_ref,
     sums_ref,
-    half_ref,
-    other_ref,
     ext_ref,
     query_ref,
     key_ref,
@@ -231,14 +233,17 @@
     gate_ref,
     tproj_ref,
     sems,
+    mid_ref,
+    tmid_ref,
+    state_ref,
+    tkv_ref,
+    out_sems,
 ):
     copies = fetch(
-        (half_hbm, other_hbm, ext_hbm, query_hbm, key_hbm, value_hbm, gate_hbm, tproj_hbm),
-        (half_ref, other_ref, ext_ref, query_ref, key_ref, value_ref, gate_ref, tproj_ref),
+        (ext_hbm, query_hbm, key_hbm, value_hbm, gate_hbm, tproj_hbm),
+        (ext_ref, query_ref, key_ref, value_ref, gate_ref, tproj_ref),
         sems,
     )
-    for copy in copies[:-1]:
-        copy.wait()
     row, col, row_count = place[0], place[1], place[2]
     total = ext_ref.shape[0]
     atoms = query_ref.shape[0]
@@ -255,6 +260,8 @@
         bias_ref[:, base + 2 * KW : base + 3 * KW] = jnp.concatenate(
             [first[REACH - HALO :], jnp.zeros((rows - 2 * HALO, KW), bf16), second[:HALO]], axis=0
         )
+    for copy in copies[:-1]:
+        copy.wait()
     lane = lax.broadcasted_iota(jnp.int32, (KW, 3 * KW), 1)
     for t in range(total // KW):
         at = slice(t * KW, (t + 1) * KW)
@@ -324,6 +331,7 @@
     counts = lax.fori_loop(0, atoms // GROUP, group, jnp.zeros((rows, 1), f32))
     token_mid = (single_ref[...].astype(f32) + sums_ref[...] / counts).astype(bf16)
     tmid_ref[...] = token_mid
+    stores = fetch((mid_ref, tmid_ref), (mid_hbm, tmid_hbm), out_sems)
     normed = (scaled(centered(token_mid.astype(f32))) * gain_ref[...]).astype(bf16)
 
     copies[-1].wait()
@@ -336,9 +344,14 @@
         return pltpu.roll(wide, lax.rem(2 * KW - (start - base), 2 * KW), 1)[:, :KW]
 
     state_ref[...] = jnp.concatenate([head_part(0), sigmoid(head_part(1))], axis=1)
-    keyvals = jnp.concatenate([head_part(2).T[:HDT], head_part(3).T[:HDT]], axis=0).astype(bf16)
-    for k in range(tkv_ref.shape[0]):
-        tkv_ref[k] = keyvals
+    keyvals = jnp.concatenate([head_part(2).T[:HDT], head_part(3).T[:HDT]], axis=0)
+    tkv_ref[...] = keyvals.astype(bf16)
+    last = [(state_ref, state_hbm)] + [(tkv_ref, tkv_hbm.at[k]) for k in range(tkv_hbm.shape[0])]
+    for i, (source, target) in enumerate(last):
+        stores.append(pltpu.make_async_copy(source, target, out_sems.at[2 + i]))
+        stores[-1].start()
+    for copy in stores:
+        copy.wait()
 
 
 def atom_attention(place, bands, parts, tokens, exit_w, pool, single, gain, tproj, copies):
@@ -346,7 +359,7 @@
     atoms = total - 2 * HALO
     rows = single.shape[0]
     operands = (tokens, exit_w, pool, single, gain)
-    fetched = (*bands, *parts, tproj)
+    fetched = (*parts, tproj)
     out_shape = [
         jax.ShapeDtypeStruct((atoms, CA), bf16),
         jax.ShapeDtypeStruct((rows, CS), bf16),
@@ -356,21 +369,26 @@
     return pl.pallas_call(
         atoms_body,
         grid=(1,),
-        in_specs=[SMEM] + [full(array) for array in operands] + [ANY] * len(fetched),
-        out_specs=[full(shape) for shape in out_shape],
+        in_specs=[SMEM]
+        + [full(array) for array in operands]
+        + [VMEM] * len(bands)
+        + [HBM] * len(fetched),
+        out_specs=[HBM] * len(out_shape),
         out_shape=out_shape,
         scratch_shapes=[
             pltpu.VMEM((rows, HA * 3 * KW), bf16),
             pltpu.VMEM((total, CA + 3 * KW), bf16),
             pltpu.VMEM((rows, CS), f32),
         ]
-        + held(fetched),
+        + held(fetched)
+        + [pltpu.VMEM(a.shape, a.dtype) for a in out_shape[:3]]
+        + [pltpu.VMEM((2 * HDT, rows), bf16), pltpu.SemaphoreType.DMA((3 + copies,))],
         compiler_params=pltpu.CompilerParams(vmem_limit_bytes=44 * 2**20),
         cost_estimate=pl.CostEstimate(
             flops=10**10, bytes_accessed=2**24, transcendentals=2**22
         ),
         name="atoms",
-    )(place, *operands, *fetched)
+    )(place, *operands, *bands, *fetched)
 
 
 def tokens_body(
@@ -516,15 +534,8 @@
     at = lambda r, k, core: r * col_count + 2 * k + core
     last = col_count - 1
 
-    last = col_count - 1
-    halo = lax.ppermute(
-        jnp.where(col == last, atom_single[-HALO:], atom_single[:HALO]),
-        both,
-        [(r * col_count + last, (r + 1) * col_count) for r in range(row_count - 1)]
-        + [((r + 1) * col_count, r * col_count + last) for r in range(row_count - 1)],
-    )
-    packed = jnp.concatenate([atom_single, halo], axis=0)
-    spread = jnp.broadcast_to(packed[None], (col_count,) + packed.shape)
+    spread = jnp.broadcast_to(atom_single[None], (col_count,) + atom_single.shape)
+    shards = lax.all_to_all(spread, "col", 0, 0)
     ext_tokens = lax.dynamic_slice_in_dim(
         jnp.pad(atom_token, (HALO, HALO)), row * row_atoms, row_atoms + 2 * HALO
     )
@@ -536,8 +547,6 @@
 
     flip = ((col == 2 * row + 1) | (col == 2 * row + 2)).astype(jnp.int32)
     place = jnp.stack([row, col, jnp.int32(row_count), flip]).astype(jnp.int32)
-    spread, place = lax.optimization_barrier((spread, place))
-    shards = lax.all_to_all(spread, "col", 0, 0)
     center = jnp.asarray((np.eye(CZ) - 1.0 / CZ).astype(bf16))
     weights = (pair_up, pair_down, bias_heads.T, center)
     token_bias, band, edge = pair_rows(place, pair_tensor, weights, (), 0, PART, 2, True)
@@ -595,13 +604,18 @@
         )
         for step in range(1, ring)
     ]
-    parts = project_atoms(shards, atom_gain[None], atom_proj)
+    atoms, _ = lax.optimization_barrier((shards.reshape(row_atoms, CA), band))
+    before = lax.ppermute(
+        atoms[-HALO:], "row", [(i, i + 1) for i in range(row_count - 1)]
+    )
+    after = lax.ppermute(atoms[:HALO], "row", [(i + 1, i) for i in range(row_count - 1)])
+    parts = project_atoms(atoms, before, after, atom_gain[None], atom_proj)
     gain = token_gain[None]
+    parts, token_bias = lax.optimization_barrier((parts, token_bias))
+    head_bias = lax.all_to_all(token_bias, "col", 0, 0)
     sent, parts, gain, ext_tokens = lax.optimization_barrier((sent, parts, gain, ext_tokens))
     band = band + sent[0] + sent[1] + sent[2]
     other = lax.ppermute(band, "col", [(i, i ^ 1) for i in range(col_count)])
-    token_bias, band = lax.optimization_barrier((token_bias, band))
-    head_bias = lax.all_to_all(token_bias, "col", 0, 0)
 
     atom_mid, token_mid, state, keyvals = atom_attention(
         place,

time: 138 us -> 137 us (level)
  blocking collectives: 13.9 us -> 19.6 us
  waiting for transfers between devices: 12.5 us -> 9.88 us
  local copies, waits for them, and re-layouts: 17 us -> 15.4 us
  other arithmetic: 4.26 us -> 2.74 us
    all_to_all x1, starting transfers between devices: 17.2 us -> 9.46 us  [local(): shards = lax.all_to_all(spread, 'col', 0, 0)]
    all_to_all x1, blocking collectives: 13.9 us -> 19.6 us  [local(): keyvals = lax.all_to_all(keyvals, 'row', 0, 0)]
    ppermute x1 -> x2, starting transfers between devices: 0.65 us -> 6.07 us  [the longest x1 4.78 us: local(): lax.ppermute(atoms[-HALO:], 'row', [(i, i + 1) for i in range(row_count -...]
    ppermute x3, waiting for transfers between devices: 3.36 us -> 0.01 us  [local(): lax.ppermute(band, both, [(at(r, k, core), at(r, flat(k, step), core)) fo...]
    unnamed x58 -> x54, local copies, waits for them, and re-layouts: 15.9 us -> 13.7 us
    ppermute x1, starting transfers between devices: 0.68 us -> 2.53 us  [local(): other = lax.ppermute(band, 'col', [(i, i ^ 1) for i in range(col_count)])]
  transfers between devices with their start and end apart: 11 -> 12, of which waited for: 2 -> 2; matrix products, arithmetic and copies ran while one was open for 1% -> 1% of each run, Pallas kernels for 28% -> 29%
where the time goes in v5:
time: 137 us; the launch traced here: 136 us
  Pallas kernels  45.7 us (33%)
  starting transfers between devices  41.7 us (30%)
  blocking collectives  19.6 us (14%)
  local copies, waits for them, and re-layouts  15.4 us (11%)
  waiting for transfers between devices  9.88 us (7%)
  other arithmetic  2.74 us (2%)
    pallas_call x2, Pallas kernels, pair_rows(): pl.pallas_call(functools.partial(pair_body, bands=bands), grid_spec=pltpu...  26.9 us
    all_to_all x1, blocking collectives, local(): keyvals = lax.all_to_all(keyvals, 'row', 0, 0)  19.6 us
    unnamed x54, local copies, waits for them, and re-layouts  13.7 us
    pallas_call x1, Pallas kernels, atom_attention(): pl.pallas_call(atoms_body, grid=(1,), in_specs=[SMEM] + [full(array) for...  11.1 us
    all_to_all x1, starting transfers between devices, local(): shards = lax.all_to_all(spread, 'col', 0, 0)  9.46 us
    all_to_all x1, waiting for transfers between devices, local(): gated = lax.all_to_all(gated, 'col', 0, 0).reshape(CS, rows)  9.13 us
    all_to_all x1, starting transfers between devices, local(): gated = lax.all_to_all(gated, 'col', 0, 0).reshape(CS, rows)  8.57 us
    ppermute x1, starting transfers between devices, local(): lax.ppermute(band, both, [(at(r, r, core), at(r, across(r), core)) for r...  4.81 us
  transfers between devices with their start and end apart: 12, of which 2 were waited for; matrix products, arithmetic and copies ran while one was open for 1% of the time, Pallas kernels for 29%

profile of v5, /device:TPU:1, one launch (start us, length us, event | category | flops | bytes accessed | tf_op | source)
XLA Modules:
  0.0 136.2 jit_solution(9443471183712751529)
XLA Ops:
  0.6 1.7 %broadcast_in_dim.27 = bf16[16,128,128]{2,1,0:T(8,128)(2,1)} broadcast(bf16[128,128]{1,0:T(8,128)(2,1)} %param.20), dimensions={1,2} | broadcast | bytes 557056 | tf_op jit(solution)/shard_map/broadcast_in_dim | solution.py:537
  2.3 9.5 %all-to-all-start = ((bf16[16,128,128]{2,1,0:T(8,128)(2,1)}), bf16[16,128,128]{2,1,0:T(8,128)(2,1)S(1)}, u32[]{:S(2)}, u32[]{:S(2)}) async-start(bf16[16,128,128]{2,1,0:T(8,128)(2,1)} %broadcast_in_dim.27), calls=%async_computation | async-start | bytes 1048576 | tf_op jit(solution)/shard_map/all_to_all | solution.py:538
  11.8 0.6 pad_add_fusion.place
  12.3 21.3 %pair.2 = (bf16[16,256,128]{2,1,0:T(8,128)(2,1)}, bf16[4,224,128]{2,1,0:T(8,128)(2,1)}, bf16[4,64,128]{2,1,0:T(8,128)(2,1)}) custom-call(s32[4]{0:T(128)} %pad_add_fusion.place, bf16[256,128,128]{2,1,0:T(8,128)(2,1)} %pair_ref.3, bf16[128,512]{1,0:T(8,128)(2,1)} %up_ref.3, bf16[256,128]{1,0:T(8,128)(2,1)} %down_ref.3, bf16[20,128]{1,0:T(8,128)(2,1)} %bitcast.15, ...), custom_call_target="tpu_custom_call" | custom-call | flops 14336000000 | bytes 8601600 | tf_op jit(solution)/shard_map/pair/pallas_call | solution.py:146
  33.7 0.0 all-to-all-done
  33.7 1.1 select_select_fusion.1
  34.8 4.8 %collective-permute-start = (bf16[4,208,128]{2,1,0:T(8,128)(2,1)S(1)}, bf16[4,208,128]{2,1,0:T(8,128)(2,1)S(1)}, u32[]{:S(2)}, u32[]{:S(2)}) collective-permute-start(bf16[4,208,128]{2,1,0:T(8,128)(2,1)S(1)} %select_select_fusion.1), channel_id=1, source_target_pairs={{0,8},{1,9},{18,26},{19,27},{36,44},{37,45},{54,62},{55,63},{72,64... | collective-permute-start | bytes 638984 | tf_op jit(solution)/shard_map/ppermute | solution.py:565
  39.6 0.0 copy-start.24
  39.6 0.0 copy-start.25
  39.6 0.0 copy-start.26
  39.7 0.0 copy-start.9
  39.7 0.0 copy-start.12
  39.7 0.8 collective-permute-start.2
  40.5 1.5 %collective-permute-start.1 = (bf16[4,64,128]{2,1,0:T(8,128)(2,1)}, bf16[4,64,128]{2,1,0:T(8,128)(2,1)S(1)}, u32[]{:S(2)}, u32[]{:S(2)}) collective-permute-start(bf16[4,64,128]{2,1,0:T(8,128)(2,1)} %get-tuple-element.45), channel_id=1, source_target_pairs={{17,18},{35,36},{53,54},{71,72},{89,90},{107,108},{125,126},{2,1},... | collective-permute-start | bytes 196616 | tf_op jit(solution)/shard_map/ppermute | solution.py:571
  42.0 5.6 %pair.3 = bf16[16,256,128]{2,1,0:T(8,128)(2,1)} custom-call(s32[4]{0:T(128)} %pad_add_fusion.place, bf16[256,128,128]{2,1,0:T(8,128)(2,1)} %pair_ref.3, bf16[128,512]{1,0:T(8,128)(2,1)} %up_ref.3, bf16[256,128]{1,0:T(8,128)(2,1)} %down_ref.3, bf16[20,128]{1,0:T(8,128)(2,1)} %bitcast.16, ...), custom_call_target="tpu_custom_call", output_to_operand_aliasing={{}: (6, {})} | custom-call | flops 2048000000 | bytes 1228800 | tf_op jit(solution)/shard_map/pair/pallas_call | solution.py:146
  47.6 0.0 collective-permute-done.2
  47.6 0.0 collective-permute-done.1
  47.6 0.0 collective-permute-done
  47.6 0.0 copy-done.24
  47.6 0.2 select_select_fusion
  47.8 1.3 collective-permute-start.5
  49.1 1.3 collective-permute-start.4
  50.4 1.3 collective-permute-start.3
  51.7 1.3 collective-permute-start.7
  53.0 4.8 %collective-permute-start.6 = (bf16[64,128]{1,0:T(8,128)(2,1)S(1)}, bf16[64,128]{1,0:T(8,128)(2,1)S(1)}, u32[]{:S(2)}, u32[]{:S(2)}) collective-permute-start(bf16[64,128]{1,0:T(8,128)(2,1)S(1)} %get-tuple-element.81), channel_id=1, source_target_pairs={{0,16},{16,32},{32,48},{48,64},{64,80},{80,96},{96,112},{1,17},{17... | collective-permute-start | bytes 49160 | tf_op jit(solution)/shard_map/ppermute | solution.py:608
  57.8 0.0 copy-done.25
  57.8 0.1 fusion
  58.0 0.0 collective-permute-done.7.after_ref
  58.0 0.7 collective-permute-done.6.before_ref
  58.7 1.5 %atom_projections.1 = (bf16[2176,128]{1,0:T(8,128)(2,1)S(1)}, bf16[2048,128]{1,0:T(8,128)(2,1)S(1)}, bf16[2176,128]{1,0:T(8,128)(2,1)S(1)}, bf16[2176,128]{1,0:T(8,128)(2,1)S(1)}, f32[2048,128]{1,0:T(8,128)S(1)}) custom-call(bf16[2048,128]{1,0:T(8,128)(2,1)S(1)} %bitcast.12, bf16[64,128]{1,0:T(8,128)(2,1)S(1)} %collective-permute-done.6.before_ref, ...), custom_call_target="tpu_custom_call" | custom-call | flops 1000000000 | bytes 4194304 | tf_op jit(solution)/shard_map/atom_projections/pallas_call | solution.py:194
  60.2 0.0 copy-start.18
  60.2 0.8 copy-done.18
  61.1 0.8 copy-done.20
  61.9 0.8 copy-done.22
  62.7 0.0 collective-permute-done.5
  62.7 0.0 collective-permute-done.4
  62.7 0.0 collective-permute-done.3
  62.7 0.0 copy-start.1
  62.7 2.5 %collective-permute-start.8 = (bf16[4,208,128]{2,1,0:T(8,128)(2,1)S(1)}, bf16[4,208,128]{2,1,0:T(8,128)(2,1)S(1)}, u32[]{:S(2)}, u32[]{:S(2)}) collective-permute-start(bf16[4,208,128]{2,1,0:T(8,128)(2,1)S(1)} %add_add_fusion.half_ref), channel_id=1, source_target_pairs={{0,1},{1,0},{2,3},{3,2},{4,5},{5,4},{6,7},{7,6},{8,9},{9,8},{10,11... | collective-permute-start | bytes 638984 | tf_op jit(solution)/shard_map/ppermute | solution.py:618
  65.3 4.1 %all-to-all-start.1 = ((bf16[16,256,128]{2,1,0:T(8,128)(2,1)}), bf16[16,256,128]{2,1,0:T(8,128)(2,1)S(1)}, u32[]{:S(2)}, u32[]{:S(2)}) async-start(bf16[16,256,128]{2,1,0:T(8,128)(2,1)} %pair.3), calls=%async_computation.1 | async-start | bytes 2097152 | tf_op jit(solution)/shard_map/all_to_all | solution.py:615
  69.4 0.0 collective-permute-done.8.other_ref
  69.4 0.0 copy-start.6
  69.4 0.7 copy-done.6
  70.1 0.0 copy-done.10
  70.1 0.9 copy-done.2
  71.0 1.0 copy-done.5
  72.0 0.9 copy-done.7
  72.9 0.9 copy-done.8
  73.9 1.1 copy-done.17
  74.9 1.1 copy-done.19
  76.0 1.1 copy-done.21
  77.0 1.0 copy-done.23
  78.1 11.1 %atoms.1 = (bf16[2048,128]{1,0:T(8,128)(2,1)S(1)}, bf16[256,768]{1,0:T(8,128)(2,1)S(1)}, f32[256,256]{1,0:T(8,128)S(1)}, bf16[8,96,256]{2,1,0:T(8,128)(2,1)S(1)}) custom-call(s32[4]{0:T(128)S(1)} %copy-done.4, s32[1,2176]{1,0:T(1,128)S(1)} %broadcast_in_dim.31.tokens_ref, bf16[128,128]{1,0:T(8,128)(2,1)S(1)} %copy-done.10, bf16[128,768]{1,0:T(8,128)(2,1)S(1)} %copy-done.8, ...), custom_call_target="tpu_custom_call" | custom-call | flops 10000000000 | bytes 16777216 | tf_op jit(solution)/shard_map/atoms/pallas_call | solution.py:369
  89.1 0.0 copy-start.14
  89.1 0.7 copy-done.14
  89.8 0.0 all-to-all-done.1.bias_hbm
  89.8 19.6 %all_to_all.20.kv_hbm = bf16[8,96,256]{2,1,0:T(8,128)(2,1)S(1)} all-to-all(bf16[8,96,256]{2,1,0:T(8,128)(2,1)S(1)} %get-tuple-element.76), channel_id=1, replica_groups=mesh['row'=8,'col'=16] {'row'}, dimensions={0} | all-to-all | bytes 786432 | tf_op jit(solution)/shard_map/all_to_all | solution.py:633
  109.5 0.9 copy-done.15
  110.4 3.2 %tokens.1 = bf16[16,48,256]{2,1,0:T(8,128)(2,1)} custom-call(s32[4]{0:T(128)S(1)} %copy-done.4, f32[16]{0:T(128)S(1)} %copy-done.13, s32[1,2048]{1,0:T(1,128)S(1)} %bitcast.13, f32[256,256]{1,0:T(8,128)S(1)} %copy-done.15, bf16[8,96,256]{2,1,0:T(8,128)(2,1)S(1)} %all_to_all.20.kv_hbm, bf16[16,256,128]{2,1,0:T(8,128)(2,1)S(1)} %all-to-all-done.1.bias_hbm), custom_call_target="tpu_custom_call" | custom-call | flops 1000000000 | bytes 4194304 | tf_op jit(solution)/shard_map/tokens/pallas_call | solution.py:438
  113.7 8.6 %all-to-all-start.3 = ((bf16[16,48,256]{2,1,0:T(8,128)(2,1)}), bf16[16,48,256]{2,1,0:T(8,128)(2,1)S(1)}, u32[]{:S(2)}, u32[]{:S(2)}) async-start(bf16[16,48,256]{2,1,0:T(8,128)(2,1)} %tokens.1), calls=%async_computation.3 | async-start | bytes 786432 | tf_op jit(solution)/shard_map/all_to_all | solution.py:635
  122.2 0.8 subtract_bitcast_fusion.tokens_ref
  123.0 9.1 %all-to-all-done.3 = bf16[16,48,256]{2,1,0:T(8,128)(2,1)S(1)} async-done(((bf16[16,48,256]{2,1,0:T(8,128)(2,1)}), bf16[16,48,256]{2,1,0:T(8,128)(2,1)S(1)}, u32[]{:S(2)}, u32[]{:S(2)}) %all-to-all-start.3) | async-done | bytes 393248 | tf_op jit(solution)/shard_map/all_to_all | solution.py:635
  132.1 0.9 copy-done.3
  133.0 3.0 %updates.1 = (bf16[256,768]{1,0:T(8,128)(2,1)}, bf16[128,128]{1,0:T(8,128)(2,1)}) custom-call(s32[4]{0:T(128)S(1)} %copy-done.4, s32[1,128]{1,0:T(1,128)S(1)} %subtract_bitcast_fusion.tokens_ref, bf16[768,256]{1,0:T(8,128)(2,1)S(1)} %bitcast.10, bf16[768,768]{1,0:T(8,128)(2,1)S(1)} %copy-done, bf16[256,768]{1,0:T(8,128)(2,1)S(1)} %get-tuple-element.78.tmid_hbm, ...), custom_call_target="tpu_custom_call" | custom-call | tf_op jit(solution)/shard_map/updates/pallas_call | solution.py:493
  (34 shorter events, 0.1 us)
Async XLA Ops:
  2.3 31.4 %all-to-all-start = ((bf16[16,128,128]{2,1,0:T(8,128)(2,1)}), bf16[16,128,128]{2,1,0:T(8,128)(2,1)S(1)}, u32[]{:S(2)}, u32[]{:S(2)}) async-start(bf16[16,128,128]{2,1,0:T(8,128)(2,1)} %broadcast_in_dim.27), calls=%async_computation | async-start | bytes 1048576 | tf_op jit(solution)/shard_map/all_to_all | solution.py:538
  34.8 12.8 %collective-permute-start = (bf16[4,208,128]{2,1,0:T(8,128)(2,1)S(1)}, bf16[4,208,128]{2,1,0:T(8,128)(2,1)S(1)}, u32[]{:S(2)}, u32[]{:S(2)}) collective-permute-start(bf16[4,208,128]{2,1,0:T(8,128)(2,1)S(1)} %select_select_fusion.1), channel_id=1, source_target_pairs={{0,8},{1,9},{18,26},{19,27},{36,44},{37,45},{54,62},{55,63},{72,64... | collective-permute-start | bytes 638984 | tf_op jit(solution)/shard_map/ppermute | solution.py:565
  39.6 8.0 %copy-start.24 = (bf16[4,224,128]{2,1,0:T(8,128)(2,1)S(1)}, bf16[4,224,128]{2,1,0:T(8,128)(2,1)}, u32[]{:S(2)}) copy-start(bf16[4,224,128]{2,1,0:T(8,128)(2,1)} %get-tuple-element.44) | copy-start | bytes 688132
  39.6 18.2 %copy-start.25 = (s32[16384]{0:T(1024)S(1)}, s32[16384]{0:T(1024)}, u32[]{:S(2)}) copy-start(s32[16384]{0:T(1024)} %param.21) | copy-start | bytes 196612
  39.6 18.3 %copy-start.26 = (f32[768]{0:T(1024)S(1)}, f32[768]{0:T(1024)}, u32[]{:S(2)}) copy-start(f32[768]{0:T(1024)} %param.30) | copy-start | bytes 9220
  39.7 19.0 %copy-start.9 = (bf16[128,512]{1,0:T(8,128)(2,1)S(1)}, bf16[128,512]{1,0:T(8,128)(2,1)}, u32[]{:S(2)}) copy-start(bf16[128,512]{1,0:T(8,128)(2,1)} %proj_ref.1) | copy-start | bytes 393220
  39.7 19.0 %copy-start.12 = (f32[128]{0:T(128)S(1)}, f32[128]{0:T(128)}, u32[]{:S(2)}) copy-start(f32[128]{0:T(128)} %param.26) | copy-start | bytes 1540
  39.7 7.9 %collective-permute-start.2 = (bf16[4,64,128]{2,1,0:T(8,128)(2,1)}, bf16[4,64,128]{2,1,0:T(8,128)(2,1)S(1)}, u32[]{:S(2)}, u32[]{:S(2)}) collective-permute-start(bf16[4,64,128]{2,1,0:T(8,128)(2,1)} %get-tuple-element.45), channel_id=1, source_target_pairs={{17,26},{35,44},{53,62},{71,64},{89,82},{107,100},{125,118},{2,9},... | collective-permute-start | bytes 196616 | tf_op jit(solution)/shard_map/ppermute | solution.py:571
  40.5 7.1 %collective-permute-start.1 = (bf16[4,64,128]{2,1,0:T(8,128)(2,1)}, bf16[4,64,128]{2,1,0:T(8,128)(2,1)S(1)}, u32[]{:S(2)}, u32[]{:S(2)}) collective-permute-start(bf16[4,64,128]{2,1,0:T(8,128)(2,1)} %get-tuple-element.45), channel_id=1, source_target_pairs={{17,18},{35,36},{53,54},{71,72},{89,90},{107,108},{125,126},{2,1},... | collective-permute-start | bytes 196616 | tf_op jit(solution)/shard_map/ppermute | solution.py:571
  47.6 22.5 %copy-start.4 = (s32[4]{0:T(128)S(1)}, s32[4]{0:T(128)}, u32[]{:S(2)}) copy-start(s32[4]{0:T(128)} %pad_add_fusion.place) | copy-start | bytes 52
  47.6 22.5 %copy-start.10 = (bf16[128,128]{1,0:T(8,128)(2,1)S(1)}, bf16[128,128]{1,0:T(8,128)(2,1)}, u32[]{:S(2)}) copy-start(bf16[128,128]{1,0:T(8,128)(2,1)} %exit_ref.1) | copy-start | bytes 98308
  47.8 14.9 %collective-permute-start.5 = (bf16[4,208,128]{2,1,0:T(8,128)(2,1)S(1)}, bf16[4,208,128]{2,1,0:T(8,128)(2,1)S(1)}, u32[]{:S(2)}, u32[]{:S(2)}) collective-permute-start(bf16[4,208,128]{2,1,0:T(8,128)(2,1)S(1)} %select_select_fusion), channel_id=1, source_target_pairs={{0,6},{1,7},{8,14},{9,15},{18,16},{19,17},{26,24},{27,25},{36,34},... | collective-permute-start | bytes 638984 | tf_op jit(solution)/shard_map/ppermute | solution.py:595
  49.1 13.6 %collective-permute-start.4 = (bf16[4,208,128]{2,1,0:T(8,128)(2,1)S(1)}, bf16[4,208,128]{2,1,0:T(8,128)(2,1)S(1)}, u32[]{:S(2)}, u32[]{:S(2)}) collective-permute-start(bf16[4,208,128]{2,1,0:T(8,128)(2,1)S(1)} %select_select_fusion), channel_id=1, source_target_pairs={{0,4},{1,5},{8,12},{9,13},{18,22},{19,23},{26,30},{27,31},{36,32},... | collective-permute-start | bytes 638984 | tf_op jit(solution)/shard_map/ppermute | solution.py:595
  50.4 12.2 %collective-permute-start.3 = (bf16[4,208,128]{2,1,0:T(8,128)(2,1)S(1)}, bf16[4,208,128]{2,1,0:T(8,128)(2,1)S(1)}, u32[]{:S(2)}, u32[]{:S(2)}) collective-permute-start(bf16[4,208,128]{2,1,0:T(8,128)(2,1)S(1)} %select_select_fusion), channel_id=1, source_target_pairs={{0,2},{1,3},{8,10},{9,11},{18,20},{19,21},{26,28},{27,29},{36,38},... | collective-permute-start | bytes 638984 | tf_op jit(solution)/shard_map/ppermute | solution.py:595
  51.7 6.2 %collective-permute-start.7 = (bf16[64,128]{1,0:T(8,128)(2,1)S(1)}, bf16[64,128]{1,0:T(8,128)(2,1)S(1)}, u32[]{:S(2)}, u32[]{:S(2)}) collective-permute-start(bf16[64,128]{1,0:T(8,128)(2,1)S(1)} %get-tuple-element.80), channel_id=1, source_target_pairs={{16,0},{32,16},{48,32},{64,48},{80,64},{96,80},{112,96},{17,1},{33... | collective-permute-start | bytes 49160 | tf_op jit(solution)/shard_map/ppermute | solution.py:611
  53.0 5.6 %collective-permute-start.6 = (bf16[64,128]{1,0:T(8,128)(2,1)S(1)}, bf16[64,128]{1,0:T(8,128)(2,1)S(1)}, u32[]{:S(2)}, u32[]{:S(2)}) collective-permute-start(bf16[64,128]{1,0:T(8,128)(2,1)S(1)} %get-tuple-element.81), channel_id=1, source_target_pairs={{0,16},{16,32},{32,48},{48,64},{64,80},{80,96},{96,112},{1,17},{17... | collective-permute-start | bytes 49160 | tf_op jit(solution)/shard_map/ppermute | solution.py:608
  60.2 0.8 copy-start.18
  61.1 0.8 copy-start.20
  61.9 0.8 copy-start.22
  62.7 2.6 %copy-start.16 = (bf16[2176,128]{1,0:T(8,128)(2,1)}, bf16[2176,128]{1,0:T(8,128)(2,1)S(1)}, u32[]{:S(2)}) copy-start(bf16[2176,128]{1,0:T(8,128)(2,1)S(1)} %get-tuple-element.68.ext_hbm) | copy-start | bytes 1671172
  62.7 6.6 %copy-start.1 = (bf16[4,208,128]{2,1,0:T(8,128)(2,1)}, bf16[4,208,128]{2,1,0:T(8,128)(2,1)S(1)}, u32[]{:S(2)}) copy-start(bf16[4,208,128]{2,1,0:T(8,128)(2,1)S(1)} %add_add_fusion.half_ref) | copy-start | bytes 638980
  62.7 6.6 %collective-permute-start.8 = (bf16[4,208,128]{2,1,0:T(8,128)(2,1)S(1)}, bf16[4,208,128]{2,1,0:T(8,128)(2,1)S(1)}, u32[]{:S(2)}, u32[]{:S(2)}) collective-permute-start(bf16[4,208,128]{2,1,0:T(8,128)(2,1)S(1)} %add_add_fusion.half_ref), channel_id=1, source_target_pairs={{0,1},{1,0},{2,3},{3,2},{4,5},{5,4},{6,7},{7,6},{8,9},{9,8},{10,11... | collective-permute-start | bytes 638984 | tf_op jit(solution)/shard_map/ppermute | solution.py:618
  65.3 24.6 %all-to-all-start.1 = ((bf16[16,256,128]{2,1,0:T(8,128)(2,1)}), bf16[16,256,128]{2,1,0:T(8,128)(2,1)S(1)}, u32[]{:S(2)}, u32[]{:S(2)}) async-start(bf16[16,256,128]{2,1,0:T(8,128)(2,1)} %pair.3), calls=%async_computation.1 | async-start | bytes 2097152 | tf_op jit(solution)/shard_map/all_to_all | solution.py:615
  69.4 0.7 copy-start.6
  70.1 0.9 copy-start.2
  71.0 1.0 copy-start.5
  72.0 0.9 copy-start.7
  72.9 0.9 copy-start.8
  73.8 1.1 copy-start.17
  74.9 1.1 copy-start.19
  76.0 1.1 copy-start.21
  77.0 1.0 copy-start.23
  78.1 31.4 %copy-start.11 = (s32[2048]{0:T(1024)S(1)}, s32[2048]{0:T(1024)}, u32[]{:S(2)}) copy-start(s32[2048]{0:T(1024)} %param.22) | copy-start | bytes 24580
  78.1 31.4 %copy-start.13 = (f32[16]{0:T(128)S(1)}, f32[16]{0:T(128)}, u32[]{:S(2)}) copy-start(f32[16]{0:T(128)} %strength.1) | copy-start | bytes 196
  89.1 0.7 copy-start.14
  89.8 42.3 %copy-start = (bf16[768,768]{1,0:T(8,128)(2,1)S(1)}, bf16[768,768]{1,0:T(8,128)(2,1)}, u32[]{:S(2)}) copy-start(bf16[768,768]{1,0:T(8,128)(2,1)} %exit_hbm.1) | copy-start | bytes 3538948
  109.4 1.0 copy-start.15
  113.7 18.5 %all-to-all-start.3 = ((bf16[16,48,256]{2,1,0:T(8,128)(2,1)}), bf16[16,48,256]{2,1,0:T(8,128)(2,1)S(1)}, u32[]{:S(2)}, u32[]{:S(2)}) async-start(bf16[16,48,256]{2,1,0:T(8,128)(2,1)} %tokens.1), calls=%async_computation.3 | async-start | bytes 786432 | tf_op jit(solution)/shard_map/all_to_all | solution.py:635
  132.1 0.9 copy-start.3

commit v6 on v5

--- a/solution.py
+++ b/solution.py
@@ -24,6 +24,7 @@
 REACH = 208
 GROUP = 1024
 EPS = 1e-05
+GRANT = 60 * 2**20
 
 bf16 = jnp.bfloat16
 f32 = jnp.float32
@@ -162,58 +163,54 @@
     )(place, pair, *weights, *before)
 
 
-def project_body(
-    atoms_ref, before_ref, after_ref, gain_ref, proj_ref, *refs
-):
-    outs, (ext_ref, query_ref, key_ref, value_ref, gate_ref, sems) = refs[:5], refs[5:]
-    atoms = atoms_ref.shape[0]
-    ext_ref[:HALO] = before_ref[...]
-    ext_ref[HALO : HALO + atoms] = atoms_ref[...]
-    ext_ref[HALO + atoms :] = after_ref[...]
-    normed = (scaled(centered(ext_ref[...].astype(f32))) * gain_ref[...]).astype(bf16)
-    own = normed[HALO : HALO + atoms]
-    query_ref[...] = (dot(own, proj_ref[:, :CA]) * HDA ** (-0.5)).astype(bf16)
+def project_body(place, mine_ref, theirs_ref, gain_ref, proj_ref, *refs):
+    outs, (atoms_ref, query_ref, key_ref, value_ref, gate_ref, sems) = refs[:5], refs[5:]
+    even = lax.rem(place[1], 2) == 0
+    per = mine_ref.shape[1]
+    for k in range(mine_ref.shape[0]):
+        mine, theirs = mine_ref[k], theirs_ref[k]
+        start = 2 * k * per
+        atoms_ref[start : start + per] = jnp.where(even, mine, theirs)
+        atoms_ref[start + per : start + 2 * per] = jnp.where(even, theirs, mine)
+    normed = (scaled(centered(atoms_ref[...].astype(f32))) * gain_ref[...]).astype(bf16)
+    query_ref[...] = (dot(normed, proj_ref[:, :CA]) * HDA ** (-0.5)).astype(bf16)
     key_ref[...] = dot(normed, proj_ref[:, CA : 2 * CA]).astype(bf16)
     value_ref[...] = dot(normed, proj_ref[:, 2 * CA : 3 * CA]).astype(bf16)
-    gate_ref[...] = sigmoid(dot(own, proj_ref[:, 3 * CA :]))
-    for copy in fetch((ext_ref, query_ref, key_ref, value_ref, gate_ref), outs, sems):
+    gate_ref[...] = sigmoid(dot(normed, proj_ref[:, 3 * CA :]))
+    for copy in fetch((atoms_ref, query_ref, key_ref, value_ref, gate_ref), outs, sems):
         copy.wait()
 
 
-def project_atoms(atoms, before, after, gain, proj):
-    count = atoms.shape[0]
-    total = count + 2 * HALO
-    operands = (atoms, before, after, gain, proj)
-    out_shape = [
-        jax.ShapeDtypeStruct((total, CA), bf16),
-        jax.ShapeDtypeStruct((count, CA), bf16),
-        jax.ShapeDtypeStruct((total, CA), bf16),
-        jax.ShapeDtypeStruct((total, CA), bf16),
-        jax.ShapeDtypeStruct((count, CA), f32),
-    ]
+def project_atoms(place, mine, theirs, gain, proj):
+    count = 2 * mine.shape[0] * mine.shape[1]
+    operands = (mine, theirs, gain, proj)
+    out_shape = [jax.ShapeDtypeStruct((count, CA), bf16)] * 4
+    out_shape += [jax.ShapeDtypeStruct((count, CA), f32)]
     return pl.pallas_call(
         project_body,
         grid=(1,),
-        in_specs=[full(array) for array in operands],
+        in_specs=[SMEM] + [full(array) for array in operands],
         out_specs=[HBM] * len(out_shape),
         out_shape=out_shape,
         scratch_shapes=held(out_shape),
-        compiler_params=pltpu.CompilerParams(vmem_limit_bytes=24 * 2**20),
+        compiler_params=pltpu.CompilerParams(vmem_limit_bytes=GRANT),
         cost_estimate=pl.CostEstimate(flops=10**9, bytes_accessed=2**22, transcendentals=2**18),
         name="atom_projections",
-    )(*operands)
+    )(place, *operands)
 
 
 def atoms_body(
     place,
     tokens_ref,
+    atom_gain_ref,
+    proj_ref,
     exit_ref,
     pool_ref,
     single_ref,
     gain_ref,
     half_ref,
     other_ref,
-    ext_hbm,
+    atoms_hbm,
     query_hbm,
     key_hbm,
     value_hbm,
@@ -226,10 +223,10 @@
     bias_ref,
     look_ref,
     sums_ref,
-    ext_ref,
+    value_ref,
+    atoms_ref,
     query_ref,
     key_ref,
-    value_ref,
     gate_ref,
     tproj_ref,
     sems,
@@ -240,28 +237,47 @@
     out_sems,
 ):
     copies = fetch(
-        (ext_hbm, query_hbm, key_hbm, value_hbm, gate_hbm, tproj_hbm),
-        (ext_ref, query_ref, key_ref, value_ref, gate_ref, tproj_ref),
+        (atoms_hbm, query_hbm, key_hbm, value_hbm, gate_hbm, tproj_hbm),
+        (
+            atoms_ref,
+            query_ref,
+            key_ref,
+            value_ref.at[HALO : HALO + atoms_ref.shape[0]],
+            gate_ref,
+            tproj_ref,
+        ),
         sems,
     )
     row, col, row_count = place[0], place[1], place[2]
-    total = ext_ref.shape[0]
+    total = look_ref.shape[0]
     atoms = query_ref.shape[0]
     rows = single_ref.shape[0]
     even = lax.rem(col, 2) == 0
     rest = jnp.zeros((rows - REACH, KW), bf16)
+    before, after = [], []
     for h in range(HA):
         mine, theirs = half_ref[h], other_ref[h]
-        first = jnp.where(even, mine, theirs)
-        second = jnp.where(even, theirs, mine)
+        mine, theirs = jnp.where(even, mine, theirs), jnp.where(even, theirs, mine)
+        first, second = mine[:REACH], theirs[:REACH]
+        before.append(mine[REACH:])
+        after.append(theirs[REACH:])
         base = h * 3 * KW
         bias_ref[:, base : base + KW] = jnp.concatenate([first, rest], axis=0)
         bias_ref[:, base + KW : base + 2 * KW] = jnp.concatenate([rest, second], axis=0)
         bias_ref[:, base + 2 * KW : base + 3 * KW] = jnp.concatenate(
             [first[REACH - HALO :], jnp.zeros((rows - 2 * HALO, KW), bf16), second[:HALO]], axis=0
         )
+    near = jnp.concatenate(before + after, axis=0).astype(f32)
+    near = (scaled(centered(near)) * atom_gain_ref[...]).astype(bf16)
+    near_keys = dot(near, proj_ref[:, CA : 2 * CA]).astype(bf16)
+    near_values = dot(near, proj_ref[:, 2 * CA : 3 * CA]).astype(bf16)
     for copy in copies[:-1]:
         copy.wait()
+    look_ref[:HALO, :CA] = near_keys[:HALO]
+    look_ref[HALO : HALO + atoms, :CA] = key_ref[...]
+    look_ref[HALO + atoms :, :CA] = near_keys[HALO:]
+    value_ref[:HALO] = near_values[:HALO]
+    value_ref[HALO + atoms :] = near_values[HALO:]
     lane = lax.broadcasted_iota(jnp.int32, (KW, 3 * KW), 1)
     for t in range(total // KW):
         at = slice(t * KW, (t + 1) * KW)
@@ -272,7 +288,6 @@
             tokens + 2 * KW + HALO,
             jnp.where(tokens < 2 * KW, tokens, tokens + HALO),
         )
-        look_ref[at, :CA] = key_ref[at, :]
         look_ref[at, CA:] = (tokens == lane).astype(f32).astype(bf16)
     head_of = lax.broadcasted_iota(jnp.int32, (QB, CA), 1) // HDA
     sums_ref[...] = jnp.zeros_like(sums_ref)
@@ -321,7 +336,7 @@
             attended.append(merged)
         attended = jnp.concatenate(attended, axis=0)
         gated = (attended * gate_ref[own, :]).astype(bf16)
-        single = ext_ref[pl.ds(pl.multiple_of(start + HALO, HALO), GROUP), :].astype(f32)
+        single = atoms_ref[own, :].astype(f32)
         mid = (single + dot(gated, exit_ref[...])).astype(bf16)
         mid_ref[own, :] = mid
         pooled = jnp.maximum(dot(mid, pool_ref[...]), 0.0).astype(bf16)
@@ -354,11 +369,13 @@
         copy.wait()
 
 
-def atom_attention(place, bands, parts, tokens, exit_w, pool, single, gain, tproj, copies):
-    total = parts[0].shape[0]
-    atoms = total - 2 * HALO
+def atom_attention(
+    place, bands, parts, tokens, atom_gain, proj, exit_w, pool, single, gain, tproj, copies
+):
+    atoms = parts[0].shape[0]
+    total = atoms + 2 * HALO
     rows = single.shape[0]
-    operands = (tokens, exit_w, pool, single, gain)
+    operands = (tokens, atom_gain, proj, exit_w, pool, single, gain)
     fetched = (*parts, tproj)
     out_shape = [
         jax.ShapeDtypeStruct((atoms, CA), bf16),
@@ -379,11 +396,13 @@
             pltpu.VMEM((rows, HA * 3 * KW), bf16),
             pltpu.VMEM((total, CA + 3 * KW), bf16),
             pltpu.VMEM((rows, CS), f32),
+            pltpu.VMEM((total, CA), bf16),
         ]
-        + held(fetched)
+        + held((*parts[:3], *parts[4:], tproj))[:-1]
+        + [pltpu.SemaphoreType.DMA((len(fetched),))]
         + [pltpu.VMEM(a.shape, a.dtype) for a in out_shape[:3]]
         + [pltpu.VMEM((2 * HDT, rows), bf16), pltpu.SemaphoreType.DMA((3 + copies,))],
-        compiler_params=pltpu.CompilerParams(vmem_limit_bytes=44 * 2**20),
+        compiler_params=pltpu.CompilerParams(vmem_limit_bytes=GRANT),
         cost_estimate=pl.CostEstimate(
             flops=10**10, bytes_accessed=2**24, transcendentals=2**22
         ),
@@ -442,7 +461,7 @@
         out_specs=full(out_shape),
         out_shape=out_shape,
         scratch_shapes=held((state, kv, bias)),
-        compiler_params=pltpu.CompilerParams(vmem_limit_bytes=24 * 2**20),
+        compiler_params=pltpu.CompilerParams(vmem_limit_bytes=GRANT),
         cost_estimate=pl.CostEstimate(flops=10**9, bytes_accessed=2**22, transcendentals=2**19),
         name="tokens",
     )(place, strength, chain, state, kv, bias)
@@ -497,7 +516,7 @@
         out_specs=[full(shape) for shape in out_shape],
         out_shape=out_shape,
         scratch_shapes=held((gated, exit_w, tmid, back, jax.ShapeDtypeStruct((atoms, CA), bf16))),
-        compiler_params=pltpu.CompilerParams(vmem_limit_bytes=24 * 2**20),
+        compiler_params=pltpu.CompilerParams(vmem_limit_bytes=GRANT),
         name="updates",
     )(place, tokens, gated, exit_w, tmid, back, mid)
 
@@ -534,8 +553,13 @@
     at = lambda r, k, core: r * col_count + 2 * k + core
     last = col_count - 1
 
-    spread = jnp.broadcast_to(atom_single[None], (col_count,) + atom_single.shape)
-    shards = lax.all_to_all(spread, "col", 0, 0)
+    last = col_count - 1
+    halo = lax.ppermute(
+        jnp.where(col == last, atom_single[-HALO:], atom_single[:HALO]),
+        both,
+        [(r * col_count + last, at(r + 1, r + 1, 0)) for r in range(row_count - 1)]
+        + [((r + 1) * col_count, at(r, r, 1)) for r in range(row_count - 1)],
+    )
     ext_tokens = lax.dynamic_slice_in_dim(
         jnp.pad(atom_token, (HALO, HALO)), row * row_atoms, row_atoms + 2 * HALO
     )
@@ -550,18 +574,18 @@
     center = jnp.asarray((np.eye(CZ) - 1.0 / CZ).astype(bf16))
     weights = (pair_up, pair_down, bias_heads.T, center)
     token_bias, band, edge = pair_rows(place, pair_tensor, weights, (), 0, PART, 2, True)
-    shards, band, edge, token_bias = lax.optimization_barrier((shards, band, edge, token_bias))
+    halo, band, edge, token_bias, own_atoms = lax.optimization_barrier(
+        (halo, band, edge, token_bias, atom_single)
+    )
 
     here = col // 2 == row
     even = col % 2 == 0
     ring = chips // 2
     flat = lambda k, step: k // ring * ring + (k + step) % ring
     across = lambda k: (k + ring) % chips
-    band = jnp.where(
-        here & even,
-        band[:, :REACH],
-        jnp.where(here, band[:, 2 * PART - REACH :], jnp.zeros_like(band[:, :REACH])),
-    )
+    band = jnp.where(even, band[:, :REACH], band[:, 2 * PART - REACH :])
+    band = jnp.concatenate([band, halo.reshape(HA, HALO // HA, CA)], axis=1)
+    band = jnp.where(here, band, jnp.zeros_like(band))
     band_y = lax.ppermute(
         band,
         both,
@@ -576,21 +600,28 @@
         )
         for to in (lambda r: r, across)
     ]
-    (token_bias,) = pair_rows(
-        place, pair_tensor, weights, (token_bias,), 2 * PART, rows - 2 * PART, 1, False
-    )
-    band_y, edges, token_bias = lax.optimization_barrier((band_y, edges, token_bias))
+    cores = [[at(0, k, core) for k in range(chips)] for core in range(2)]
+    own_atoms = jnp.broadcast_to(own_atoms[None], (chips,) + own_atoms.shape)
+    shards = lax.all_to_all(own_atoms, "col", 0, 0, axis_index_groups=cores)
+    swap = [(i, i ^ 1) for i in range(col_count)]
+    band_y, edges = lax.optimization_barrier((band_y, edges))
     edge = edges[0] + edges[1]
-    blank = jnp.zeros((HA, REACH - HALO, cols), bf16)
+    blank = jnp.zeros((HA, band.shape[1] - HALO, cols), bf16)
+    split = REACH - HALO
     edge = jnp.where(
-        even, jnp.concatenate([blank, edge], axis=1), jnp.concatenate([edge, blank], axis=1)
+        even,
+        jnp.concatenate([blank[:, :split], edge, blank[:, split:]], axis=1),
+        jnp.concatenate([edge, blank], axis=1),
     )
     place_in = lax.broadcasted_iota(jnp.int32, band.shape, 1)
     lane = lax.broadcasted_iota(jnp.int32, band.shape, 2)
     spare = jnp.where(
-        even, (place_in >= REACH - HALO) & (lane < HALO), (place_in < HALO) & (lane >= HALO)
+        even,
+        (place_in >= split) & (place_in < REACH) & (lane < HALO),
+        (place_in < HALO) & (lane >= HALO),
     )
     band = jnp.where(spare, edge, band + band_y)
+    band, token_bias = lax.optimization_barrier((band, token_bias))
     sent = [
         lax.ppermute(
             band,
@@ -604,24 +635,25 @@
         )
         for step in range(1, ring)
     ]
-    atoms, _ = lax.optimization_barrier((shards.reshape(row_atoms, CA), band))
-    before = lax.ppermute(
-        atoms[-HALO:], "row", [(i, i + 1) for i in range(row_count - 1)]
-    )
-    after = lax.ppermute(atoms[:HALO], "row", [(i + 1, i) for i in range(row_count - 1)])
-    parts = project_atoms(atoms, before, after, atom_gain[None], atom_proj)
+    (token_bias,) = pair_rows(
+        place, pair_tensor, weights, (token_bias,), 2 * PART, rows - 2 * PART, 1, False
+    )
+    theirs = lax.ppermute(shards, "col", swap)
+    parts = project_atoms(place, shards, theirs, atom_gain[None], atom_proj)
     gain = token_gain[None]
     parts, token_bias = lax.optimization_barrier((parts, token_bias))
     head_bias = lax.all_to_all(token_bias, "col", 0, 0)
     sent, parts, gain, ext_tokens = lax.optimization_barrier((sent, parts, gain, ext_tokens))
     band = band + sent[0] + sent[1] + sent[2]
-    other = lax.ppermute(band, "col", [(i, i ^ 1) for i in range(col_count)])
+    other = lax.ppermute(band, "col", swap)
 
     atom_mid, token_mid, state, keyvals = atom_attention(
         place,
         (band, other),
         parts,
         ext_tokens,
+        atom_gain[None],
+        atom_proj,
         atom_exit,
         atom_pool,
         token_single,

time: 137 us -> 127 us (0.927)
  starting transfers between devices: 41.7 us -> 30 us
  local copies, waits for them, and re-layouts: 15.4 us -> 4.21 us
  waiting for transfers between devices: 9.88 us -> 20.5 us
  Pallas kernels: 45.7 us -> 51.8 us
  blocking collectives: 19.6 us -> 14.9 us
    unnamed x54 -> x18, local copies, waits for them, and re-layouts: 13.7 us -> 2.19 us
    ppermute x2, waiting for transfers between devices: 0.01 us -> 7.77 us  [local(): lax.ppermute(edge, both, [(at(r, r - 1, 1), at(r, to(r), 0)) for r in ran...]
    ppermute x3, starting transfers between devices: 8.61 us -> 1.95 us  [the longest x1 1.28 us: local(): lax.ppermute(jnp.where(col == last, atom_single[-HALO:], atom_single[:HAL...]
    all_to_all x1, blocking collectives: 19.6 us -> 14.9 us  [local(): keyvals = lax.all_to_all(keyvals, 'row', 0, 0)]
    all_to_all x1, waiting for transfers between devices: 0.01 us -> 3.37 us  [local(): head_bias = lax.all_to_all(token_bias, 'col', 0, 0)]
    all_to_all x1, starting transfers between devices: 9.46 us -> 6.28 us  [local(): shards = lax.all_to_all(own_atoms, 'col', 0, 0, axis_index_groups=cores)]
    pallas_call x1, Pallas kernels: 11.1 us -> 13.1 us  [atom_attention(): pl.pallas_call(atoms_body, grid=(1,), in_specs=[SMEM] + [full(array) for...]
    pallas_call x1, Pallas kernels: 1.52 us -> 3.46 us  [project_atoms(): pl.pallas_call(project_body, grid=(1,), in_specs=[SMEM] + [full(array) fo...]
  transfers between devices with their start and end apart: 12 -> 12, of which waited for: 2 -> 3; matrix products, arithmetic and copies ran while one was open for 1% -> 3% of each run, Pallas kernels for 29% -> 35%
where the time goes in v6:
time: 127 us; the launch traced here: 126 us
  Pallas kernels  51.8 us (41%)
  starting transfers between devices  30 us (24%)
  waiting for transfers between devices  20.5 us (16%)
  blocking collectives  14.9 us (12%)
  local copies, waits for them, and re-layouts  4.21 us (3%)
  other arithmetic  3.47 us (3%)
    pallas_call x2, Pallas kernels, pair_rows(): pl.pallas_call(functools.partial(pair_body, bands=bands), grid_spec=pltpu...  27.1 us
    all_to_all x1, blocking collectives, local(): keyvals = lax.all_to_all(keyvals, 'row', 0, 0)  14.9 us
    pallas_call x1, Pallas kernels, atom_attention(): pl.pallas_call(atoms_body, grid=(1,), in_specs=[SMEM] + [full(array) for...  13.1 us
    all_to_all x1, waiting for transfers between devices, local(): gated = lax.all_to_all(gated, 'col', 0, 0).reshape(CS, rows)  9.31 us
    ppermute x2, waiting for transfers between devices, local(): lax.ppermute(edge, both, [(at(r, r - 1, 1), at(r, to(r), 0)) for r in ran...  7.77 us
    all_to_all x1, starting transfers between devices, local(): gated = lax.all_to_all(gated, 'col', 0, 0).reshape(CS, rows)  6.78 us
    all_to_all x1, starting transfers between devices, local(): shards = lax.all_to_all(own_atoms, 'col', 0, 0, axis_index_groups=cores)  6.28 us
    ppermute x1, starting transfers between devices, local(): lax.ppermute(band, both, [(at(r, r, core), at(r, across(r), core)) for r...  5.03 us
  transfers between devices with their start and end apart: 12, of which 3 were waited for; matrix products, arithmetic and copies ran while one was open for 3% of the time, Pallas kernels for 35%

profile of v6, /device:TPU:1, one launch (start us, length us, event | category | flops | bytes accessed | tf_op | source)
XLA Modules:
  0.0 125.9 jit_solution(6231582359575494511)
XLA Ops:
  0.6 0.7 slice_select_fusion.1
  1.4 1.3 %collective-permute-start = (bf16[64,128]{1,0:T(8,128)(2,1)S(1)}, bf16[64,128]{1,0:T(8,128)(2,1)S(1)}, u32[]{:S(2)}, u32[]{:S(2)}) collective-permute-start(bf16[64,128]{1,0:T(8,128)(2,1)S(1)} %slice_select_fusion.1), channel_id=1, source_target_pairs={{15,18},{31,36},{47,54},{63,72},{79,90},{95,108},{111,126},{16,1},... | collective-permute-start | bytes 49160 | tf_op jit(solution)/shard_map/ppermute | solution.py:557
  2.7 0.7 pad_add_fusion.place
  3.3 0.0 copy-start.4
  3.3 0.0 copy-start.5
  3.3 0.0 copy-start.6
  3.3 21.5 %pair.2 = (bf16[16,256,128]{2,1,0:T(8,128)(2,1)}, bf16[4,224,128]{2,1,0:T(8,128)(2,1)}, bf16[4,64,128]{2,1,0:T(8,128)(2,1)}) custom-call(s32[4]{0:T(128)} %pad_add_fusion.place, bf16[256,128,128]{2,1,0:T(8,128)(2,1)} %pair_ref.3, bf16[128,512]{1,0:T(8,128)(2,1)} %up_ref.3, bf16[256,128]{1,0:T(8,128)(2,1)} %down_ref.3, bf16[20,128]{1,0:T(8,128)(2,1)} %bitcast.12, ...), custom_call_target="tpu_custom_call" | custom-call | flops 14336000000 | bytes 8601600 | tf_op jit(solution)/shard_map/pair/pallas_call | solution.py:147
  24.8 0.0 collective-permute-done
  24.8 1.1 slice_select_fusion
  26.0 5.0 %collective-permute-start.1 = (bf16[4,224,128]{2,1,0:T(8,128)(2,1)S(1)}, bf16[4,224,128]{2,1,0:T(8,128)(2,1)S(1)}, u32[]{:S(2)}, u32[]{:S(2)}) collective-permute-start(bf16[4,224,128]{2,1,0:T(8,128)(2,1)S(1)} %maximum_select_fusion), channel_id=1, source_target_pairs={{0,8},{1,9},{18,26},{19,27},{36,44},{37,45},{54,62},{55,63},{72,64... | collective-permute-start | bytes 688136 | tf_op jit(solution)/shard_map/ppermute | solution.py:589
  31.0 0.0 copy-done.4
  31.0 0.7 broadcast_in_dim.29
  31.8 6.3 %all-to-all-start = ((bf16[8,128,128]{2,1,0:T(8,128)(2,1)}), bf16[8,128,128]{2,1,0:T(8,128)(2,1)S(1)}, u32[]{:S(2)}, u32[]{:S(2)}) async-start(bf16[8,128,128]{2,1,0:T(8,128)(2,1)} %broadcast_in_dim.29), calls=%async_computation | async-start | bytes 524288 | tf_op jit(solution)/shard_map/all_to_all | solution.py:605
  38.0 0.0 copy-done.5
  38.0 0.1 fusion
  38.1 0.1 pad.8.clone
  38.2 0.0 copy-done.6
  38.2 0.6 broadcast_in_dim.31.gain_ref
  38.8 0.6 broadcast_in_dim.32.tokens_ref
  39.4 0.7 collective-permute-start.3
  40.1 1.3 %collective-permute-start.2 = (bf16[4,64,128]{2,1,0:T(8,128)(2,1)}, bf16[4,64,128]{2,1,0:T(8,128)(2,1)S(1)}, u32[]{:S(2)}, u32[]{:S(2)}) collective-permute-start(bf16[4,64,128]{2,1,0:T(8,128)(2,1)} %get-tuple-element.47), channel_id=1, source_target_pairs={{17,18},{35,36},{53,54},{71,72},{89,90},{107,108},{125,126},{2,1},... | collective-permute-start | bytes 196616 | tf_op jit(solution)/shard_map/ppermute | solution.py:595
  41.4 0.0 collective-permute-done.3
  41.4 7.8 %collective-permute-done.2 = bf16[4,64,128]{2,1,0:T(8,128)(2,1)S(1)} collective-permute-done((bf16[4,64,128]{2,1,0:T(8,128)(2,1)}, bf16[4,64,128]{2,1,0:T(8,128)(2,1)S(1)}, u32[]{:S(2)}, u32[]{:S(2)}) %collective-permute-start.2) | collective-permute-done | bytes 65568 | tf_op jit(solution)/shard_map/ppermute | solution.py:595
  49.2 0.0 collective-permute-done.1
  49.2 0.0 all-to-all-done.mine_ref
  49.2 0.0 copy-start.2
  49.2 0.1 collective-permute-start.7
  49.3 0.2 select_select_fusion
  49.5 1.3 %collective-permute-start.6 = (bf16[4,224,128]{2,1,0:T(8,128)(2,1)S(1)}, bf16[4,224,128]{2,1,0:T(8,128)(2,1)S(1)}, u32[]{:S(2)}, u32[]{:S(2)}) collective-permute-start(bf16[4,224,128]{2,1,0:T(8,128)(2,1)S(1)} %select_select_fusion), channel_id=1, source_target_pairs={{0,6},{1,7},{8,14},{9,15},{18,16},{19,17},{26,24},{27,25},{36,34},... | collective-permute-start | bytes 688136 | tf_op jit(solution)/shard_map/ppermute | solution.py:626
  50.9 1.3 %collective-permute-start.5 = (bf16[4,224,128]{2,1,0:T(8,128)(2,1)S(1)}, bf16[4,224,128]{2,1,0:T(8,128)(2,1)S(1)}, u32[]{:S(2)}, u32[]{:S(2)}) collective-permute-start(bf16[4,224,128]{2,1,0:T(8,128)(2,1)S(1)} %select_select_fusion), channel_id=1, source_target_pairs={{0,4},{1,5},{8,12},{9,13},{18,22},{19,23},{26,30},{27,31},{36,32},... | collective-permute-start | bytes 688136 | tf_op jit(solution)/shard_map/ppermute | solution.py:626
  52.2 1.5 %collective-permute-start.4 = (bf16[4,224,128]{2,1,0:T(8,128)(2,1)S(1)}, bf16[4,224,128]{2,1,0:T(8,128)(2,1)S(1)}, u32[]{:S(2)}, u32[]{:S(2)}) collective-permute-start(bf16[4,224,128]{2,1,0:T(8,128)(2,1)S(1)} %select_select_fusion), channel_id=1, source_target_pairs={{0,2},{1,3},{8,10},{9,11},{18,20},{19,21},{26,28},{27,29},{36,38},... | collective-permute-start | bytes 688136 | tf_op jit(solution)/shard_map/ppermute | solution.py:626
  53.7 5.6 %pair.3 = bf16[16,256,128]{2,1,0:T(8,128)(2,1)} custom-call(s32[4]{0:T(128)} %pad_add_fusion.place, bf16[256,128,128]{2,1,0:T(8,128)(2,1)} %pair_ref.3, bf16[128,512]{1,0:T(8,128)(2,1)} %up_ref.3, bf16[256,128]{1,0:T(8,128)(2,1)} %down_ref.3, bf16[20,128]{1,0:T(8,128)(2,1)} %bitcast.13, ...), custom_call_target="tpu_custom_call", output_to_operand_aliasing={{}: (6, {})} | custom-call | flops 2048000000 | bytes 1228800 | tf_op jit(solution)/shard_map/pair/pallas_call | solution.py:147
  59.2 0.0 copy-done.2
  59.2 0.0 collective-permute-done.7.theirs_ref
  59.2 0.0 copy-start.7
  59.2 0.7 copy-done.7
  59.9 3.5 %atom_projections.1 = (bf16[2048,128]{1,0:T(8,128)(2,1)}, bf16[2048,128]{1,0:T(8,128)(2,1)}, bf16[2048,128]{1,0:T(8,128)(2,1)}, bf16[2048,128]{1,0:T(8,128)(2,1)}, f32[2048,128]{1,0:T(8,128)}) custom-call(s32[4]{0:T(128)} %pad_add_fusion.place, bf16[8,128,128]{2,1,0:T(8,128)(2,1)} %copy-done.2, bf16[8,128,128]{2,1,0:T(8,128)(2,1)} %copy-done.7, ...), custom_call_target="tpu_custom_call" | custom-call | flops 1000000000 | bytes 4194304 | tf_op jit(solution)/shard_map/atom_projections/pallas_call | solution.py:189
  63.4 0.0 collective-permute-done.6
  63.4 0.0 collective-permute-done.5
  63.4 0.0 collective-permute-done.4
  63.5 0.0 copy-start.3
  63.5 0.6 collective-permute-start.8
  64.1 3.9 %all-to-all-start.1 = ((bf16[16,256,128]{2,1,0:T(8,128)(2,1)}), bf16[16,256,128]{2,1,0:T(8,128)(2,1)S(1)}, u32[]{:S(2)}, u32[]{:S(2)}) async-start(bf16[16,256,128]{2,1,0:T(8,128)(2,1)} %pair.3), calls=%async_computation.1 | async-start | bytes 2097152 | tf_op jit(solution)/shard_map/all_to_all | solution.py:645
  68.0 0.0 collective-permute-done.8.other_ref
  68.0 0.0 copy-done.3
  68.0 0.0 copy-start.8
  68.0 0.7 copy-done.8
  68.7 13.1 %atoms.1 = (bf16[2048,128]{1,0:T(8,128)(2,1)}, bf16[256,768]{1,0:T(8,128)(2,1)}, f32[256,256]{1,0:T(8,128)}, bf16[8,96,256]{2,1,0:T(8,128)(2,1)}) custom-call(s32[4]{0:T(128)} %pad_add_fusion.place, s32[1,2176]{1,0:T(1,128)} %broadcast_in_dim.32.tokens_ref, f32[1,128]{1,0:T(1,128)} %bitcast.16, bf16[128,512]{1,0:T(8,128)(2,1)} %proj_ref.3, ...), custom_call_target="tpu_custom_call" | custom-call | flops 10000000000 | bytes 16777216 | tf_op jit(solution)/shard_map/atoms/pallas_call | solution.py:386
  81.8 3.4 %all-to-all-done.1.bias_hbm = bf16[16,256,128]{2,1,0:T(8,128)(2,1)S(1)} async-done(((bf16[16,256,128]{2,1,0:T(8,128)(2,1)}), bf16[16,256,128]{2,1,0:T(8,128)(2,1)S(1)}, u32[]{:S(2)}, u32[]{:S(2)}) %all-to-all-start.1) | async-done | bytes 1048608 | tf_op jit(solution)/shard_map/all_to_all | solution.py:645
  85.2 0.0 copy-start.1
  85.2 14.9 %all_to_all.20.kv_hbm = bf16[8,96,256]{2,1,0:T(8,128)(2,1)} all-to-all(bf16[8,96,256]{2,1,0:T(8,128)(2,1)} %get-tuple-element.78), channel_id=1, replica_groups=mesh['row'=8,'col'=16] {'row'}, dimensions={0} | all-to-all | bytes 786432 | tf_op jit(solution)/shard_map/all_to_all | solution.py:665
  100.1 0.0 copy-done.1
  100.1 4.5 %tokens.1 = bf16[16,48,256]{2,1,0:T(8,128)(2,1)} custom-call(s32[4]{0:T(128)} %pad_add_fusion.place, f32[16]{0:T(128)} %strength.1, s32[1,2048]{1,0:T(1,128)} %bitcast.14, f32[256,256]{1,0:T(8,128)} %get-tuple-element.75.state_hbm, bf16[8,96,256]{2,1,0:T(8,128)(2,1)} %all_to_all.20.kv_hbm, bf16[16,256,128]{2,1,0:T(8,128)(2,1)} %copy-done.1), custom_call_target="tpu_custom_call" | custom-call | flops 1000000000 | bytes 4194304 | tf_op jit(solution)/shard_map/tokens/pallas_call | solution.py:457
  104.6 6.8 %all-to-all-start.3 = ((bf16[16,48,256]{2,1,0:T(8,128)(2,1)}), bf16[16,48,256]{2,1,0:T(8,128)(2,1)S(1)}, u32[]{:S(2)}, u32[]{:S(2)}) async-start(bf16[16,48,256]{2,1,0:T(8,128)(2,1)} %tokens.1), calls=%async_computation.3 | async-start | bytes 786432 | tf_op jit(solution)/shard_map/all_to_all | solution.py:667
  111.4 0.6 subtract_bitcast_fusion.tokens_ref
  111.9 9.3 %all-to-all-done.3 = bf16[16,48,256]{2,1,0:T(8,128)(2,1)S(1)} async-done(((bf16[16,48,256]{2,1,0:T(8,128)(2,1)}), bf16[16,48,256]{2,1,0:T(8,128)(2,1)S(1)}, u32[]{:S(2)}, u32[]{:S(2)}) %all-to-all-start.3) | async-done | bytes 393248 | tf_op jit(solution)/shard_map/all_to_all | solution.py:667
  121.2 0.0 copy-start
  121.2 0.8 copy-done
  122.0 3.7 %updates.1 = (bf16[256,768]{1,0:T(8,128)(2,1)}, bf16[128,128]{1,0:T(8,128)(2,1)}) custom-call(s32[4]{0:T(128)} %pad_add_fusion.place, s32[1,128]{1,0:T(1,128)} %subtract_bitcast_fusion.tokens_ref, bf16[768,256]{1,0:T(8,128)(2,1)} %bitcast.10, bf16[768,768]{1,0:T(8,128)(2,1)} %exit_hbm.1, bf16[256,768]{1,0:T(8,128)(2,1)} %get-tuple-element.80.tmid_hbm, ...), custom_call_target="tpu_custom_call" | custom-call | tf_op jit(solution)/shard_map/updates/pallas_call | solution.py:512
  (8 shorter events, 0.1 us)
Async XLA Ops:
  1.4 23.5 %collective-permute-start = (bf16[64,128]{1,0:T(8,128)(2,1)S(1)}, bf16[64,128]{1,0:T(8,128)(2,1)S(1)}, u32[]{:S(2)}, u32[]{:S(2)}) collective-permute-start(bf16[64,128]{1,0:T(8,128)(2,1)S(1)} %slice_select_fusion.1), channel_id=1, source_target_pairs={{15,18},{31,36},{47,54},{63,72},{79,90},{95,108},{111,126},{16,1},... | collective-permute-start | bytes 49160 | tf_op jit(solution)/shard_map/ppermute | solution.py:557
  3.3 27.7 %copy-start.4 = (bf16[128,128]{1,0:T(8,128)(2,1)S(1)}, bf16[128,128]{1,0:T(8,128)(2,1)}, u32[]{:S(2)}) copy-start(bf16[128,128]{1,0:T(8,128)(2,1)} %param.20) | copy-start | bytes 98308
  3.3 34.7 %copy-start.5 = (s32[16384]{0:T(1024)S(1)}, s32[16384]{0:T(1024)}, u32[]{:S(2)}) copy-start(s32[16384]{0:T(1024)} %param.21) | copy-start | bytes 196612
  3.3 34.9 %copy-start.6 = (f32[768]{0:T(1024)S(1)}, f32[768]{0:T(1024)}, u32[]{:S(2)}) copy-start(f32[768]{0:T(1024)} %param.30) | copy-start | bytes 9220
  26.0 23.2 %collective-permute-start.1 = (bf16[4,224,128]{2,1,0:T(8,128)(2,1)S(1)}, bf16[4,224,128]{2,1,0:T(8,128)(2,1)S(1)}, u32[]{:S(2)}, u32[]{:S(2)}) collective-permute-start(bf16[4,224,128]{2,1,0:T(8,128)(2,1)S(1)} %maximum_select_fusion), channel_id=1, source_target_pairs={{0,8},{1,9},{18,26},{19,27},{36,44},{37,45},{54,62},{55,63},{72,64... | collective-permute-start | bytes 688136 | tf_op jit(solution)/shard_map/ppermute | solution.py:589
  31.8 17.5 %all-to-all-start = ((bf16[8,128,128]{2,1,0:T(8,128)(2,1)}), bf16[8,128,128]{2,1,0:T(8,128)(2,1)S(1)}, u32[]{:S(2)}, u32[]{:S(2)}) async-start(bf16[8,128,128]{2,1,0:T(8,128)(2,1)} %broadcast_in_dim.29), calls=%async_computation | async-start | bytes 524288 | tf_op jit(solution)/shard_map/all_to_all | solution.py:605
  39.4 2.0 %collective-permute-start.3 = (bf16[4,64,128]{2,1,0:T(8,128)(2,1)}, bf16[4,64,128]{2,1,0:T(8,128)(2,1)S(1)}, u32[]{:S(2)}, u32[]{:S(2)}) collective-permute-start(bf16[4,64,128]{2,1,0:T(8,128)(2,1)} %get-tuple-element.47), channel_id=1, source_target_pairs={{17,26},{35,44},{53,62},{71,64},{89,82},{107,100},{125,118},{2,9},... | collective-permute-start | bytes 196616 | tf_op jit(solution)/shard_map/ppermute | solution.py:595
  40.1 9.1 %collective-permute-start.2 = (bf16[4,64,128]{2,1,0:T(8,128)(2,1)}, bf16[4,64,128]{2,1,0:T(8,128)(2,1)S(1)}, u32[]{:S(2)}, u32[]{:S(2)}) collective-permute-start(bf16[4,64,128]{2,1,0:T(8,128)(2,1)} %get-tuple-element.47), channel_id=1, source_target_pairs={{17,18},{35,36},{53,54},{71,72},{89,90},{107,108},{125,126},{2,1},... | collective-permute-start | bytes 196616 | tf_op jit(solution)/shard_map/ppermute | solution.py:595
  49.2 10.0 %copy-start.2 = (bf16[8,128,128]{2,1,0:T(8,128)(2,1)}, bf16[8,128,128]{2,1,0:T(8,128)(2,1)S(1)}, u32[]{:S(2)}) copy-start(bf16[8,128,128]{2,1,0:T(8,128)(2,1)S(1)} %all-to-all-done.mine_ref) | copy-start | bytes 786436
  49.2 10.0 %collective-permute-start.7 = (bf16[8,128,128]{2,1,0:T(8,128)(2,1)S(1)}, bf16[8,128,128]{2,1,0:T(8,128)(2,1)S(1)}, u32[]{:S(2)}, u32[]{:S(2)}) collective-permute-start(bf16[8,128,128]{2,1,0:T(8,128)(2,1)S(1)} %all-to-all-done.mine_ref), channel_id=1, source_target_pairs={{0,1},{1,0},{2,3},{3,2},{4,5},{5,4},{6,7},{7,6},{8,9},{9,8},{10,11... | collective-permute-start | bytes 786440 | tf_op jit(solution)/shard_map/ppermute | solution.py:641
  49.5 13.9 %collective-permute-start.6 = (bf16[4,224,128]{2,1,0:T(8,128)(2,1)S(1)}, bf16[4,224,128]{2,1,0:T(8,128)(2,1)S(1)}, u32[]{:S(2)}, u32[]{:S(2)}) collective-permute-start(bf16[4,224,128]{2,1,0:T(8,128)(2,1)S(1)} %select_select_fusion), channel_id=1, source_target_pairs={{0,6},{1,7},{8,14},{9,15},{18,16},{19,17},{26,24},{27,25},{36,34},... | collective-permute-start | bytes 688136 | tf_op jit(solution)/shard_map/ppermute | solution.py:626
  50.9 12.6 %collective-permute-start.5 = (bf16[4,224,128]{2,1,0:T(8,128)(2,1)S(1)}, bf16[4,224,128]{2,1,0:T(8,128)(2,1)S(1)}, u32[]{:S(2)}, u32[]{:S(2)}) collective-permute-start(bf16[4,224,128]{2,1,0:T(8,128)(2,1)S(1)} %select_select_fusion), channel_id=1, source_target_pairs={{0,4},{1,5},{8,12},{9,13},{18,22},{19,23},{26,30},{27,31},{36,32},... | collective-permute-start | bytes 688136 | tf_op jit(solution)/shard_map/ppermute | solution.py:626
  52.2 11.3 %collective-permute-start.4 = (bf16[4,224,128]{2,1,0:T(8,128)(2,1)S(1)}, bf16[4,224,128]{2,1,0:T(8,128)(2,1)S(1)}, u32[]{:S(2)}, u32[]{:S(2)}) collective-permute-start(bf16[4,224,128]{2,1,0:T(8,128)(2,1)S(1)} %select_select_fusion), channel_id=1, source_target_pairs={{0,2},{1,3},{8,10},{9,11},{18,20},{19,21},{26,28},{27,29},{36,38},... | collective-permute-start | bytes 688136 | tf_op jit(solution)/shard_map/ppermute | solution.py:626
  59.2 0.7 copy-start.7
  63.5 4.5 %copy-start.3 = (bf16[4,224,128]{2,1,0:T(8,128)(2,1)}, bf16[4,224,128]{2,1,0:T(8,128)(2,1)S(1)}, u32[]{:S(2)}) copy-start(bf16[4,224,128]{2,1,0:T(8,128)(2,1)S(1)} %add_add_fusion.half_ref) | copy-start | bytes 688132
  63.5 4.5 %collective-permute-start.8 = (bf16[4,224,128]{2,1,0:T(8,128)(2,1)S(1)}, bf16[4,224,128]{2,1,0:T(8,128)(2,1)S(1)}, u32[]{:S(2)}, u32[]{:S(2)}) collective-permute-start(bf16[4,224,128]{2,1,0:T(8,128)(2,1)S(1)} %add_add_fusion.half_ref), channel_id=1, source_target_pairs={{0,1},{1,0},{2,3},{3,2},{4,5},{5,4},{6,7},{7,6},{8,9},{9,8},{10,11... | collective-permute-start | bytes 688136 | tf_op jit(solution)/shard_map/ppermute | solution.py:648
  64.1 21.1 %all-to-all-start.1 = ((bf16[16,256,128]{2,1,0:T(8,128)(2,1)}), bf16[16,256,128]{2,1,0:T(8,128)(2,1)S(1)}, u32[]{:S(2)}, u32[]{:S(2)}) async-start(bf16[16,256,128]{2,1,0:T(8,128)(2,1)} %pair.3), calls=%async_computation.1 | async-start | bytes 2097152 | tf_op jit(solution)/shard_map/all_to_all | solution.py:645
  68.0 0.7 copy-start.8
  85.2 14.9 %copy-start.1 = (bf16[16,256,128]{2,1,0:T(8,128)(2,1)}, bf16[16,256,128]{2,1,0:T(8,128)(2,1)S(1)}, u32[]{:S(2)}) copy-start(bf16[16,256,128]{2,1,0:T(8,128)(2,1)S(1)} %all-to-all-done.1.bias_hbm) | copy-start | bytes 3145732
  104.6 16.7 %all-to-all-start.3 = ((bf16[16,48,256]{2,1,0:T(8,128)(2,1)}), bf16[16,48,256]{2,1,0:T(8,128)(2,1)S(1)}, u32[]{:S(2)}, u32[]{:S(2)}) async-start(bf16[16,48,256]{2,1,0:T(8,128)(2,1)} %tokens.1), calls=%async_computation.3 | async-start | bytes 786432 | tf_op jit(solution)/shard_map/all_to_all | solution.py:667
  121.2 0.8 copy-start

commit v7 on v6

--- a/solution.py
+++ b/solution.py
@@ -103,9 +103,15 @@
 
         @pl.when(pl.program_id(0) == 0)
         def _():
-            edge = jnp.where(place[3] == 1, stacked[:HA, rows - HALO :], stacked[:HA, :HALO])
-            edge = pltpu.roll(edge.reshape(HA * HALO, CZ), HALO, 1)
-            outs[2][...] = edge.reshape(HA, HALO, CZ).astype(bf16)
+            flip = place[3] == 1
+            edge = jnp.where(flip, stacked[:HA, rows - HALO :], stacked[:HA, :HALO])
+            edge = edge.reshape(HA * HALO, CZ)
+            turned = pltpu.roll(edge, HALO, 1)
+            half = HA * HALO // 2
+            low = jnp.where(flip, edge[:half], turned[:half])
+            high = jnp.where(flip, turned[half:], edge[half:])
+            lane = lax.broadcasted_iota(jnp.int32, (half, CZ), 1)
+            outs[2][...] = jnp.where(lane < HALO, low, high).astype(bf16)
 
 
 def pair_rows(place, pair, weights, before, first, size, count, bands):
@@ -137,7 +143,7 @@
                 lambda i, place: (0, i + place[3] * (count - 1 - 2 * i), 0),
             )
         )
-        out_shape.append(jax.ShapeDtypeStruct((HA, HALO, cols), bf16))
+        out_shape.append(jax.ShapeDtypeStruct((HA * HALO // 2, cols), bf16))
         out_specs.append(full(out_shape[-1]))
     aliases = {}
     if before:
@@ -163,42 +169,6 @@
     )(place, pair, *weights, *before)
 
 
-def project_body(place, mine_ref, theirs_ref, gain_ref, proj_ref, *refs):
-    outs, (atoms_ref, query_ref, key_ref, value_ref, gate_ref, sems) = refs[:5], refs[5:]
-    even = lax.rem(place[1], 2) == 0
-    per = mine_ref.shape[1]
-    for k in range(mine_ref.shape[0]):
-        mine, theirs = mine_ref[k], theirs_ref[k]
-        start = 2 * k * per
-        atoms_ref[start : start + per] = jnp.where(even, mine, theirs)
-        atoms_ref[start + per : start + 2 * per] = jnp.where(even, theirs, mine)
-    normed = (scaled(centered(atoms_ref[...].astype(f32))) * gain_ref[...]).astype(bf16)
-    query_ref[...] = (dot(normed, proj_ref[:, :CA]) * HDA ** (-0.5)).astype(bf16)
-    key_ref[...] = dot(normed, proj_ref[:, CA : 2 * CA]).astype(bf16)
-    value_ref[...] = dot(normed, proj_ref[:, 2 * CA : 3 * CA]).astype(bf16)
-    gate_ref[...] = sigmoid(dot(normed, proj_ref[:, 3 * CA :]))
-    for copy in fetch((atoms_ref, query_ref, key_ref, value_ref, gate_ref), outs, sems):
-        copy.wait()
-
-
-def project_atoms(place, mine, theirs, gain, proj):
-    count = 2 * mine.shape[0] * mine.shape[1]
-    operands = (mine, theirs, gain, proj)
-    out_shape = [jax.ShapeDtypeStruct((count, CA), bf16)] * 4
-    out_shape += [jax.ShapeDtypeStruct((count, CA), f32)]
-    return pl.pallas_call(
-        project_body,
-        grid=(1,),
-        in_specs=[SMEM] + [full(array) for array in operands],
-        out_specs=[HBM] * len(out_shape),
-        out_shape=out_shape,
-        scratch_shapes=held(out_shape),
-        compiler_params=pltpu.CompilerParams(vmem_limit_bytes=GRANT),
-        cost_estimate=pl.CostEstimate(flops=10**9, bytes_accessed=2**22, transcendentals=2**18),
-        name="atom_projections",
-    )(place, *operands)
-
-
 def atoms_body(
     place,
     tokens_ref,
@@ -210,11 +180,8 @@
     gain_ref,
     half_ref,
     other_ref,
-    atoms_hbm,
-    query_hbm,
-    key_hbm,
-    value_hbm,
-    gate_hbm,
+    mine_hbm,
+    theirs_hbm,
     tproj_hbm,
     mid_hbm,
     tmid_hbm,
@@ -224,10 +191,11 @@
     look_ref,
     sums_ref,
     value_ref,
-    atoms_ref,
+    ext_ref,
     query_ref,
-    key_ref,
     gate_ref,
+    mine_ref,
+    theirs_ref,
     tproj_ref,
     sems,
     mid_ref,
@@ -237,47 +205,52 @@
     out_sems,
 ):
     copies = fetch(
-        (atoms_hbm, query_hbm, key_hbm, value_hbm, gate_hbm, tproj_hbm),
-        (
-            atoms_ref,
-            query_ref,
-            key_ref,
-            value_ref.at[HALO : HALO + atoms_ref.shape[0]],
-            gate_ref,
-            tproj_ref,
-        ),
-        sems,
+        (mine_hbm, theirs_hbm, tproj_hbm), (mine_ref, theirs_ref, tproj_ref), sems
     )
     row, col, row_count = place[0], place[1], place[2]
     total = look_ref.shape[0]
     atoms = query_ref.shape[0]
     rows = single_ref.shape[0]
+    chips = mine_ref.shape[0]
+    per = atoms // (2 * chips)
     even = lax.rem(col, 2) == 0
+    copies[0].wait()
+    copies[1].wait()
     rest = jnp.zeros((rows - REACH, KW), bf16)
+    middle = jnp.zeros((rows - 2 * HALO, KW), bf16)
+    left = jnp.maximum(row - 1, 0)
+    right = jnp.minimum(row + 1, chips - 1)
+    left = jnp.where(even, theirs_ref[left, per:], mine_ref[left, per:])
+    right = jnp.where(even, mine_ref[right, per:], theirs_ref[right, per:])
+    left_turned = pltpu.roll(left.astype(f32), HALO, 1).astype(bf16)
+    right_turned = pltpu.roll(right.astype(f32), HALO, 1).astype(bf16)
     before, after = [], []
     for h in range(HA):
         mine, theirs = half_ref[h], other_ref[h]
         mine, theirs = jnp.where(even, mine, theirs), jnp.where(even, theirs, mine)
-        first, second = mine[:REACH], theirs[:REACH]
         before.append(mine[REACH:])
         after.append(theirs[REACH:])
         base = h * 3 * KW
-        bias_ref[:, base : base + KW] = jnp.concatenate([first, rest], axis=0)
-        bias_ref[:, base + KW : base + 2 * KW] = jnp.concatenate([rest, second], axis=0)
+        part = slice(h % 2 * HALO, (h % 2 + 1) * HALO)
+        edges = (left, right_turned) if h < HA // 2 else (left_turned, right)
+        bias_ref[:, base : base + KW] = jnp.concatenate([mine[:REACH], rest], axis=0)
+        bias_ref[:, base + KW : base + 2 * KW] = jnp.concatenate([rest, theirs[:REACH]], axis=0)
         bias_ref[:, base + 2 * KW : base + 3 * KW] = jnp.concatenate(
-            [first[REACH - HALO :], jnp.zeros((rows - 2 * HALO, KW), bf16), second[:HALO]], axis=0
+            [edges[0][part], middle, edges[1][part]], axis=0
         )
-    near = jnp.concatenate(before + after, axis=0).astype(f32)
-    near = (scaled(centered(near)) * atom_gain_ref[...]).astype(bf16)
-    near_keys = dot(near, proj_ref[:, CA : 2 * CA]).astype(bf16)
-    near_values = dot(near, proj_ref[:, 2 * CA : 3 * CA]).astype(bf16)
-    for copy in copies[:-1]:
-        copy.wait()
-    look_ref[:HALO, :CA] = near_keys[:HALO]
-    look_ref[HALO : HALO + atoms, :CA] = key_ref[...]
-    look_ref[HALO + atoms :, :CA] = near_keys[HALO:]
-    value_ref[:HALO] = near_values[:HALO]
-    value_ref[HALO + atoms :] = near_values[HALO:]
+    ext_ref[:HALO] = jnp.concatenate(before, axis=0)
+    ext_ref[HALO + atoms :] = jnp.concatenate(after, axis=0)
+    for k in range(chips):
+        mine, theirs = mine_ref[k, :per], theirs_ref[k, :per]
+        at = HALO + 2 * k * per
+        ext_ref[at : at + per] = jnp.where(even, mine, theirs)
+        ext_ref[at + per : at + 2 * per] = jnp.where(even, theirs, mine)
+    normed = (scaled(centered(ext_ref[...].astype(f32))) * atom_gain_ref[...]).astype(bf16)
+    own = normed[HALO : HALO + atoms]
+    query_ref[...] = (dot(own, proj_ref[:, :CA]) * HDA ** (-0.5)).astype(bf16)
+    look_ref[:, :CA] = dot(normed, proj_ref[:, CA : 2 * CA]).astype(bf16)
+    value_ref[...] = dot(normed, proj_ref[:, 2 * CA : 3 * CA]).astype(bf16)
+    gate_ref[...] = sigmoid(dot(own, proj_ref[:, 3 * CA :]))
     lane = lax.broadcasted_iota(jnp.int32, (KW, 3 * KW), 1)
     for t in range(total // KW):
         at = slice(t * KW, (t + 1) * KW)
@@ -336,7 +309,7 @@
             attended.append(merged)
         attended = jnp.concatenate(attended, axis=0)
         gated = (attended * gate_ref[own, :]).astype(bf16)
-        single = atoms_ref[own, :].astype(f32)
+        single = ext_ref[pl.ds(pl.multiple_of(start + HALO, HALO), GROUP), :].astype(f32)
         mid = (single + dot(gated, exit_ref[...])).astype(bf16)
         mid_ref[own, :] = mid
         pooled = jnp.maximum(dot(mid, pool_ref[...]), 0.0).astype(bf16)
@@ -370,13 +343,13 @@
 
 
 def atom_attention(
-    place, bands, parts, tokens, atom_gain, proj, exit_w, pool, single, gain, tproj, copies
+    place, bands, shards, tokens, atom_gain, proj, exit_w, pool, single, gain, tproj, copies
 ):
-    atoms = parts[0].shape[0]
-    total = atoms + 2 * HALO
+    total = tokens.shape[1]
+    atoms = total - 2 * HALO
     rows = single.shape[0]
     operands = (tokens, atom_gain, proj, exit_w, pool, single, gain)
-    fetched = (*parts, tproj)
+    fetched = (*shards, tproj)
     out_shape = [
         jax.ShapeDtypeStruct((atoms, CA), bf16),
         jax.ShapeDtypeStruct((rows, CS), bf16),
@@ -397,14 +370,16 @@
             pltpu.VMEM((total, CA + 3 * KW), bf16),
             pltpu.VMEM((rows, CS), f32),
             pltpu.VMEM((total, CA), bf16),
+            pltpu.VMEM((total, CA), bf16),
+            pltpu.VMEM((atoms, CA), bf16),
+            pltpu.VMEM((atoms, CA), f32),
         ]
-        + held((*parts[:3], *parts[4:], tproj))[:-1]
-        + [pltpu.SemaphoreType.DMA((len(fetched),))]
+        + held(fetched)
         + [pltpu.VMEM(a.shape, a.dtype) for a in out_shape[:3]]
         + [pltpu.VMEM((2 * HDT, rows), bf16), pltpu.SemaphoreType.DMA((3 + copies,))],
         compiler_params=pltpu.CompilerParams(vmem_limit_bytes=GRANT),
         cost_estimate=pl.CostEstimate(
-            flops=10**10, bytes_accessed=2**24, transcendentals=2**22
+            flops=10**7, bytes_accessed=2**14, transcendentals=2**10
         ),
         name="atoms",
     )(place, *operands, *bands, *fetched)
@@ -413,22 +388,28 @@
 def tokens_body(
     place, strength, chain_ref, state_hbm, kv_hbm, bias_hbm, out_ref, state_ref, kv_ref, bias_ref, sems
 ):
-    copies = fetch((state_hbm, kv_hbm, bias_hbm), (state_ref, kv_ref, bias_ref), sems)
+    per = state_hbm.shape[0] // bias_hbm.shape[2]
+    groups = kv_hbm.shape[0]
+    bias_parts = [pl.ds(r * per, per) for r in range(groups)]
+    copies = fetch(
+        [state_hbm, kv_hbm] + [bias_hbm.at[part] for part in bias_parts],
+        [state_ref, kv_ref] + [bias_ref.at[part] for part in bias_parts],
+        sems,
+    )
     col = place[1]
     rows = state_ref.shape[0]
     own = pl.multiple_of(place[0] * rows, rows)
     mine = chain_ref[:, pl.ds(own, rows)].astype(f32)
     mine = jnp.broadcast_to(mine, (KW, rows)).T
     mine = jnp.concatenate([mine] * (rows // KW), axis=1).astype(jnp.int32)
-    for copy in copies:
-        copy.wait()
+    copies[0].wait()
+    copies[1].wait()
     query = state_ref[:, :HDT].astype(bf16)
-    shards, cols = bias_ref.shape[0], bias_ref.shape[2]
     strong = strength[col]
+    raws = [dot(query, kv_ref[r, :HDT, :]) * HDT ** (-0.5) for r in range(groups)]
     scores = []
-    for r in range(kv_ref.shape[0]):
-        raw = dot(query, kv_ref[r, :HDT, :]) * HDT ** (-0.5)
-        per = rows // cols
+    for r, raw in enumerate(raws):
+        copies[2 + r].wait()
         bias = jnp.concatenate([bias_ref[r * per + k].astype(f32) for k in range(per)], axis=1)
         same = mine == chain_ref[:, r * rows : (r + 1) * rows]
         scores.append(raw + bias + jnp.where(same, strong, 0.0))
@@ -460,7 +441,8 @@
         in_specs=[SMEM] * 2 + [full(chain)] + [HBM] * 3,
         out_specs=full(out_shape),
         out_shape=out_shape,
-        scratch_shapes=held((state, kv, bias)),
+        scratch_shapes=held((state, kv, bias))[:-1]
+        + [pltpu.SemaphoreType.DMA((2 + kv.shape[0],))],
         compiler_params=pltpu.CompilerParams(vmem_limit_bytes=GRANT),
         cost_estimate=pl.CostEstimate(flops=10**9, bytes_accessed=2**22, transcendentals=2**19),
         name="tokens",
@@ -468,39 +450,18 @@
 
 
 def update_body(
-    place,
-    tokens_ref,
-    gated_hbm,
-    exit_hbm,
-    tmid_hbm,
-    back_hbm,
-    mid_hbm,
-    tout_ref,
-    aout_ref,
-    gated_ref,
-    exit_ref,
-    tmid_ref,
-    back_ref,
-    mid_ref,
-    sems,
+    place, tokens_ref, gated_ref, exit_ref, tmid_ref, back_ref, mid_ref, tout_ref, aout_ref
 ):
     col = place[1]
     atoms, rows = aout_ref.shape[0], tmid_ref.shape[0]
     at = pl.multiple_of(col * atoms, atoms)
-    copies = fetch(
-        (gated_hbm, exit_hbm, tmid_hbm, back_hbm, mid_hbm.at[pl.ds(at, atoms)]),
-        (gated_ref, exit_ref, tmid_ref, back_ref, mid_ref),
-        sems,
-    )
-    for copy in copies:
-        copy.wait()
     added = dot_tn(gated_ref[...], exit_ref[...])
     update = (tmid_ref[...].astype(f32) + added).astype(bf16)
     tout_ref[...] = update
     sent = dot(update, back_ref[...]).astype(bf16)
     own = tokens_ref[...]
     onehot = (lax.broadcasted_iota(jnp.int32, (rows, atoms), 0) == own).astype(f32).astype(bf16)
-    aout_ref[...] = (mid_ref[...].astype(f32) + dot_tn(onehot, sent)).astype(bf16)
+    aout_ref[...] = (mid_ref[pl.ds(at, atoms), :].astype(f32) + dot_tn(onehot, sent)).astype(bf16)
 
 
 def updates(place, gated, exit_w, tmid, back, mid, tokens, atoms):
@@ -512,11 +473,10 @@
     return pl.pallas_call(
         update_body,
         grid=(1,),
-        in_specs=[SMEM, full(tokens)] + [HBM] * 5,
+        in_specs=[SMEM] + [VMEM] * 6,
         out_specs=[full(shape) for shape in out_shape],
         out_shape=out_shape,
-        scratch_shapes=held((gated, exit_w, tmid, back, jax.ShapeDtypeStruct((atoms, CA), bf16))),
-        compiler_params=pltpu.CompilerParams(vmem_limit_bytes=GRANT),
+        compiler_params=pltpu.CompilerParams(vmem_limit_bytes=16 * 2**20),
         name="updates",
     )(place, tokens, gated, exit_w, tmid, back, mid)
 
@@ -591,36 +551,12 @@
         both,
         [(at(r, r, core), at(r, across(r), core)) for r in range(row_count) for core in range(2)],
     )
-    edges = [
-        lax.ppermute(
-            edge,
-            both,
-            [(at(r, r - 1, 1), at(r, to(r), 0)) for r in range(1, row_count)]
-            + [(at(r, r + 1, 0), at(r, to(r), 1)) for r in range(row_count - 1)],
-        )
-        for to in (lambda r: r, across)
-    ]
     cores = [[at(0, k, core) for k in range(chips)] for core in range(2)]
-    own_atoms = jnp.broadcast_to(own_atoms[None], (chips,) + own_atoms.shape)
-    shards = lax.all_to_all(own_atoms, "col", 0, 0, axis_index_groups=cores)
+    own_part = jnp.concatenate([own_atoms, edge], axis=0)
+    own_part = jnp.broadcast_to(own_part[None], (chips,) + own_part.shape)
+    shards = lax.all_to_all(own_part, "col", 0, 0, axis_index_groups=cores)
     swap = [(i, i ^ 1) for i in range(col_count)]
-    band_y, edges = lax.optimization_barrier((band_y, edges))
-    edge = edges[0] + edges[1]
-    blank = jnp.zeros((HA, band.shape[1] - HALO, cols), bf16)
-    split = REACH - HALO
-    edge = jnp.where(
-        even,
-        jnp.concatenate([blank[:, :split], edge, blank[:, split:]], axis=1),
-        jnp.concatenate([edge, blank], axis=1),
-    )
-    place_in = lax.broadcasted_iota(jnp.int32, band.shape, 1)
-    lane = lax.broadcasted_iota(jnp.int32, band.shape, 2)
-    spare = jnp.where(
-        even,
-        (place_in >= split) & (place_in < REACH) & (lane < HALO),
-        (place_in < HALO) & (lane >= HALO),
-    )
-    band = jnp.where(spare, edge, band + band_y)
+    band = band + band_y
     band, token_bias = lax.optimization_barrier((band, token_bias))
     sent = [
         lax.ppermute(
@@ -639,18 +575,16 @@
         place, pair_tensor, weights, (token_bias,), 2 * PART, rows - 2 * PART, 1, False
     )
     theirs = lax.ppermute(shards, "col", swap)
-    parts = project_atoms(place, shards, theirs, atom_gain[None], atom_proj)
     gain = token_gain[None]
-    parts, token_bias = lax.optimization_barrier((parts, token_bias))
     head_bias = lax.all_to_all(token_bias, "col", 0, 0)
-    sent, parts, gain, ext_tokens = lax.optimization_barrier((sent, parts, gain, ext_tokens))
+    sent, theirs, gain, ext_tokens = lax.optimization_barrier((sent, theirs, gain, ext_tokens))
     band = band + sent[0] + sent[1] + sent[2]
     other = lax.ppermute(band, "col", swap)
 
     atom_mid, token_mid, state, keyvals = atom_attention(
         place,
         (band, other),
-        parts,
+        (shards, theirs),
         ext_tokens,
         atom_gain[None],
         atom_proj,

time: 127 us -> 140 us (1.10)
  starting transfers between devices: 30 us -> 40.8 us
  waiting for transfers between devices: 20.5 us -> 29.2 us
  Pallas kernels: 51.8 us -> 47.4 us
    ppermute x3, waiting for transfers between devices: 0.01 us -> 14 us  [local(): lax.ppermute(band, both, [(at(r, k, core), at(r, flat(k, step), core)) fo...]
    ppermute x2 -> x0, waiting for transfers between devices: 7.77 us -> none  [local(): lax.ppermute(edge, both, [(at(r, r - 1, 1), at(r, to(r), 0)) for r in ran...]
    pallas_call x2 -> x1, Pallas kernels: 7.17 us -> 2.03 us  [updates(): pl.pallas_call(update_body, grid=(1,), in_specs=[SMEM] + [VMEM] * 6, out_...]
    all_to_all x1, starting transfers between devices: 6.28 us -> 10.6 us  [local(): shards = lax.all_to_all(own_part, 'col', 0, 0, axis_index_groups=cores)]
    ppermute x1, waiting for transfers between devices: 0.01 us -> 4.31 us  [local(): lax.ppermute(band, both, [(at(r, r, core), at(r, across(r), core)) for r...]
    all_to_all x1, starting transfers between devices: 6.78 us -> 10.5 us  [local(): gated = lax.all_to_all(gated, 'col', 0, 0).reshape(CS, rows)]
    all_to_all x1, waiting for transfers between devices: 3.37 us -> 0.01 us  [local(): head_bias = lax.all_to_all(token_bias, 'col', 0, 0)]
    ppermute x3, starting transfers between devices: 4.09 us -> 7.11 us  [local(): lax.ppermute(band, both, [(at(r, k, core), at(r, flat(k, step), core)) fo...]
  transfers between devices with their start and end apart: 12 -> 10, of which waited for: 3 -> 6; matrix products, arithmetic and copies ran while one was open for 3% -> 2% of each run, Pallas kernels for 35% -> 29%
where the time goes in v7:
time: 140 us; the launch traced here: 139 us
  Pallas kernels  47.4 us (34%)
  starting transfers between devices  40.8 us (29%)
  waiting for transfers between devices  29.2 us (21%)
  blocking collectives  14.2 us (10%)
  other arithmetic  3.55 us (3%)
  local copies, waits for them, and re-layouts  2.82 us (2%)
    pallas_call x2, Pallas kernels, pair_rows(): pl.pallas_call(functools.partial(pair_body, bands=bands), grid_spec=pltpu...  27.1 us
    all_to_all x1, blocking collectives, local(): keyvals = lax.all_to_all(keyvals, 'row', 0, 0)  14.2 us
    ppermute x3, waiting for transfers between devices, local(): lax.ppermute(band, both, [(at(r, k, core), at(r, flat(k, step), core)) fo...  14 us
    pallas_call x1, Pallas kernels, atom_attention(): pl.pallas_call(atoms_body, grid=(1,), in_specs=[SMEM] + [full(array) for...  13.5 us
    all_to_all x1, starting transfers between devices, local(): shards = lax.all_to_all(own_part, 'col', 0, 0, axis_index_groups=cores)  10.6 us
    all_to_all x1, starting transfers between devices, local(): gated = lax.all_to_all(gated, 'col', 0, 0).reshape(CS, rows)  10.5 us
    all_to_all x1, waiting for transfers between devices, local(): gated = lax.all_to_all(gated, 'col', 0, 0).reshape(CS, rows)  9.82 us
    ppermute x3, starting transfers between devices, local(): lax.ppermute(band, both, [(at(r, k, core), at(r, flat(k, step), core)) fo...  7.11 us
  transfers between devices with their start and end apart: 10, of which 6 were waited for; matrix products, arithmetic and copies ran while one was open for 2% of the time, Pallas kernels for 29%

profile of v7, /device:TPU:1, one launch (start us, length us, event | category | flops | bytes accessed | tf_op | source)
XLA Modules:
  0.0 138.8 jit_solution(673592268439482760)
XLA Ops:
  0.6 0.7 slice_select_fusion.1
  1.4 1.3 collective-permute-start
  2.7 0.7 pad_add_fusion.place
  3.4 0.0 copy-start.10
  3.4 21.5 %pair.2 = (bf16[16,256,128]{2,1,0:T(8,128)(2,1)}, bf16[4,224,128]{2,1,0:T(8,128)(2,1)}, bf16[128,128]{1,0:T(8,128)(2,1)}) custom-call(s32[4]{0:T(128)} %pad_add_fusion.place, bf16[256,128,128]{2,1,0:T(8,128)(2,1)} %pair_ref.3, bf16[128,512]{1,0:T(8,128)(2,1)} %up_ref.3, bf16[256,128]{1,0:T(8,128)(2,1)} %down_ref.3, bf16[20,128]{1,0:T(8,128)(2,1)} %bitcast.12, ...), custom_call_target="tpu_custom_call" | custom-call | flops 14336000000 | bytes 8601600 | tf_op jit(solution)/shard_map/pair/pallas_call | solution.py:153
  24.8 0.0 collective-permute-done
  24.9 0.0 copy-done.10
  24.9 0.8 pad_maximum_fusion
  25.6 0.9 broadcast_in_dim.27
  26.5 10.6 %all-to-all-start = ((bf16[8,256,128]{2,1,0:T(8,128)(2,1)}), bf16[8,256,128]{2,1,0:T(8,128)(2,1)S(1)}, u32[]{:S(2)}, u32[]{:S(2)}) async-start(bf16[8,256,128]{2,1,0:T(8,128)(2,1)} %broadcast_in_dim.27), calls=%async_computation | async-start | bytes 1048576 | tf_op jit(solution)/shard_map/all_to_all | solution.py:557
  37.1 1.1 slice_select_fusion
  38.3 4.9 %collective-permute-start.1 = (bf16[4,224,128]{2,1,0:T(8,128)(2,1)S(1)}, bf16[4,224,128]{2,1,0:T(8,128)(2,1)S(1)}, u32[]{:S(2)}, u32[]{:S(2)}) collective-permute-start(bf16[4,224,128]{2,1,0:T(8,128)(2,1)S(1)} %maximum_select_fusion), channel_id=1, source_target_pairs={{0,8},{1,9},{18,26},{19,27},{36,44},{37,45},{54,62},{55,63},{72,64... | collective-permute-start | bytes 688136 | tf_op jit(solution)/shard_map/ppermute | solution.py:549
  43.2 4.3 %collective-permute-done.1 = bf16[4,224,128]{2,1,0:T(8,128)(2,1)S(1)} collective-permute-done((bf16[4,224,128]{2,1,0:T(8,128)(2,1)S(1)}, bf16[4,224,128]{2,1,0:T(8,128)(2,1)S(1)}, u32[]{:S(2)}, u32[]{:S(2)}) %collective-permute-start.1) | collective-permute-done | bytes 229408 | tf_op jit(solution)/shard_map/ppermute | solution.py:549
  47.5 0.1 add.39
  47.5 0.0 copy-start.12
  47.5 0.0 copy-start.11
  47.6 0.0 all-to-all-done.mine_hbm
  47.6 0.0 copy-start.5
  47.6 0.3 collective-permute-start.5
  47.8 5.6 %pair.3 = bf16[16,256,128]{2,1,0:T(8,128)(2,1)} custom-call(s32[4]{0:T(128)} %pad_add_fusion.place, bf16[256,128,128]{2,1,0:T(8,128)(2,1)} %pair_ref.3, bf16[128,512]{1,0:T(8,128)(2,1)} %up_ref.3, bf16[256,128]{1,0:T(8,128)(2,1)} %down_ref.3, bf16[20,128]{1,0:T(8,128)(2,1)} %bitcast.13, ...), custom_call_target="tpu_custom_call", output_to_operand_aliasing={{}: (6, {})} | custom-call | flops 2048000000 | bytes 1228800 | tf_op jit(solution)/shard_map/pair/pallas_call | solution.py:153
  53.4 0.0 copy-done.5
  53.4 5.4 %all-to-all-start.1 = ((bf16[16,256,128]{2,1,0:T(8,128)(2,1)}), bf16[16,256,128]{2,1,0:T(8,128)(2,1)S(1)}, u32[]{:S(2)}, u32[]{:S(2)}) async-start(bf16[16,256,128]{2,1,0:T(8,128)(2,1)} %pair.3), calls=%async_computation.1 | async-start | bytes 2097152 | tf_op jit(solution)/shard_map/all_to_all | solution.py:579
  58.9 4.5 %collective-permute-start.4 = (bf16[4,224,128]{2,1,0:T(8,128)(2,1)S(1)}, bf16[4,224,128]{2,1,0:T(8,128)(2,1)S(1)}, u32[]{:S(2)}, u32[]{:S(2)}) collective-permute-start(bf16[4,224,128]{2,1,0:T(8,128)(2,1)S(1)} %add.39), channel_id=1, source_target_pairs={{0,6},{1,7},{8,14},{9,15},{18,16},{19,17},{26,24},{27,25},{36,34},... | collective-permute-start | bytes 688136 | tf_op jit(solution)/shard_map/ppermute | solution.py:562
  63.4 1.3 collective-permute-start.3
  64.7 1.3 collective-permute-start.2
  66.0 0.0 copy-done.12
  66.0 0.6 broadcast_in_dim.28.gain_ref
  66.6 0.0 copy-done.11
  66.6 0.1 fusion
  66.7 0.6 broadcast_in_dim.29.tokens_ref
  67.3 5.2 %collective-permute-done.4 = bf16[4,224,128]{2,1,0:T(8,128)(2,1)S(1)} collective-permute-done((bf16[4,224,128]{2,1,0:T(8,128)(2,1)S(1)}, bf16[4,224,128]{2,1,0:T(8,128)(2,1)S(1)}, u32[]{:S(2)}, u32[]{:S(2)}) %collective-permute-start.4) | collective-permute-done | bytes 229408 | tf_op jit(solution)/shard_map/ppermute | solution.py:562
  72.5 3.9 %collective-permute-done.3 = bf16[4,224,128]{2,1,0:T(8,128)(2,1)S(1)} collective-permute-done((bf16[4,224,128]{2,1,0:T(8,128)(2,1)S(1)}, bf16[4,224,128]{2,1,0:T(8,128)(2,1)S(1)}, u32[]{:S(2)}, u32[]{:S(2)}) %collective-permute-start.3) | collective-permute-done | bytes 229408 | tf_op jit(solution)/shard_map/ppermute | solution.py:562
  76.4 4.9 %collective-permute-done.2 = bf16[4,224,128]{2,1,0:T(8,128)(2,1)S(1)} collective-permute-done((bf16[4,224,128]{2,1,0:T(8,128)(2,1)S(1)}, bf16[4,224,128]{2,1,0:T(8,128)(2,1)S(1)}, u32[]{:S(2)}, u32[]{:S(2)}) %collective-permute-start.2) | collective-permute-done | bytes 229408 | tf_op jit(solution)/shard_map/ppermute | solution.py:562
  81.3 0.0 collective-permute-done.5.theirs_hbm
  81.3 0.0 copy-start.8
  81.3 0.0 copy-start.7
  81.3 0.7 collective-permute-start.6
  82.0 1.1 collective-permute-done.6.other_ref
  83.1 0.0 copy-done.8
  83.1 0.0 copy-start.9
  83.1 0.0 copy-done.7
  83.1 0.7 copy-done.9
  83.8 0.0 copy-start
  83.8 0.0 copy-start.3
  83.8 0.0 copy-start.4
  83.8 13.5 %atoms.1 = (bf16[2048,128]{1,0:T(8,128)(2,1)}, bf16[256,768]{1,0:T(8,128)(2,1)}, f32[256,256]{1,0:T(8,128)}, bf16[8,96,256]{2,1,0:T(8,128)(2,1)}) custom-call(s32[4]{0:T(128)} %pad_add_fusion.place, s32[1,2176]{1,0:T(1,128)} %broadcast_in_dim.29.tokens_ref, f32[1,128]{1,0:T(1,128)} %bitcast.14, bf16[128,512]{1,0:T(8,128)(2,1)} %proj_ref.1, ...), custom_call_target="tpu_custom_call" | custom-call | flops 10000000 | bytes 16384 | tf_op jit(solution)/shard_map/atoms/pallas_call | solution.py:359
  97.4 0.0 copy-start.1
  97.4 0.0 copy-start.2
  97.4 0.0 all-to-all-done.1.bias_hbm
  97.4 0.0 copy-start.6
  97.4 14.2 %all_to_all.20.kv_hbm = bf16[8,96,256]{2,1,0:T(8,128)(2,1)} all-to-all(bf16[8,96,256]{2,1,0:T(8,128)(2,1)} %get-tuple-element.42), channel_id=1, replica_groups=mesh['row'=8,'col'=16] {'row'}, dimensions={0} | all-to-all | bytes 786432 | tf_op jit(solution)/shard_map/all_to_all | solution.py:599
  111.6 0.0 copy-done.6
  111.6 4.7 %tokens.1 = bf16[16,48,256]{2,1,0:T(8,128)(2,1)} custom-call(s32[4]{0:T(128)} %pad_add_fusion.place, f32[16]{0:T(128)} %strength.1, s32[1,2048]{1,0:T(1,128)} %bitcast.15, f32[256,256]{1,0:T(8,128)} %get-tuple-element.39.state_hbm, bf16[8,96,256]{2,1,0:T(8,128)(2,1)} %all_to_all.20.kv_hbm, bf16[16,256,128]{2,1,0:T(8,128)(2,1)} %copy-done.6), custom_call_target="tpu_custom_call" | custom-call | flops 1000000000 | bytes 4194304 | tf_op jit(solution)/shard_map/tokens/pallas_call | solution.py:438
  116.3 10.5 %all-to-all-start.3 = ((bf16[16,48,256]{2,1,0:T(8,128)(2,1)}), bf16[16,48,256]{2,1,0:T(8,128)(2,1)S(1)}, u32[]{:S(2)}, u32[]{:S(2)}) async-start(bf16[16,48,256]{2,1,0:T(8,128)(2,1)} %tokens.1), calls=%async_computation.3 | async-start | bytes 786432 | tf_op jit(solution)/shard_map/all_to_all | solution.py:601
  126.8 0.1 subtract_bitcast_fusion.tokens_ref
  126.9 9.8 %all-to-all-done.3 = bf16[16,48,256]{2,1,0:T(8,128)(2,1)S(1)} async-done(((bf16[16,48,256]{2,1,0:T(8,128)(2,1)}), bf16[16,48,256]{2,1,0:T(8,128)(2,1)S(1)}, u32[]{:S(2)}, u32[]{:S(2)}) %all-to-all-start.3) | async-done | bytes 393248 | tf_op jit(solution)/shard_map/all_to_all | solution.py:601
  136.7 0.0 copy-done
  136.7 0.0 copy-done.3
  136.7 0.0 copy-done.4
  136.8 0.0 copy-done.1
  136.8 0.0 copy-done.2
  136.8 2.0 %updates.1 = (bf16[256,768]{1,0:T(8,128)(2,1)}, bf16[128,128]{1,0:T(8,128)(2,1)}) custom-call(s32[4]{0:T(128)S(1)} %copy-done.4, s32[1,128]{1,0:T(1,128)S(1)} %subtract_bitcast_fusion.tokens_ref, bf16[768,256]{1,0:T(8,128)(2,1)S(1)} %bitcast.10, bf16[768,768]{1,0:T(8,128)(2,1)S(1)} %copy-done, bf16[256,768]{1,0:T(8,128)(2,1)S(1)} %copy-done.2, ...), custom_call_target="tpu_custom_call" | custom-call | tf_op jit(solution)/shard_map/updates/pallas_call | solution.py:473
  (2 shorter events, 0.1 us)
Async XLA Ops:
  1.4 23.5 %collective-permute-start = (bf16[64,128]{1,0:T(8,128)(2,1)S(1)}, bf16[64,128]{1,0:T(8,128)(2,1)S(1)}, u32[]{:S(2)}, u32[]{:S(2)}) collective-permute-start(bf16[64,128]{1,0:T(8,128)(2,1)S(1)} %slice_select_fusion.1), channel_id=1, source_target_pairs={{15,18},{31,36},{47,54},{63,72},{79,90},{95,108},{111,126},{16,1},... | collective-permute-start | bytes 49160 | tf_op jit(solution)/shard_map/ppermute | solution.py:517
  3.4 21.5 %copy-start.10 = (bf16[128,128]{1,0:T(8,128)(2,1)S(1)}, bf16[128,128]{1,0:T(8,128)(2,1)}, u32[]{:S(2)}) copy-start(bf16[128,128]{1,0:T(8,128)(2,1)} %param.20) | copy-start | bytes 98308
  26.5 21.1 %all-to-all-start = ((bf16[8,256,128]{2,1,0:T(8,128)(2,1)}), bf16[8,256,128]{2,1,0:T(8,128)(2,1)S(1)}, u32[]{:S(2)}, u32[]{:S(2)}) async-start(bf16[8,256,128]{2,1,0:T(8,128)(2,1)} %broadcast_in_dim.27), calls=%async_computation | async-start | bytes 1048576 | tf_op jit(solution)/shard_map/all_to_all | solution.py:557
  38.3 9.2 %collective-permute-start.1 = (bf16[4,224,128]{2,1,0:T(8,128)(2,1)S(1)}, bf16[4,224,128]{2,1,0:T(8,128)(2,1)S(1)}, u32[]{:S(2)}, u32[]{:S(2)}) collective-permute-start(bf16[4,224,128]{2,1,0:T(8,128)(2,1)S(1)} %maximum_select_fusion), channel_id=1, source_target_pairs={{0,8},{1,9},{18,26},{19,27},{36,44},{37,45},{54,62},{55,63},{72,64... | collective-permute-start | bytes 688136 | tf_op jit(solution)/shard_map/ppermute | solution.py:549
  47.5 18.5 %copy-start.12 = (f32[768]{0:T(1024)S(1)}, f32[768]{0:T(1024)}, u32[]{:S(2)}) copy-start(f32[768]{0:T(1024)} %param.30) | copy-start | bytes 9220
  47.5 19.1 %copy-start.11 = (s32[16384]{0:T(1024)S(1)}, s32[16384]{0:T(1024)}, u32[]{:S(2)}) copy-start(s32[16384]{0:T(1024)} %param.21) | copy-start | bytes 196612
  47.6 5.9 %copy-start.5 = (bf16[8,256,128]{2,1,0:T(8,128)(2,1)}, bf16[8,256,128]{2,1,0:T(8,128)(2,1)S(1)}, u32[]{:S(2)}) copy-start(bf16[8,256,128]{2,1,0:T(8,128)(2,1)S(1)} %all-to-all-done.mine_hbm) | copy-start | bytes 1572868
  47.6 33.7 %collective-permute-start.5 = (bf16[8,256,128]{2,1,0:T(8,128)(2,1)S(1)}, bf16[8,256,128]{2,1,0:T(8,128)(2,1)S(1)}, u32[]{:S(2)}, u32[]{:S(2)}) collective-permute-start(bf16[8,256,128]{2,1,0:T(8,128)(2,1)S(1)} %all-to-all-done.mine_hbm), channel_id=1, source_target_pairs={{0,1},{1,0},{2,3},{3,2},{4,5},{5,4},{6,7},{7,6},{8,9},{9,8},{10,11... | collective-permute-start | bytes 1572872 | tf_op jit(solution)/shard_map/ppermute | solution.py:577
  53.4 44.0 %all-to-all-start.1 = ((bf16[16,256,128]{2,1,0:T(8,128)(2,1)}), bf16[16,256,128]{2,1,0:T(8,128)(2,1)S(1)}, u32[]{:S(2)}, u32[]{:S(2)}) async-start(bf16[16,256,128]{2,1,0:T(8,128)(2,1)} %pair.3), calls=%async_computation.1 | async-start | bytes 2097152 | tf_op jit(solution)/shard_map/all_to_all | solution.py:579
  58.9 13.6 %collective-permute-start.4 = (bf16[4,224,128]{2,1,0:T(8,128)(2,1)S(1)}, bf16[4,224,128]{2,1,0:T(8,128)(2,1)S(1)}, u32[]{:S(2)}, u32[]{:S(2)}) collective-permute-start(bf16[4,224,128]{2,1,0:T(8,128)(2,1)S(1)} %add.39), channel_id=1, source_target_pairs={{0,6},{1,7},{8,14},{9,15},{18,16},{19,17},{26,24},{27,25},{36,34},... | collective-permute-start | bytes 688136 | tf_op jit(solution)/shard_map/ppermute | solution.py:562
  63.4 13.0 %collective-permute-start.3 = (bf16[4,224,128]{2,1,0:T(8,128)(2,1)S(1)}, bf16[4,224,128]{2,1,0:T(8,128)(2,1)S(1)}, u32[]{:S(2)}, u32[]{:S(2)}) collective-permute-start(bf16[4,224,128]{2,1,0:T(8,128)(2,1)S(1)} %add.39), channel_id=1, source_target_pairs={{0,4},{1,5},{8,12},{9,13},{18,22},{19,23},{26,30},{27,31},{36,32},... | collective-permute-start | bytes 688136 | tf_op jit(solution)/shard_map/ppermute | solution.py:562
  64.7 16.6 %collective-permute-start.2 = (bf16[4,224,128]{2,1,0:T(8,128)(2,1)S(1)}, bf16[4,224,128]{2,1,0:T(8,128)(2,1)S(1)}, u32[]{:S(2)}, u32[]{:S(2)}) collective-permute-start(bf16[4,224,128]{2,1,0:T(8,128)(2,1)S(1)} %add.39), channel_id=1, source_target_pairs={{0,2},{1,3},{8,10},{9,11},{18,20},{19,21},{26,28},{27,29},{36,38},... | collective-permute-start | bytes 688136 | tf_op jit(solution)/shard_map/ppermute | solution.py:562
  81.3 1.8 %copy-start.8 = (bf16[8,256,128]{2,1,0:T(8,128)(2,1)}, bf16[8,256,128]{2,1,0:T(8,128)(2,1)S(1)}, u32[]{:S(2)}) copy-start(bf16[8,256,128]{2,1,0:T(8,128)(2,1)S(1)} %collective-permute-done.5.theirs_hbm) | copy-start | bytes 1572868
  81.3 1.8 %copy-start.7 = (bf16[4,224,128]{2,1,0:T(8,128)(2,1)}, bf16[4,224,128]{2,1,0:T(8,128)(2,1)S(1)}, u32[]{:S(2)}) copy-start(bf16[4,224,128]{2,1,0:T(8,128)(2,1)S(1)} %add_add_fusion.half_ref) | copy-start | bytes 688132
  81.3 1.8 %collective-permute-start.6 = (bf16[4,224,128]{2,1,0:T(8,128)(2,1)S(1)}, bf16[4,224,128]{2,1,0:T(8,128)(2,1)S(1)}, u32[]{:S(2)}, u32[]{:S(2)}) collective-permute-start(bf16[4,224,128]{2,1,0:T(8,128)(2,1)S(1)} %add_add_fusion.half_ref), channel_id=1, source_target_pairs={{0,1},{1,0},{2,3},{3,2},{4,5},{5,4},{6,7},{7,6},{8,9},{9,8},{10,11... | collective-permute-start | bytes 688136 | tf_op jit(solution)/shard_map/ppermute | solution.py:582
  83.1 0.7 copy-start.9
  83.8 52.9 %copy-start = (bf16[768,768]{1,0:T(8,128)(2,1)S(1)}, bf16[768,768]{1,0:T(8,128)(2,1)}, u32[]{:S(2)}) copy-start(bf16[768,768]{1,0:T(8,128)(2,1)} %exit_ref.3) | copy-start | bytes 3538948
  83.8 52.9 %copy-start.3 = (bf16[768,128]{1,0:T(8,128)(2,1)S(1)}, bf16[768,128]{1,0:T(8,128)(2,1)}, u32[]{:S(2)}) copy-start(bf16[768,128]{1,0:T(8,128)(2,1)} %back_ref.1) | copy-start | bytes 589828
  83.8 52.9 %copy-start.4 = (s32[4]{0:T(128)S(1)}, s32[4]{0:T(128)}, u32[]{:S(2)}) copy-start(s32[4]{0:T(128)} %pad_add_fusion.place) | copy-start | bytes 52
  97.4 39.4 %copy-start.1 = (bf16[2048,128]{1,0:T(8,128)(2,1)S(1)}, bf16[2048,128]{1,0:T(8,128)(2,1)}, u32[]{:S(2)}) copy-start(bf16[2048,128]{1,0:T(8,128)(2,1)} %get-tuple-element.45.mid_ref) | copy-start | bytes 1572868
  97.4 39.4 %copy-start.2 = (bf16[256,768]{1,0:T(8,128)(2,1)S(1)}, bf16[256,768]{1,0:T(8,128)(2,1)}, u32[]{:S(2)}) copy-start(bf16[256,768]{1,0:T(8,128)(2,1)} %get-tuple-element.44.tmid_ref) | copy-start | bytes 1179652
  97.4 14.2 %copy-start.6 = (bf16[16,256,128]{2,1,0:T(8,128)(2,1)}, bf16[16,256,128]{2,1,0:T(8,128)(2,1)S(1)}, u32[]{:S(2)}) copy-start(bf16[16,256,128]{2,1,0:T(8,128)(2,1)S(1)} %all-to-all-done.1.bias_hbm) | copy-start | bytes 3145732
  116.3 20.4 %all-to-all-start.3 = ((bf16[16,48,256]{2,1,0:T(8,128)(2,1)}), bf16[16,48,256]{2,1,0:T(8,128)(2,1)S(1)}, u32[]{:S(2)}, u32[]{:S(2)}) async-start(bf16[16,48,256]{2,1,0:T(8,128)(2,1)} %tokens.1), calls=%async_computation.3 | async-start | bytes 786432 | tf_op jit(solution)/shard_map/all_to_all | solution.py:601

commit v8 on v7

--- a/solution.py
+++ b/solution.py
@@ -379,7 +379,7 @@
         + [pltpu.VMEM((2 * HDT, rows), bf16), pltpu.SemaphoreType.DMA((3 + copies,))],
         compiler_params=pltpu.CompilerParams(vmem_limit_bytes=GRANT),
         cost_estimate=pl.CostEstimate(
-            flops=10**7, bytes_accessed=2**14, transcendentals=2**10
+            flops=10**10, bytes_accessed=2**24, transcendentals=2**22
         ),
         name="atoms",
     )(place, *operands, *bands, *fetched)
@@ -546,6 +546,7 @@
     band = jnp.where(even, band[:, :REACH], band[:, 2 * PART - REACH :])
     band = jnp.concatenate([band, halo.reshape(HA, HALO // HA, CA)], axis=1)
     band = jnp.where(here, band, jnp.zeros_like(band))
+    band, own_atoms, edge = lax.optimization_barrier((band, own_atoms, edge))
     band_y = lax.ppermute(
         band,
         both,
@@ -576,10 +577,11 @@
     )
     theirs = lax.ppermute(shards, "col", swap)
     gain = token_gain[None]
-    head_bias = lax.all_to_all(token_bias, "col", 0, 0)
     sent, theirs, gain, ext_tokens = lax.optimization_barrier((sent, theirs, gain, ext_tokens))
     band = band + sent[0] + sent[1] + sent[2]
     other = lax.ppermute(band, "col", swap)
+    band, token_bias = lax.optimization_barrier((band, token_bias))
+    head_bias = lax.all_to_all(token_bias, "col", 0, 0)
 
     atom_mid, token_mid, state, keyvals = atom_attention(
         place,

time: 140 us -> 135 us (0.964)
  blocking collectives: 14.2 us -> 32.3 us
  starting transfers between devices: 40.8 us -> 24.5 us
  waiting for transfers between devices: 29.2 us -> 23.4 us
    all_to_all x0 -> x1, blocking collectives: none -> 20.9 us  [local(): shards = lax.all_to_all(own_part, 'col', 0, 0, axis_index_groups=cores)]
    all_to_all x1 -> x0, starting transfers between devices: 10.6 us -> none  [local(): shards = lax.all_to_all(own_part, 'col', 0, 0, axis_index_groups=cores)]
    ppermute x3, waiting for transfers between devices: 14 us -> 6.11 us  [local(): lax.ppermute(band, both, [(at(r, k, core), at(r, flat(k, step), core)) fo...]
    ppermute x3, starting transfers between devices: 7.11 us -> 3.91 us  [local(): lax.ppermute(band, both, [(at(r, k, core), at(r, flat(k, step), core)) fo...]
    all_to_all x1, starting transfers between devices: 10.5 us -> 7.41 us  [local(): gated = lax.all_to_all(gated, 'col', 0, 0).reshape(CS, rows)]
    all_to_all x1, waiting for transfers between devices: 0.01 us -> 3 us  [local(): head_bias = lax.all_to_all(token_bias, 'col', 0, 0)]
    all_to_all x1, blocking collectives: 14.2 us -> 11.4 us  [local(): keyvals = lax.all_to_all(keyvals, 'row', 0, 0)]
    ppermute x1, starting transfers between devices: 4.88 us -> 2.28 us  [local(): lax.ppermute(band, both, [(at(r, r, core), at(r, across(r), core)) for r...]
  transfers between devices with their start and end apart: 10 -> 9, of which waited for: 6 -> 5; matrix products, arithmetic and copies ran while one was open for 2% -> 1% of each run, Pallas kernels for 29% -> 30%
where the time goes in v8:
time: 135 us; the launch traced here: 134 us
  Pallas kernels  47.2 us (35%)
  blocking collectives  32.3 us (24%)
  starting transfers between devices  24.5 us (18%)
  waiting for transfers between devices  23.4 us (17%)
  other arithmetic  3.48 us (3%)
  local copies, waits for them, and re-layouts  1.99 us (1%)
    pallas_call x2, Pallas kernels, pair_rows(): pl.pallas_call(functools.partial(pair_body, bands=bands), grid_spec=pltpu...  27 us
    all_to_all x1, blocking collectives, local(): shards = lax.all_to_all(own_part, 'col', 0, 0, axis_index_groups=cores)  20.9 us
    pallas_call x1, Pallas kernels, atom_attention(): pl.pallas_call(atoms_body, grid=(1,), in_specs=[SMEM] + [full(array) for...  13.4 us
    all_to_all x1, blocking collectives, local(): keyvals = lax.all_to_all(keyvals, 'row', 0, 0)  11.4 us
    all_to_all x1, waiting for transfers between devices, local(): gated = lax.all_to_all(gated, 'col', 0, 0).reshape(CS, rows)  9.82 us
    all_to_all x1, starting transfers between devices, local(): gated = lax.all_to_all(gated, 'col', 0, 0).reshape(CS, rows)  7.41 us
    all_to_all x1, starting transfers between devices, local(): head_bias = lax.all_to_all(token_bias, 'col', 0, 0)  7.35 us
    ppermute x3, waiting for transfers between devices, local(): lax.ppermute(band, both, [(at(r, k, core), at(r, flat(k, step), core)) fo...  6.11 us
  transfers between devices with their start and end apart: 9, of which 5 were waited for; matrix products, arithmetic and copies ran while one was open for 1% of the time, Pallas kernels for 30%

profile of v8, /device:TPU:1, one launch (start us, length us, event | category | flops | bytes accessed | tf_op | source)
XLA Modules:
  0.0 133.7 jit_solution(10424327296058534048)
XLA Ops:
  0.6 0.7 slice_select_fusion.1
  1.4 1.3 collective-permute-start
  2.7 0.6 pad_add_fusion.place
  3.3 0.0 copy-start.8
  3.3 0.0 copy-start.10
  3.3 0.0 copy-start.9
  3.3 21.5 %pair.2 = (bf16[16,256,128]{2,1,0:T(8,128)(2,1)}, bf16[4,224,128]{2,1,0:T(8,128)(2,1)}, bf16[128,128]{1,0:T(8,128)(2,1)}) custom-call(s32[4]{0:T(128)} %pad_add_fusion.place, bf16[256,128,128]{2,1,0:T(8,128)(2,1)} %pair_ref.3, bf16[128,512]{1,0:T(8,128)(2,1)} %up_ref.3, bf16[256,128]{1,0:T(8,128)(2,1)} %down_ref.3, bf16[20,128]{1,0:T(8,128)(2,1)} %bitcast.12, ...), custom_call_target="tpu_custom_call" | custom-call | flops 14336000000 | bytes 8601600 | tf_op jit(solution)/shard_map/pair/pallas_call | solution.py:153
  24.8 0.0 collective-permute-done
  24.8 1.1 slice_select_fusion
  25.9 0.0 copy-done.8
  25.9 0.8 pad_maximum_fusion
  26.7 0.1 broadcast_in_dim.27
  26.8 20.9 %all_to_all.20.mine_hbm = bf16[8,256,128]{2,1,0:T(8,128)(2,1)S(1)} all-to-all(bf16[8,256,128]{2,1,0:T(8,128)(2,1)S(1)} %broadcast_in_dim.27), channel_id=1, replica_groups={{0,2,4,6,8,10,12,14},{1,3,5,7,9,11,13,15},{16,18,20,22,24,26,28,30},{17..., dimensions={0} | all-to-all | bytes 1048576 | tf_op jit(solution)/shard_map/all_to_all | solution.py:558
  47.6 0.0 copy-start.6
  47.6 0.0 collective-permute-start.5
  47.6 2.3 %collective-permute-start.1 = (bf16[4,224,128]{2,1,0:T(8,128)(2,1)S(1)}, bf16[4,224,128]{2,1,0:T(8,128)(2,1)S(1)}, u32[]{:S(2)}, u32[]{:S(2)}) collective-permute-start(bf16[4,224,128]{2,1,0:T(8,128)(2,1)S(1)} %maximum_select_fusion), channel_id=1, source_target_pairs={{0,8},{1,9},{18,26},{19,27},{36,44},{37,45},{54,62},{55,63},{72,64... | collective-permute-start | bytes 688136 | tf_op jit(solution)/shard_map/ppermute | solution.py:550
  49.9 4.4 %collective-permute-done.1 = bf16[4,224,128]{2,1,0:T(8,128)(2,1)S(1)} collective-permute-done((bf16[4,224,128]{2,1,0:T(8,128)(2,1)S(1)}, bf16[4,224,128]{2,1,0:T(8,128)(2,1)S(1)}, u32[]{:S(2)}, u32[]{:S(2)}) %collective-permute-start.1) | collective-permute-done | bytes 229408 | tf_op jit(solution)/shard_map/ppermute | solution.py:550
  54.3 0.1 add.39
  54.4 1.3 collective-permute-start.4
  55.7 1.3 collective-permute-start.3
  57.0 1.3 collective-permute-start.2
  58.3 0.0 copy-done.10
  58.4 0.6 broadcast_in_dim.28.gain_ref
  58.9 0.0 copy-done.9
  58.9 0.1 fusion
  59.0 0.6 broadcast_in_dim.29.tokens_ref
  59.6 0.0 collective-permute-done.4
  59.6 1.2 collective-permute-done.3
  60.8 4.9 %collective-permute-done.2 = bf16[4,224,128]{2,1,0:T(8,128)(2,1)S(1)} collective-permute-done((bf16[4,224,128]{2,1,0:T(8,128)(2,1)S(1)}, bf16[4,224,128]{2,1,0:T(8,128)(2,1)S(1)}, u32[]{:S(2)}, u32[]{:S(2)}) %collective-permute-start.2) | collective-permute-done | bytes 229408 | tf_op jit(solution)/shard_map/ppermute | solution.py:563
  65.7 0.0 collective-permute-done.5.theirs_hbm
  65.7 0.0 copy-start.11
  65.8 0.0 copy-start.7
  65.8 2.3 %collective-permute-start.6 = (bf16[4,224,128]{2,1,0:T(8,128)(2,1)S(1)}, bf16[4,224,128]{2,1,0:T(8,128)(2,1)S(1)}, u32[]{:S(2)}, u32[]{:S(2)}) collective-permute-start(bf16[4,224,128]{2,1,0:T(8,128)(2,1)S(1)} %add_add_fusion.half_ref), channel_id=1, source_target_pairs={{0,1},{1,0},{2,3},{3,2},{4,5},{5,4},{6,7},{7,6},{8,9},{9,8},{10,11... | collective-permute-start | bytes 688136 | tf_op jit(solution)/shard_map/ppermute | solution.py:582
  68.1 5.5 %pair.3 = bf16[16,256,128]{2,1,0:T(8,128)(2,1)} custom-call(s32[4]{0:T(128)} %pad_add_fusion.place, bf16[256,128,128]{2,1,0:T(8,128)(2,1)} %pair_ref.3, bf16[128,512]{1,0:T(8,128)(2,1)} %up_ref.3, bf16[256,128]{1,0:T(8,128)(2,1)} %down_ref.3, bf16[20,128]{1,0:T(8,128)(2,1)} %bitcast.13, ...), custom_call_target="tpu_custom_call", output_to_operand_aliasing={{}: (6, {})} | custom-call | flops 2048000000 | bytes 1228800 | tf_op jit(solution)/shard_map/pair/pallas_call | solution.py:153
  73.6 0.0 copy-done.6
  73.6 0.0 copy-done.11
  73.6 0.0 copy-done.7
  73.6 7.3 %all-to-all-start.1 = ((bf16[16,256,128]{2,1,0:T(8,128)(2,1)}), bf16[16,256,128]{2,1,0:T(8,128)(2,1)S(1)}, u32[]{:S(2)}, u32[]{:S(2)}) async-start(bf16[16,256,128]{2,1,0:T(8,128)(2,1)} %pair.3), calls=%async_computation.1 | async-start | bytes 2097152 | tf_op jit(solution)/shard_map/all_to_all | solution.py:584
  81.0 0.0 collective-permute-done.6.other_ref
  81.0 0.0 copy-start.12
  81.0 0.7 copy-done.12
  81.7 13.4 %atoms.1 = (bf16[2048,128]{1,0:T(8,128)(2,1)}, bf16[256,768]{1,0:T(8,128)(2,1)}, f32[256,256]{1,0:T(8,128)}, bf16[8,96,256]{2,1,0:T(8,128)(2,1)}) custom-call(s32[4]{0:T(128)} %pad_add_fusion.place, s32[1,2176]{1,0:T(1,128)} %broadcast_in_dim.29.tokens_ref, f32[1,128]{1,0:T(1,128)} %bitcast.15, bf16[128,512]{1,0:T(8,128)(2,1)} %proj_ref.1, ...), custom_call_target="tpu_custom_call" | custom-call | flops 10000000000 | bytes 16777216 | tf_op jit(solution)/shard_map/atoms/pallas_call | solution.py:359
  95.1 0.0 copy-start
  95.1 0.0 copy-start.1
  95.1 0.0 copy-start.2
  95.1 0.0 copy-start.3
  95.2 0.0 copy-start.4
  95.2 3.0 %all-to-all-done.1.bias_hbm = bf16[16,256,128]{2,1,0:T(8,128)(2,1)S(1)} async-done(((bf16[16,256,128]{2,1,0:T(8,128)(2,1)}), bf16[16,256,128]{2,1,0:T(8,128)(2,1)S(1)}, u32[]{:S(2)}, u32[]{:S(2)}) %all-to-all-start.1) | async-done | bytes 1048608 | tf_op jit(solution)/shard_map/all_to_all | solution.py:584
  98.2 0.0 copy-start.5
  98.2 11.4 %all_to_all.21.kv_hbm = bf16[8,96,256]{2,1,0:T(8,128)(2,1)} all-to-all(bf16[8,96,256]{2,1,0:T(8,128)(2,1)} %get-tuple-element.52), channel_id=1, replica_groups=mesh['row'=8,'col'=16] {'row'}, dimensions={0} | all-to-all | bytes 786432 | tf_op jit(solution)/shard_map/all_to_all | solution.py:601
  109.6 0.0 copy-done.5
  109.6 4.7 %tokens.1 = bf16[16,48,256]{2,1,0:T(8,128)(2,1)} custom-call(s32[4]{0:T(128)} %pad_add_fusion.place, f32[16]{0:T(128)} %strength.1, s32[1,2048]{1,0:T(1,128)} %bitcast.14, f32[256,256]{1,0:T(8,128)} %get-tuple-element.49.state_hbm, bf16[8,96,256]{2,1,0:T(8,128)(2,1)} %all_to_all.21.kv_hbm, bf16[16,256,128]{2,1,0:T(8,128)(2,1)} %copy-done.5), custom_call_target="tpu_custom_call" | custom-call | flops 1000000000 | bytes 4194304 | tf_op jit(solution)/shard_map/tokens/pallas_call | solution.py:438
  114.3 7.4 %all-to-all-start.3 = ((bf16[16,48,256]{2,1,0:T(8,128)(2,1)}), bf16[16,48,256]{2,1,0:T(8,128)(2,1)S(1)}, u32[]{:S(2)}, u32[]{:S(2)}) async-start(bf16[16,48,256]{2,1,0:T(8,128)(2,1)} %tokens.1), calls=%async_computation.3 | async-start | bytes 786432 | tf_op jit(solution)/shard_map/all_to_all | solution.py:603
  121.7 0.1 subtract_bitcast_fusion.tokens_ref
  121.8 9.8 %all-to-all-done.3 = bf16[16,48,256]{2,1,0:T(8,128)(2,1)S(1)} async-done(((bf16[16,48,256]{2,1,0:T(8,128)(2,1)}), bf16[16,48,256]{2,1,0:T(8,128)(2,1)S(1)}, u32[]{:S(2)}, u32[]{:S(2)}) %all-to-all-start.3) | async-done | bytes 393248 | tf_op jit(solution)/shard_map/all_to_all | solution.py:603
  131.6 0.0 copy-done
  131.6 0.0 copy-done.1
  131.6 0.0 copy-done.2
  131.6 0.0 copy-done.3
  131.6 0.0 copy-done.4
  131.7 2.0 %updates.1 = (bf16[256,768]{1,0:T(8,128)(2,1)}, bf16[128,128]{1,0:T(8,128)(2,1)}) custom-call(s32[4]{0:T(128)S(1)} %copy-done.4, s32[1,128]{1,0:T(1,128)S(1)} %subtract_bitcast_fusion.tokens_ref, bf16[768,256]{1,0:T(8,128)(2,1)S(1)} %bitcast.10, bf16[768,768]{1,0:T(8,128)(2,1)S(1)} %copy-done, bf16[256,768]{1,0:T(8,128)(2,1)S(1)} %copy-done.2, ...), custom_call_target="tpu_custom_call" | custom-call | tf_op jit(solution)/shard_map/updates/pallas_call | solution.py:473
  (2 shorter events, 0.1 us)
Async XLA Ops:
  1.4 23.4 %collective-permute-start = (bf16[64,128]{1,0:T(8,128)(2,1)S(1)}, bf16[64,128]{1,0:T(8,128)(2,1)S(1)}, u32[]{:S(2)}, u32[]{:S(2)}) collective-permute-start(bf16[64,128]{1,0:T(8,128)(2,1)S(1)} %slice_select_fusion.1), channel_id=1, source_target_pairs={{15,18},{31,36},{47,54},{63,72},{79,90},{95,108},{111,126},{16,1},... | collective-permute-start | bytes 49160 | tf_op jit(solution)/shard_map/ppermute | solution.py:517
  3.3 22.6 %copy-start.8 = (bf16[128,128]{1,0:T(8,128)(2,1)S(1)}, bf16[128,128]{1,0:T(8,128)(2,1)}, u32[]{:S(2)}) copy-start(bf16[128,128]{1,0:T(8,128)(2,1)} %param.20) | copy-start | bytes 98308
  3.3 55.1 %copy-start.10 = (f32[768]{0:T(1024)S(1)}, f32[768]{0:T(1024)}, u32[]{:S(2)}) copy-start(f32[768]{0:T(1024)} %param.30) | copy-start | bytes 9220
  3.3 55.7 %copy-start.9 = (s32[16384]{0:T(1024)S(1)}, s32[16384]{0:T(1024)}, u32[]{:S(2)}) copy-start(s32[16384]{0:T(1024)} %param.21) | copy-start | bytes 196612
  47.6 26.0 %copy-start.6 = (bf16[8,256,128]{2,1,0:T(8,128)(2,1)}, bf16[8,256,128]{2,1,0:T(8,128)(2,1)S(1)}, u32[]{:S(2)}) copy-start(bf16[8,256,128]{2,1,0:T(8,128)(2,1)S(1)} %all_to_all.20.mine_hbm) | copy-start | bytes 1572868
  47.6 18.1 %collective-permute-start.5 = (bf16[8,256,128]{2,1,0:T(8,128)(2,1)S(1)}, bf16[8,256,128]{2,1,0:T(8,128)(2,1)S(1)}, u32[]{:S(2)}, u32[]{:S(2)}) collective-permute-start(bf16[8,256,128]{2,1,0:T(8,128)(2,1)S(1)} %all_to_all.20.mine_hbm), channel_id=1, source_target_pairs={{0,1},{1,0},{2,3},{3,2},{4,5},{5,4},{6,7},{7,6},{8,9},{9,8},{10,11... | collective-permute-start | bytes 1572872 | tf_op jit(solution)/shard_map/ppermute | solution.py:578
  47.6 6.7 %collective-permute-start.1 = (bf16[4,224,128]{2,1,0:T(8,128)(2,1)S(1)}, bf16[4,224,128]{2,1,0:T(8,128)(2,1)S(1)}, u32[]{:S(2)}, u32[]{:S(2)}) collective-permute-start(bf16[4,224,128]{2,1,0:T(8,128)(2,1)S(1)} %maximum_select_fusion), channel_id=1, source_target_pairs={{0,8},{1,9},{18,26},{19,27},{36,44},{37,45},{54,62},{55,63},{72,64... | collective-permute-start | bytes 688136 | tf_op jit(solution)/shard_map/ppermute | solution.py:550
  54.4 5.2 %collective-permute-start.4 = (bf16[4,224,128]{2,1,0:T(8,128)(2,1)S(1)}, bf16[4,224,128]{2,1,0:T(8,128)(2,1)S(1)}, u32[]{:S(2)}, u32[]{:S(2)}) collective-permute-start(bf16[4,224,128]{2,1,0:T(8,128)(2,1)S(1)} %add.39), channel_id=1, source_target_pairs={{0,6},{1,7},{8,14},{9,15},{18,16},{19,17},{26,24},{27,25},{36,34},... | collective-permute-start | bytes 688136 | tf_op jit(solution)/shard_map/ppermute | solution.py:563
  55.7 5.1 %collective-permute-start.3 = (bf16[4,224,128]{2,1,0:T(8,128)(2,1)S(1)}, bf16[4,224,128]{2,1,0:T(8,128)(2,1)S(1)}, u32[]{:S(2)}, u32[]{:S(2)}) collective-permute-start(bf16[4,224,128]{2,1,0:T(8,128)(2,1)S(1)} %add.39), channel_id=1, source_target_pairs={{0,4},{1,5},{8,12},{9,13},{18,22},{19,23},{26,30},{27,31},{36,32},... | collective-permute-start | bytes 688136 | tf_op jit(solution)/shard_map/ppermute | solution.py:563
  57.0 8.7 %collective-permute-start.2 = (bf16[4,224,128]{2,1,0:T(8,128)(2,1)S(1)}, bf16[4,224,128]{2,1,0:T(8,128)(2,1)S(1)}, u32[]{:S(2)}, u32[]{:S(2)}) collective-permute-start(bf16[4,224,128]{2,1,0:T(8,128)(2,1)S(1)} %add.39), channel_id=1, source_target_pairs={{0,2},{1,3},{8,10},{9,11},{18,20},{19,21},{26,28},{27,29},{36,38},... | collective-permute-start | bytes 688136 | tf_op jit(solution)/shard_map/ppermute | solution.py:563
  65.7 7.9 %copy-start.11 = (bf16[8,256,128]{2,1,0:T(8,128)(2,1)}, bf16[8,256,128]{2,1,0:T(8,128)(2,1)S(1)}, u32[]{:S(2)}) copy-start(bf16[8,256,128]{2,1,0:T(8,128)(2,1)S(1)} %collective-permute-done.5.theirs_hbm) | copy-start | bytes 1572868
  65.8 7.8 %copy-start.7 = (bf16[4,224,128]{2,1,0:T(8,128)(2,1)}, bf16[4,224,128]{2,1,0:T(8,128)(2,1)S(1)}, u32[]{:S(2)}) copy-start(bf16[4,224,128]{2,1,0:T(8,128)(2,1)S(1)} %add_add_fusion.half_ref) | copy-start | bytes 688132
  65.8 15.2 %collective-permute-start.6 = (bf16[4,224,128]{2,1,0:T(8,128)(2,1)S(1)}, bf16[4,224,128]{2,1,0:T(8,128)(2,1)S(1)}, u32[]{:S(2)}, u32[]{:S(2)}) collective-permute-start(bf16[4,224,128]{2,1,0:T(8,128)(2,1)S(1)} %add_add_fusion.half_ref), channel_id=1, source_target_pairs={{0,1},{1,0},{2,3},{3,2},{4,5},{5,4},{6,7},{7,6},{8,9},{9,8},{10,11... | collective-permute-start | bytes 688136 | tf_op jit(solution)/shard_map/ppermute | solution.py:582
  73.6 24.6 %all-to-all-start.1 = ((bf16[16,256,128]{2,1,0:T(8,128)(2,1)}), bf16[16,256,128]{2,1,0:T(8,128)(2,1)S(1)}, u32[]{:S(2)}, u32[]{:S(2)}) async-start(bf16[16,256,128]{2,1,0:T(8,128)(2,1)} %pair.3), calls=%async_computation.1 | async-start | bytes 2097152 | tf_op jit(solution)/shard_map/all_to_all | solution.py:584
  81.0 0.7 copy-start.12
  95.1 36.5 %copy-start = (bf16[768,768]{1,0:T(8,128)(2,1)S(1)}, bf16[768,768]{1,0:T(8,128)(2,1)}, u32[]{:S(2)}) copy-start(bf16[768,768]{1,0:T(8,128)(2,1)} %exit_ref.3) | copy-start | bytes 3538948
  95.1 36.5 %copy-start.1 = (bf16[2048,128]{1,0:T(8,128)(2,1)S(1)}, bf16[2048,128]{1,0:T(8,128)(2,1)}, u32[]{:S(2)}) copy-start(bf16[2048,128]{1,0:T(8,128)(2,1)} %get-tuple-element.55.mid_ref) | copy-start | bytes 1572868
  95.1 36.5 %copy-start.2 = (bf16[256,768]{1,0:T(8,128)(2,1)S(1)}, bf16[256,768]{1,0:T(8,128)(2,1)}, u32[]{:S(2)}) copy-start(bf16[256,768]{1,0:T(8,128)(2,1)} %get-tuple-element.54.tmid_ref) | copy-start | bytes 1179652
  95.1 36.5 %copy-start.3 = (bf16[768,128]{1,0:T(8,128)(2,1)S(1)}, bf16[768,128]{1,0:T(8,128)(2,1)}, u32[]{:S(2)}) copy-start(bf16[768,128]{1,0:T(8,128)(2,1)} %back_ref.1) | copy-start | bytes 589828
  95.2 36.5 %copy-start.4 = (s32[4]{0:T(128)S(1)}, s32[4]{0:T(128)}, u32[]{:S(2)}) copy-start(s32[4]{0:T(128)} %pad_add_fusion.place) | copy-start | bytes 52
  98.2 11.4 %copy-start.5 = (bf16[16,256,128]{2,1,0:T(8,128)(2,1)}, bf16[16,256,128]{2,1,0:T(8,128)(2,1)S(1)}, u32[]{:S(2)}) copy-start(bf16[16,256,128]{2,1,0:T(8,128)(2,1)S(1)} %all-to-all-done.1.bias_hbm) | copy-start | bytes 3145732
  114.3 17.3 %all-to-all-start.3 = ((bf16[16,48,256]{2,1,0:T(8,128)(2,1)}), bf16[16,48,256]{2,1,0:T(8,128)(2,1)S(1)}, u32[]{:S(2)}, u32[]{:S(2)}) async-start(bf16[16,48,256]{2,1,0:T(8,128)(2,1)} %tokens.1), calls=%async_computation.3 | async-start | bytes 786432 | tf_op jit(solution)/shard_map/all_to_all | solution.py:603

commit v9 on v7

--- a/solution.py
+++ b/solution.py
@@ -103,15 +103,9 @@
 
         @pl.when(pl.program_id(0) == 0)
         def _():
-            flip = place[3] == 1
-            edge = jnp.where(flip, stacked[:HA, rows - HALO :], stacked[:HA, :HALO])
-            edge = edge.reshape(HA * HALO, CZ)
-            turned = pltpu.roll(edge, HALO, 1)
-            half = HA * HALO // 2
-            low = jnp.where(flip, edge[:half], turned[:half])
-            high = jnp.where(flip, turned[half:], edge[half:])
-            lane = lax.broadcasted_iota(jnp.int32, (half, CZ), 1)
-            outs[2][...] = jnp.where(lane < HALO, low, high).astype(bf16)
+            edge = jnp.where(place[3] == 1, stacked[:HA, rows - HALO :], stacked[:HA, :HALO])
+            edge = pltpu.roll(edge.reshape(HA * HALO, CZ), HALO, 1)
+            outs[2][...] = edge.reshape(HA, HALO, CZ).astype(bf16)
 
 
 def pair_rows(place, pair, weights, before, first, size, count, bands):
@@ -143,7 +137,7 @@
                 lambda i, place: (0, i + place[3] * (count - 1 - 2 * i), 0),
             )
         )
-        out_shape.append(jax.ShapeDtypeStruct((HA * HALO // 2, cols), bf16))
+        out_shape.append(jax.ShapeDtypeStruct((HA, HALO, cols), bf16))
         out_specs.append(full(out_shape[-1]))
     aliases = {}
     if before:
@@ -218,12 +212,6 @@
     copies[1].wait()
     rest = jnp.zeros((rows - REACH, KW), bf16)
     middle = jnp.zeros((rows - 2 * HALO, KW), bf16)
-    left = jnp.maximum(row - 1, 0)
-    right = jnp.minimum(row + 1, chips - 1)
-    left = jnp.where(even, theirs_ref[left, per:], mine_ref[left, per:])
-    right = jnp.where(even, mine_ref[right, per:], theirs_ref[right, per:])
-    left_turned = pltpu.roll(left.astype(f32), HALO, 1).astype(bf16)
-    right_turned = pltpu.roll(right.astype(f32), HALO, 1).astype(bf16)
     before, after = [], []
     for h in range(HA):
         mine, theirs = half_ref[h], other_ref[h]
@@ -231,17 +219,15 @@
         before.append(mine[REACH:])
         after.append(theirs[REACH:])
         base = h * 3 * KW
-        part = slice(h % 2 * HALO, (h % 2 + 1) * HALO)
-        edges = (left, right_turned) if h < HA // 2 else (left_turned, right)
         bias_ref[:, base : base + KW] = jnp.concatenate([mine[:REACH], rest], axis=0)
         bias_ref[:, base + KW : base + 2 * KW] = jnp.concatenate([rest, theirs[:REACH]], axis=0)
         bias_ref[:, base + 2 * KW : base + 3 * KW] = jnp.concatenate(
-            [edges[0][part], middle, edges[1][part]], axis=0
+            [mine[REACH - HALO : REACH], middle, theirs[:HALO]], axis=0
         )
     ext_ref[:HALO] = jnp.concatenate(before, axis=0)
     ext_ref[HALO + atoms :] = jnp.concatenate(after, axis=0)
     for k in range(chips):
-        mine, theirs = mine_ref[k, :per], theirs_ref[k, :per]
+        mine, theirs = mine_ref[k], theirs_ref[k]
         at = HALO + 2 * k * per
         ext_ref[at : at + per] = jnp.where(even, mine, theirs)
         ext_ref[at + per : at + 2 * per] = jnp.where(even, theirs, mine)
@@ -379,7 +365,7 @@
         + [pltpu.VMEM((2 * HDT, rows), bf16), pltpu.SemaphoreType.DMA((3 + copies,))],
         compiler_params=pltpu.CompilerParams(vmem_limit_bytes=GRANT),
         cost_estimate=pl.CostEstimate(
-            flops=10**7, bytes_accessed=2**14, transcendentals=2**10
+            flops=10**10, bytes_accessed=2**24, transcendentals=2**22
         ),
         name="atoms",
     )(place, *operands, *bands, *fetched)
@@ -543,20 +529,37 @@
     ring = chips // 2
     flat = lambda k, step: k // ring * ring + (k + step) % ring
     across = lambda k: (k + ring) % chips
+    split = REACH - HALO
     band = jnp.where(even, band[:, :REACH], band[:, 2 * PART - REACH :])
     band = jnp.concatenate([band, halo.reshape(HA, HALO // HA, CA)], axis=1)
-    band = jnp.where(here, band, jnp.zeros_like(band))
-    band_y = lax.ppermute(
-        band,
-        both,
-        [(at(r, r, core), at(r, across(r), core)) for r in range(row_count) for core in range(2)],
-    )
+    none = jnp.zeros_like(band)
+    place_in = lax.broadcasted_iota(jnp.int32, band.shape, 1)
+    lane = lax.broadcasted_iota(jnp.int32, band.shape, 2)
+    late = (place_in >= split) & (place_in < REACH) & (lane < HALO)
+    early = (place_in < HALO) & (lane >= HALO)
+    late_edge = jnp.concatenate([none[:, :split], edge, none[:, REACH:]], axis=1)
+    early_edge = jnp.concatenate([edge, none[:, HALO:]], axis=1)
+    band = jnp.where(jnp.where(even, late, early), none, band)
+    edge = jnp.where(
+        even, jnp.where(early, early_edge, none), jnp.where(late, late_edge, none)
+    )
+    band = jnp.where(here, band, edge)
+    over_y = [
+        (at(r, r, core), at(r, across(r), core)) for r in range(row_count) for core in range(2)
+    ]
+    beside = lambda to: [(at(r, r - 1, 1), at(r, to(r), 0)) for r in range(1, row_count)] + [
+        (at(r, r + 1, 0), at(r, to(r), 1)) for r in range(row_count - 1)
+    ]
+    arrived = [
+        lax.ppermute(band, both, over_y + beside(lambda r: r)),
+        lax.ppermute(band, both, beside(across)),
+    ]
     cores = [[at(0, k, core) for k in range(chips)] for core in range(2)]
-    own_part = jnp.concatenate([own_atoms, edge], axis=0)
-    own_part = jnp.broadcast_to(own_part[None], (chips,) + own_part.shape)
-    shards = lax.all_to_all(own_part, "col", 0, 0, axis_index_groups=cores)
+    own_atoms = jnp.broadcast_to(own_atoms[None], (chips,) + own_atoms.shape)
+    shards = lax.all_to_all(own_atoms, "col", 0, 0, axis_index_groups=cores)
     swap = [(i, i ^ 1) for i in range(col_count)]
-    band = band + band_y
+    arrived = lax.optimization_barrier(arrived)
+    band = jnp.where(here, band, none) + arrived[0] + arrived[1]
     band, token_bias = lax.optimization_barrier((band, token_bias))
     sent = [
         lax.ppermute(
@@ -576,6 +579,7 @@
     )
     theirs = lax.ppermute(shards, "col", swap)
     gain = token_gain[None]
+    theirs, token_bias = lax.optimization_barrier((theirs, token_bias))
     head_bias = lax.all_to_all(token_bias, "col", 0, 0)
     sent, theirs, gain, ext_tokens = lax.optimization_barrier((sent, theirs, gain, ext_tokens))
     band = band + sent[0] + sent[1] + sent[2]

time: 140 us -> 117 us (0.84)
  waiting for transfers between devices: 29.2 us -> 14.1 us
  starting transfers between devices: 40.8 us -> 34.1 us
    ppermute x3, waiting for transfers between devices: 14 us -> 0.69 us  [local(): lax.ppermute(band, both, [(at(r, k, core), at(r, flat(k, step), core)) fo...]
    all_to_all x1, starting transfers between devices: 10.6 us -> 5.68 us  [local(): shards = lax.all_to_all(own_atoms, 'col', 0, 0, axis_index_groups=cores)]
    ppermute x1 -> x2, waiting for transfers between devices: 4.31 us -> 0.01 us  [the longest x1 0.01 us: local(): lax.ppermute(band, both, over_y + beside(lambda r: r))]
    all_to_all x1, starting transfers between devices: 10.5 us -> 7.21 us  [local(): gated = lax.all_to_all(gated, 'col', 0, 0).reshape(CS, rows)]
    all_to_all x1, waiting for transfers between devices: 0.01 us -> 3.21 us  [local(): head_bias = lax.all_to_all(token_bias, 'col', 0, 0)]
    ppermute x1 -> x2, starting transfers between devices: 4.88 us -> 6.31 us  [the longest x1 5.64 us: local(): lax.ppermute(band, both, over_y + beside(lambda r: r))]
  transfers between devices with their start and end apart: 10 -> 11, of which waited for: 6 -> 4; matrix products, arithmetic and copies ran while one was open for 2% -> 2% of each run, Pallas kernels for 29% -> 35%
where the time goes in v9:
time: 117 us
  Pallas kernels  47 us (40%)
  starting transfers between devices  34.1 us (29%)
  waiting for transfers between devices  14.1 us (12%)
  blocking collectives  13.8 us (12%)
  other arithmetic  3.84 us (3%)
  local copies, waits for them, and re-layouts  2.73 us (2%)
    pallas_call x2, Pallas kernels, pair_rows(): pl.pallas_call(functools.partial(pair_body, bands=bands), grid_spec=pltpu...  27 us
    all_to_all x1, blocking collectives, local(): keyvals = lax.all_to_all(keyvals, 'row', 0, 0)  13.8 us
    pallas_call x1, Pallas kernels, atom_attention(): pl.pallas_call(atoms_body, grid=(1,), in_specs=[SMEM] + [full(array) for...  13.2 us
    all_to_all x1, waiting for transfers between devices, local(): gated = lax.all_to_all(gated, 'col', 0, 0).reshape(CS, rows)  9.82 us
    all_to_all x1, starting transfers between devices, local(): gated = lax.all_to_all(gated, 'col', 0, 0).reshape(CS, rows)  7.21 us
    ppermute x3, starting transfers between devices, local(): lax.ppermute(band, both, [(at(r, k, core), at(r, flat(k, step), core)) fo...  7.19 us
    all_to_all x1, starting transfers between devices, local(): head_bias = lax.all_to_all(token_bias, 'col', 0, 0)  6.38 us
    all_to_all x1, starting transfers between devices, local(): shards = lax.all_to_all(own_atoms, 'col', 0, 0, axis_index_groups=cores)  5.68 us
  transfers between devices with their start and end apart: 11, of which 4 were waited for; matrix products, arithmetic and copies ran while one was open for 2% of the time, Pallas kernels for 35%

profile of v9, /device:TPU:1, one launch (start us, length us, event | category | flops | bytes accessed | tf_op | source)
XLA Modules:
  0.0 116.5 jit_solution(5264692835896513046)
XLA Ops:
  0.6 0.7 slice_select_fusion.1
  1.4 1.3 %collective-permute-start = (bf16[64,128]{1,0:T(8,128)(2,1)S(1)}, bf16[64,128]{1,0:T(8,128)(2,1)S(1)}, u32[]{:S(2)}, u32[]{:S(2)}) collective-permute-start(bf16[64,128]{1,0:T(8,128)(2,1)S(1)} %slice_select_fusion.1), channel_id=1, source_target_pairs={{15,18},{31,36},{47,54},{63,72},{79,90},{95,108},{111,126},{16,1},... | collective-permute-start | bytes 49160 | tf_op jit(solution)/shard_map/ppermute | solution.py:503
  2.7 0.6 pad_add_fusion.place
  3.3 0.0 copy-start.8
  3.3 0.0 copy-start.9
  3.3 0.0 copy-start.10
  3.3 21.5 %pair.2 = (bf16[16,256,128]{2,1,0:T(8,128)(2,1)}, bf16[4,224,128]{2,1,0:T(8,128)(2,1)}, bf16[4,64,128]{2,1,0:T(8,128)(2,1)}) custom-call(s32[4]{0:T(128)} %pad_add_fusion.place, bf16[256,128,128]{2,1,0:T(8,128)(2,1)} %pair_ref.3, bf16[128,512]{1,0:T(8,128)(2,1)} %up_ref.3, bf16[256,128]{1,0:T(8,128)(2,1)} %down_ref.3, bf16[20,128]{1,0:T(8,128)(2,1)} %bitcast.12, ...), custom_call_target="tpu_custom_call" | custom-call | flops 14336000000 | bytes 8601600 | tf_op jit(solution)/shard_map/pair/pallas_call | solution.py:147
  24.8 0.1 pad.8.clone
  24.9 0.0 collective-permute-done
  24.9 1.1 slice_select_fusion
  26.0 1.1 fusion.1
  27.2 0.7 collective-permute-start.2
  27.8 5.6 %collective-permute-start.1 = (bf16[4,224,128]{2,1,0:T(8,128)(2,1)S(1)}, bf16[4,224,128]{2,1,0:T(8,128)(2,1)S(1)}, u32[]{:S(2)}, u32[]{:S(2)}) collective-permute-start(bf16[4,224,128]{2,1,0:T(8,128)(2,1)S(1)} %fusion.1), channel_id=1, source_target_pairs={{0,8},{1,9},{18,26},{19,27},{36,44},{37,45},{54,62},{55,63},{72,64... | collective-permute-start | bytes 688136 | tf_op jit(solution)/shard_map/ppermute | solution.py:554
  33.5 0.0 copy-done.8
  33.5 0.7 broadcast_in_dim.27
  34.2 5.7 %all-to-all-start = ((bf16[8,128,128]{2,1,0:T(8,128)(2,1)}), bf16[8,128,128]{2,1,0:T(8,128)(2,1)S(1)}, u32[]{:S(2)}, u32[]{:S(2)}) async-start(bf16[8,128,128]{2,1,0:T(8,128)(2,1)} %broadcast_in_dim.27), calls=%async_computation | async-start | bytes 524288 | tf_op jit(solution)/shard_map/all_to_all | solution.py:559
  39.9 0.0 collective-permute-done.2
  39.9 0.0 collective-permute-done.1
  40.0 4.6 %collective-permute-start.5 = (bf16[4,224,128]{2,1,0:T(8,128)(2,1)S(1)}, bf16[4,224,128]{2,1,0:T(8,128)(2,1)S(1)}, u32[]{:S(2)}, u32[]{:S(2)}) collective-permute-start(bf16[4,224,128]{2,1,0:T(8,128)(2,1)S(1)} %add_add_fusion.1), channel_id=1, source_target_pairs={{0,6},{1,7},{8,14},{9,15},{18,16},{19,17},{26,24},{27,25},{36,34},... | collective-permute-start | bytes 688136 | tf_op jit(solution)/shard_map/ppermute | solution.py:565
  44.6 1.3 %collective-permute-start.4 = (bf16[4,224,128]{2,1,0:T(8,128)(2,1)S(1)}, bf16[4,224,128]{2,1,0:T(8,128)(2,1)S(1)}, u32[]{:S(2)}, u32[]{:S(2)}) collective-permute-start(bf16[4,224,128]{2,1,0:T(8,128)(2,1)S(1)} %add_add_fusion.1), channel_id=1, source_target_pairs={{0,4},{1,5},{8,12},{9,13},{18,22},{19,23},{26,30},{27,31},{36,32},... | collective-permute-start | bytes 688136 | tf_op jit(solution)/shard_map/ppermute | solution.py:565
  45.9 1.3 %collective-permute-start.3 = (bf16[4,224,128]{2,1,0:T(8,128)(2,1)S(1)}, bf16[4,224,128]{2,1,0:T(8,128)(2,1)S(1)}, u32[]{:S(2)}, u32[]{:S(2)}) collective-permute-start(bf16[4,224,128]{2,1,0:T(8,128)(2,1)S(1)} %add_add_fusion.1), channel_id=1, source_target_pairs={{0,2},{1,3},{8,10},{9,11},{18,20},{19,21},{26,28},{27,29},{36,38},... | collective-permute-start | bytes 688136 | tf_op jit(solution)/shard_map/ppermute | solution.py:565
  47.2 0.4 all-to-all-done.mine_hbm
  47.5 0.0 copy-start.6
  47.5 0.0 collective-permute-start.6
  47.5 0.0 copy-done.9
  47.5 0.1 fusion.3
  47.6 0.0 copy-done.10
  47.6 0.6 broadcast_in_dim.28.gain_ref
  48.2 0.6 broadcast_in_dim.29.tokens_ref
  48.8 5.5 %pair.3 = bf16[16,256,128]{2,1,0:T(8,128)(2,1)} custom-call(s32[4]{0:T(128)} %pad_add_fusion.place, bf16[256,128,128]{2,1,0:T(8,128)(2,1)} %pair_ref.3, bf16[128,512]{1,0:T(8,128)(2,1)} %up_ref.3, bf16[256,128]{1,0:T(8,128)(2,1)} %down_ref.3, bf16[20,128]{1,0:T(8,128)(2,1)} %bitcast.13, ...), custom_call_target="tpu_custom_call", output_to_operand_aliasing={{}: (6, {})} | custom-call | flops 2048000000 | bytes 1228800 | tf_op jit(solution)/shard_map/pair/pallas_call | solution.py:147
  54.4 0.0 copy-done.6
  54.4 0.0 collective-permute-done.6.theirs_hbm
  54.4 0.0 copy-start.11
  54.4 0.0 collective-permute-done.5
  54.4 0.0 collective-permute-done.4
  54.4 0.7 collective-permute-done.3
  55.2 0.0 copy-start.7
  55.2 0.1 collective-permute-start.7
  55.3 6.4 %all-to-all-start.1 = ((bf16[16,256,128]{2,1,0:T(8,128)(2,1)}), bf16[16,256,128]{2,1,0:T(8,128)(2,1)S(1)}, u32[]{:S(2)}, u32[]{:S(2)}) async-start(bf16[16,256,128]{2,1,0:T(8,128)(2,1)} %pair.3), calls=%async_computation.1 | async-start | bytes 2097152 | tf_op jit(solution)/shard_map/all_to_all | solution.py:583
  61.6 0.0 collective-permute-done.7.other_ref
  61.6 0.0 copy-start.12
  61.6 0.0 copy-done.11
  61.7 0.0 copy-done.7
  61.7 0.6 copy-done.12
  62.3 13.2 %atoms.1 = (bf16[2048,128]{1,0:T(8,128)(2,1)}, bf16[256,768]{1,0:T(8,128)(2,1)}, f32[256,256]{1,0:T(8,128)}, bf16[8,96,256]{2,1,0:T(8,128)(2,1)}) custom-call(s32[4]{0:T(128)} %pad_add_fusion.place, s32[1,2176]{1,0:T(1,128)} %broadcast_in_dim.29.tokens_ref, f32[1,128]{1,0:T(1,128)} %bitcast.15, bf16[128,512]{1,0:T(8,128)(2,1)} %proj_ref.1, ...), custom_call_target="tpu_custom_call" | custom-call | flops 10000000000 | bytes 16777216 | tf_op jit(solution)/shard_map/atoms/pallas_call | solution.py:345
  75.6 0.0 copy-start
  75.6 0.0 copy-start.1
  75.6 0.0 copy-start.2
  75.6 0.0 copy-start.3
  75.6 0.0 copy-start.4
  75.6 3.2 %all-to-all-done.1.bias_hbm = bf16[16,256,128]{2,1,0:T(8,128)(2,1)S(1)} async-done(((bf16[16,256,128]{2,1,0:T(8,128)(2,1)}), bf16[16,256,128]{2,1,0:T(8,128)(2,1)S(1)}, u32[]{:S(2)}, u32[]{:S(2)}) %all-to-all-start.1) | async-done | bytes 1048608 | tf_op jit(solution)/shard_map/all_to_all | solution.py:583
  78.8 0.0 copy-start.5
  78.8 13.8 %all_to_all.20.kv_hbm = bf16[8,96,256]{2,1,0:T(8,128)(2,1)} all-to-all(bf16[8,96,256]{2,1,0:T(8,128)(2,1)} %get-tuple-element.50), channel_id=1, replica_groups=mesh['row'=8,'col'=16] {'row'}, dimensions={0} | all-to-all | bytes 786432 | tf_op jit(solution)/shard_map/all_to_all | solution.py:603
  92.6 0.0 copy-done.5
  92.6 4.7 %tokens.1 = bf16[16,48,256]{2,1,0:T(8,128)(2,1)} custom-call(s32[4]{0:T(128)} %pad_add_fusion.place, f32[16]{0:T(128)} %strength.1, s32[1,2048]{1,0:T(1,128)} %bitcast.14, f32[256,256]{1,0:T(8,128)} %get-tuple-element.47.state_hbm, bf16[8,96,256]{2,1,0:T(8,128)(2,1)} %all_to_all.20.kv_hbm, bf16[16,256,128]{2,1,0:T(8,128)(2,1)} %copy-done.5), custom_call_target="tpu_custom_call" | custom-call | flops 1000000000 | bytes 4194304 | tf_op jit(solution)/shard_map/tokens/pallas_call | solution.py:424
  97.4 7.2 %all-to-all-start.3 = ((bf16[16,48,256]{2,1,0:T(8,128)(2,1)}), bf16[16,48,256]{2,1,0:T(8,128)(2,1)S(1)}, u32[]{:S(2)}, u32[]{:S(2)}) async-start(bf16[16,48,256]{2,1,0:T(8,128)(2,1)} %tokens.1), calls=%async_computation.3 | async-start | bytes 786432 | tf_op jit(solution)/shard_map/all_to_all | solution.py:605
  104.6 0.1 subtract_bitcast_fusion.tokens_ref
  104.7 9.8 %all-to-all-done.3 = bf16[16,48,256]{2,1,0:T(8,128)(2,1)S(1)} async-done(((bf16[16,48,256]{2,1,0:T(8,128)(2,1)}), bf16[16,48,256]{2,1,0:T(8,128)(2,1)S(1)}, u32[]{:S(2)}, u32[]{:S(2)}) %all-to-all-start.3) | async-done | bytes 393248 | tf_op jit(solution)/shard_map/all_to_all | solution.py:605
  114.5 0.0 copy-done
  114.5 0.0 copy-done.1
  114.5 0.0 copy-done.2
  114.5 0.0 copy-done.3
  114.5 0.0 copy-done.4
  114.5 2.0 %updates.1 = (bf16[256,768]{1,0:T(8,128)(2,1)}, bf16[128,128]{1,0:T(8,128)(2,1)}) custom-call(s32[4]{0:T(128)S(1)} %copy-done.4, s32[1,128]{1,0:T(1,128)S(1)} %subtract_bitcast_fusion.tokens_ref, bf16[768,256]{1,0:T(8,128)(2,1)S(1)} %bitcast.10, bf16[768,768]{1,0:T(8,128)(2,1)S(1)} %copy-done, bf16[256,768]{1,0:T(8,128)(2,1)S(1)} %copy-done.2, ...), custom_call_target="tpu_custom_call" | custom-call | tf_op jit(solution)/shard_map/updates/pallas_call | solution.py:459
  (7 shorter events, 0.1 us)
Async XLA Ops:
  1.4 23.6 %collective-permute-start = (bf16[64,128]{1,0:T(8,128)(2,1)S(1)}, bf16[64,128]{1,0:T(8,128)(2,1)S(1)}, u32[]{:S(2)}, u32[]{:S(2)}) collective-permute-start(bf16[64,128]{1,0:T(8,128)(2,1)S(1)} %slice_select_fusion.1), channel_id=1, source_target_pairs={{15,18},{31,36},{47,54},{63,72},{79,90},{95,108},{111,126},{16,1},... | collective-permute-start | bytes 49160 | tf_op jit(solution)/shard_map/ppermute | solution.py:503
  3.3 30.2 %copy-start.8 = (bf16[128,128]{1,0:T(8,128)(2,1)S(1)}, bf16[128,128]{1,0:T(8,128)(2,1)}, u32[]{:S(2)}) copy-start(bf16[128,128]{1,0:T(8,128)(2,1)} %param.20) | copy-start | bytes 98308
  3.3 44.2 %copy-start.9 = (s32[16384]{0:T(1024)S(1)}, s32[16384]{0:T(1024)}, u32[]{:S(2)}) copy-start(s32[16384]{0:T(1024)} %param.21) | copy-start | bytes 196612
  3.3 44.3 %copy-start.10 = (f32[768]{0:T(1024)S(1)}, f32[768]{0:T(1024)}, u32[]{:S(2)}) copy-start(f32[768]{0:T(1024)} %param.30) | copy-start | bytes 9220
  27.2 12.8 %collective-permute-start.2 = (bf16[4,224,128]{2,1,0:T(8,128)(2,1)S(1)}, bf16[4,224,128]{2,1,0:T(8,128)(2,1)S(1)}, u32[]{:S(2)}, u32[]{:S(2)}) collective-permute-start(bf16[4,224,128]{2,1,0:T(8,128)(2,1)S(1)} %fusion.1), channel_id=1, source_target_pairs={{17,26},{35,44},{53,62},{71,64},{89,82},{107,100},{125,118},{2,9},... | collective-permute-start | bytes 688136 | tf_op jit(solution)/shard_map/ppermute | solution.py:555
  27.8 12.1 %collective-permute-start.1 = (bf16[4,224,128]{2,1,0:T(8,128)(2,1)S(1)}, bf16[4,224,128]{2,1,0:T(8,128)(2,1)S(1)}, u32[]{:S(2)}, u32[]{:S(2)}) collective-permute-start(bf16[4,224,128]{2,1,0:T(8,128)(2,1)S(1)} %fusion.1), channel_id=1, source_target_pairs={{0,8},{1,9},{18,26},{19,27},{36,44},{37,45},{54,62},{55,63},{72,64... | collective-permute-start | bytes 688136 | tf_op jit(solution)/shard_map/ppermute | solution.py:554
  34.2 13.3 %all-to-all-start = ((bf16[8,128,128]{2,1,0:T(8,128)(2,1)}), bf16[8,128,128]{2,1,0:T(8,128)(2,1)S(1)}, u32[]{:S(2)}, u32[]{:S(2)}) async-start(bf16[8,128,128]{2,1,0:T(8,128)(2,1)} %broadcast_in_dim.27), calls=%async_computation | async-start | bytes 524288 | tf_op jit(solution)/shard_map/all_to_all | solution.py:559
  40.0 14.4 %collective-permute-start.5 = (bf16[4,224,128]{2,1,0:T(8,128)(2,1)S(1)}, bf16[4,224,128]{2,1,0:T(8,128)(2,1)S(1)}, u32[]{:S(2)}, u32[]{:S(2)}) collective-permute-start(bf16[4,224,128]{2,1,0:T(8,128)(2,1)S(1)} %add_add_fusion.1), channel_id=1, source_target_pairs={{0,6},{1,7},{8,14},{9,15},{18,16},{19,17},{26,24},{27,25},{36,34},... | collective-permute-start | bytes 688136 | tf_op jit(solution)/shard_map/ppermute | solution.py:565
  44.6 9.8 %collective-permute-start.4 = (bf16[4,224,128]{2,1,0:T(8,128)(2,1)S(1)}, bf16[4,224,128]{2,1,0:T(8,128)(2,1)S(1)}, u32[]{:S(2)}, u32[]{:S(2)}) collective-permute-start(bf16[4,224,128]{2,1,0:T(8,128)(2,1)S(1)} %add_add_fusion.1), channel_id=1, source_target_pairs={{0,4},{1,5},{8,12},{9,13},{18,22},{19,23},{26,30},{27,31},{36,32},... | collective-permute-start | bytes 688136 | tf_op jit(solution)/shard_map/ppermute | solution.py:565
  45.9 9.2 %collective-permute-start.3 = (bf16[4,224,128]{2,1,0:T(8,128)(2,1)S(1)}, bf16[4,224,128]{2,1,0:T(8,128)(2,1)S(1)}, u32[]{:S(2)}, u32[]{:S(2)}) collective-permute-start(bf16[4,224,128]{2,1,0:T(8,128)(2,1)S(1)} %add_add_fusion.1), channel_id=1, source_target_pairs={{0,2},{1,3},{8,10},{9,11},{18,20},{19,21},{26,28},{27,29},{36,38},... | collective-permute-start | bytes 688136 | tf_op jit(solution)/shard_map/ppermute | solution.py:565
  47.5 6.9 %copy-start.6 = (bf16[8,128,128]{2,1,0:T(8,128)(2,1)}, bf16[8,128,128]{2,1,0:T(8,128)(2,1)S(1)}, u32[]{:S(2)}) copy-start(bf16[8,128,128]{2,1,0:T(8,128)(2,1)S(1)} %all-to-all-done.mine_hbm) | copy-start | bytes 786436
  47.5 6.9 %collective-permute-start.6 = (bf16[8,128,128]{2,1,0:T(8,128)(2,1)S(1)}, bf16[8,128,128]{2,1,0:T(8,128)(2,1)S(1)}, u32[]{:S(2)}, u32[]{:S(2)}) collective-permute-start(bf16[8,128,128]{2,1,0:T(8,128)(2,1)S(1)} %all-to-all-done.mine_hbm), channel_id=1, source_target_pairs={{0,1},{1,0},{2,3},{3,2},{4,5},{5,4},{6,7},{7,6},{8,9},{9,8},{10,11... | collective-permute-start | bytes 786440 | tf_op jit(solution)/shard_map/ppermute | solution.py:580
  54.4 7.3 %copy-start.11 = (bf16[8,128,128]{2,1,0:T(8,128)(2,1)}, bf16[8,128,128]{2,1,0:T(8,128)(2,1)S(1)}, u32[]{:S(2)}) copy-start(bf16[8,128,128]{2,1,0:T(8,128)(2,1)S(1)} %collective-permute-done.6.theirs_hbm) | copy-start | bytes 786436
  55.2 6.5 %copy-start.7 = (bf16[4,224,128]{2,1,0:T(8,128)(2,1)}, bf16[4,224,128]{2,1,0:T(8,128)(2,1)S(1)}, u32[]{:S(2)}) copy-start(bf16[4,224,128]{2,1,0:T(8,128)(2,1)S(1)} %add_add_fusion.half_ref) | copy-start | bytes 688132
  55.2 6.5 %collective-permute-start.7 = (bf16[4,224,128]{2,1,0:T(8,128)(2,1)S(1)}, bf16[4,224,128]{2,1,0:T(8,128)(2,1)S(1)}, u32[]{:S(2)}, u32[]{:S(2)}) collective-permute-start(bf16[4,224,128]{2,1,0:T(8,128)(2,1)S(1)} %add_add_fusion.half_ref), channel_id=1, source_target_pairs={{0,1},{1,0},{2,3},{3,2},{4,5},{5,4},{6,7},{7,6},{8,9},{9,8},{10,11... | collective-permute-start | bytes 688136 | tf_op jit(solution)/shard_map/ppermute | solution.py:586
  55.3 23.6 %all-to-all-start.1 = ((bf16[16,256,128]{2,1,0:T(8,128)(2,1)}), bf16[16,256,128]{2,1,0:T(8,128)(2,1)S(1)}, u32[]{:S(2)}, u32[]{:S(2)}) async-start(bf16[16,256,128]{2,1,0:T(8,128)(2,1)} %pair.3), calls=%async_computation.1 | async-start | bytes 2097152 | tf_op jit(solution)/shard_map/all_to_all | solution.py:583
  61.6 0.7 copy-start.12
  75.6 38.9 %copy-start = (bf16[768,768]{1,0:T(8,128)(2,1)S(1)}, bf16[768,768]{1,0:T(8,128)(2,1)}, u32[]{:S(2)}) copy-start(bf16[768,768]{1,0:T(8,128)(2,1)} %exit_ref.3) | copy-start | bytes 3538948
  75.6 38.9 %copy-start.1 = (bf16[2048,128]{1,0:T(8,128)(2,1)S(1)}, bf16[2048,128]{1,0:T(8,128)(2,1)}, u32[]{:S(2)}) copy-start(bf16[2048,128]{1,0:T(8,128)(2,1)} %get-tuple-element.53.mid_ref) | copy-start | bytes 1572868
  75.6 38.9 %copy-start.2 = (bf16[256,768]{1,0:T(8,128)(2,1)S(1)}, bf16[256,768]{1,0:T(8,128)(2,1)}, u32[]{:S(2)}) copy-start(bf16[256,768]{1,0:T(8,128)(2,1)} %get-tuple-element.52.tmid_ref) | copy-start | bytes 1179652
  75.6 38.9 %copy-start.3 = (bf16[768,128]{1,0:T(8,128)(2,1)S(1)}, bf16[768,128]{1,0:T(8,128)(2,1)}, u32[]{:S(2)}) copy-start(bf16[768,128]{1,0:T(8,128)(2,1)} %back_ref.1) | copy-start | bytes 589828
  75.6 38.9 %copy-start.4 = (s32[4]{0:T(128)S(1)}, s32[4]{0:T(128)}, u32[]{:S(2)}) copy-start(s32[4]{0:T(128)} %pad_add_fusion.place) | copy-start | bytes 52
  78.8 13.8 %copy-start.5 = (bf16[16,256,128]{2,1,0:T(8,128)(2,1)}, bf16[16,256,128]{2,1,0:T(8,128)(2,1)S(1)}, u32[]{:S(2)}) copy-start(bf16[16,256,128]{2,1,0:T(8,128)(2,1)S(1)} %all-to-all-done.1.bias_hbm) | copy-start | bytes 3145732
  97.4 17.1 %all-to-all-start.3 = ((bf16[16,48,256]{2,1,0:T(8,128)(2,1)}), bf16[16,48,256]{2,1,0:T(8,128)(2,1)S(1)}, u32[]{:S(2)}, u32[]{:S(2)}) async-start(bf16[16,48,256]{2,1,0:T(8,128)(2,1)} %tokens.1), calls=%async_computation.3 | async-start | bytes 786432 | tf_op jit(solution)/shard_map/all_to_all | solution.py:605

commit v10 on v9

--- a/solution.py
+++ b/solution.py
@@ -82,8 +82,10 @@
 
 
 def pair_body(place, pair_ref, up_ref, down_ref, heads_ref, center_ref, *refs, bands):
-    padded = refs[-1]
-    outs = refs[-4:-1] if bands else refs[-2:-1]
+    if bands:
+        *_, bias_ref, band_ref, padded, saved = refs
+    else:
+        *_, bias_ref, padded = refs
     pair_part = pair_ref[...].reshape(-1, CZ)
     normed = scaled(dot(pair_part, center_ref[...])).astype(bf16)
     gate = dot(normed, up_ref[:, :PH] * bf16(0.5))
@@ -97,15 +99,32 @@
     rows = pair_ref.shape[0]
     stacked = jnp.stack([biases[:, i * CZ : (i + 1) * CZ] for i in range(rows)], axis=0)
     stacked = jnp.swapaxes(stacked, 0, 1)
-    outs[0][...] = stacked[HA:HB].astype(bf16)
+    bias_ref[...] = stacked[HA:HB].astype(bf16)
     if bands:
-        outs[1][...] = stacked[:HA].astype(bf16)
-
-        @pl.when(pl.program_id(0) == 0)
+        step = pl.program_id(0)
+        flip, here = place[3] == 1, place[4] == 1
+
+        @pl.when(step == 0)
         def _():
-            edge = jnp.where(place[3] == 1, stacked[:HA, rows - HALO :], stacked[:HA, :HALO])
+            edge = jnp.where(flip, stacked[:HA, rows - HALO :], stacked[:HA, :HALO])
             edge = pltpu.roll(edge.reshape(HA * HALO, CZ), HALO, 1)
-            outs[2][...] = edge.reshape(HA, HALO, CZ).astype(bf16)
+            saved[...] = edge.reshape(HA, HALO, CZ)
+
+        low = REACH - HALO - rows
+        high = rows - HALO - low
+        edge = saved[...]
+        blank = jnp.zeros((HA, rows, CZ), f32)
+        placed = jnp.where(
+            flip,
+            jnp.concatenate([blank[:, :high], edge, blank[:, :low]], axis=1),
+            jnp.concatenate([blank[:, :low], edge, blank[:, :high]], axis=1),
+        )
+        at = lax.broadcasted_iota(jnp.int32, (HA, rows, CZ), 1) - jnp.where(flip, high, low)
+        lane = lax.broadcasted_iota(jnp.int32, (HA, rows, CZ), 2)
+        side = jnp.where(flip, lane - HALO, lane)
+        spare = (at >= 0) & (at < HALO) & (side >= 0) & (side < HALO) & (step == 1)
+        own = jnp.where(here, stacked[:HA], 0.0)
+        band_ref[...] = jnp.where(spare, jnp.where(here, 0.0, placed), own).astype(bf16)
 
 
 def pair_rows(place, pair, weights, before, first, size, count, bands):
@@ -137,8 +156,6 @@
                 lambda i, place: (0, i + place[3] * (count - 1 - 2 * i), 0),
             )
         )
-        out_shape.append(jax.ShapeDtypeStruct((HA, HALO, cols), bf16))
-        out_specs.append(full(out_shape[-1]))
     aliases = {}
     if before:
         aliases = {2 + len(weights): 0}
@@ -151,7 +168,8 @@
             grid=(count,),
             in_specs=in_specs,
             out_specs=out_specs,
-            scratch_shapes=[pltpu.VMEM((32, CZ), f32)],
+            scratch_shapes=[pltpu.VMEM((32, CZ), f32)]
+            + [pltpu.VMEM((HA, HALO, CZ), f32)] * bands,
         ),
         out_shape=out_shape,
         input_output_aliases=aliases,
@@ -211,23 +229,22 @@
     copies[0].wait()
     copies[1].wait()
     rest = jnp.zeros((rows - REACH, KW), bf16)
+    skip = 2 * PART - REACH
     middle = jnp.zeros((rows - 2 * HALO, KW), bf16)
-    before, after = [], []
     for h in range(HA):
         mine, theirs = half_ref[h], other_ref[h]
         mine, theirs = jnp.where(even, mine, theirs), jnp.where(even, theirs, mine)
-        before.append(mine[REACH:])
-        after.append(theirs[REACH:])
         base = h * 3 * KW
         bias_ref[:, base : base + KW] = jnp.concatenate([mine[:REACH], rest], axis=0)
-        bias_ref[:, base + KW : base + 2 * KW] = jnp.concatenate([rest, theirs[:REACH]], axis=0)
+        bias_ref[:, base + KW : base + 2 * KW] = jnp.concatenate([rest, theirs[skip:]], axis=0)
         bias_ref[:, base + 2 * KW : base + 3 * KW] = jnp.concatenate(
-            [mine[REACH - HALO : REACH], middle, theirs[:HALO]], axis=0
-        )
-    ext_ref[:HALO] = jnp.concatenate(before, axis=0)
-    ext_ref[HALO + atoms :] = jnp.concatenate(after, axis=0)
+            [mine[REACH - HALO : REACH], middle, theirs[skip : skip + HALO]], axis=0
+        )
+    mine, theirs = mine_ref[row, per:], theirs_ref[row, per:]
+    ext_ref[:HALO] = jnp.where(even, mine, theirs)
+    ext_ref[HALO + atoms :] = jnp.where(even, theirs, mine)
     for k in range(chips):
-        mine, theirs = mine_ref[k], theirs_ref[k]
+        mine, theirs = mine_ref[k, :per], theirs_ref[k, :per]
         at = HALO + 2 * k * per
         ext_ref[at : at + per] = jnp.where(even, mine, theirs)
         ext_ref[at + per : at + 2 * per] = jnp.where(even, theirs, mine)
@@ -240,7 +257,7 @@
     lane = lax.broadcasted_iota(jnp.int32, (KW, 3 * KW), 1)
     for t in range(total // KW):
         at = slice(t * KW, (t + 1) * KW)
-        tokens = jnp.broadcast_to(tokens_ref[:, at], (KW, KW)).astype(f32).T.astype(jnp.int32)
+        tokens = jnp.broadcast_to(tokens_ref[t : t + 1, :], (KW, KW)).astype(f32).T.astype(jnp.int32)
         tokens = jnp.concatenate([tokens] * 3, axis=1)
         tokens = jnp.where(
             tokens < 0,
@@ -302,11 +319,12 @@
         sums_ref[...] += dot_tn(onehot, pooled)
         return counts + jnp.sum(onehot.astype(f32).T, axis=1, keepdims=True)
 
-    counts = lax.fori_loop(0, atoms // GROUP, group, jnp.zeros((rows, 1), f32))
+    counts = lax.fori_loop(0, atoms // GROUP, group, jnp.zeros((rows, 1), f32), unroll=True)
     token_mid = (single_ref[...].astype(f32) + sums_ref[...] / counts).astype(bf16)
     tmid_ref[...] = token_mid
     stores = fetch((mid_ref, tmid_ref), (mid_hbm, tmid_hbm), out_sems)
-    normed = (scaled(centered(token_mid.astype(f32))) * gain_ref[...]).astype(bf16)
+    gain = jnp.concatenate([gain_ref[k : k + 1, :] for k in range(gain_ref.shape[0])], axis=1)
+    normed = (scaled(centered(token_mid.astype(f32))) * gain).astype(bf16)
 
     copies[-1].wait()
 
@@ -331,7 +349,7 @@
 def atom_attention(
     place, bands, shards, tokens, atom_gain, proj, exit_w, pool, single, gain, tproj, copies
 ):
-    total = tokens.shape[1]
+    total = tokens.size
     atoms = total - 2 * HALO
     rows = single.shape[0]
     operands = (tokens, atom_gain, proj, exit_w, pool, single, gain)
@@ -509,41 +527,25 @@
     ext_tokens = lax.dynamic_slice_in_dim(
         jnp.pad(atom_token, (HALO, HALO)), row * row_atoms, row_atoms + 2 * HALO
     )
-    ext_tokens = (ext_tokens - row * rows)[None, :]
+    ext_tokens = (ext_tokens - row * rows).reshape(-1, KW)
     own_tokens = lax.dynamic_slice_in_dim(
         atom_token, row * row_atoms + col * atom_rows, atom_rows
     )
     own_tokens = (own_tokens - row * rows)[None, :]
 
     flip = ((col == 2 * row + 1) | (col == 2 * row + 2)).astype(jnp.int32)
-    place = jnp.stack([row, col, jnp.int32(row_count), flip]).astype(jnp.int32)
+    here = col // 2 == row
+    place = jnp.stack([row, col, jnp.int32(row_count), flip, here.astype(jnp.int32)])
     center = jnp.asarray((np.eye(CZ) - 1.0 / CZ).astype(bf16))
     weights = (pair_up, pair_down, bias_heads.T, center)
-    token_bias, band, edge = pair_rows(place, pair_tensor, weights, (), 0, PART, 2, True)
-    halo, band, edge, token_bias, own_atoms = lax.optimization_barrier(
-        (halo, band, edge, token_bias, atom_single)
-    )
-
-    here = col // 2 == row
-    even = col % 2 == 0
+    token_bias, band = pair_rows(place, pair_tensor, weights, (), 0, PART, 2, True)
+    own_atoms, halo, band, token_bias = lax.optimization_barrier(
+        (atom_single, halo, band, token_bias)
+    )
+
     ring = chips // 2
     flat = lambda k, step: k // ring * ring + (k + step) % ring
     across = lambda k: (k + ring) % chips
-    split = REACH - HALO
-    band = jnp.where(even, band[:, :REACH], band[:, 2 * PART - REACH :])
-    band = jnp.concatenate([band, halo.reshape(HA, HALO // HA, CA)], axis=1)
-    none = jnp.zeros_like(band)
-    place_in = lax.broadcasted_iota(jnp.int32, band.shape, 1)
-    lane = lax.broadcasted_iota(jnp.int32, band.shape, 2)
-    late = (place_in >= split) & (place_in < REACH) & (lane < HALO)
-    early = (place_in < HALO) & (lane >= HALO)
-    late_edge = jnp.concatenate([none[:, :split], edge, none[:, REACH:]], axis=1)
-    early_edge = jnp.concatenate([edge, none[:, HALO:]], axis=1)
-    band = jnp.where(jnp.where(even, late, early), none, band)
-    edge = jnp.where(
-        even, jnp.where(early, early_edge, none), jnp.where(late, late_edge, none)
-    )
-    band = jnp.where(here, band, edge)
     over_y = [
         (at(r, r, core), at(r, across(r), core)) for r in range(row_count) for core in range(2)
     ]
@@ -555,11 +557,12 @@
         lax.ppermute(band, both, beside(across)),
     ]
     cores = [[at(0, k, core) for k in range(chips)] for core in range(2)]
-    own_atoms = jnp.broadcast_to(own_atoms[None], (chips,) + own_atoms.shape)
-    shards = lax.all_to_all(own_atoms, "col", 0, 0, axis_index_groups=cores)
+    own_part = jnp.concatenate([own_atoms, halo], axis=0)
+    own_part = jnp.broadcast_to(own_part[None], (chips,) + own_part.shape)
+    shards = lax.all_to_all(own_part, "col", 0, 0, axis_index_groups=cores)
     swap = [(i, i ^ 1) for i in range(col_count)]
     arrived = lax.optimization_barrier(arrived)
-    band = jnp.where(here, band, none) + arrived[0] + arrived[1]
+    band = jnp.where(here, band, jnp.zeros_like(band)) + arrived[0] + arrived[1]
     band, token_bias = lax.optimization_barrier((band, token_bias))
     sent = [
         lax.ppermute(
@@ -578,7 +581,7 @@
         place, pair_tensor, weights, (token_bias,), 2 * PART, rows - 2 * PART, 1, False
     )
     theirs = lax.ppermute(shards, "col", swap)
-    gain = token_gain[None]
+    gain = token_gain.reshape(-1, KW)
     theirs, token_bias = lax.optimization_barrier((theirs, token_bias))
     head_bias = lax.all_to_all(token_bias, "col", 0, 0)
     sent, theirs, gain, ext_tokens = lax.optimization_barrier((sent, theirs, gain, ext_tokens))

time: 117 us -> 121 us (1.034)
  waiting for transfers between devices: 14.1 us -> 21.1 us
    ppermute x1, waiting for transfers between devices: 0.01 us -> 5.35 us  [local(): lax.ppermute(band, both, over_y + beside(lambda r: r))]
    all_to_all x1, starting transfers between devices: 5.68 us -> 10.6 us  [local(): shards = lax.all_to_all(own_part, 'col', 0, 0, axis_index_groups=cores)]
    ppermute x3, starting transfers between devices: 7.19 us -> 4.09 us  [local(): lax.ppermute(band, both, [(at(r, k, core), at(r, flat(k, step), core)) fo...]
    select_n x2 -> x0, other arithmetic: 2.21 us -> none  [the longest x1 1.14 us: local(): band = jnp.where(here, band, edge)]
    all_to_all x1, starting transfers between devices: 6.38 us -> 4.49 us  [local(): head_bias = lax.all_to_all(token_bias, 'col', 0, 0)]
    ppermute x3, waiting for transfers between devices: 0.69 us -> 2.03 us  [local(): lax.ppermute(band, both, [(at(r, k, core), at(r, flat(k, step), core)) fo...]
  transfers between devices with their start and end apart: 11 -> 11, of which waited for: 4 -> 4; matrix products, arithmetic and copies ran while one was open for 2% -> 2% of each run, Pallas kernels for 35% -> 33%
where the time goes in v10:
time: 121 us; the launch traced here: 120 us
  Pallas kernels  46.6 us (39%)
  starting transfers between devices  33.7 us (28%)
  waiting for transfers between devices  21.1 us (17%)
  blocking collectives  13.2 us (11%)
  other arithmetic  2.68 us (2%)
  local copies, waits for them, and re-layouts  2.13 us (2%)
    pallas_call x2, Pallas kernels, pair_rows(): pl.pallas_call(functools.partial(pair_body, bands=bands), grid_spec=pltpu...  27.2 us
    all_to_all x1, blocking collectives, local(): keyvals = lax.all_to_all(keyvals, 'row', 0, 0)  13.2 us
    pallas_call x1, Pallas kernels, atom_attention(): pl.pallas_call(atoms_body, grid=(1,), in_specs=[SMEM] + [full(array) for...  12.6 us
    all_to_all x1, starting transfers between devices, local(): shards = lax.all_to_all(own_part, 'col', 0, 0, axis_index_groups=cores)  10.6 us
    all_to_all x1, waiting for transfers between devices, local(): gated = lax.all_to_all(gated, 'col', 0, 0).reshape(CS, rows)  9.82 us
    all_to_all x1, starting transfers between devices, local(): gated = lax.all_to_all(gated, 'col', 0, 0).reshape(CS, rows)  6.14 us
    ppermute x1, starting transfers between devices, local(): lax.ppermute(band, both, over_y + beside(lambda r: r))  5.49 us
    ppermute x1, waiting for transfers between devices, local(): lax.ppermute(band, both, over_y + beside(lambda r: r))  5.35 us
  transfers between devices with their start and end apart: 11, of which 4 were waited for; matrix products, arithmetic and copies ran while one was open for 2% of the time, Pallas kernels for 33%

profile of v10, /device:TPU:1, one launch (start us, length us, event | category | flops | bytes accessed | tf_op | source)
XLA Modules:
  0.0 120.3 jit_solution(1283533901287099317)
XLA Ops:
  0.6 0.7 slice_select_fusion
  1.4 1.3 %collective-permute-start = (bf16[64,128]{1,0:T(8,128)(2,1)S(1)}, bf16[64,128]{1,0:T(8,128)(2,1)S(1)}, u32[]{:S(2)}, u32[]{:S(2)}) collective-permute-start(bf16[64,128]{1,0:T(8,128)(2,1)S(1)} %slice_select_fusion), channel_id=1, source_target_pairs={{15,18},{31,36},{47,54},{63,72},{79,90},{95,108},{111,126},{16,1},... | collective-permute-start | bytes 49160 | tf_op jit(solution)/shard_map/ppermute | solution.py:521
  2.7 0.6 stack.27.place
  3.3 0.0 copy-start.8
  3.3 0.0 copy-start.9
  3.3 21.6 %pair.2 = (bf16[16,256,128]{2,1,0:T(8,128)(2,1)}, bf16[4,224,128]{2,1,0:T(8,128)(2,1)}) custom-call(s32[5]{0:T(128)} %stack.27.place, bf16[256,128,128]{2,1,0:T(8,128)(2,1)} %pair_ref.3, bf16[128,512]{1,0:T(8,128)(2,1)} %up_ref.3, bf16[256,128]{1,0:T(8,128)(2,1)} %down_ref.3, bf16[20,128]{1,0:T(8,128)(2,1)} %bitcast.14, ...), custom_call_target="tpu_custom_call" | custom-call | flops 14336000000 | bytes 8601600 | tf_op jit(solution)/shard_map/pair/pallas_call | solution.py:164
  25.0 0.0 collective-permute-done
  25.0 0.0 copy-done.8
  25.0 0.8 broadcast_in_dim.21
  25.8 10.6 %all-to-all-start = ((bf16[8,192,128]{2,1,0:T(8,128)(2,1)}), bf16[8,192,128]{2,1,0:T(8,128)(2,1)S(1)}, u32[]{:S(2)}, u32[]{:S(2)}) async-start(bf16[8,192,128]{2,1,0:T(8,128)(2,1)} %broadcast_in_dim.21), calls=%async_computation | async-start | bytes 786432 | tf_op jit(solution)/shard_map/all_to_all | solution.py:562
  36.4 0.7 collective-permute-start.2
  37.1 5.5 %collective-permute-start.1 = (bf16[4,224,128]{2,1,0:T(8,128)(2,1)}, bf16[4,224,128]{2,1,0:T(8,128)(2,1)S(1)}, u32[]{:S(2)}, u32[]{:S(2)}) collective-permute-start(bf16[4,224,128]{2,1,0:T(8,128)(2,1)} %get-tuple-element.28), channel_id=1, source_target_pairs={{0,8},{1,9},{18,26},{19,27},{36,44},{37,45},{54,62},{55,63},{72,64... | collective-permute-start | bytes 688136 | tf_op jit(solution)/shard_map/ppermute | solution.py:556
  42.6 0.0 collective-permute-done.2
  42.6 5.4 %collective-permute-done.1 = bf16[4,224,128]{2,1,0:T(8,128)(2,1)S(1)} collective-permute-done((bf16[4,224,128]{2,1,0:T(8,128)(2,1)}, bf16[4,224,128]{2,1,0:T(8,128)(2,1)S(1)}, u32[]{:S(2)}, u32[]{:S(2)}) %collective-permute-start.1) | collective-permute-done | bytes 229408 | tf_op jit(solution)/shard_map/ppermute | solution.py:556
  47.9 0.0 all-to-all-done.mine_hbm
  47.9 0.0 copy-start.6
  47.9 0.0 collective-permute-start.6
  47.9 1.1 add_add_fusion.1
  49.1 1.3 %collective-permute-start.5 = (bf16[4,224,128]{2,1,0:T(8,128)(2,1)S(1)}, bf16[4,224,128]{2,1,0:T(8,128)(2,1)S(1)}, u32[]{:S(2)}, u32[]{:S(2)}) collective-permute-start(bf16[4,224,128]{2,1,0:T(8,128)(2,1)S(1)} %add_add_fusion.1), channel_id=1, source_target_pairs={{0,6},{1,7},{8,14},{9,15},{18,16},{19,17},{26,24},{27,25},{36,34},... | collective-permute-start | bytes 688136 | tf_op jit(solution)/shard_map/ppermute | solution.py:568
  50.4 1.3 %collective-permute-start.4 = (bf16[4,224,128]{2,1,0:T(8,128)(2,1)S(1)}, bf16[4,224,128]{2,1,0:T(8,128)(2,1)S(1)}, u32[]{:S(2)}, u32[]{:S(2)}) collective-permute-start(bf16[4,224,128]{2,1,0:T(8,128)(2,1)S(1)} %add_add_fusion.1), channel_id=1, source_target_pairs={{0,4},{1,5},{8,12},{9,13},{18,22},{19,23},{26,30},{27,31},{36,32},... | collective-permute-start | bytes 688136 | tf_op jit(solution)/shard_map/ppermute | solution.py:568
  51.7 1.5 %collective-permute-start.3 = (bf16[4,224,128]{2,1,0:T(8,128)(2,1)S(1)}, bf16[4,224,128]{2,1,0:T(8,128)(2,1)S(1)}, u32[]{:S(2)}, u32[]{:S(2)}) collective-permute-start(bf16[4,224,128]{2,1,0:T(8,128)(2,1)S(1)} %add_add_fusion.1), channel_id=1, source_target_pairs={{0,2},{1,3},{8,10},{9,11},{18,20},{19,21},{26,28},{27,29},{36,38},... | collective-permute-start | bytes 688136 | tf_op jit(solution)/shard_map/ppermute | solution.py:568
  53.2 0.0 copy-done.9
  53.2 0.7 fusion.1.tokens_ref
  53.9 5.6 %pair.3 = bf16[16,256,128]{2,1,0:T(8,128)(2,1)} custom-call(s32[5]{0:T(128)} %stack.27.place, bf16[256,128,128]{2,1,0:T(8,128)(2,1)} %pair_ref.3, bf16[128,512]{1,0:T(8,128)(2,1)} %up_ref.3, bf16[256,128]{1,0:T(8,128)(2,1)} %down_ref.3, bf16[20,128]{1,0:T(8,128)(2,1)} %bitcast.15, ...), custom_call_target="tpu_custom_call", output_to_operand_aliasing={{}: (6, {})} | custom-call | flops 2048000000 | bytes 1228800 | tf_op jit(solution)/shard_map/pair/pallas_call | solution.py:164
  59.5 0.0 copy-done.6
  59.5 0.0 collective-permute-done.6.theirs_hbm
  59.5 0.0 copy-start.10
  59.5 0.0 collective-permute-done.5
  59.5 0.0 collective-permute-done.4
  59.5 2.0 %collective-permute-done.3 = bf16[4,224,128]{2,1,0:T(8,128)(2,1)S(1)} collective-permute-done((bf16[4,224,128]{2,1,0:T(8,128)(2,1)S(1)}, bf16[4,224,128]{2,1,0:T(8,128)(2,1)S(1)}, u32[]{:S(2)}, u32[]{:S(2)}) %collective-permute-start.3) | collective-permute-done | bytes 229408 | tf_op jit(solution)/shard_map/ppermute | solution.py:568
  61.6 0.0 copy-start.7
  61.6 0.9 collective-permute-start.7
  62.5 4.5 %all-to-all-start.1 = ((bf16[16,256,128]{2,1,0:T(8,128)(2,1)}), bf16[16,256,128]{2,1,0:T(8,128)(2,1)S(1)}, u32[]{:S(2)}, u32[]{:S(2)}) async-start(bf16[16,256,128]{2,1,0:T(8,128)(2,1)} %pair.3), calls=%async_computation.1 | async-start | bytes 2097152 | tf_op jit(solution)/shard_map/all_to_all | solution.py:586
  67.0 0.0 collective-permute-done.7.other_ref
  67.0 0.0 copy-start.11
  67.0 0.0 copy-done.10
  67.1 0.0 copy-done.7
  67.1 0.7 copy-done.11
  67.7 12.6 %atoms.1 = (bf16[2048,128]{1,0:T(8,128)(2,1)}, bf16[256,768]{1,0:T(8,128)(2,1)}, f32[256,256]{1,0:T(8,128)}, bf16[8,96,256]{2,1,0:T(8,128)(2,1)}) custom-call(s32[5]{0:T(128)} %stack.27.place, s32[17,128]{1,0:T(8,128)} %fusion.1.tokens_ref, f32[1,128]{1,0:T(1,128)} %bitcast.18, bf16[128,512]{1,0:T(8,128)(2,1)} %proj_ref.1, bf16[128,128]{1,0:T(8,128)(2,1)} %exit_ref.2, ...), custom_call_target="tpu_custom_call" | custom-call | flops 10000000000 | bytes 16777216 | tf_op jit(solution)/shard_map/atoms/pallas_call | solution.py:363
  80.3 0.0 copy-start
  80.3 0.0 copy-start.1
  80.3 0.0 copy-start.2
  80.4 0.0 copy-start.3
  80.4 0.0 copy-start.4
  80.4 3.9 %all-to-all-done.1.bias_hbm = bf16[16,256,128]{2,1,0:T(8,128)(2,1)S(1)} async-done(((bf16[16,256,128]{2,1,0:T(8,128)(2,1)}), bf16[16,256,128]{2,1,0:T(8,128)(2,1)S(1)}, u32[]{:S(2)}, u32[]{:S(2)}) %all-to-all-start.1) | async-done | bytes 1048608 | tf_op jit(solution)/shard_map/all_to_all | solution.py:586
  84.2 0.0 copy-start.5
  84.2 13.2 %all_to_all.20.kv_hbm = bf16[8,96,256]{2,1,0:T(8,128)(2,1)} all-to-all(bf16[8,96,256]{2,1,0:T(8,128)(2,1)} %get-tuple-element.46), channel_id=1, replica_groups=mesh['row'=8,'col'=16] {'row'}, dimensions={0} | all-to-all | bytes 786432 | tf_op jit(solution)/shard_map/all_to_all | solution.py:606
  97.5 0.0 copy-done.5
  97.5 4.7 %tokens.1 = bf16[16,48,256]{2,1,0:T(8,128)(2,1)} custom-call(s32[5]{0:T(128)} %stack.27.place, f32[16]{0:T(128)} %strength.1, s32[1,2048]{1,0:T(1,128)} %bitcast.16, f32[256,256]{1,0:T(8,128)} %get-tuple-element.43.state_hbm, bf16[8,96,256]{2,1,0:T(8,128)(2,1)} %all_to_all.20.kv_hbm, bf16[16,256,128]{2,1,0:T(8,128)(2,1)} %copy-done.5), custom_call_target="tpu_custom_call" | custom-call | flops 1000000000 | bytes 4194304 | tf_op jit(solution)/shard_map/tokens/pallas_call | solution.py:442
  102.2 6.1 %all-to-all-start.3 = ((bf16[16,48,256]{2,1,0:T(8,128)(2,1)}), bf16[16,48,256]{2,1,0:T(8,128)(2,1)S(1)}, u32[]{:S(2)}, u32[]{:S(2)}) async-start(bf16[16,48,256]{2,1,0:T(8,128)(2,1)} %tokens.1), calls=%async_computation.3 | async-start | bytes 786432 | tf_op jit(solution)/shard_map/all_to_all | solution.py:608
  108.4 0.1 subtract_bitcast_fusion.tokens_ref
  108.4 9.8 %all-to-all-done.3 = bf16[16,48,256]{2,1,0:T(8,128)(2,1)S(1)} async-done(((bf16[16,48,256]{2,1,0:T(8,128)(2,1)}), bf16[16,48,256]{2,1,0:T(8,128)(2,1)S(1)}, u32[]{:S(2)}, u32[]{:S(2)}) %all-to-all-start.3) | async-done | bytes 393248 | tf_op jit(solution)/shard_map/all_to_all | solution.py:608
  118.3 0.0 copy-done
  118.3 0.0 copy-done.1
  118.3 0.0 copy-done.2
  118.3 0.0 copy-done.3
  118.3 0.0 copy-done.4
  118.3 2.0 %updates.1 = (bf16[256,768]{1,0:T(8,128)(2,1)}, bf16[128,128]{1,0:T(8,128)(2,1)}) custom-call(s32[5]{0:T(128)S(1)} %copy-done.4, s32[1,128]{1,0:T(1,128)S(1)} %subtract_bitcast_fusion.tokens_ref, bf16[768,256]{1,0:T(8,128)(2,1)S(1)} %bitcast.13, bf16[768,768]{1,0:T(8,128)(2,1)S(1)} %copy-done, bf16[256,768]{1,0:T(8,128)(2,1)S(1)} %copy-done.2, ...), custom_call_target="tpu_custom_call" | custom-call | tf_op jit(solution)/shard_map/updates/pallas_call | solution.py:477
  (2 shorter events, 0.1 us)
Async XLA Ops:
  1.4 23.6 %collective-permute-start = (bf16[64,128]{1,0:T(8,128)(2,1)S(1)}, bf16[64,128]{1,0:T(8,128)(2,1)S(1)}, u32[]{:S(2)}, u32[]{:S(2)}) collective-permute-start(bf16[64,128]{1,0:T(8,128)(2,1)S(1)} %slice_select_fusion), channel_id=1, source_target_pairs={{15,18},{31,36},{47,54},{63,72},{79,90},{95,108},{111,126},{16,1},... | collective-permute-start | bytes 49160 | tf_op jit(solution)/shard_map/ppermute | solution.py:521
  3.3 21.6 %copy-start.8 = (bf16[128,128]{1,0:T(8,128)(2,1)S(1)}, bf16[128,128]{1,0:T(8,128)(2,1)}, u32[]{:S(2)}) copy-start(bf16[128,128]{1,0:T(8,128)(2,1)} %param.20) | copy-start | bytes 98308
  3.3 49.9 %copy-start.9 = (s32[16384]{0:T(1024)S(1)}, s32[16384]{0:T(1024)}, u32[]{:S(2)}) copy-start(s32[16384]{0:T(1024)} %param.21) | copy-start | bytes 196612
  25.8 22.2 %all-to-all-start = ((bf16[8,192,128]{2,1,0:T(8,128)(2,1)}), bf16[8,192,128]{2,1,0:T(8,128)(2,1)S(1)}, u32[]{:S(2)}, u32[]{:S(2)}) async-start(bf16[8,192,128]{2,1,0:T(8,128)(2,1)} %broadcast_in_dim.21), calls=%async_computation | async-start | bytes 786432 | tf_op jit(solution)/shard_map/all_to_all | solution.py:562
  36.4 6.2 %collective-permute-start.2 = (bf16[4,224,128]{2,1,0:T(8,128)(2,1)}, bf16[4,224,128]{2,1,0:T(8,128)(2,1)S(1)}, u32[]{:S(2)}, u32[]{:S(2)}) collective-permute-start(bf16[4,224,128]{2,1,0:T(8,128)(2,1)} %get-tuple-element.28), channel_id=1, source_target_pairs={{17,26},{35,44},{53,62},{71,64},{89,82},{107,100},{125,118},{2,9},... | collective-permute-start | bytes 688136 | tf_op jit(solution)/shard_map/ppermute | solution.py:557
  37.1 10.9 %collective-permute-start.1 = (bf16[4,224,128]{2,1,0:T(8,128)(2,1)}, bf16[4,224,128]{2,1,0:T(8,128)(2,1)S(1)}, u32[]{:S(2)}, u32[]{:S(2)}) collective-permute-start(bf16[4,224,128]{2,1,0:T(8,128)(2,1)} %get-tuple-element.28), channel_id=1, source_target_pairs={{0,8},{1,9},{18,26},{19,27},{36,44},{37,45},{54,62},{55,63},{72,64... | collective-permute-start | bytes 688136 | tf_op jit(solution)/shard_map/ppermute | solution.py:556
  47.9 11.5 %copy-start.6 = (bf16[8,192,128]{2,1,0:T(8,128)(2,1)}, bf16[8,192,128]{2,1,0:T(8,128)(2,1)S(1)}, u32[]{:S(2)}) copy-start(bf16[8,192,128]{2,1,0:T(8,128)(2,1)S(1)} %all-to-all-done.mine_hbm) | copy-start | bytes 1179652
  47.9 11.5 %collective-permute-start.6 = (bf16[8,192,128]{2,1,0:T(8,128)(2,1)S(1)}, bf16[8,192,128]{2,1,0:T(8,128)(2,1)S(1)}, u32[]{:S(2)}, u32[]{:S(2)}) collective-permute-start(bf16[8,192,128]{2,1,0:T(8,128)(2,1)S(1)} %all-to-all-done.mine_hbm), channel_id=1, source_target_pairs={{0,1},{1,0},{2,3},{3,2},{4,5},{5,4},{6,7},{7,6},{8,9},{9,8},{10,11... | collective-permute-start | bytes 1179656 | tf_op jit(solution)/shard_map/ppermute | solution.py:583
  49.1 10.4 %collective-permute-start.5 = (bf16[4,224,128]{2,1,0:T(8,128)(2,1)S(1)}, bf16[4,224,128]{2,1,0:T(8,128)(2,1)S(1)}, u32[]{:S(2)}, u32[]{:S(2)}) collective-permute-start(bf16[4,224,128]{2,1,0:T(8,128)(2,1)S(1)} %add_add_fusion.1), channel_id=1, source_target_pairs={{0,6},{1,7},{8,14},{9,15},{18,16},{19,17},{26,24},{27,25},{36,34},... | collective-permute-start | bytes 688136 | tf_op jit(solution)/shard_map/ppermute | solution.py:568
  50.4 9.1 %collective-permute-start.4 = (bf16[4,224,128]{2,1,0:T(8,128)(2,1)S(1)}, bf16[4,224,128]{2,1,0:T(8,128)(2,1)S(1)}, u32[]{:S(2)}, u32[]{:S(2)}) collective-permute-start(bf16[4,224,128]{2,1,0:T(8,128)(2,1)S(1)} %add_add_fusion.1), channel_id=1, source_target_pairs={{0,4},{1,5},{8,12},{9,13},{18,22},{19,23},{26,30},{27,31},{36,32},... | collective-permute-start | bytes 688136 | tf_op jit(solution)/shard_map/ppermute | solution.py:568
  51.7 9.8 %collective-permute-start.3 = (bf16[4,224,128]{2,1,0:T(8,128)(2,1)S(1)}, bf16[4,224,128]{2,1,0:T(8,128)(2,1)S(1)}, u32[]{:S(2)}, u32[]{:S(2)}) collective-permute-start(bf16[4,224,128]{2,1,0:T(8,128)(2,1)S(1)} %add_add_fusion.1), channel_id=1, source_target_pairs={{0,2},{1,3},{8,10},{9,11},{18,20},{19,21},{26,28},{27,29},{36,38},... | collective-permute-start | bytes 688136 | tf_op jit(solution)/shard_map/ppermute | solution.py:568
  59.5 7.6 %copy-start.10 = (bf16[8,192,128]{2,1,0:T(8,128)(2,1)}, bf16[8,192,128]{2,1,0:T(8,128)(2,1)S(1)}, u32[]{:S(2)}) copy-start(bf16[8,192,128]{2,1,0:T(8,128)(2,1)S(1)} %collective-permute-done.6.theirs_hbm) | copy-start | bytes 1179652
  61.6 5.5 %copy-start.7 = (bf16[4,224,128]{2,1,0:T(8,128)(2,1)}, bf16[4,224,128]{2,1,0:T(8,128)(2,1)S(1)}, u32[]{:S(2)}) copy-start(bf16[4,224,128]{2,1,0:T(8,128)(2,1)S(1)} %add_add_fusion.half_ref) | copy-start | bytes 688132
  61.6 5.4 %collective-permute-start.7 = (bf16[4,224,128]{2,1,0:T(8,128)(2,1)S(1)}, bf16[4,224,128]{2,1,0:T(8,128)(2,1)S(1)}, u32[]{:S(2)}, u32[]{:S(2)}) collective-permute-start(bf16[4,224,128]{2,1,0:T(8,128)(2,1)S(1)} %add_add_fusion.half_ref), channel_id=1, source_target_pairs={{0,1},{1,0},{2,3},{3,2},{4,5},{5,4},{6,7},{7,6},{8,9},{9,8},{10,11... | collective-permute-start | bytes 688136 | tf_op jit(solution)/shard_map/ppermute | solution.py:589
  62.5 21.7 %all-to-all-start.1 = ((bf16[16,256,128]{2,1,0:T(8,128)(2,1)}), bf16[16,256,128]{2,1,0:T(8,128)(2,1)S(1)}, u32[]{:S(2)}, u32[]{:S(2)}) async-start(bf16[16,256,128]{2,1,0:T(8,128)(2,1)} %pair.3), calls=%async_computation.1 | async-start | bytes 2097152 | tf_op jit(solution)/shard_map/all_to_all | solution.py:586
  67.0 0.7 copy-start.11
  80.3 37.9 %copy-start = (bf16[768,768]{1,0:T(8,128)(2,1)S(1)}, bf16[768,768]{1,0:T(8,128)(2,1)}, u32[]{:S(2)}) copy-start(bf16[768,768]{1,0:T(8,128)(2,1)} %exit_ref.3) | copy-start | bytes 3538948
  80.3 37.9 %copy-start.1 = (bf16[2048,128]{1,0:T(8,128)(2,1)S(1)}, bf16[2048,128]{1,0:T(8,128)(2,1)}, u32[]{:S(2)}) copy-start(bf16[2048,128]{1,0:T(8,128)(2,1)} %get-tuple-element.49.mid_ref) | copy-start | bytes 1572868
  80.3 37.9 %copy-start.2 = (bf16[256,768]{1,0:T(8,128)(2,1)S(1)}, bf16[256,768]{1,0:T(8,128)(2,1)}, u32[]{:S(2)}) copy-start(bf16[256,768]{1,0:T(8,128)(2,1)} %get-tuple-element.48.tmid_ref) | copy-start | bytes 1179652
  80.4 37.9 %copy-start.3 = (bf16[768,128]{1,0:T(8,128)(2,1)S(1)}, bf16[768,128]{1,0:T(8,128)(2,1)}, u32[]{:S(2)}) copy-start(bf16[768,128]{1,0:T(8,128)(2,1)} %back_ref.1) | copy-start | bytes 589828
  80.4 37.9 %copy-start.4 = (s32[5]{0:T(128)S(1)}, s32[5]{0:T(128)}, u32[]{:S(2)}) copy-start(s32[5]{0:T(128)} %stack.27.place) | copy-start | bytes 64
  84.2 13.2 %copy-start.5 = (bf16[16,256,128]{2,1,0:T(8,128)(2,1)}, bf16[16,256,128]{2,1,0:T(8,128)(2,1)S(1)}, u32[]{:S(2)}) copy-start(bf16[16,256,128]{2,1,0:T(8,128)(2,1)S(1)} %all-to-all-done.1.bias_hbm) | copy-start | bytes 3145732
  102.2 16.0 %all-to-all-start.3 = ((bf16[16,48,256]{2,1,0:T(8,128)(2,1)}), bf16[16,48,256]{2,1,0:T(8,128)(2,1)S(1)}, u32[]{:S(2)}, u32[]{:S(2)}) async-start(bf16[16,48,256]{2,1,0:T(8,128)(2,1)} %tokens.1), calls=%async_computation.3 | async-start | bytes 786432 | tf_op jit(solution)/shard_map/all_to_all | solution.py:608

commit v11 on v9

--- a/solution.py
+++ b/solution.py
@@ -240,7 +240,7 @@
     lane = lax.broadcasted_iota(jnp.int32, (KW, 3 * KW), 1)
     for t in range(total // KW):
         at = slice(t * KW, (t + 1) * KW)
-        tokens = jnp.broadcast_to(tokens_ref[:, at], (KW, KW)).astype(f32).T.astype(jnp.int32)
+        tokens = jnp.broadcast_to(tokens_ref[t : t + 1, :], (KW, KW)).astype(f32).T.astype(jnp.int32)
         tokens = jnp.concatenate([tokens] * 3, axis=1)
         tokens = jnp.where(
             tokens < 0,
@@ -302,11 +302,12 @@
         sums_ref[...] += dot_tn(onehot, pooled)
         return counts + jnp.sum(onehot.astype(f32).T, axis=1, keepdims=True)
 
-    counts = lax.fori_loop(0, atoms // GROUP, group, jnp.zeros((rows, 1), f32))
+    counts = lax.fori_loop(0, atoms // GROUP, group, jnp.zeros((rows, 1), f32), unroll=True)
     token_mid = (single_ref[...].astype(f32) + sums_ref[...] / counts).astype(bf16)
     tmid_ref[...] = token_mid
     stores = fetch((mid_ref, tmid_ref), (mid_hbm, tmid_hbm), out_sems)
-    normed = (scaled(centered(token_mid.astype(f32))) * gain_ref[...]).astype(bf16)
+    gain = jnp.concatenate([gain_ref[k : k + 1, :] for k in range(gain_ref.shape[0])], axis=1)
+    normed = (scaled(centered(token_mid.astype(f32))) * gain).astype(bf16)
 
     copies[-1].wait()
 
@@ -331,7 +332,7 @@
 def atom_attention(
     place, bands, shards, tokens, atom_gain, proj, exit_w, pool, single, gain, tproj, copies
 ):
-    total = tokens.shape[1]
+    total = tokens.size
     atoms = total - 2 * HALO
     rows = single.shape[0]
     operands = (tokens, atom_gain, proj, exit_w, pool, single, gain)
@@ -420,7 +421,7 @@
 
 def token_attention(place, state, kv, bias, chain, strength):
     rows = state.shape[0]
-    out_shape = jax.ShapeDtypeStruct((bias.shape[0], HDT, rows), bf16)
+    out_shape = jax.ShapeDtypeStruct((bias.shape[0] // 2, HDT, rows), bf16)
     return pl.pallas_call(
         tokens_body,
         grid=(1,),
@@ -436,8 +437,25 @@
 
 
 def update_body(
-    place, tokens_ref, gated_ref, exit_ref, tmid_ref, back_ref, mid_ref, tout_ref, aout_ref
+    place,
+    tokens_ref,
+    mine_ref,
+    theirs_ref,
+    exit_ref,
+    tmid_ref,
+    back_ref,
+    mid_ref,
+    tout_ref,
+    aout_ref,
+    gated_ref,
 ):
+    even = lax.rem(place[1], 2) == 0
+    for k in range(mine_ref.shape[0]):
+        mine, theirs = mine_ref[k], theirs_ref[k]
+        first = slice(2 * k * HDT, (2 * k + 1) * HDT)
+        second = slice((2 * k + 1) * HDT, (2 * k + 2) * HDT)
+        gated_ref[first, :] = jnp.where(even, mine, theirs)
+        gated_ref[second, :] = jnp.where(even, theirs, mine)
     col = place[1]
     atoms, rows = aout_ref.shape[0], tmid_ref.shape[0]
     at = pl.multiple_of(col * atoms, atoms)
@@ -459,12 +477,13 @@
     return pl.pallas_call(
         update_body,
         grid=(1,),
-        in_specs=[SMEM] + [VMEM] * 6,
+        in_specs=[SMEM] + [VMEM] * 7,
         out_specs=[full(shape) for shape in out_shape],
         out_shape=out_shape,
+        scratch_shapes=[pltpu.VMEM((CS, rows), bf16)],
         compiler_params=pltpu.CompilerParams(vmem_limit_bytes=16 * 2**20),
         name="updates",
-    )(place, tokens, gated, exit_w, tmid, back, mid)
+    )(place, tokens, *gated, exit_w, tmid, back, mid)
 
 
 def local(
@@ -509,7 +528,7 @@
     ext_tokens = lax.dynamic_slice_in_dim(
         jnp.pad(atom_token, (HALO, HALO)), row * row_atoms, row_atoms + 2 * HALO
     )
-    ext_tokens = (ext_tokens - row * rows)[None, :]
+    ext_tokens = (ext_tokens - row * rows).reshape(-1, KW)
     own_tokens = lax.dynamic_slice_in_dim(
         atom_token, row * row_atoms + col * atom_rows, atom_rows
     )
@@ -578,7 +597,7 @@
         place, pair_tensor, weights, (token_bias,), 2 * PART, rows - 2 * PART, 1, False
     )
     theirs = lax.ppermute(shards, "col", swap)
-    gain = token_gain[None]
+    gain = token_gain.reshape(-1, KW)
     theirs, token_bias = lax.optimization_barrier((theirs, token_bias))
     head_bias = lax.all_to_all(token_bias, "col", 0, 0)
     sent, theirs, gain, ext_tokens = lax.optimization_barrier((sent, theirs, gain, ext_tokens))
@@ -602,7 +621,8 @@
     keyvals, head_bias = lax.optimization_barrier((keyvals, head_bias))
     keyvals = lax.all_to_all(keyvals, "row", 0, 0)
     gated = token_attention(place, state, keyvals, head_bias, chain_index[None], chain_bias)
-    gated = lax.all_to_all(gated, "col", 0, 0).reshape(CS, rows)
+    gated = lax.all_to_all(gated, "col", 0, 0, axis_index_groups=cores)
+    gated = (gated, lax.ppermute(gated, "col", swap))
     return tuple(
         updates(
             place, gated, token_exit, token_mid, token_back, atom_mid, own_tokens, atom_rows

time: 117 us -> 116 us (level)
  blocking collectives: 13.8 us -> 26.2 us
  waiting for transfers between devices: 14.1 us -> 6.56 us
  starting transfers between devices: 34.1 us -> 29.5 us
  local copies, waits for them, and re-layouts: 2.73 us -> 1.55 us
    all_to_all x0 -> x1, blocking collectives: none -> 12.4 us  [local(): gated = lax.all_to_all(gated, 'col', 0, 0, axis_index_groups=cores)]
    all_to_all x1 -> x0, waiting for transfers between devices: 9.82 us -> none  [local(): gated = lax.all_to_all(gated, 'col', 0, 0).reshape(CS, rows)]
    all_to_all x1 -> x0, starting transfers between devices: 7.21 us -> none  [local(): gated = lax.all_to_all(gated, 'col', 0, 0).reshape(CS, rows)]
    ppermute x0 -> x1, starting transfers between devices: none -> 2.62 us  [local(): gated = (gated, lax.ppermute(gated, 'col', swap))]
    broadcast_in_dim x2 -> x0, local copies, waits for them, and re-layouts: 1.2 us -> none  [the longest x1 0.6 us: local(): ext_tokens = (ext_tokens - row * rows)[None, :]]
  transfers between devices with their start and end apart: 11 -> 11, of which waited for: 4 -> 4; matrix products, arithmetic and copies ran while one was open for 2% -> 2% of each run, Pallas kernels for 35% -> 34%
where the time goes in v11:
time: 116 us
  Pallas kernels  46.2 us (40%)
  starting transfers between devices  29.5 us (25%)
  blocking collectives  26.2 us (23%)
  waiting for transfers between devices  6.56 us (6%)
  other arithmetic  4.49 us (4%)
  local copies, waits for them, and re-layouts  1.55 us (1%)
    pallas_call x2, Pallas kernels, pair_rows(): pl.pallas_call(functools.partial(pair_body, bands=bands), grid_spec=pltpu...  27 us
    all_to_all x1, blocking collectives, local(): keyvals = lax.all_to_all(keyvals, 'row', 0, 0)  13.8 us
    pallas_call x1, Pallas kernels, atom_attention(): pl.pallas_call(atoms_body, grid=(1,), in_specs=[SMEM] + [full(array) for...  12.5 us
    all_to_all x1, blocking collectives, local(): gated = lax.all_to_all(gated, 'col', 0, 0, axis_index_groups=cores)  12.4 us
    ppermute x3, starting transfers between devices, local(): lax.ppermute(band, both, [(at(r, k, core), at(r, flat(k, step), core)) fo...  7.19 us
    all_to_all x1, starting transfers between devices, local(): head_bias = lax.all_to_all(token_bias, 'col', 0, 0)  6.38 us
    all_to_all x1, starting transfers between devices, local(): shards = lax.all_to_all(own_atoms, 'col', 0, 0, axis_index_groups=cores)  5.68 us
    ppermute x1, starting transfers between devices, local(): lax.ppermute(band, both, over_y + beside(lambda r: r))  5.64 us
  transfers between devices with their start and end apart: 11, of which 4 were waited for; matrix products, arithmetic and copies ran while one was open for 2% of the time, Pallas kernels for 34%

profile of v11, /device:TPU:1, one launch (start us, length us, event | category | flops | bytes accessed | tf_op | source)
XLA Modules:
  0.0 115.5 jit_solution(15101201413750124044)
XLA Ops:
  0.6 0.7 slice_select_fusion.1
  1.4 1.3 %collective-permute-start = (bf16[64,128]{1,0:T(8,128)(2,1)S(1)}, bf16[64,128]{1,0:T(8,128)(2,1)S(1)}, u32[]{:S(2)}, u32[]{:S(2)}) collective-permute-start(bf16[64,128]{1,0:T(8,128)(2,1)S(1)} %slice_select_fusion.1), channel_id=1, source_target_pairs={{15,18},{31,36},{47,54},{63,72},{79,90},{95,108},{111,126},{16,1},... | collective-permute-start | bytes 49160 | tf_op jit(solution)/shard_map/ppermute | solution.py:522
  2.7 0.7 pad_add_fusion.place
  3.4 0.0 copy-start.8
  3.4 0.0 copy-start.9
  3.4 21.5 %pair.2 = (bf16[16,256,128]{2,1,0:T(8,128)(2,1)}, bf16[4,224,128]{2,1,0:T(8,128)(2,1)}, bf16[4,64,128]{2,1,0:T(8,128)(2,1)}) custom-call(s32[4]{0:T(128)} %pad_add_fusion.place, bf16[256,128,128]{2,1,0:T(8,128)(2,1)} %pair_ref.3, bf16[128,512]{1,0:T(8,128)(2,1)} %up_ref.3, bf16[256,128]{1,0:T(8,128)(2,1)} %down_ref.3, bf16[20,128]{1,0:T(8,128)(2,1)} %bitcast.13, ...), custom_call_target="tpu_custom_call" | custom-call | flops 14336000000 | bytes 8601600 | tf_op jit(solution)/shard_map/pair/pallas_call | solution.py:147
  24.9 0.1 pad.8.clone
  25.0 0.0 collective-permute-done
  25.0 1.1 slice_select_fusion
  26.0 1.1 fusion.1
  27.2 0.7 collective-permute-start.2
  27.9 5.6 %collective-permute-start.1 = (bf16[4,224,128]{2,1,0:T(8,128)(2,1)S(1)}, bf16[4,224,128]{2,1,0:T(8,128)(2,1)S(1)}, u32[]{:S(2)}, u32[]{:S(2)}) collective-permute-start(bf16[4,224,128]{2,1,0:T(8,128)(2,1)S(1)} %fusion.1), channel_id=1, source_target_pairs={{0,8},{1,9},{18,26},{19,27},{36,44},{37,45},{54,62},{55,63},{72,64... | collective-permute-start | bytes 688136 | tf_op jit(solution)/shard_map/ppermute | solution.py:573
  33.5 0.0 copy-done.8
  33.5 0.7 broadcast_in_dim.21
  34.3 5.7 %all-to-all-start = ((bf16[8,128,128]{2,1,0:T(8,128)(2,1)}), bf16[8,128,128]{2,1,0:T(8,128)(2,1)S(1)}, u32[]{:S(2)}, u32[]{:S(2)}) async-start(bf16[8,128,128]{2,1,0:T(8,128)(2,1)} %broadcast_in_dim.21), calls=%async_computation | async-start | bytes 524288 | tf_op jit(solution)/shard_map/all_to_all | solution.py:578
  40.0 0.0 collective-permute-done.2
  40.0 0.0 collective-permute-done.1
  40.0 4.6 %collective-permute-start.5 = (bf16[4,224,128]{2,1,0:T(8,128)(2,1)S(1)}, bf16[4,224,128]{2,1,0:T(8,128)(2,1)S(1)}, u32[]{:S(2)}, u32[]{:S(2)}) collective-permute-start(bf16[4,224,128]{2,1,0:T(8,128)(2,1)S(1)} %add_add_fusion.1), channel_id=1, source_target_pairs={{0,6},{1,7},{8,14},{9,15},{18,16},{19,17},{26,24},{27,25},{36,34},... | collective-permute-start | bytes 688136 | tf_op jit(solution)/shard_map/ppermute | solution.py:584
  44.6 1.3 %collective-permute-start.4 = (bf16[4,224,128]{2,1,0:T(8,128)(2,1)S(1)}, bf16[4,224,128]{2,1,0:T(8,128)(2,1)S(1)}, u32[]{:S(2)}, u32[]{:S(2)}) collective-permute-start(bf16[4,224,128]{2,1,0:T(8,128)(2,1)S(1)} %add_add_fusion.1), channel_id=1, source_target_pairs={{0,4},{1,5},{8,12},{9,13},{18,22},{19,23},{26,30},{27,31},{36,32},... | collective-permute-start | bytes 688136 | tf_op jit(solution)/shard_map/ppermute | solution.py:584
  45.9 1.3 %collective-permute-start.3 = (bf16[4,224,128]{2,1,0:T(8,128)(2,1)S(1)}, bf16[4,224,128]{2,1,0:T(8,128)(2,1)S(1)}, u32[]{:S(2)}, u32[]{:S(2)}) collective-permute-start(bf16[4,224,128]{2,1,0:T(8,128)(2,1)S(1)} %add_add_fusion.1), channel_id=1, source_target_pairs={{0,2},{1,3},{8,10},{9,11},{18,20},{19,21},{26,28},{27,29},{36,38},... | collective-permute-start | bytes 688136 | tf_op jit(solution)/shard_map/ppermute | solution.py:584
  47.2 0.3 all-to-all-done.mine_hbm
  47.6 0.0 copy-start.6
  47.6 0.0 collective-permute-start.6
  47.6 0.0 copy-done.9
  47.6 0.7 fusion.4.tokens_ref
  48.3 5.6 %pair.3 = bf16[16,256,128]{2,1,0:T(8,128)(2,1)} custom-call(s32[4]{0:T(128)} %pad_add_fusion.place, bf16[256,128,128]{2,1,0:T(8,128)(2,1)} %pair_ref.3, bf16[128,512]{1,0:T(8,128)(2,1)} %up_ref.3, bf16[256,128]{1,0:T(8,128)(2,1)} %down_ref.3, bf16[20,128]{1,0:T(8,128)(2,1)} %bitcast.14, ...), custom_call_target="tpu_custom_call", output_to_operand_aliasing={{}: (6, {})} | custom-call | flops 2048000000 | bytes 1228800 | tf_op jit(solution)/shard_map/pair/pallas_call | solution.py:147
  53.8 0.0 copy-done.6
  53.8 0.0 collective-permute-done.6.theirs_hbm
  53.8 0.0 copy-start.10
  53.8 0.0 collective-permute-done.5
  53.9 0.0 collective-permute-done.4
  53.9 1.3 %collective-permute-done.3 = bf16[4,224,128]{2,1,0:T(8,128)(2,1)S(1)} collective-permute-done((bf16[4,224,128]{2,1,0:T(8,128)(2,1)S(1)}, bf16[4,224,128]{2,1,0:T(8,128)(2,1)S(1)}, u32[]{:S(2)}, u32[]{:S(2)}) %collective-permute-start.3) | collective-permute-done | bytes 229408 | tf_op jit(solution)/shard_map/ppermute | solution.py:584
  55.2 0.0 copy-start.7
  55.2 0.1 collective-permute-start.7
  55.3 6.4 %all-to-all-start.1 = ((bf16[16,256,128]{2,1,0:T(8,128)(2,1)}), bf16[16,256,128]{2,1,0:T(8,128)(2,1)S(1)}, u32[]{:S(2)}, u32[]{:S(2)}) async-start(bf16[16,256,128]{2,1,0:T(8,128)(2,1)} %pair.3), calls=%async_computation.1 | async-start | bytes 2097152 | tf_op jit(solution)/shard_map/all_to_all | solution.py:602
  61.7 0.0 collective-permute-done.7.other_ref
  61.7 0.0 copy-start.11
  61.7 0.0 copy-done.10
  61.7 0.0 copy-done.7
  61.7 0.7 copy-done.11
  62.4 12.5 %atoms.1 = (bf16[2048,128]{1,0:T(8,128)(2,1)}, bf16[256,768]{1,0:T(8,128)(2,1)}, f32[256,256]{1,0:T(8,128)}, bf16[8,96,256]{2,1,0:T(8,128)(2,1)}) custom-call(s32[4]{0:T(128)} %pad_add_fusion.place, s32[17,128]{1,0:T(8,128)} %fusion.4.tokens_ref, f32[1,128]{1,0:T(1,128)} %bitcast.17, bf16[128,512]{1,0:T(8,128)(2,1)} %proj_ref.1, bf16[128,128]{1,0:T(8,128)(2,1)} %exit_ref.2, ...), custom_call_target="tpu_custom_call" | custom-call | flops 10000000000 | bytes 16777216 | tf_op jit(solution)/shard_map/atoms/pallas_call | solution.py:346
  74.9 0.0 copy-start
  74.9 0.0 copy-start.1
  74.9 0.0 copy-start.2
  74.9 0.0 copy-start.3
  74.9 0.0 copy-start.4
  74.9 3.9 %all-to-all-done.1.bias_hbm = bf16[16,256,128]{2,1,0:T(8,128)(2,1)S(1)} async-done(((bf16[16,256,128]{2,1,0:T(8,128)(2,1)}), bf16[16,256,128]{2,1,0:T(8,128)(2,1)S(1)}, u32[]{:S(2)}, u32[]{:S(2)}) %all-to-all-start.1) | async-done | bytes 1048608 | tf_op jit(solution)/shard_map/all_to_all | solution.py:602
  78.9 0.0 copy-start.5
  78.9 13.8 %all_to_all.20.kv_hbm = bf16[8,96,256]{2,1,0:T(8,128)(2,1)} all-to-all(bf16[8,96,256]{2,1,0:T(8,128)(2,1)} %get-tuple-element.50), channel_id=1, replica_groups=mesh['row'=8,'col'=16] {'row'}, dimensions={0} | all-to-all | bytes 786432 | tf_op jit(solution)/shard_map/all_to_all | solution.py:622
  92.7 0.0 copy-done.5
  92.7 4.7 %tokens.1 = bf16[8,48,256]{2,1,0:T(8,128)(2,1)} custom-call(s32[4]{0:T(128)} %pad_add_fusion.place, f32[16]{0:T(128)} %strength.1, s32[1,2048]{1,0:T(1,128)} %bitcast.15, f32[256,256]{1,0:T(8,128)} %get-tuple-element.47.state_hbm, bf16[8,96,256]{2,1,0:T(8,128)(2,1)} %all_to_all.20.kv_hbm, bf16[16,256,128]{2,1,0:T(8,128)(2,1)} %copy-done.5), custom_call_target="tpu_custom_call" | custom-call | flops 1000000000 | bytes 4194304 | tf_op jit(solution)/shard_map/tokens/pallas_call | solution.py:425
  97.3 12.4 %all_to_all.21.mine_ref = bf16[8,48,256]{2,1,0:T(8,128)(2,1)S(1)} all-to-all(bf16[8,48,256]{2,1,0:T(8,128)(2,1)} %tokens.1), channel_id=1, replica_groups={{0,2,4,6,8,10,12,14},{1,3,5,7,9,11,13,15},{16,18,20,22,24,26,28,30},{17..., dimensions={0} | all-to-all | bytes 393216 | tf_op jit(solution)/shard_map/all_to_all | solution.py:624
  109.8 2.6 %collective-permute-start.8 = (bf16[8,48,256]{2,1,0:T(8,128)(2,1)S(1)}, bf16[8,48,256]{2,1,0:T(8,128)(2,1)S(1)}, u32[]{:S(2)}, u32[]{:S(2)}) collective-permute-start(bf16[8,48,256]{2,1,0:T(8,128)(2,1)S(1)} %all_to_all.21.mine_ref), channel_id=1, source_target_pairs={{0,1},{1,0},{2,3},{3,2},{4,5},{5,4},{6,7},{7,6},{8,9},{9,8},{10,11... | collective-permute-start | bytes 589832 | tf_op jit(solution)/shard_map/ppermute | solution.py:625
  112.4 0.1 subtract_bitcast_fusion.tokens_ref
  112.4 1.0 collective-permute-done.8.theirs_ref
  113.4 0.0 copy-done
  113.4 0.0 copy-done.1
  113.4 0.0 copy-done.2
  113.4 0.0 copy-done.3
  113.5 0.0 copy-done.4
  113.5 2.0 %updates.1 = (bf16[256,768]{1,0:T(8,128)(2,1)}, bf16[128,128]{1,0:T(8,128)(2,1)}) custom-call(s32[4]{0:T(128)S(1)} %copy-done.4, s32[1,128]{1,0:T(1,128)S(1)} %subtract_bitcast_fusion.tokens_ref, bf16[8,48,256]{2,1,0:T(8,128)(2,1)S(1)} %all_to_all.21.mine_ref, bf16[8,48,256]{2,1,0:T(8,128)(2,1)S(1)} %collective-permute-done.8.theirs_ref, ...), custom_call_target="tpu_custom_call" | custom-call | tf_op jit(solution)/shard_map/updates/pallas_call | solution.py:477
  (7 shorter events, 0.1 us)
Async XLA Ops:
  1.4 23.6 %collective-permute-start = (bf16[64,128]{1,0:T(8,128)(2,1)S(1)}, bf16[64,128]{1,0:T(8,128)(2,1)S(1)}, u32[]{:S(2)}, u32[]{:S(2)}) collective-permute-start(bf16[64,128]{1,0:T(8,128)(2,1)S(1)} %slice_select_fusion.1), channel_id=1, source_target_pairs={{15,18},{31,36},{47,54},{63,72},{79,90},{95,108},{111,126},{16,1},... | collective-permute-start | bytes 49160 | tf_op jit(solution)/shard_map/ppermute | solution.py:522
  3.4 30.2 %copy-start.8 = (bf16[128,128]{1,0:T(8,128)(2,1)S(1)}, bf16[128,128]{1,0:T(8,128)(2,1)}, u32[]{:S(2)}) copy-start(bf16[128,128]{1,0:T(8,128)(2,1)} %param.20) | copy-start | bytes 98308
  3.4 44.2 %copy-start.9 = (s32[16384]{0:T(1024)S(1)}, s32[16384]{0:T(1024)}, u32[]{:S(2)}) copy-start(s32[16384]{0:T(1024)} %param.21) | copy-start | bytes 196612
  27.2 12.8 %collective-permute-start.2 = (bf16[4,224,128]{2,1,0:T(8,128)(2,1)S(1)}, bf16[4,224,128]{2,1,0:T(8,128)(2,1)S(1)}, u32[]{:S(2)}, u32[]{:S(2)}) collective-permute-start(bf16[4,224,128]{2,1,0:T(8,128)(2,1)S(1)} %fusion.1), channel_id=1, source_target_pairs={{17,26},{35,44},{53,62},{71,64},{89,82},{107,100},{125,118},{2,9},... | collective-permute-start | bytes 688136 | tf_op jit(solution)/shard_map/ppermute | solution.py:574
  27.9 12.1 %collective-permute-start.1 = (bf16[4,224,128]{2,1,0:T(8,128)(2,1)S(1)}, bf16[4,224,128]{2,1,0:T(8,128)(2,1)S(1)}, u32[]{:S(2)}, u32[]{:S(2)}) collective-permute-start(bf16[4,224,128]{2,1,0:T(8,128)(2,1)S(1)} %fusion.1), channel_id=1, source_target_pairs={{0,8},{1,9},{18,26},{19,27},{36,44},{37,45},{54,62},{55,63},{72,64... | collective-permute-start | bytes 688136 | tf_op jit(solution)/shard_map/ppermute | solution.py:573
  34.3 13.3 %all-to-all-start = ((bf16[8,128,128]{2,1,0:T(8,128)(2,1)}), bf16[8,128,128]{2,1,0:T(8,128)(2,1)S(1)}, u32[]{:S(2)}, u32[]{:S(2)}) async-start(bf16[8,128,128]{2,1,0:T(8,128)(2,1)} %broadcast_in_dim.21), calls=%async_computation | async-start | bytes 524288 | tf_op jit(solution)/shard_map/all_to_all | solution.py:578
  40.0 13.8 %collective-permute-start.5 = (bf16[4,224,128]{2,1,0:T(8,128)(2,1)S(1)}, bf16[4,224,128]{2,1,0:T(8,128)(2,1)S(1)}, u32[]{:S(2)}, u32[]{:S(2)}) collective-permute-start(bf16[4,224,128]{2,1,0:T(8,128)(2,1)S(1)} %add_add_fusion.1), channel_id=1, source_target_pairs={{0,6},{1,7},{8,14},{9,15},{18,16},{19,17},{26,24},{27,25},{36,34},... | collective-permute-start | bytes 688136 | tf_op jit(solution)/shard_map/ppermute | solution.py:584
  44.6 9.3 %collective-permute-start.4 = (bf16[4,224,128]{2,1,0:T(8,128)(2,1)S(1)}, bf16[4,224,128]{2,1,0:T(8,128)(2,1)S(1)}, u32[]{:S(2)}, u32[]{:S(2)}) collective-permute-start(bf16[4,224,128]{2,1,0:T(8,128)(2,1)S(1)} %add_add_fusion.1), channel_id=1, source_target_pairs={{0,4},{1,5},{8,12},{9,13},{18,22},{19,23},{26,30},{27,31},{36,32},... | collective-permute-start | bytes 688136 | tf_op jit(solution)/shard_map/ppermute | solution.py:584
  45.9 9.2 %collective-permute-start.3 = (bf16[4,224,128]{2,1,0:T(8,128)(2,1)S(1)}, bf16[4,224,128]{2,1,0:T(8,128)(2,1)S(1)}, u32[]{:S(2)}, u32[]{:S(2)}) collective-permute-start(bf16[4,224,128]{2,1,0:T(8,128)(2,1)S(1)} %add_add_fusion.1), channel_id=1, source_target_pairs={{0,2},{1,3},{8,10},{9,11},{18,20},{19,21},{26,28},{27,29},{36,38},... | collective-permute-start | bytes 688136 | tf_op jit(solution)/shard_map/ppermute | solution.py:584
  47.6 6.3 %copy-start.6 = (bf16[8,128,128]{2,1,0:T(8,128)(2,1)}, bf16[8,128,128]{2,1,0:T(8,128)(2,1)S(1)}, u32[]{:S(2)}) copy-start(bf16[8,128,128]{2,1,0:T(8,128)(2,1)S(1)} %all-to-all-done.mine_hbm) | copy-start | bytes 786436
  47.6 6.3 %collective-permute-start.6 = (bf16[8,128,128]{2,1,0:T(8,128)(2,1)S(1)}, bf16[8,128,128]{2,1,0:T(8,128)(2,1)S(1)}, u32[]{:S(2)}, u32[]{:S(2)}) collective-permute-start(bf16[8,128,128]{2,1,0:T(8,128)(2,1)S(1)} %all-to-all-done.mine_hbm), channel_id=1, source_target_pairs={{0,1},{1,0},{2,3},{3,2},{4,5},{5,4},{6,7},{7,6},{8,9},{9,8},{10,11... | collective-permute-start | bytes 786440 | tf_op jit(solution)/shard_map/ppermute | solution.py:599
  53.8 7.8 %copy-start.10 = (bf16[8,128,128]{2,1,0:T(8,128)(2,1)}, bf16[8,128,128]{2,1,0:T(8,128)(2,1)S(1)}, u32[]{:S(2)}) copy-start(bf16[8,128,128]{2,1,0:T(8,128)(2,1)S(1)} %collective-permute-done.6.theirs_hbm) | copy-start | bytes 786436
  55.2 6.5 %copy-start.7 = (bf16[4,224,128]{2,1,0:T(8,128)(2,1)}, bf16[4,224,128]{2,1,0:T(8,128)(2,1)S(1)}, u32[]{:S(2)}) copy-start(bf16[4,224,128]{2,1,0:T(8,128)(2,1)S(1)} %add_add_fusion.half_ref) | copy-start | bytes 688132
  55.2 6.5 %collective-permute-start.7 = (bf16[4,224,128]{2,1,0:T(8,128)(2,1)S(1)}, bf16[4,224,128]{2,1,0:T(8,128)(2,1)S(1)}, u32[]{:S(2)}, u32[]{:S(2)}) collective-permute-start(bf16[4,224,128]{2,1,0:T(8,128)(2,1)S(1)} %add_add_fusion.half_ref), channel_id=1, source_target_pairs={{0,1},{1,0},{2,3},{3,2},{4,5},{5,4},{6,7},{7,6},{8,9},{9,8},{10,11... | collective-permute-start | bytes 688136 | tf_op jit(solution)/shard_map/ppermute | solution.py:605
  55.3 23.6 %all-to-all-start.1 = ((bf16[16,256,128]{2,1,0:T(8,128)(2,1)}), bf16[16,256,128]{2,1,0:T(8,128)(2,1)S(1)}, u32[]{:S(2)}, u32[]{:S(2)}) async-start(bf16[16,256,128]{2,1,0:T(8,128)(2,1)} %pair.3), calls=%async_computation.1 | async-start | bytes 2097152 | tf_op jit(solution)/shard_map/all_to_all | solution.py:602
  61.7 0.7 copy-start.11
  74.9 38.6 %copy-start = (bf16[768,768]{1,0:T(8,128)(2,1)S(1)}, bf16[768,768]{1,0:T(8,128)(2,1)}, u32[]{:S(2)}) copy-start(bf16[768,768]{1,0:T(8,128)(2,1)} %exit_ref.3) | copy-start | bytes 3538948
  74.9 38.5 %copy-start.1 = (bf16[2048,128]{1,0:T(8,128)(2,1)S(1)}, bf16[2048,128]{1,0:T(8,128)(2,1)}, u32[]{:S(2)}) copy-start(bf16[2048,128]{1,0:T(8,128)(2,1)} %get-tuple-element.53.mid_ref) | copy-start | bytes 1572868
  74.9 38.5 %copy-start.2 = (bf16[256,768]{1,0:T(8,128)(2,1)S(1)}, bf16[256,768]{1,0:T(8,128)(2,1)}, u32[]{:S(2)}) copy-start(bf16[256,768]{1,0:T(8,128)(2,1)} %get-tuple-element.52.tmid_ref) | copy-start | bytes 1179652
  74.9 38.5 %copy-start.3 = (bf16[768,128]{1,0:T(8,128)(2,1)S(1)}, bf16[768,128]{1,0:T(8,128)(2,1)}, u32[]{:S(2)}) copy-start(bf16[768,128]{1,0:T(8,128)(2,1)} %back_ref.1) | copy-start | bytes 589828
  74.9 38.5 %copy-start.4 = (s32[4]{0:T(128)S(1)}, s32[4]{0:T(128)}, u32[]{:S(2)}) copy-start(s32[4]{0:T(128)} %pad_add_fusion.place) | copy-start | bytes 52
  78.9 13.8 %copy-start.5 = (bf16[16,256,128]{2,1,0:T(8,128)(2,1)}, bf16[16,256,128]{2,1,0:T(8,128)(2,1)S(1)}, u32[]{:S(2)}) copy-start(bf16[16,256,128]{2,1,0:T(8,128)(2,1)S(1)} %all-to-all-done.1.bias_hbm) | copy-start | bytes 3145732
  109.8 3.7 %collective-permute-start.8 = (bf16[8,48,256]{2,1,0:T(8,128)(2,1)S(1)}, bf16[8,48,256]{2,1,0:T(8,128)(2,1)S(1)}, u32[]{:S(2)}, u32[]{:S(2)}) collective-permute-start(bf16[8,48,256]{2,1,0:T(8,128)(2,1)S(1)} %all_to_all.21.mine_ref), channel_id=1, source_target_pairs={{0,1},{1,0},{2,3},{3,2},{4,5},{5,4},{6,7},{7,6},{8,9},{9,8},{10,11... | collective-permute-start | bytes 589832 | tf_op jit(solution)/shard_map/ppermute | solution.py:625

commit v12 on v11

--- a/solution.py
+++ b/solution.py
@@ -364,7 +364,7 @@
         + held(fetched)
         + [pltpu.VMEM(a.shape, a.dtype) for a in out_shape[:3]]
         + [pltpu.VMEM((2 * HDT, rows), bf16), pltpu.SemaphoreType.DMA((3 + copies,))],
-        compiler_params=pltpu.CompilerParams(vmem_limit_bytes=GRANT),
+        compiler_params=pltpu.CompilerParams(vmem_limit_bytes=52 * 2**20),
         cost_estimate=pl.CostEstimate(
             flops=10**10, bytes_accessed=2**24, transcendentals=2**22
         ),

time: 116 us -> 116 us (level)
  waiting for transfers between devices: 6.56 us -> 8.05 us
  transfers between devices with their start and end apart: 11 -> 11, of which waited for: 4 -> 4; matrix products, arithmetic and copies ran while one was open for 2% -> 1% of each run, Pallas kernels for 34% -> 33%
where the time goes in v12:
time: 116 us; the launch traced here: 115 us
  Pallas kernels  45.3 us (39%)
  starting transfers between devices  29.5 us (25%)
  blocking collectives  26.2 us (23%)
  waiting for transfers between devices  8.05 us (7%)
  other arithmetic  3.89 us (3%)
  local copies, waits for them, and re-layouts  1.59 us (1%)
    pallas_call x2, Pallas kernels, pair_rows(): pl.pallas_call(functools.partial(pair_body, bands=bands), grid_spec=pltpu...  27.1 us
    all_to_all x1, blocking collectives, local(): keyvals = lax.all_to_all(keyvals, 'row', 0, 0)  13.8 us
    all_to_all x1, blocking collectives, local(): gated = lax.all_to_all(gated, 'col', 0, 0, axis_index_groups=cores)  12.4 us
    pallas_call x1, Pallas kernels, atom_attention(): pl.pallas_call(atoms_body, grid=(1,), in_specs=[SMEM] + [full(array) for...  11.5 us
    ppermute x3, starting transfers between devices, local(): lax.ppermute(band, both, [(at(r, k, core), at(r, flat(k, step), core)) fo...  7.19 us
    all_to_all x1, starting transfers between devices, local(): head_bias = lax.all_to_all(token_bias, 'col', 0, 0)  6.38 us
    all_to_all x1, starting transfers between devices, local(): shards = lax.all_to_all(own_atoms, 'col', 0, 0, axis_index_groups=cores)  5.68 us
    ppermute x1, starting transfers between devices, local(): lax.ppermute(band, both, over_y + beside(lambda r: r))  5.64 us
  transfers between devices with their start and end apart: 11, of which 4 were waited for; matrix products, arithmetic and copies ran while one was open for 1% of the time, Pallas kernels for 33%

profile of v12, /device:TPU:1, one launch (start us, length us, event | category | flops | bytes accessed | tf_op | source)
XLA Modules:
  0.0 115.4 jit_solution(13257250655246035283)
XLA Ops:
  0.6 0.7 slice_select_fusion.1
  1.4 1.3 %collective-permute-start = (bf16[64,128]{1,0:T(8,128)(2,1)S(1)}, bf16[64,128]{1,0:T(8,128)(2,1)S(1)}, u32[]{:S(2)}, u32[]{:S(2)}) collective-permute-start(bf16[64,128]{1,0:T(8,128)(2,1)S(1)} %slice_select_fusion.1), channel_id=1, source_target_pairs={{15,18},{31,36},{47,54},{63,72},{79,90},{95,108},{111,126},{16,1},... | collective-permute-start | bytes 49160 | tf_op jit(solution)/shard_map/ppermute | solution.py:522
  2.7 0.7 pad_add_fusion.place
  3.4 0.0 copy-start.12
  3.4 0.0 copy-start.13
  3.4 21.5 %pair.2 = (bf16[16,256,128]{2,1,0:T(8,128)(2,1)}, bf16[4,224,128]{2,1,0:T(8,128)(2,1)}, bf16[4,64,128]{2,1,0:T(8,128)(2,1)}) custom-call(s32[4]{0:T(128)} %pad_add_fusion.place, bf16[256,128,128]{2,1,0:T(8,128)(2,1)} %pair_ref.3, bf16[128,512]{1,0:T(8,128)(2,1)} %up_ref.3, bf16[256,128]{1,0:T(8,128)(2,1)} %down_ref.3, bf16[20,128]{1,0:T(8,128)(2,1)} %bitcast.15, ...), custom_call_target="tpu_custom_call" | custom-call | flops 14336000000 | bytes 8601600 | tf_op jit(solution)/shard_map/pair/pallas_call | solution.py:147
  24.9 0.1 pad.8.clone
  25.0 0.0 collective-permute-done
  25.0 1.1 slice_select_fusion
  26.0 1.1 fusion.1
  27.2 0.7 collective-permute-start.2
  27.9 5.6 %collective-permute-start.1 = (bf16[4,224,128]{2,1,0:T(8,128)(2,1)S(1)}, bf16[4,224,128]{2,1,0:T(8,128)(2,1)S(1)}, u32[]{:S(2)}, u32[]{:S(2)}) collective-permute-start(bf16[4,224,128]{2,1,0:T(8,128)(2,1)S(1)} %fusion.1), channel_id=1, source_target_pairs={{0,8},{1,9},{18,26},{19,27},{36,44},{37,45},{54,62},{55,63},{72,64... | collective-permute-start | bytes 688136 | tf_op jit(solution)/shard_map/ppermute | solution.py:573
  33.5 0.0 copy-done.12
  33.5 0.7 broadcast_in_dim.21
  34.3 5.7 %all-to-all-start = ((bf16[8,128,128]{2,1,0:T(8,128)(2,1)}), bf16[8,128,128]{2,1,0:T(8,128)(2,1)S(1)}, u32[]{:S(2)}, u32[]{:S(2)}) async-start(bf16[8,128,128]{2,1,0:T(8,128)(2,1)} %broadcast_in_dim.21), calls=%async_computation | async-start | bytes 524288 | tf_op jit(solution)/shard_map/all_to_all | solution.py:578
  39.9 0.0 collective-permute-done.2
  40.0 0.0 collective-permute-done.1
  40.0 4.6 %collective-permute-start.5 = (bf16[4,224,128]{2,1,0:T(8,128)(2,1)S(1)}, bf16[4,224,128]{2,1,0:T(8,128)(2,1)S(1)}, u32[]{:S(2)}, u32[]{:S(2)}) collective-permute-start(bf16[4,224,128]{2,1,0:T(8,128)(2,1)S(1)} %add_add_fusion.1), channel_id=1, source_target_pairs={{0,6},{1,7},{8,14},{9,15},{18,16},{19,17},{26,24},{27,25},{36,34},... | collective-permute-start | bytes 688136 | tf_op jit(solution)/shard_map/ppermute | solution.py:584
  44.6 1.3 %collective-permute-start.4 = (bf16[4,224,128]{2,1,0:T(8,128)(2,1)S(1)}, bf16[4,224,128]{2,1,0:T(8,128)(2,1)S(1)}, u32[]{:S(2)}, u32[]{:S(2)}) collective-permute-start(bf16[4,224,128]{2,1,0:T(8,128)(2,1)S(1)} %add_add_fusion.1), channel_id=1, source_target_pairs={{0,4},{1,5},{8,12},{9,13},{18,22},{19,23},{26,30},{27,31},{36,32},... | collective-permute-start | bytes 688136 | tf_op jit(solution)/shard_map/ppermute | solution.py:584
  45.9 1.3 %collective-permute-start.3 = (bf16[4,224,128]{2,1,0:T(8,128)(2,1)S(1)}, bf16[4,224,128]{2,1,0:T(8,128)(2,1)S(1)}, u32[]{:S(2)}, u32[]{:S(2)}) collective-permute-start(bf16[4,224,128]{2,1,0:T(8,128)(2,1)S(1)} %add_add_fusion.1), channel_id=1, source_target_pairs={{0,2},{1,3},{8,10},{9,11},{18,20},{19,21},{26,28},{27,29},{36,38},... | collective-permute-start | bytes 688136 | tf_op jit(solution)/shard_map/ppermute | solution.py:584
  47.2 0.4 all-to-all-done.mine_hbm
  47.6 0.0 collective-permute-start.6
  47.6 0.0 copy-done.13
  47.6 0.1 fusion.4.tokens_ref
  47.7 0.0 copy-start.3
  47.7 0.0 copy-start.6
  47.7 0.0 copy-start.7
  47.7 0.0 copy-start.8
  47.7 0.0 copy-start.9
  47.7 5.7 %pair.3 = bf16[16,256,128]{2,1,0:T(8,128)(2,1)} custom-call(s32[4]{0:T(128)} %pad_add_fusion.place, bf16[256,128,128]{2,1,0:T(8,128)(2,1)} %pair_ref.3, bf16[128,512]{1,0:T(8,128)(2,1)} %up_ref.3, bf16[256,128]{1,0:T(8,128)(2,1)} %down_ref.3, bf16[20,128]{1,0:T(8,128)(2,1)} %bitcast.16, ...), custom_call_target="tpu_custom_call", output_to_operand_aliasing={{}: (6, {})} | custom-call | flops 2048000000 | bytes 1228800 | tf_op jit(solution)/shard_map/pair/pallas_call | solution.py:147
  53.4 0.0 collective-permute-done.6.theirs_hbm
  53.4 0.0 collective-permute-done.5
  53.4 0.0 collective-permute-done.4
  53.4 1.7 %collective-permute-done.3 = bf16[4,224,128]{2,1,0:T(8,128)(2,1)S(1)} collective-permute-done((bf16[4,224,128]{2,1,0:T(8,128)(2,1)S(1)}, bf16[4,224,128]{2,1,0:T(8,128)(2,1)S(1)}, u32[]{:S(2)}, u32[]{:S(2)}) %collective-permute-start.3) | collective-permute-done | bytes 229408 | tf_op jit(solution)/shard_map/ppermute | solution.py:584
  55.1 0.1 add_add_fusion.half_ref
  55.2 0.1 collective-permute-start.7
  55.3 6.4 %all-to-all-start.1 = ((bf16[16,256,128]{2,1,0:T(8,128)(2,1)}), bf16[16,256,128]{2,1,0:T(8,128)(2,1)S(1)}, u32[]{:S(2)}, u32[]{:S(2)}) async-start(bf16[16,256,128]{2,1,0:T(8,128)(2,1)} %pair.3), calls=%async_computation.1 | async-start | bytes 2097152 | tf_op jit(solution)/shard_map/all_to_all | solution.py:602
  61.7 0.0 collective-permute-done.7.other_ref
  61.7 0.0 copy-done.3
  61.7 0.0 copy-done.5
  61.7 0.0 copy-done.6
  61.7 0.0 copy-done.7
  61.7 0.0 copy-done.8
  61.7 0.0 copy-done.9
  61.7 11.5 %atoms.1 = (bf16[2048,128]{1,0:T(8,128)(2,1)}, bf16[256,768]{1,0:T(8,128)(2,1)S(1)}, f32[256,256]{1,0:T(8,128)S(1)}, bf16[8,96,256]{2,1,0:T(8,128)(2,1)}) custom-call(s32[4]{0:T(128)S(1)} %copy-done.3, s32[17,128]{1,0:T(8,128)S(1)} %fusion.4.tokens_ref, f32[1,128]{1,0:T(1,128)S(1)} %bitcast.13, bf16[128,512]{1,0:T(8,128)(2,1)S(1)} %copy-done.6, ...), custom_call_target="tpu_custom_call" | custom-call | flops 10000000000 | bytes 16777216 | tf_op jit(solution)/shard_map/atoms/pallas_call | solution.py:346
  73.2 0.0 copy-start.10
  73.2 0.7 copy-done.10
  73.9 0.0 copy-start
  73.9 0.0 copy-start.1
  73.9 0.0 copy-start.2
  73.9 0.0 copy-start.4
  73.9 5.0 %all-to-all-done.1.bias_hbm = bf16[16,256,128]{2,1,0:T(8,128)(2,1)S(1)} async-done(((bf16[16,256,128]{2,1,0:T(8,128)(2,1)}), bf16[16,256,128]{2,1,0:T(8,128)(2,1)S(1)}, u32[]{:S(2)}, u32[]{:S(2)}) %all-to-all-start.1) | async-done | bytes 1048608 | tf_op jit(solution)/shard_map/all_to_all | solution.py:602
  78.9 13.8 %all_to_all.20.kv_hbm = bf16[8,96,256]{2,1,0:T(8,128)(2,1)} all-to-all(bf16[8,96,256]{2,1,0:T(8,128)(2,1)} %get-tuple-element.50), channel_id=1, replica_groups=mesh['row'=8,'col'=16] {'row'}, dimensions={0} | all-to-all | bytes 786432 | tf_op jit(solution)/shard_map/all_to_all | solution.py:622
  92.7 0.0 copy-done.11
  92.7 4.7 %tokens.1 = bf16[8,48,256]{2,1,0:T(8,128)(2,1)} custom-call(s32[4]{0:T(128)} %pad_add_fusion.place, f32[16]{0:T(128)} %strength.1, s32[1,2048]{1,0:T(1,128)} %bitcast.17, f32[256,256]{1,0:T(8,128)} %copy-done.10, bf16[8,96,256]{2,1,0:T(8,128)(2,1)} %all_to_all.20.kv_hbm, bf16[16,256,128]{2,1,0:T(8,128)(2,1)} %copy-done.11), custom_call_target="tpu_custom_call" | custom-call | flops 1000000000 | bytes 4194304 | tf_op jit(solution)/shard_map/tokens/pallas_call | solution.py:425
  97.3 12.4 %all_to_all.21.mine_ref = bf16[8,48,256]{2,1,0:T(8,128)(2,1)S(1)} all-to-all(bf16[8,48,256]{2,1,0:T(8,128)(2,1)} %tokens.1), channel_id=1, replica_groups={{0,2,4,6,8,10,12,14},{1,3,5,7,9,11,13,15},{16,18,20,22,24,26,28,30},{17..., dimensions={0} | all-to-all | bytes 393216 | tf_op jit(solution)/shard_map/all_to_all | solution.py:624
  109.8 2.6 %collective-permute-start.8 = (bf16[8,48,256]{2,1,0:T(8,128)(2,1)S(1)}, bf16[8,48,256]{2,1,0:T(8,128)(2,1)S(1)}, u32[]{:S(2)}, u32[]{:S(2)}) collective-permute-start(bf16[8,48,256]{2,1,0:T(8,128)(2,1)S(1)} %all_to_all.21.mine_ref), channel_id=1, source_target_pairs={{0,1},{1,0},{2,3},{3,2},{4,5},{5,4},{6,7},{7,6},{8,9},{9,8},{10,11... | collective-permute-start | bytes 589832 | tf_op jit(solution)/shard_map/ppermute | solution.py:625
  112.3 0.1 subtract_bitcast_fusion.tokens_ref
  112.4 1.0 collective-permute-done.8.theirs_ref
  113.4 0.0 copy-done
  113.4 0.0 copy-done.1
  113.4 0.0 copy-done.2
  113.4 0.0 copy-done.4
  113.4 2.0 %updates.1 = (bf16[256,768]{1,0:T(8,128)(2,1)}, bf16[128,128]{1,0:T(8,128)(2,1)}) custom-call(s32[4]{0:T(128)S(1)} %copy-done.4, s32[1,128]{1,0:T(1,128)S(1)} %subtract_bitcast_fusion.tokens_ref, bf16[8,48,256]{2,1,0:T(8,128)(2,1)S(1)} %all_to_all.21.mine_ref, bf16[8,48,256]{2,1,0:T(8,128)(2,1)S(1)} %collective-permute-done.8.theirs_ref, ...), custom_call_target="tpu_custom_call" | custom-call | tf_op jit(solution)/shard_map/updates/pallas_call | solution.py:477
  (8 shorter events, 0.1 us)
Async XLA Ops:
  1.4 23.6 %collective-permute-start = (bf16[64,128]{1,0:T(8,128)(2,1)S(1)}, bf16[64,128]{1,0:T(8,128)(2,1)S(1)}, u32[]{:S(2)}, u32[]{:S(2)}) collective-permute-start(bf16[64,128]{1,0:T(8,128)(2,1)S(1)} %slice_select_fusion.1), channel_id=1, source_target_pairs={{15,18},{31,36},{47,54},{63,72},{79,90},{95,108},{111,126},{16,1},... | collective-permute-start | bytes 49160 | tf_op jit(solution)/shard_map/ppermute | solution.py:522
  3.4 30.2 %copy-start.12 = (bf16[128,128]{1,0:T(8,128)(2,1)S(1)}, bf16[128,128]{1,0:T(8,128)(2,1)}, u32[]{:S(2)}) copy-start(bf16[128,128]{1,0:T(8,128)(2,1)} %param.20) | copy-start | bytes 98308
  3.4 44.2 %copy-start.13 = (s32[16384]{0:T(1024)S(1)}, s32[16384]{0:T(1024)}, u32[]{:S(2)}) copy-start(s32[16384]{0:T(1024)} %param.21) | copy-start | bytes 196612
  27.2 12.8 %collective-permute-start.2 = (bf16[4,224,128]{2,1,0:T(8,128)(2,1)S(1)}, bf16[4,224,128]{2,1,0:T(8,128)(2,1)S(1)}, u32[]{:S(2)}, u32[]{:S(2)}) collective-permute-start(bf16[4,224,128]{2,1,0:T(8,128)(2,1)S(1)} %fusion.1), channel_id=1, source_target_pairs={{17,26},{35,44},{53,62},{71,64},{89,82},{107,100},{125,118},{2,9},... | collective-permute-start | bytes 688136 | tf_op jit(solution)/shard_map/ppermute | solution.py:574
  27.9 12.1 %collective-permute-start.1 = (bf16[4,224,128]{2,1,0:T(8,128)(2,1)S(1)}, bf16[4,224,128]{2,1,0:T(8,128)(2,1)S(1)}, u32[]{:S(2)}, u32[]{:S(2)}) collective-permute-start(bf16[4,224,128]{2,1,0:T(8,128)(2,1)S(1)} %fusion.1), channel_id=1, source_target_pairs={{0,8},{1,9},{18,26},{19,27},{36,44},{37,45},{54,62},{55,63},{72,64... | collective-permute-start | bytes 688136 | tf_op jit(solution)/shard_map/ppermute | solution.py:573
  34.3 13.3 %all-to-all-start = ((bf16[8,128,128]{2,1,0:T(8,128)(2,1)}), bf16[8,128,128]{2,1,0:T(8,128)(2,1)S(1)}, u32[]{:S(2)}, u32[]{:S(2)}) async-start(bf16[8,128,128]{2,1,0:T(8,128)(2,1)} %broadcast_in_dim.21), calls=%async_computation | async-start | bytes 524288 | tf_op jit(solution)/shard_map/all_to_all | solution.py:578
  40.0 13.4 %collective-permute-start.5 = (bf16[4,224,128]{2,1,0:T(8,128)(2,1)S(1)}, bf16[4,224,128]{2,1,0:T(8,128)(2,1)S(1)}, u32[]{:S(2)}, u32[]{:S(2)}) collective-permute-start(bf16[4,224,128]{2,1,0:T(8,128)(2,1)S(1)} %add_add_fusion.1), channel_id=1, source_target_pairs={{0,6},{1,7},{8,14},{9,15},{18,16},{19,17},{26,24},{27,25},{36,34},... | collective-permute-start | bytes 688136 | tf_op jit(solution)/shard_map/ppermute | solution.py:584
  44.6 8.8 %collective-permute-start.4 = (bf16[4,224,128]{2,1,0:T(8,128)(2,1)S(1)}, bf16[4,224,128]{2,1,0:T(8,128)(2,1)S(1)}, u32[]{:S(2)}, u32[]{:S(2)}) collective-permute-start(bf16[4,224,128]{2,1,0:T(8,128)(2,1)S(1)} %add_add_fusion.1), channel_id=1, source_target_pairs={{0,4},{1,5},{8,12},{9,13},{18,22},{19,23},{26,30},{27,31},{36,32},... | collective-permute-start | bytes 688136 | tf_op jit(solution)/shard_map/ppermute | solution.py:584
  45.9 9.2 %collective-permute-start.3 = (bf16[4,224,128]{2,1,0:T(8,128)(2,1)S(1)}, bf16[4,224,128]{2,1,0:T(8,128)(2,1)S(1)}, u32[]{:S(2)}, u32[]{:S(2)}) collective-permute-start(bf16[4,224,128]{2,1,0:T(8,128)(2,1)S(1)} %add_add_fusion.1), channel_id=1, source_target_pairs={{0,2},{1,3},{8,10},{9,11},{18,20},{19,21},{26,28},{27,29},{36,38},... | collective-permute-start | bytes 688136 | tf_op jit(solution)/shard_map/ppermute | solution.py:584
  47.6 5.8 %collective-permute-start.6 = (bf16[8,128,128]{2,1,0:T(8,128)(2,1)S(1)}, bf16[8,128,128]{2,1,0:T(8,128)(2,1)S(1)}, u32[]{:S(2)}, u32[]{:S(2)}) collective-permute-start(bf16[8,128,128]{2,1,0:T(8,128)(2,1)S(1)} %all-to-all-done.mine_hbm), channel_id=1, source_target_pairs={{0,1},{1,0},{2,3},{3,2},{4,5},{5,4},{6,7},{7,6},{8,9},{9,8},{10,11... | collective-permute-start | bytes 786440 | tf_op jit(solution)/shard_map/ppermute | solution.py:599
  47.7 14.0 %copy-start.3 = (s32[4]{0:T(128)S(1)}, s32[4]{0:T(128)}, u32[]{:S(2)}) copy-start(s32[4]{0:T(128)} %pad_add_fusion.place) | copy-start | bytes 52
  47.7 14.0 %copy-start.5 = (bf16[128,768]{1,0:T(8,128)(2,1)S(1)}, bf16[128,768]{1,0:T(8,128)(2,1)}, u32[]{:S(2)}) copy-start(bf16[128,768]{1,0:T(8,128)(2,1)} %pool_ref.1) | copy-start | bytes 589828
  47.7 14.0 %copy-start.6 = (bf16[128,512]{1,0:T(8,128)(2,1)S(1)}, bf16[128,512]{1,0:T(8,128)(2,1)}, u32[]{:S(2)}) copy-start(bf16[128,512]{1,0:T(8,128)(2,1)} %proj_ref.1) | copy-start | bytes 393220
  47.7 14.0 %copy-start.7 = (bf16[128,128]{1,0:T(8,128)(2,1)S(1)}, bf16[128,128]{1,0:T(8,128)(2,1)}, u32[]{:S(2)}) copy-start(bf16[128,128]{1,0:T(8,128)(2,1)} %exit_ref.2) | copy-start | bytes 98308
  47.7 14.0 %copy-start.8 = (f32[768]{0:T(1024)S(1)}, f32[768]{0:T(1024)}, u32[]{:S(2)}) copy-start(f32[768]{0:T(1024)} %param.30) | copy-start | bytes 9220
  47.7 14.0 %copy-start.9 = (f32[128]{0:T(128)S(1)}, f32[128]{0:T(128)}, u32[]{:S(2)}) copy-start(f32[128]{0:T(128)} %param.26) | copy-start | bytes 1540
  55.2 6.5 %collective-permute-start.7 = (bf16[4,224,128]{2,1,0:T(8,128)(2,1)S(1)}, bf16[4,224,128]{2,1,0:T(8,128)(2,1)S(1)}, u32[]{:S(2)}, u32[]{:S(2)}) collective-permute-start(bf16[4,224,128]{2,1,0:T(8,128)(2,1)S(1)} %add_add_fusion.half_ref), channel_id=1, source_target_pairs={{0,1},{1,0},{2,3},{3,2},{4,5},{5,4},{6,7},{7,6},{8,9},{9,8},{10,11... | collective-permute-start | bytes 688136 | tf_op jit(solution)/shard_map/ppermute | solution.py:605
  55.3 23.6 %all-to-all-start.1 = ((bf16[16,256,128]{2,1,0:T(8,128)(2,1)}), bf16[16,256,128]{2,1,0:T(8,128)(2,1)S(1)}, u32[]{:S(2)}, u32[]{:S(2)}) async-start(bf16[16,256,128]{2,1,0:T(8,128)(2,1)} %pair.3), calls=%async_computation.1 | async-start | bytes 2097152 | tf_op jit(solution)/shard_map/all_to_all | solution.py:602
  73.2 0.7 copy-start.10
  73.9 39.5 %copy-start = (bf16[768,768]{1,0:T(8,128)(2,1)S(1)}, bf16[768,768]{1,0:T(8,128)(2,1)}, u32[]{:S(2)}) copy-start(bf16[768,768]{1,0:T(8,128)(2,1)} %exit_ref.3) | copy-start | bytes 3538948
  73.9 39.5 %copy-start.1 = (bf16[2048,128]{1,0:T(8,128)(2,1)S(1)}, bf16[2048,128]{1,0:T(8,128)(2,1)}, u32[]{:S(2)}) copy-start(bf16[2048,128]{1,0:T(8,128)(2,1)} %get-tuple-element.53.mid_ref) | copy-start | bytes 1572868
  73.9 39.5 %copy-start.2 = (bf16[768,128]{1,0:T(8,128)(2,1)S(1)}, bf16[768,128]{1,0:T(8,128)(2,1)}, u32[]{:S(2)}) copy-start(bf16[768,128]{1,0:T(8,128)(2,1)} %back_ref.1) | copy-start | bytes 589828
  73.9 39.5 %copy-start.4 = (s32[4]{0:T(128)S(1)}, s32[4]{0:T(128)}, u32[]{:S(2)}) copy-start(s32[4]{0:T(128)} %pad_add_fusion.place) | copy-start | bytes 52
  78.9 13.8 %copy-start.11 = (bf16[16,256,128]{2,1,0:T(8,128)(2,1)}, bf16[16,256,128]{2,1,0:T(8,128)(2,1)S(1)}, u32[]{:S(2)}) copy-start(bf16[16,256,128]{2,1,0:T(8,128)(2,1)S(1)} %all-to-all-done.1.bias_hbm) | copy-start | bytes 3145732
  109.8 3.6 %collective-permute-start.8 = (bf16[8,48,256]{2,1,0:T(8,128)(2,1)S(1)}, bf16[8,48,256]{2,1,0:T(8,128)(2,1)S(1)}, u32[]{:S(2)}, u32[]{:S(2)}) collective-permute-start(bf16[8,48,256]{2,1,0:T(8,128)(2,1)S(1)} %all_to_all.21.mine_ref), channel_id=1, source_target_pairs={{0,1},{1,0},{2,3},{3,2},{4,5},{5,4},{6,7},{7,6},{8,9},{9,8},{10,11... | collective-permute-start | bytes 589832 | tf_op jit(solution)/shard_map/ppermute | solution.py:625
